TPU v7x, 32 devices: a whole 2x2x4 slice. The times are simulated.
32 devices in a mesh: seq: 8 (over z, core), utt: 4 (over y, x).
Axes of the slice: x: 2, y: 2, z: 4, core: 2. Of those that a mesh axis runs over, the one named last changes fastest.
Arguments:
- feats: bfloat16 [4, 2048, 512], P('utt', 'seq'), may hold values from -6 to 6
- mask_starts: int32 [4, 85], P('utt'), may hold values from 0 to 1014, as said below
- grad_out: bfloat16 [4, 1024, 1024], P('utt', 'seq'), may hold values from -6 to 6
- conv_weight: bfloat16 [1024, 512], P('utt'), may hold values from -0.1875 to 0.1875
- conv_gain: float32 [512], P('utt'), may hold values from 0.5 to 1.5
- conv_shift: float32 [512], P('utt'), may hold values from -1.75 to 1.75
- norm_gain: float32 [512], P('utt'), may hold values from 0.5 to 1.5
- norm_shift: float32 [512], P('utt'), may hold values from -1.75 to 1.75
- proj_weight: bfloat16 [512, 1024], P('utt'), may hold values from -0.25 to 0.25
- proj_bias: float32 [1024], P('utt'), may hold values from -1.75 to 1.75
- mask_embed: float32 [1024], P('utt'), may hold values from -6 to 6
- pos_weight: bfloat16 [128, 64, 1024], P(None, None, 'utt'), may hold values from -0.0625 to 0.0625
- pos_bias: float32 [1024], P('utt'), may hold values from -1.75 to 1.75
- attn_gain: float32 [1024], P('utt'), may hold values from 0.5 to 1.5
- attn_shift: float32 [1024], P('utt'), may hold values from -1.75 to 1.75
- qkv_weight: bfloat16 [1024, 3072], P('utt'), may hold values from -0.1875 to 0.1875
- query_bias: float32 [1024], P('utt'), may hold values from -1.75 to 1.75
- value_bias: float32 [1024], P('utt'), may hold values from -1.75 to 1.75
- out_weight: bfloat16 [1024, 1024], P('utt'), may hold values from -0.5 to 0.5
- out_bias: float32 [1024], P('utt'), may hold values from -1.75 to 1.75
- ffn_gain: float32 [1024], P('utt'), may hold values from 0.5 to 1.5
- ffn_shift: float32 [1024], P('utt'), may hold values from -1.75 to 1.75
- up_weight: bfloat16 [1024, 4096], P('utt'), may hold values from -0.1875 to 0.1875
- up_bias: float32 [4096], P('utt'), may hold values from -1.75 to 1.75
- down_weight: bfloat16 [4096, 1024], P('utt'), may hold values from -0.09375 to 0.09375
- down_bias: float32 [1024], P('utt'), may hold values from -1.75 to 1.75
Outputs:
- layer_out: bfloat16 [4, 1024, 1024], P('utt', 'seq')
- feat_grad: bfloat16 [4, 2048, 512], P('utt', 'seq')
- convweight_grad: float32 [1024, 512], P('utt')
- convgain_grad: float32 [512], P('utt')
- convshift_grad: float32 [512], P('utt')
- normgain_grad: float32 [512], P('utt')
- normshift_grad: float32 [512], P('utt')
- projweight_grad: float32 [512, 1024], P('utt')
- projbias_grad: float32 [1024], P('utt')
- maskembed_grad: float32 [1024], P('utt')
- posweight_grad: float32 [128, 64, 1024], P(None, None, 'utt')
- posbias_grad: float32 [1024], P('utt')
- attngain_grad: float32 [1024], P('utt')
- attnshift_grad: float32 [1024], P('utt')
- qkvweight_grad: float32 [1024, 3072], P('utt')
- querybias_grad: float32 [1024], P('utt')
- valuebias_grad: float32 [1024], P('utt')
- outweight_grad: float32 [1024, 1024], P('utt')
- outbias_grad: float32 [1024], P('utt')
- ffngain_grad: float32 [1024], P('utt')
- ffnshift_grad: float32 [1024], P('utt')
- upweight_grad: float32 [1024, 4096], P('utt')
- upbias_grad: float32 [4096], P('utt')
- downweight_grad: float32 [4096, 1024], P('utt')
- downbias_grad: float32 [1024], P('utt')
Inputs may be any that keep to these rules, and one draw needn't show every extreme that they name: `mask_starts`: start frames of 85 mask spans of each utterance; a start may repeat; every span ends inside its utterance; the number of distinct spans may differ between utterances.
All inputs are finite; a program needn't handle non-finite values.
Results may differ from a plain program's by a relative error of at most 0.024.
Values may be sent and summed in bfloat16 or wider, within the bound.
A program may use at most 320 MiB of HBM per device.

v0:
```python
import jax
import jax.numpy as jnp
from jax import lax
from jax.sharding import PartitionSpec as P

D = 1024
H = 16
HEAD_DIM = 64
C = 512
KPOS = 128
G = 16
GW = 64
SPAN = 10


EPS = 1e-05


def padded_2(cells, sides, width):
    for axis, dim in sides:
        count = lax.axis_size(axis)
        ends = count - 1
        head = lax.slice_in_dim(cells, 0, width, axis=dim)
        tail = lax.slice_in_dim(cells, cells.shape[dim] - width, cells.shape[dim], axis=dim)
        cells = jnp.concatenate(
            [
                lax.ppermute(tail, axis, [(i, (i + 1) % count) for i in range(ends)]),
                cells,
                lax.ppermute(head, axis, [((i + 1) % count, i) for i in range(ends)]),
            ],
            axis=dim,
        )
    return cells


def layer_norm(values, gain, shift):
    center = values - jnp.mean(values, -1, keepdims=True)
    spread = jnp.mean(center * center, -1, keepdims=True)
    return center * lax.rsqrt(spread + EPS) * gain + shift


def gelu_exact(values):
    return jax.nn.gelu(values, approximate=False)


def front_norms(conv_pre, conv_gain, conv_shift, norm_gain, norm_shift):
    return layer_norm(
        gelu_exact(layer_norm(conv_pre, conv_gain, conv_shift)), norm_gain, norm_shift
    )


def inner_dot(first_mat, second_mat):
    return lax.dot_general(
        first_mat, second_mat, (((0,), (0,)), ((), ())), preferred_element_type=jnp.float32
    )


def back_dot(values, weight):
    return lax.dot_general(
        values, weight, (((1,), (1,)), ((), ())), preferred_element_type=jnp.float32
    )


def block_rows(length):
    chosen = 1
    for option in range(1, min(512, length) + 1):
        if length % option == 0:
            chosen = option
    return chosen


def empty_state(num_utts, row_count, heads):
    return (
        jnp.full((num_utts, heads, row_count), -1e30, jnp.float32),
        jnp.zeros((num_utts, heads, row_count), jnp.float32),
        jnp.zeros((num_utts, row_count, heads, HEAD_DIM), jnp.float32),
    )


def attend_forward(queries, key_rows, value_rows, soft_state, heads, score_scale):
    q_heads = queries.reshape(queries.shape[0], queries.shape[1], heads, HEAD_DIM)
    length = key_rows.shape[1]
    step_len = block_rows(length)

    def absorb(block_id, running_state):
        running, totals, accumulated = running_state
        k_block = lax.dynamic_slice_in_dim(key_rows, block_id * step_len, step_len, 1)
        v_block = lax.dynamic_slice_in_dim(value_rows, block_id * step_len, step_len, 1)
        k_block = k_block.reshape(k_block.shape[0], step_len, heads, HEAD_DIM)
        v_block = v_block.reshape(v_block.shape[0], step_len, heads, HEAD_DIM)
        scores = (
            jnp.einsum("uqhe,ukhe->uhqk", q_heads, k_block, preferred_element_type=jnp.float32)
            * score_scale
        )
        highest = jnp.maximum(running, jnp.max(scores, -1))
        shrink = jnp.exp(running - highest)
        weights = jnp.exp(scores - highest[..., None])
        totals = totals * shrink + jnp.sum(weights, -1)
        accumulated = accumulated * jnp.transpose(shrink, (0, 2, 1))[..., None] + jnp.einsum(
            "uhqk,ukhe->uqhe",
            weights.astype(jnp.bfloat16),
            v_block,
            preferred_element_type=jnp.float32,
        )
        return (highest, totals, accumulated)

    return lax.fori_loop(0, length // step_len, absorb, soft_state)


def finish_softmax(soft_state):
    running, totals, accumulated = soft_state
    log_total = running + jnp.log(totals)
    output = accumulated / jnp.transpose(totals, (0, 2, 1))[..., None]
    return (log_total, output.reshape(output.shape[0], output.shape[1], -1))


def row_inner(out_grad, output, heads):
    product = (out_grad.astype(jnp.float32) * output).reshape(
        output.shape[0], output.shape[1], heads, HEAD_DIM
    )
    return jnp.transpose(jnp.sum(product, -1), (0, 2, 1))


def attend_backward(
    queries, key_rows, value_rows, out_grad, log_total, inner_sums, heads, score_scale
):
    q_heads = queries.reshape(queries.shape[0], queries.shape[1], heads, HEAD_DIM)
    g_heads = out_grad.reshape(out_grad.shape[0], out_grad.shape[1], heads, HEAD_DIM)
    length = key_rows.shape[1]
    step_len = block_rows(length)

    def absorb(block_id, running_state):
        query_grad, key_grad, value_grad = running_state
        first_row = block_id * step_len
        k_block = lax.dynamic_slice_in_dim(key_rows, first_row, step_len, 1)
        v_block = lax.dynamic_slice_in_dim(value_rows, first_row, step_len, 1)
        k_block = k_block.reshape(k_block.shape[0], step_len, heads, HEAD_DIM)
        v_block = v_block.reshape(v_block.shape[0], step_len, heads, HEAD_DIM)
        scores = (
            jnp.einsum("uqhe,ukhe->uhqk", q_heads, k_block, preferred_element_type=jnp.float32)
            * score_scale
        )
        softmax_rows = jnp.exp(scores - log_total[..., None])
        value_part = jnp.einsum(
            "uhqk,uqhe->ukhe",
            softmax_rows.astype(jnp.bfloat16),
            g_heads,
            preferred_element_type=jnp.float32,
        )
        prob_grad = jnp.einsum(
            "uqhe,ukhe->uhqk", g_heads, v_block, preferred_element_type=jnp.float32
        )
        score_grad = (softmax_rows * (prob_grad - inner_sums[..., None])).astype(jnp.bfloat16)
        query_grad = (
            query_grad
            + jnp.einsum("uhqk,ukhe->uqhe", score_grad, k_block, preferred_element_type=jnp.float32)
            * score_scale
        )
        key_part = (
            jnp.einsum("uhqk,uqhe->ukhe", score_grad, q_heads, preferred_element_type=jnp.float32)
            * score_scale
        )
        key_grad = lax.dynamic_update_slice_in_dim(
            key_grad, key_part.reshape(key_part.shape[0], step_len, -1), first_row, 1
        )
        value_grad = lax.dynamic_update_slice_in_dim(
            value_grad, value_part.reshape(value_part.shape[0], step_len, -1), first_row, 1
        )
        return (query_grad, key_grad, value_grad)

    start_state = (
        jnp.zeros(q_heads.shape, jnp.float32),
        jnp.zeros(key_rows.shape, jnp.float32),
        jnp.zeros(value_rows.shape, jnp.float32),
    )
    query_grad, key_grad, value_grad = lax.fori_loop(0, length // step_len, absorb, start_state)
    return (query_grad.reshape(queries.shape), key_grad, value_grad)


def tap_conv(padded, tap_weights, row_count):
    num_utts = padded.shape[0]
    group_taps = 8

    def absorb(block_id, accumulated):
        columns = jnp.stack(
            [
                lax.dynamic_slice_in_dim(padded, block_id * group_taps + offset, row_count, 1)
                for offset in range(group_taps)
            ],
            axis=2,
        )
        columns = columns.reshape(num_utts, row_count, group_taps, G, GW)
        weight = lax.dynamic_slice_in_dim(tap_weights, block_id * group_taps, group_taps, 0)
        return accumulated + jnp.einsum(
            "utjgi,jigo->utgo", columns, weight, preferred_element_type=jnp.float32
        )

    accumulated = lax.fori_loop(
        0, KPOS // group_taps, absorb, jnp.zeros((num_utts, row_count, G, GW), jnp.float32)
    )
    return accumulated.reshape(num_utts * row_count, G * GW)


def tap_grad(padded, grad_rows):
    num_utts, row_count = (grad_rows.shape[0], grad_rows.shape[1])
    group_taps = 8
    grad_groups = grad_rows.reshape(num_utts, row_count, G, GW)

    def absorb(block_id, summed):
        columns = jnp.stack(
            [
                lax.dynamic_slice_in_dim(padded, block_id * group_taps + offset, row_count, 1)
                for offset in range(group_taps)
            ],
            axis=2,
        )
        columns = columns.reshape(num_utts, row_count, group_taps, G, GW)
        partial_value = jnp.einsum(
            "utjgi,utgo->jigo", columns, grad_groups, preferred_element_type=jnp.float32
        )
        return lax.dynamic_update_slice_in_dim(summed, partial_value, block_id * group_taps, 0)

    summed = lax.fori_loop(0, KPOS // group_taps, absorb, jnp.zeros((KPOS, GW, G, GW), jnp.float32))
    return summed.reshape(KPOS, GW, G * GW)


def shards(
    feats,
    mask_starts,
    grad_out,
    conv_weight,
    conv_gain,
    conv_shift,
    norm_gain,
    norm_shift,
    proj_weight,
    proj_bias,
    mask_embed,
    pos_weight,
    pos_bias,
    attn_gain,
    attn_shift,
    qkv_weight,
    query_bias,
    value_bias,
    out_weight,
    out_bias,
    ffn_gain,
    ffn_shift,
    up_weight,
    up_bias,
    down_weight,
    down_bias,
):
    conv_weight, proj_weight, pos_weight, qkv_weight, out_weight, up_weight, down_weight = (
        lax.all_gather(conv_weight, "utt", axis=0, tiled=True),
        lax.all_gather(proj_weight, "utt", axis=0, tiled=True),
        lax.all_gather(pos_weight, "utt", axis=2, tiled=True),
        lax.all_gather(qkv_weight, "utt", axis=0, tiled=True),
        lax.all_gather(out_weight, "utt", axis=0, tiled=True),
        lax.all_gather(up_weight, "utt", axis=0, tiled=True),
        lax.all_gather(down_weight, "utt", axis=0, tiled=True),
    )
    (
        conv_gain,
        conv_shift,
        norm_gain,
        norm_shift,
        proj_bias,
        mask_embed,
        pos_bias,
        attn_gain,
        attn_shift,
        query_bias,
        value_bias,
        out_bias,
        ffn_gain,
        ffn_shift,
        up_bias,
        down_bias,
    ) = (
        lax.all_gather(conv_gain, "utt", axis=0, tiled=True),
        lax.all_gather(conv_shift, "utt", axis=0, tiled=True),
        lax.all_gather(norm_gain, "utt", axis=0, tiled=True),
        lax.all_gather(norm_shift, "utt", axis=0, tiled=True),
        lax.all_gather(proj_bias, "utt", axis=0, tiled=True),
        lax.all_gather(mask_embed, "utt", axis=0, tiled=True),
        lax.all_gather(pos_bias, "utt", axis=0, tiled=True),
        lax.all_gather(attn_gain, "utt", axis=0, tiled=True),
        lax.all_gather(attn_shift, "utt", axis=0, tiled=True),
        lax.all_gather(query_bias, "utt", axis=0, tiled=True),
        lax.all_gather(value_bias, "utt", axis=0, tiled=True),
        lax.all_gather(out_bias, "utt", axis=0, tiled=True),
        lax.all_gather(ffn_gain, "utt", axis=0, tiled=True),
        lax.all_gather(ffn_shift, "utt", axis=0, tiled=True),
        lax.all_gather(up_bias, "utt", axis=0, tiled=True),
        lax.all_gather(down_bias, "utt", axis=0, tiled=True),
    )
    num_utts = feats.shape[0]
    frames = grad_out.shape[1]
    row_count = num_utts * frames
    score_scale = HEAD_DIM ** (-0.5)
    steps_in = feats.reshape(row_count, 2 * C)
    conv_pre = jnp.dot(steps_in, conv_weight, preferred_element_type=jnp.float32)
    feat_norm, front_pull = jax.vjp(
        front_norms, conv_pre, conv_gain, conv_shift, norm_gain, norm_shift
    )
    feat_low = feat_norm.astype(jnp.bfloat16)
    proj_out = jnp.dot(feat_low, proj_weight, preferred_element_type=jnp.float32) + proj_bias
    frame_pos = lax.axis_index("seq") * frames + jnp.arange(frames, dtype=jnp.int32)
    inside = (frame_pos[None, :, None] >= mask_starts[:, None, :]) & (
        frame_pos[None, :, None] < mask_starts[:, None, :] + SPAN
    )
    masked = jnp.any(inside, -1).reshape(row_count, 1)
    embed = jnp.where(masked, mask_embed[None, :], proj_out)
    embed_low = embed.astype(jnp.bfloat16).reshape(num_utts, frames, D)
    embed_rim = padded_2(embed_low, (("seq", 1),), KPOS // 2)
    tap_weights = pos_weight.reshape(KPOS, GW, G, GW)
    pos_pre = tap_conv(embed_rim, tap_weights, frames) + pos_bias
    pos_act, pos_pull = jax.vjp(gelu_exact, pos_pre)
    resid_one = embed + pos_act
    attn_norm, attn_pull = jax.vjp(layer_norm, resid_one, attn_gain, attn_shift)
    attn_in = attn_norm.astype(jnp.bfloat16)
    projected = jnp.dot(attn_in, qkv_weight, preferred_element_type=jnp.float32)
    queries = (projected[:, :D] + query_bias).astype(jnp.bfloat16).reshape(num_utts, frames, D)
    key_rows = projected[:, D : 2 * D].astype(jnp.bfloat16).reshape(num_utts, frames, D)
    value_rows = (
        (projected[:, 2 * D :] + value_bias).astype(jnp.bfloat16).reshape(num_utts, frames, D)
    )
    soft_state = attend_forward(
        queries,
        lax.all_gather(key_rows, "seq", axis=1, tiled=True),
        lax.all_gather(value_rows, "seq", axis=1, tiled=True),
        empty_state(num_utts, frames, H),
        H,
        score_scale,
    )
    log_total, attn_f32 = finish_softmax(soft_state)
    attn_rows = attn_f32.astype(jnp.bfloat16)
    attn_flat = attn_rows.reshape(row_count, D)
    resid_two = (
        resid_one + jnp.dot(attn_flat, out_weight, preferred_element_type=jnp.float32) + out_bias
    )
    ffn_norm, ffn_pull = jax.vjp(layer_norm, resid_two, ffn_gain, ffn_shift)
    ffn_in = ffn_norm.astype(jnp.bfloat16)
    hidden_pre = jnp.dot(ffn_in, up_weight, preferred_element_type=jnp.float32) + up_bias
    hidden_act, hidden_pull = jax.vjp(gelu_exact, hidden_pre)
    hidden_low = hidden_act.astype(jnp.bfloat16)
    layer_value = (
        resid_two + jnp.dot(hidden_low, down_weight, preferred_element_type=jnp.float32) + down_bias
    )
    layer_out = layer_value.astype(jnp.bfloat16).reshape(num_utts, frames, D)
    out_rows = grad_out.reshape(row_count, D)
    downweight_grad = inner_dot(hidden_low, out_rows)
    downbias_grad = jnp.sum(out_rows, 0, dtype=jnp.float32)
    (hidden_grad,) = hidden_pull(back_dot(out_rows, down_weight))
    hidden_grad = hidden_grad.astype(jnp.bfloat16)
    upweight_grad = inner_dot(ffn_in, hidden_grad)
    upbias_grad = jnp.sum(hidden_grad, 0, dtype=jnp.float32)
    ffn_back, ffngain_grad, ffnshift_grad = ffn_pull(back_dot(hidden_grad, up_weight))
    resid2_grad = out_rows.astype(jnp.float32) + ffn_back
    attn_grad = resid2_grad.astype(jnp.bfloat16)
    outweight_grad = inner_dot(attn_flat, attn_grad)
    outbias_grad = jnp.sum(attn_grad, 0, dtype=jnp.float32)
    out_grad = back_dot(attn_grad, out_weight).astype(jnp.bfloat16).reshape(num_utts, frames, D)
    inner_sums = row_inner(out_grad, attn_f32, H)
    all_keys, all_values = (
        lax.all_gather(key_rows, "seq", axis=1, tiled=True),
        lax.all_gather(value_rows, "seq", axis=1, tiled=True),
    )
    query_grad, key_part, value_part = attend_backward(
        queries, all_keys, all_values, out_grad, log_total, inner_sums, H, score_scale
    )
    key_grad, value_grad = (
        lax.psum_scatter(
            key_part.astype(jnp.bfloat16), "seq", scatter_dimension=1, tiled=True
        ).astype(jnp.float32),
        lax.psum_scatter(
            value_part.astype(jnp.bfloat16), "seq", scatter_dimension=1, tiled=True
        ).astype(jnp.float32),
    )
    query_low = query_grad.astype(jnp.bfloat16)
    key_low = key_grad.astype(jnp.bfloat16)
    value_low = value_grad.astype(jnp.bfloat16)
    qkv_grad = jnp.concatenate(
        [
            query_low.reshape(row_count, D),
            key_low.reshape(row_count, D),
            value_low.reshape(row_count, D),
        ],
        axis=1,
    )
    qkvweight_grad = inner_dot(attn_in, qkv_grad)
    querybias_grad = jnp.sum(qkv_grad[:, :D], 0, dtype=jnp.float32)
    valuebias_grad = jnp.sum(qkv_grad[:, 2 * D :], 0, dtype=jnp.float32)
    attn_back, attngain_grad, attnshift_grad = attn_pull(back_dot(qkv_grad, qkv_weight))
    resid1_grad = resid2_grad + attn_back
    (pos_grad,) = pos_pull(resid1_grad)
    pos_low = pos_grad.astype(jnp.bfloat16)
    posbias_grad = jnp.sum(pos_low, 0, dtype=jnp.float32)
    pos_rows = pos_low.reshape(num_utts, frames, D)
    posweight_grad = tap_grad(embed_rim, pos_rows)
    grad_rim = padded_2(pos_rows, (("seq", 1),), KPOS // 2)
    flipped = jnp.flip(jnp.transpose(tap_weights, (0, 3, 2, 1)), 0)
    embed_grad = resid1_grad + tap_conv(grad_rim[:, 1:], flipped, frames)
    maskembed_grad = jnp.sum(jnp.where(masked, embed_grad, 0.0), 0)
    proj_grad = jnp.where(masked, 0.0, embed_grad).astype(jnp.bfloat16)
    projbias_grad = jnp.sum(proj_grad, 0, dtype=jnp.float32)
    projweight_grad = inner_dot(feat_low, proj_grad)
    conv_back, convgain_grad, convshift_grad, normgain_grad, normshift_grad = front_pull(
        back_dot(proj_grad, proj_weight)
    )
    conv_grad = conv_back.astype(jnp.bfloat16)
    convweight_grad = inner_dot(steps_in, conv_grad)
    feat_grad = (
        back_dot(conv_grad, conv_weight).astype(jnp.bfloat16).reshape(num_utts, 2 * frames, C)
    )
    shares = (
        lax.psum_scatter(
            convweight_grad.astype(jnp.bfloat16), "utt", scatter_dimension=0, tiled=True
        ).astype(jnp.float32),
        lax.psum_scatter(
            convgain_grad.astype(jnp.bfloat16), "utt", scatter_dimension=0, tiled=True
        ).astype(jnp.float32),
        lax.psum_scatter(
            convshift_grad.astype(jnp.bfloat16), "utt", scatter_dimension=0, tiled=True
        ).astype(jnp.float32),
        lax.psum_scatter(
            normgain_grad.astype(jnp.bfloat16), "utt", scatter_dimension=0, tiled=True
        ).astype(jnp.float32),
        lax.psum_scatter(
            normshift_grad.astype(jnp.bfloat16), "utt", scatter_dimension=0, tiled=True
        ).astype(jnp.float32),
        lax.psum_scatter(
            projweight_grad.astype(jnp.bfloat16), "utt", scatter_dimension=0, tiled=True
        ).astype(jnp.float32),
        lax.psum_scatter(
            projbias_grad.astype(jnp.bfloat16), "utt", scatter_dimension=0, tiled=True
        ).astype(jnp.float32),
        lax.psum_scatter(
            maskembed_grad.astype(jnp.bfloat16), "utt", scatter_dimension=0, tiled=True
        ).astype(jnp.float32),
        lax.psum_scatter(
            posweight_grad.astype(jnp.bfloat16), "utt", scatter_dimension=2, tiled=True
        ).astype(jnp.float32),
        lax.psum_scatter(
            posbias_grad.astype(jnp.bfloat16), "utt", scatter_dimension=0, tiled=True
        ).astype(jnp.float32),
        lax.psum_scatter(
            attngain_grad.astype(jnp.bfloat16), "utt", scatter_dimension=0, tiled=True
        ).astype(jnp.float32),
        lax.psum_scatter(
            attnshift_grad.astype(jnp.bfloat16), "utt", scatter_dimension=0, tiled=True
        ).astype(jnp.float32),
        lax.psum_scatter(
            qkvweight_grad.astype(jnp.bfloat16), "utt", scatter_dimension=0, tiled=True
        ).astype(jnp.float32),
        lax.psum_scatter(
            querybias_grad.astype(jnp.bfloat16), "utt", scatter_dimension=0, tiled=True
        ).astype(jnp.float32),
        lax.psum_scatter(
            valuebias_grad.astype(jnp.bfloat16), "utt", scatter_dimension=0, tiled=True
        ).astype(jnp.float32),
        lax.psum_scatter(
            outweight_grad.astype(jnp.bfloat16), "utt", scatter_dimension=0, tiled=True
        ).astype(jnp.float32),
        lax.psum_scatter(
            outbias_grad.astype(jnp.bfloat16), "utt", scatter_dimension=0, tiled=True
        ).astype(jnp.float32),
        lax.psum_scatter(
            ffngain_grad.astype(jnp.bfloat16), "utt", scatter_dimension=0, tiled=True
        ).astype(jnp.float32),
        lax.psum_scatter(
            ffnshift_grad.astype(jnp.bfloat16), "utt", scatter_dimension=0, tiled=True
        ).astype(jnp.float32),
        lax.psum_scatter(
            upweight_grad.astype(jnp.bfloat16), "utt", scatter_dimension=0, tiled=True
        ).astype(jnp.float32),
        lax.psum_scatter(
            upbias_grad.astype(jnp.bfloat16), "utt", scatter_dimension=0, tiled=True
        ).astype(jnp.float32),
        lax.psum_scatter(
            downweight_grad.astype(jnp.bfloat16), "utt", scatter_dimension=0, tiled=True
        ).astype(jnp.float32),
        lax.psum_scatter(
            downbias_grad.astype(jnp.bfloat16), "utt", scatter_dimension=0, tiled=True
        ).astype(jnp.float32),
    )
    totals = (
        lax.psum(shares[0].astype(jnp.bfloat16), "seq").astype(jnp.float32),
        lax.psum(shares[1].astype(jnp.bfloat16), "seq").astype(jnp.float32),
        lax.psum(shares[2].astype(jnp.bfloat16), "seq").astype(jnp.float32),
        lax.psum(shares[3].astype(jnp.bfloat16), "seq").astype(jnp.float32),
        lax.psum(shares[4].astype(jnp.bfloat16), "seq").astype(jnp.float32),
        lax.psum(shares[5].astype(jnp.bfloat16), "seq").astype(jnp.float32),
        lax.psum(shares[6].astype(jnp.bfloat16), "seq").astype(jnp.float32),
        lax.psum(shares[7].astype(jnp.bfloat16), "seq").astype(jnp.float32),
        lax.psum(shares[8].astype(jnp.bfloat16), "seq").astype(jnp.float32),
        lax.psum(shares[9].astype(jnp.bfloat16), "seq").astype(jnp.float32),
        lax.psum(shares[10].astype(jnp.bfloat16), "seq").astype(jnp.float32),
        lax.psum(shares[11].astype(jnp.bfloat16), "seq").astype(jnp.float32),
        lax.psum(shares[12].astype(jnp.bfloat16), "seq").astype(jnp.float32),
        lax.psum(shares[13].astype(jnp.bfloat16), "seq").astype(jnp.float32),
        lax.psum(shares[14].astype(jnp.bfloat16), "seq").astype(jnp.float32),
        lax.psum(shares[15].astype(jnp.bfloat16), "seq").astype(jnp.float32),
        lax.psum(shares[16].astype(jnp.bfloat16), "seq").astype(jnp.float32),
        lax.psum(shares[17].astype(jnp.bfloat16), "seq").astype(jnp.float32),
        lax.psum(shares[18].astype(jnp.bfloat16), "seq").astype(jnp.float32),
        lax.psum(shares[19].astype(jnp.bfloat16), "seq").astype(jnp.float32),
        lax.psum(shares[20].astype(jnp.bfloat16), "seq").astype(jnp.float32),
        lax.psum(shares[21].astype(jnp.bfloat16), "seq").astype(jnp.float32),
        lax.psum(shares[22].astype(jnp.bfloat16), "seq").astype(jnp.float32),
    )
    return (layer_out, feat_grad) + tuple(totals)


def solution(mesh):
    in_specs = (
        P("utt", "seq", None),
        P("utt", None),
        P("utt", "seq", None),
        P("utt", None),
        P("utt"),
        P("utt"),
        P("utt"),
        P("utt"),
        P("utt", None),
        P("utt"),
        P("utt"),
        P(None, None, "utt"),
        P("utt"),
        P("utt"),
        P("utt"),
        P("utt", None),
        P("utt"),
        P("utt"),
        P("utt", None),
        P("utt"),
        P("utt"),
        P("utt"),
        P("utt", None),
        P("utt"),
        P("utt", None),
        P("utt"),
    )
    out_specs = (
        P("utt", "seq", None),
        P("utt", "seq", None),
        P("utt", None),
        P("utt"),
        P("utt"),
        P("utt"),
        P("utt"),
        P("utt", None),
        P("utt"),
        P("utt"),
        P(None, None, "utt"),
        P("utt"),
        P("utt"),
        P("utt"),
        P("utt", None),
        P("utt"),
        P("utt"),
        P("utt", None),
        P("utt"),
        P("utt"),
        P("utt"),
        P("utt", None),
        P("utt"),
        P("utt", None),
        P("utt"),
    )
    return jax.shard_map(shards, mesh=mesh, in_specs=in_specs, out_specs=out_specs, check_vma=False)
```

profile of v0, /device:TPU:0, one launch (start us, length us, event | category | flops | bytes accessed | tf_op | source)
XLA Modules:
  0.0 1606.9 jit_solution(9901085464767323539)
XLA Ops:
  8.7 6.8 copy.112
  16.6 9.4 all-gather.4
  26.0 7.9 all-gather.3
  33.9 6.9 all-gather.6
  40.9 7.9 all-gather.5
  48.8 7.1 all-gather.7
  55.8 8.0 all-gather.2
  76.0 7.1 all-gather.8
  83.1 8.0 all-gather.10
  91.1 7.1 all-gather.9
  98.5 129.2 %all-gather.31.cloned.1.call-done = bf16[128,64,1024]{0,2,1:T(8,128)(2,1)} async-done(((bf16[128,64,256]{0,2,1:T(8,128)(2,1)}), bf16[128,64,1024]{0,2,1:T(8,128)(2,1)}) %all-gather.31.cloned.1.call-update) | async-done | bytes 16777232 | tf_op jit(solution)/shard_map/all_gather | solution.py:258
  227.7 56.3 %copy.113 = bf16[128,64,16,64]{1,3,0,2:T(8,128)(2,1)} copy(bf16[128,64,16,64]{0,3,2,1:T(8,128)(2,1)} %bitcast.382) | data formatting | bytes 33554432
  284.0 55.3 %while.84 = (s32[]{:T(128)}, f32[1,128,16,64]{1,3,2,0:T(8,128)S(1)}, bf16[128,64,16,64]{1,3,0,2:T(8,128)(2,1)}, bf16[1,256,1024]{1,2,0:T(8,128)(2,1)S(1)}, s32[]...) while((s32[]{:T(128)}, ...), condition=%wide.region_6.7_spmd.clone, body=%wide.region_5.6_spmd.clone.sunk | while | flops 134479904 | bytes 13632132 | solution.py:198
  348.2 8.1 all-gather.12
  356.3 7.1 all-gather.11
  366.6 8.0 all-gather.13
  374.7 7.1 all-gather.15
  381.7 8.0 all-gather.14
  389.8 7.6 all_gather.99
  400.5 7.6 all-gather.43.cloned.1.call-done
  412.0 20.4 %while.85 = (s32[]{:T(128)}, f32[1,16,128]{2,1,0:T(8,128)S(1)}, f32[1,16,128]{2,1,0:T(8,128)S(1)}, f32[1,128,16,64]{1,3,2,0:T(8,128)}, bf16[1,1024,1024]{1,2,0:T...) while((s32[]{:T(128)}, f32[1,16,128]{2,1,0:T(8,128)S(1)}, ...), condition=%wide.region_12.13_spmd.clone, body=%wide.region_9.12_spmd.clone.sunk | while | flops 277229568 | bytes 37093580 | solution.py:107
  434.6 10.2 all-gather.35.cloned.1.call-done
  447.3 86.9 %all-gather.37.cloned.1.call-done = bf16[1024,4096]{1,0:T(8,128)(2,1)} async-done(((bf16[256,4096]{1,0:T(8,128)(2,1)}), bf16[1024,4096]{1,0:T(8,128)(2,1)}) %all-gather.37.cloned.1.call-update) | async-done | bytes 8388624 | tf_op jit(solution)/shard_map/all_gather | solution.py:261
  534.3 9.3 multiply_convert_fusion.1
  543.6 80.2 %all-gather.39.cloned.1.call-done = bf16[4096,1024]{1,0:T(8,128)(2,1)} async-done(((bf16[1024,1024]{1,0:T(8,128)(2,1)}), bf16[4096,1024]{1,0:T(8,128)(2,1)}) %all-gather.39.cloned.1.call-update) | async-done | bytes 8388624 | tf_op jit(solution)/shard_map/all_gather | solution.py:262
  623.8 10.7 fusion.121
  646.8 25.4 %while.86 = (s32[]{:T(128)}, f32[1,128,16,64]{1,3,2,0:T(8,128)}, bf16[1,1024,1024]{1,2,0:T(8,128)(2,1)}, bf16[1,1024,1024]{1,2,0:T(8,128)(2,1)}, bf16[1,1024,102...) while((s32[]{:T(128)}, f32[1,128,16,64]{1,3,2,0:T(8,128)}, ...), condition=%wide.region_19.20_spmd.clone, body=%wide.region_18.19_spmd.clone.sunk | while | flops 680919040 | bytes 127951344 | solution.py:176
  672.2 10.7 copy.138
  688.8 7.5 copy.136
  700.7 40.8 %rev.4 = bf16[128,64,16,64]{0,1,2,3:T(8,128)(2,1)} reverse(bf16[128,64,16,64]{0,1,2,3:T(8,128)(2,1)} %bitcast.383), dimensions={0} | reverse | bytes 33554432 | tf_op jit(solution)/shard_map/jit(_flip)/rev | solution.py:404
  741.5 46.2 %copy.124 = bf16[128,64,16,64]{1,3,0,2:T(8,128)(2,1)} copy(bf16[128,64,16,64]{0,1,2,3:T(8,128)(2,1)} %rev.4) | data formatting | bytes 33554432
  792.0 5.2 multiply_reduce_fusion.1
  805.7 67.2 %while.87 = (s32[]{:T(128)}, f32[1,128,16,64]{1,3,2,0:T(8,128)}, bf16[128,64,16,64]{1,3,0,2:T(8,128)(2,1)}, bf16[1,255,1024]{1,2,0:T(8,128)(2,1)S(1)}, s32[]{:T(...) while((s32[]{:T(128)}, f32[1,128,16,64]{1,3,2,0:T(8,128)}, ...), condition=%wide.region_25.26_spmd.clone, body=%wide.region_24.25_spmd.clone.sunk | while | flops 134479904 | bytes 13632132 | solution.py:198
  886.9 5.9 convolution_convert_fusion.1
  894.1 5.7 convolution_convert_fusion
  900.0 11.3 broadcast_in_dim.118
  911.3 49.4 %while.83 = (s32[]{:T(128)}, bf16[128,64,16,64]{3,1,0,2:T(8,128)(2,1)}, bf16[1,256,1024]{1,2,0:T(8,128)(2,1)S(1)}, bf16[1,128,16,64]{1,3,2,0:T(8,128)(2,1)S(1)},...) while((s32[]{:T(128)}, ...), condition=%wide.region_53.54_spmd, body=%wide.region_52.53_spmd.sunk | while | flops 134217760 | bytes 14942842 | solution.py:223
  960.7 36.2 %copy.129 = bf16[128,64,16,64]{0,3,2,1:T(8,128)(2,1)} copy(bf16[128,64,16,64]{3,1,0,2:T(8,128)(2,1)} %get-tuple-element.678) | data formatting | bytes 33554432 | tf_op jit(solution)/shard_map/while | solution.py:223
  997.1 15.8 reduce-scatter.20.cloned.1.call-done
  1012.9 90.2 %reduce-scatter.24.cloned.1.call-done = bf16[256,4096]{1,0:T(8,128)(2,1)} async-done(((bf16[1024,4096]{1,0:T(8,128)(2,1)}), bf16[256,4096]{1,0:T(8,128)(2,1)}) %reduce-scatter.24.cloned.1.call-update) | async-done | bytes 2097168 | tf_op jit(solution)/shard_map/reduce_scatter | solution.py:476
  1103.1 89.3 %reduce-scatter.26.cloned.1.call-done = bf16[1024,1024]{1,0:T(8,128)(2,1)} async-done(((bf16[4096,1024]{1,0:T(8,128)(2,1)}), bf16[1024,1024]{1,0:T(8,128)(2,1)}) %reduce-scatter.26.cloned.1.call-update) | async-done | bytes 2097168 | tf_op jit(solution)/shard_map/reduce_scatter | solution.py:482
  1192.5 157.1 %reduce-scatter.18.cloned.1.call-done = bf16[128,64,256]{0,2,1:T(8,128)(2,1)} async-done(((bf16[128,64,1024]{0,2,1:T(8,128)(2,1)}), bf16[128,64,256]{0,2,1:T(8,128)(2,1)}) %reduce-scatter.18.cloned.1.call-update) | async-done | bytes 4194320 | tf_op jit(solution)/shard_map/reduce_scatter | solution.py:443
  1352.7 7.9 all-gather.16
  1360.7 5.5 fusion.71
  1367.7 15.7 all-reduce.18
  1384.5 15.7 all-reduce.16
  1409.1 171.7 %all-reduce.21.cloned.1.call-done = (bf16[256,512]{0,1:T(8,128)(2,1)}, bf16[128,64,256]{0,2,1:T(8,128)(2,1)}, bf16[128,1024]{1,0:T(8,128)(2,1)}, bf16[256,3072]{...) async-done(((bf16[256,512]{0,1:T(8,128)(2,1)}, bf16[128,64,256]{0,2,1:T(8,128)(2,1)}, ...) | async-done | bytes 11010064 | tf_op jit(solution)/shard_map/psum | solution.py:490
  1584.5 7.3 copy.131
  (954 shorter events, 325.7 us)
Async XLA Ops:
  7.2 56.8 %all-gather.27.cloned.1.call-start = ((), (), s32[]{:S(2)}) async-start(), calls=%async_computation.9 | async-start | bytes 1310720 | tf_op jit(solution)/shard_map/all_gather | solution.py:256
  7.9 60.6 %all-gather.29.cloned.1.call-start = ((), (), s32[]{:S(2)}) async-start(), calls=%async_computation.10 | async-start | bytes 1310720 | tf_op jit(solution)/shard_map/all_gather | solution.py:257
  8.7 219.0 %all-gather.31.cloned.1.call-start = ((), (), s32[]{:S(2)}) async-start(), calls=%async_computation.11 | async-start | bytes 20971520 | tf_op jit(solution)/shard_map/all_gather | solution.py:258
  15.6 18.3 %copy-start.115 = (f32[128]{0:T(128)S(1)}, f32[128]{0:T(128)}, u32[]{:S(2)}) copy-start(f32[128]{0:T(128)} %param.43) | copy-start | bytes 1540
  15.6 25.3 %copy-start.116 = (f32[128]{0:T(128)S(1)}, f32[128]{0:T(128)}, u32[]{:S(2)}) copy-start(f32[128]{0:T(128)} %param.42) | copy-start | bytes 1540
  15.6 33.2 %copy-start.98 = (f32[256]{0:T(256)S(1)}, f32[256]{0:T(256)}, u32[]{:S(2)}) copy-start(f32[256]{0:T(256)} %param.45) | copy-start | bytes 3076
  15.6 40.2 %copy-start.99 = (f32[256]{0:T(256)S(1)}, f32[256]{0:T(256)}, u32[]{:S(2)}) copy-start(f32[256]{0:T(256)} %param.46) | copy-start | bytes 3076
  15.6 48.2 %copy-start.117 = (s32[1,85]{1,0:T(1,128)S(1)}, s32[1,85]{1,0:T(1,128)}, u32[]{:S(2)}) copy-start(s32[1,85]{1,0:T(1,128)} %param.37) | copy-start | bytes 1024
  15.7 327.4 %all-gather.33.cloned.1.call-start = ((), (), s32[]{:S(2)}) async-start(), calls=%async_computation.12 | async-start | bytes 7864320 | tf_op jit(solution)/shard_map/all_gather | solution.py:259
  16.6 49.3 %copy-start.49 = (bf16[128,1024]{1,0:T(8,128)(2,1)}, bf16[128,1024]{1,0:T(8,128)(2,1)S(1)}, u32[]{:S(2)}) copy-start(bf16[128,1024]{1,0:T(8,128)(2,1)S(1)} %reshape.732) | copy-start | bytes 786436
  26.0 42.5 %copy-start.75 = (f32[4,1,128]{2,1,0:T(1,128)}, f32[4,1,128]{2,1,0:T(1,128)S(1)}, u32[]{:S(2)}) copy-start(f32[4,1,128]{2,1,0:T(1,128)S(1)} %all-gather.4) | copy-start | bytes 6148
  33.9 34.6 %copy-start.73 = (f32[4,1,128]{2,1,0:T(1,128)}, f32[4,1,128]{2,1,0:T(1,128)S(1)}, u32[]{:S(2)}) copy-start(f32[4,1,128]{2,1,0:T(1,128)S(1)} %all-gather.3) | copy-start | bytes 6148
  40.9 27.7 %copy-start.79 = (f32[4,1,128]{2,1,0:T(1,128)}, f32[4,1,128]{2,1,0:T(1,128)S(1)}, u32[]{:S(2)}) copy-start(f32[4,1,128]{2,1,0:T(1,128)S(1)} %all-gather.6) | copy-start | bytes 6148
  48.7 19.8 %copy-start.69 = (f32[4,1,128]{2,1,0:T(1,128)}, f32[4,1,128]{2,1,0:T(1,128)S(1)}, u32[]{:S(2)}) copy-start(f32[4,1,128]{2,1,0:T(1,128)S(1)} %all-gather.5) | copy-start | bytes 6148
  69.0 14.1 copy-start.101
  69.0 22.1 %copy-start.102 = (f32[256]{0:T(256)S(1)}, f32[256]{0:T(256)}, u32[]{:S(2)}) copy-start(f32[256]{0:T(256)} %param.49) | copy-start | bytes 3076
  71.5 26.7 %collective-permute-start.1 = (bf16[1,64,1024]{2,1,0:T(8,128)(2,1)S(1)}, bf16[1,64,1024]{2,1,0:T(8,128)(2,1)S(1)}, u32[]{:S(2)}, u32[]{:S(2)}) collective-permute-start(bf16[1,64,1024]{2,1,0:T(8,128)(2,1)S(1)} %get-tuple-element.1153), channel_id=1, source_target_pairs={{4,0},{8,4},{12,8},{16,12},{20,16},{24,20},{28,24},{5,1},{9,5},{13... | collective-permute-start | bytes 393224 | tf_op jit(solution)/shard_map/ppermute | solution.py:29
  72.8 25.4 %collective-permute-start = (bf16[1,64,1024]{2,1,0:T(8,128)(2,1)S(1)}, bf16[1,64,1024]{2,1,0:T(8,128)(2,1)S(1)}, u32[]{:S(2)}, u32[]{:S(2)}) collective-permute-start(bf16[1,64,1024]{2,1,0:T(8,128)(2,1)S(1)} %get-tuple-element.1152), channel_id=1, source_target_pairs={{0,4},{4,8},{8,12},{12,16},{16,20},{20,24},{24,28},{1,5},{5,9},{9,... | collective-permute-start | bytes 393224 | tf_op jit(solution)/shard_map/ppermute | solution.py:27
  75.9 321.7 %all-gather.41.cloned.1.call-start = ((), (), s32[]{:S(2)}) async-start(), calls=%async_computation.23 | async-start | bytes 2359296 | tf_op jit(solution)/shard_map/all_gather | solution.py:332
  83.1 256.5 %copy-start.71 = (f32[4,1,256]{2,1,0:T(1,128)}, f32[4,1,256]{2,1,0:T(1,128)S(1)}, u32[]{:S(2)}) copy-start(f32[4,1,256]{2,1,0:T(1,128)S(1)} %all-gather.8) | copy-start | bytes 12292
  91.1 252.4 %copy-start.66 = (f32[4,1,256]{2,1,0:T(1,128)}, f32[4,1,256]{2,1,0:T(1,128)S(1)}, u32[]{:S(2)}) copy-start(f32[4,1,256]{2,1,0:T(1,128)S(1)} %all-gather.10) | copy-start | bytes 12292
  98.2 245.3 %copy-start.64 = (f32[4,1,256]{2,1,0:T(1,128)}, f32[4,1,256]{2,1,0:T(1,128)S(1)}, u32[]{:S(2)}) copy-start(f32[4,1,256]{2,1,0:T(1,128)S(1)} %all-gather.9) | copy-start | bytes 12292
  343.5 12.8 copy-start.104
  348.2 59.9 %all-gather.43.cloned.1.call-start = ((), (), s32[]{:S(2)}) async-start(), calls=%async_computation.24 | async-start | bytes 2359296 | tf_op jit(solution)/shard_map/all_gather | solution.py:333
  364.2 80.5 %all-gather.35.cloned.1.call-start = ((), (), s32[]{:S(2)}) async-start(), calls=%async_computation.13 | async-start | bytes 2621440 | tf_op jit(solution)/shard_map/all_gather | solution.py:260
  365.0 16.7 %copy-start.107 = (f32[256]{0:T(256)S(1)}, f32[256]{0:T(256)}, u32[]{:S(2)}) copy-start(f32[256]{0:T(256)} %param.56) | copy-start | bytes 3076
  365.0 24.7 %copy-start.97 = (f32[1024]{0:T(1024)S(1)}, f32[1024]{0:T(1024)}, u32[]{:S(2)}) copy-start(f32[1024]{0:T(1024)} %param.59) | copy-start | bytes 12292
  365.0 169.2 %all-gather.37.cloned.1.call-start = ((), (), s32[]{:S(2)}) async-start(), calls=%async_computation.14 | async-start | bytes 10485760 | tf_op jit(solution)/shard_map/all_gather | solution.py:261
  365.8 258.0 %all-gather.39.cloned.1.call-start = ((), (), s32[]{:S(2)}) async-start(), calls=%async_computation.15 | async-start | bytes 10485760 | tf_op jit(solution)/shard_map/all_gather | solution.py:262
  366.5 421.5 %reduce-scatter.30.cloned.1.call-start = ((), (), s32[]{:S(2)}) async-start(), calls=%async_computation.26 | async-start | bytes 2359296
  432.4 12.3 copy-start.10
  433.6 11.2 copy-start.25
  447.1 190.9 %copy-start.12 = (f32[128,1024]{1,0:T(8,128)}, f32[128,1024]{1,0:T(8,128)S(1)}, u32[]{:S(2)}) copy-start(f32[128,1024]{1,0:T(8,128)S(1)} %get-tuple-element.1157) | copy-start | bytes 1572868
  534.3 89.5 %copy-start.41 = (bf16[1,128,1024]{2,1,0:T(8,128)(2,1)S(1)}, bf16[1,128,1024]{2,1,0:T(8,128)(2,1)}, u32[]{:S(2)}) copy-start(bf16[1,128,1024]{2,1,0:T(8,128)(2,1)} %param.38) | copy-start | bytes 786436
  687.2 102.9 %reduce-scatter.28.cloned.1.call-start = ((), (), s32[]{:S(2)}) async-start(), calls=%async_computation.25 | async-start | bytes 2359296
  700.7 296.4 %reduce-scatter.22.cloned.1.call-start = ((), (), s32[]{:S(2)}) async-start(), calls=%async_computation.20 | async-start | bytes 2621440 | tf_op jit(solution)/shard_map/reduce_scatter | solution.py:464
  741.5 46.2 %copy-start.14 = (f32[1,128,16,64]{1,3,2,0:T(8,128)S(1)}, f32[1,128,16,64]{1,3,2,0:T(8,128)}, u32[]{:S(2)}) copy-start(f32[1,128,16,64]{1,3,2,0:T(8,128)} %get-tuple-element.674) | copy-start | bytes 1572868
  798.9 6.5 collective-permute-start.3
  800.2 5.2 collective-permute-start.2
  805.3 191.8 %reduce-scatter.14.cloned.1.call-start = ((), (), s32[]{:S(2)}) async-start(), calls=%async_computation.16 | async-start | bytes 1310720 | tf_op jit(solution)/shard_map/reduce_scatter | solution.py:419
  805.7 68.7 %copy-start.92 = (pred[128]{0:T(512)(128)(4,1)S(1)}, pred[128]{0:T(512)(128)(4,1)}, u32[]{:S(2)}) copy-start(pred[128]{0:T(512)(128)(4,1)} %copy-done.91) | copy-start | bytes 388
  879.0 118.1 %reduce-scatter.16.cloned.1.call-start = ((), (), s32[]{:S(2)}) async-start(), calls=%async_computation.17 | async-start | bytes 1310720 | tf_op jit(solution)/shard_map/reduce_scatter | solution.py:434
  880.6 132.3 %reduce-scatter.20.cloned.1.call-start = ((), (), s32[]{:S(2)}) async-start(), calls=%async_computation.19 | async-start | bytes 7864320 | tf_op jit(solution)/shard_map/reduce_scatter | solution.py:455
  885.6 217.6 %reduce-scatter.24.cloned.1.call-start = ((), (), s32[]{:S(2)}) async-start(), calls=%async_computation.21 | async-start | bytes 10485760 | tf_op jit(solution)/shard_map/reduce_scatter | solution.py:476
  892.8 299.7 %reduce-scatter.26.cloned.1.call-start = ((), (), s32[]{:S(2)}) async-start(), calls=%async_computation.22 | async-start | bytes 10485760 | tf_op jit(solution)/shard_map/reduce_scatter | solution.py:482
  899.8 449.8 %reduce-scatter.18.cloned.1.call-start = ((), (), s32[]{:S(2)}) async-start(), calls=%async_computation.18 | async-start | bytes 20971520 | tf_op jit(solution)/shard_map/reduce_scatter | solution.py:443
  900.0 11.3 copy-start.4
  997.0 583.8 %all-reduce.21.cloned.1.call-start = ((), (), s32[]{:S(2)}) async-start(), calls=%async_computation.27 | async-start | bytes 22020096 | tf_op jit(solution)/shard_map/psum | solution.py:490
  (107 other events, 339.0 us)
Sparse Core Ops, SparseCore 0:
  9.9 29.3 all-gather.26
  41.1 26.6 all-gather.28
  70.2 157.4 all-gather.30
  229.4 70.1 all-gather.32
  348.3 29.0 all-gather.40
  379.5 28.5 all-gather.42
  409.9 34.7 all-gather.34
  446.6 87.5 all-gather.36
  536.1 87.5 all-gather.38
  687.4 35.7 reduce-scatter.29
  726.1 34.3 reduce-scatter.27
  805.4 35.2 reduce-scatter.21
  879.1 29.3 reduce-scatter.13
  911.8 27.6 reduce-scatter.15
  942.7 70.2 reduce-scatter.19
  1016.7 86.3 reduce-scatter.23
  1106.0 86.3 reduce-scatter.25
  1195.7 153.7 reduce-scatter.17
  1352.7 228.0 all-reduce.20
where the time goes:
time: 1620 us; the launch traced here: 1610 us
  waiting for transfers between devices  842 us (52%)
  local copies, waits for them, and re-layouts  329 us (20%)
  matrix products  209 us (13%)
  blocking collectives  155 us (10%)
  other arithmetic  39.6 us (2%)
  between operations  17.9 us (1%)
    psum x1, waiting for transfers between devices, shards(): lax.psum(shares[0].astype(jnp.bfloat16), 'seq').astype(jnp.float32)  172 us
    unnamed x253, local copies, waits for them, and re-layouts  166 us
    reduce_scatter x1, waiting for transfers between devices, shards(): lax.psum_scatter(posweight_grad.astype(jnp.bfloat16), 'utt', scatter_dime...  157 us
    all_gather x1, waiting for transfers between devices, shards(): lax.all_gather(pos_weight, 'utt', axis=2, tiled=True)  129 us
    reduce_scatter x1, waiting for transfers between devices, shards(): lax.psum_scatter(upweight_grad.astype(jnp.bfloat16), 'utt', scatter_dimen...  90.2 us
    reduce_scatter x1, waiting for transfers between devices, shards(): lax.psum_scatter(downweight_grad.astype(jnp.bfloat16), 'utt', scatter_dim...  89.3 us
    all_gather x1, waiting for transfers between devices, shards(): lax.all_gather(up_weight, 'utt', axis=0, tiled=True)  86.9 us
    dot_general x32, matrix products, absorb(): jnp.einsum('utjgi,jigo->utgo', columns, weight, preferred_element_type=jn...  85.3 us
  transfers between devices with their start and end apart: 23, of which 10 were waited for; matrix products, arithmetic and copies ran while one was open for 29% of the time, Pallas kernels for 0%

commit v1 on v0

v1 whole, which is shorter than its diff:
```python
import functools

import jax
import jax.numpy as jnp
from jax import lax
from jax.experimental import pallas as pl
from jax.experimental.pallas import tpu as pltpu
from jax.sharding import PartitionSpec as P

D = 1024
H = 16
HEAD_DIM = 64
C = 512
KPOS = 128
G = 16
GW = 64
SPAN = 10
PACK = 4
TILE = PACK * GW
EPS = 1e-05
MESH = pl.DeviceIdType.MESH
F32 = jnp.float32
BF16 = jnp.bfloat16
VMEM_BYTES = 56 * 1024 * 1024


def exchange(items, collective_id):
    count = len(items)
    axes = []
    for _, axis, _ in items:
        if axis not in axes:
            axes.append(axis)
    sizes = {axis: lax.axis_size(axis) for axis in axes}

    def kernel(*refs):
        ins, outs = refs[:count], refs[count : 2 * count]
        sems = refs[2 * count :]
        barrier = pltpu.get_barrier_semaphore()
        for axis in axes:
            me = lax.axis_index(axis)

            def greet(i, carry, axis=axis, me=me):
                peer = lax.rem(me + i, sizes[axis])
                pl.semaphore_signal(
                    barrier, inc=1, device_id={axis: peer}, device_id_type=MESH
                )
                return carry

            lax.fori_loop(1, sizes[axis], greet, 0)
        own = []
        for n, (_, axis, gather) in enumerate(items):
            me = lax.axis_index(axis)
            source = ins[n] if gather else ins[n].at[me]
            copy = pltpu.make_async_copy(source, outs[n].at[me], sems[3 * n + 2])
            copy.start()
            own.append(copy)
        pl.semaphore_wait(barrier, sum(sizes[axis] - 1 for axis in axes))

        def copy_to(n, i, slot_is_mine):
            _, axis, gather = items[n]
            me = lax.axis_index(axis)
            peer = lax.rem(me + i, sizes[axis])
            slot = me if slot_is_mine else peer
            return pltpu.make_async_remote_copy(
                src_ref=ins[n] if gather else ins[n].at[peer],
                dst_ref=outs[n].at[slot],
                send_sem=sems[3 * n].at[peer],
                recv_sem=sems[3 * n + 1].at[slot],
                device_id={axis: peer},
                device_id_type=MESH,
            )

        for n, (_, axis, _) in enumerate(items):

            def send(i, carry, n=n):
                copy_to(n, i, True).start()
                return carry

            lax.fori_loop(1, sizes[axis], send, 0)
        for n, (_, axis, _) in enumerate(items):
            own[n].wait()

            def finish(i, carry, n=n):
                copy_to(n, i, False).wait()
                return carry

            lax.fori_loop(1, sizes[axis], finish, 0)

    shapes, scratch = [], []
    for array, axis, gather in items:
        shape = ((sizes[axis],) + array.shape) if gather else array.shape
        shapes.append(jax.ShapeDtypeStruct(shape, array.dtype))
        scratch += [
            pltpu.SemaphoreType.DMA((sizes[axis],)),
            pltpu.SemaphoreType.DMA((sizes[axis],)),
            pltpu.SemaphoreType.DMA,
        ]
    return pl.pallas_call(
        kernel,
        out_shape=shapes,
        in_specs=[pl.BlockSpec(memory_space=pl.ANY)] * count,
        out_specs=[pl.BlockSpec(memory_space=pl.ANY)] * count,
        scratch_shapes=scratch,
        compiler_params=pltpu.CompilerParams(
            collective_id=collective_id, has_side_effects=True
        ),
    )(*[array for array, _, _ in items])


def regroup(blocks, backward, collective_id):
    num_seq, num_utt = lax.axis_size("seq"), lax.axis_size("utt")
    per_column = num_seq // num_utt
    num_blocks = per_column * num_utt
    sends = blocks.shape[0]
    receives = num_blocks if backward else num_seq

    def kernel(x_ref, o_ref, send_sem, recv_sem, own_sem):
        me_seq, me_utt = lax.axis_index("seq"), lax.axis_index("utt")

        def by_block(b):
            return lax.rem(b, per_column) * num_utt + me_utt, b // per_column

        def by_shard(f):
            return f, lax.rem(me_seq, num_utt)

        dest, origin = (by_shard, by_block) if backward else (by_block, by_shard)
        slot = me_utt * per_column + me_seq // num_utt if backward else me_seq
        own_block = me_seq if backward else me_utt * per_column + me_seq // num_utt
        is_own = (lax.rem(me_seq, num_utt) == me_utt).astype(jnp.int32)

        def not_me(where):
            return jnp.logical_or(where[0] != me_seq, where[1] != me_utt)

        def device(where):
            return {"seq": where[0], "utt": where[1]}

        barrier = pltpu.get_barrier_semaphore()

        def greet(i, carry):
            where = origin(i)

            @pl.when(not_me(where))
            def _():
                pl.semaphore_signal(
                    barrier, inc=1, device_id=device(where), device_id_type=MESH
                )

            return carry

        lax.fori_loop(0, receives, greet, 0)
        own = pltpu.make_async_copy(x_ref.at[own_block], o_ref.at[slot], own_sem)

        @pl.when(is_own == 1)
        def _():
            own.start()

        pl.semaphore_wait(barrier, sends - is_own)

        def outgoing(i):
            return pltpu.make_async_remote_copy(
                src_ref=x_ref.at[i],
                dst_ref=o_ref.at[slot],
                send_sem=send_sem.at[i],
                recv_sem=recv_sem.at[slot],
                device_id=device(dest(i)),
                device_id_type=MESH,
            )

        def incoming(i):
            return pltpu.make_async_remote_copy(
                src_ref=x_ref.at[0],
                dst_ref=o_ref.at[i],
                send_sem=send_sem.at[0],
                recv_sem=recv_sem.at[i],
                device_id=device(origin(i)),
                device_id_type=MESH,
            )

        def send(i, carry):
            @pl.when(not_me(dest(i)))
            def _():
                outgoing(i).start()

            return carry

        def sent(i, carry):
            @pl.when(not_me(dest(i)))
            def _():
                outgoing(i).wait_send()

            return carry

        def arrived(i, carry):
            @pl.when(not_me(origin(i)))
            def _():
                incoming(i).wait_recv()

            return carry

        lax.fori_loop(0, sends, send, 0)

        @pl.when(is_own == 1)
        def _():
            own.wait()

        lax.fori_loop(0, receives, arrived, 0)
        lax.fori_loop(0, sends, sent, 0)

    return pl.pallas_call(
        kernel,
        out_shape=jax.ShapeDtypeStruct((receives,) + blocks.shape[1:], blocks.dtype),
        in_specs=[pl.BlockSpec(memory_space=pl.ANY)],
        out_specs=pl.BlockSpec(memory_space=pl.ANY),
        scratch_shapes=[
            pltpu.SemaphoreType.DMA((sends,)),
            pltpu.SemaphoreType.DMA((receives,)),
            pltpu.SemaphoreType.DMA,
        ],
        compiler_params=pltpu.CompilerParams(
            collective_id=collective_id, has_side_effects=True
        ),
    )(blocks)


def permute_all(blocks):
    size = lax.axis_size("utt")
    me = lax.axis_index("utt")
    result = blocks
    for step in range(1, size):
        piece = lax.dynamic_index_in_dim(blocks, lax.rem(me + step, size), 0)
        moved = lax.ppermute(piece, "utt", [(i, (i + step) % size) for i in range(size)])
        result = lax.dynamic_update_slice_in_dim(
            result, moved, lax.rem(me + size - step, size), 0
        )
    return result


def pack_frames(wide_ref, packed_ref, rows, groups):
    for r in range(PACK):
        part = wide_ref[pl.ds(r, rows, stride=PACK), :]
        for h in range(groups):
            packed_ref[h, :, r * GW : (r + 1) * GW] = part[:, h * GW : (h + 1) * GW]


def unpack_frames(packed, wide_ref, rows, groups):
    for r in range(PACK):
        wide_ref[pl.ds(r, rows, stride=PACK), :] = jnp.concatenate(
            [packed(h, r) for h in range(groups)], axis=1
        )


def tap_tile(taps_ref, first, depth, h):
    return jnp.concatenate(
        [
            taps_ref[pl.ds(TILE + first - r * GW, depth), h * GW : (h + 1) * GW]
            for r in range(PACK)
        ],
        axis=1,
    )


STEP_TILES = 3
NUM_TILES = KPOS // PACK + 1
HALF = KPOS // 2


def fill_taps(w_ref, taps_ref):
    edge = jnp.zeros((TILE, taps_ref.shape[1]), taps_ref.dtype)
    taps_ref[0:TILE, :] = edge
    taps_ref[TILE + KPOS * GW :, :] = edge
    taps_ref[TILE : TILE + KPOS * GW, :] = w_ref[...]


def fill_frames(x_ref, wide_ref, packed_ref, frames, groups):
    edge = jnp.zeros((HALF, wide_ref.shape[1]), F32)
    wide_ref[0:HALF, :] = edge
    wide_ref[HALF + frames :, :] = edge
    wide_ref[HALF : HALF + frames, :] = x_ref[...].astype(F32)
    pack_frames(wide_ref, packed_ref, (frames + KPOS) // PACK, groups)


def pos_forward_kernel(x_ref, w_ref, b_ref, o_ref, wide_ref, packed_ref, taps_ref, acc_ref):
    frames, width = x_ref.shape
    groups = width // GW
    rows = frames // PACK
    fill_taps(w_ref, taps_ref)
    fill_frames(x_ref, wide_ref, packed_ref, frames, groups)
    for h in range(groups):
        for step in range(NUM_TILES // STEP_TILES):
            first = step * STEP_TILES
            columns = jnp.concatenate(
                [packed_ref[h, first + j : first + j + rows, :] for j in range(STEP_TILES)], axis=1
            ).astype(BF16)
            part = jnp.dot(
                columns,
                tap_tile(taps_ref, first * TILE, STEP_TILES * TILE, h),
                preferred_element_type=F32,
            )
            if step == 0:
                acc_ref[h] = part
            else:
                acc_ref[h] += part
    unpack_frames(
        lambda h, r: acc_ref[h, :, r * GW : (r + 1) * GW] + b_ref[:, h * GW : (h + 1) * GW],
        wide_ref.at[0:frames],
        rows,
        groups,
    )
    o_ref[...] = wide_ref[0:frames, :].astype(o_ref.dtype)


def pos_forward(x, taps, bias):
    frames, width = x.shape
    groups = width // GW
    return pl.pallas_call(
        pos_forward_kernel,
        out_shape=jax.ShapeDtypeStruct((frames, width), BF16),
        scratch_shapes=[
            pltpu.VMEM((frames + KPOS, width), F32),
            pltpu.VMEM((groups, (frames + KPOS) // PACK, TILE), F32),
            pltpu.VMEM((KPOS * GW + 2 * TILE, width), BF16),
            pltpu.VMEM((groups, frames // PACK, TILE), F32),
        ],
        compiler_params=pltpu.CompilerParams(vmem_limit_bytes=VMEM_BYTES),
    )(x, taps, bias)


def pos_backward_kernel(
    x_ref, g_ref, w_ref, dx_ref, dw_ref, wide_ref, packed_ref, grads_ref, taps_ref, acc_ref, sum_ref
):
    frames, width = x_ref.shape
    groups = width // GW
    rows = frames // PACK
    middle = HALF // PACK
    fill_taps(w_ref, taps_ref)
    fill_frames(x_ref, wide_ref, packed_ref, frames, groups)
    fill_frames(g_ref, wide_ref, grads_ref, frames, groups)
    sum_ref[...] = jnp.zeros_like(sum_ref)
    for tile in range(NUM_TILES):
        parts = [
            lax.dot_general(
                packed_ref[h, tile : tile + rows, :].astype(BF16),
                grads_ref[h, middle : middle + rows, :].astype(BF16),
                (((0,), (0,)), ((), ())),
                preferred_element_type=F32,
            )
            for h in range(groups)
        ]
        for r in range(PACK):
            where = TILE + tile * TILE - r * GW
            sum_ref[where : where + TILE, :] += jnp.concatenate(
                [part[:, r * GW : (r + 1) * GW] for part in parts], axis=1
            )
    dw_ref[...] = sum_ref[TILE : TILE + KPOS * GW, :].astype(dw_ref.dtype)
    for h in range(groups):
        for tile in range(NUM_TILES):
            first = 2 * middle - tile
            part = lax.dot_general(
                grads_ref[h, first : first + rows, :].astype(BF16),
                tap_tile(taps_ref, tile * TILE, TILE, h),
                (((1,), (1,)), ((), ())),
                preferred_element_type=F32,
            )
            if tile == 0:
                acc_ref[h] = part
            else:
                acc_ref[h] += part
    unpack_frames(
        lambda h, r: acc_ref[h, :, r * GW : (r + 1) * GW], wide_ref.at[0:frames], rows, groups
    )
    dx_ref[...] = wide_ref[0:frames, :].astype(dx_ref.dtype)


def pos_backward(x, grads, taps):
    frames, width = x.shape
    groups = width // GW
    padded = (groups, (frames + KPOS) // PACK, TILE)
    return pl.pallas_call(
        pos_backward_kernel,
        out_shape=[
            jax.ShapeDtypeStruct((frames, width), BF16),
            jax.ShapeDtypeStruct((KPOS * GW, width), BF16),
        ],
        scratch_shapes=[
            pltpu.VMEM((frames + KPOS, width), F32),
            pltpu.VMEM(padded, F32),
            pltpu.VMEM(padded, F32),
            pltpu.VMEM((KPOS * GW + 2 * TILE, width), BF16),
            pltpu.VMEM((groups, frames // PACK, TILE), F32),
            pltpu.VMEM((KPOS * GW + 2 * TILE, width), F32),
        ],
        compiler_params=pltpu.CompilerParams(vmem_limit_bytes=VMEM_BYTES),
    )(x, grads, taps)


SCALE = HEAD_DIM ** (-0.5)
Q_BLOCK = 256


def nt_dot(a, b):
    return lax.dot_general(a, b, (((1,), (1,)), ((), ())), preferred_element_type=F32)


def attend_kernel(q_ref, k_ref, v_ref, o_ref, lse_ref):
    frames, width = q_ref.shape
    for h in range(width // HEAD_DIM):
        lanes = slice(h * HEAD_DIM, (h + 1) * HEAD_DIM)
        keys, values = k_ref[:, lanes], v_ref[:, lanes]
        for start in range(0, frames, Q_BLOCK):
            rows = slice(start, start + Q_BLOCK)
            scores = nt_dot(q_ref[rows, lanes], keys) * SCALE
            highest = jnp.max(scores, -1, keepdims=True)
            weights = jnp.exp(scores - highest)
            total = jnp.sum(weights, -1, keepdims=True)
            summed = jnp.dot(weights.astype(BF16), values, preferred_element_type=F32)
            o_ref[rows, lanes] = summed / total
            lse_ref[rows, h : h + 1] = highest + jnp.log(total)


def attend(queries, keys, values):
    frames, width = queries.shape
    return pl.pallas_call(
        attend_kernel,
        out_shape=[
            jax.ShapeDtypeStruct((frames, width), F32),
            jax.ShapeDtypeStruct((frames, width // HEAD_DIM), F32),
        ],
        compiler_params=pltpu.CompilerParams(vmem_limit_bytes=VMEM_BYTES),
    )(queries, keys, values)


def attend_back_kernel(
    q_ref, k_ref, v_ref, g_ref, o_ref, lse_ref, dq_ref, dk_ref, dv_ref, dk_acc, dv_acc
):
    frames, width = q_ref.shape
    for h in range(width // HEAD_DIM):
        lanes = slice(h * HEAD_DIM, (h + 1) * HEAD_DIM)
        keys, values = k_ref[:, lanes], v_ref[:, lanes]
        for start in range(0, frames, Q_BLOCK):
            rows = slice(start, start + Q_BLOCK)
            queries, grads = q_ref[rows, lanes], g_ref[rows, lanes]
            inner = jnp.sum(grads.astype(F32) * o_ref[rows, lanes], -1, keepdims=True)
            probs = jnp.exp(nt_dot(queries, keys) * SCALE - lse_ref[rows, h : h + 1])
            score_grad = (probs * (nt_dot(grads, values) - inner)).astype(BF16)
            dq_ref[rows, lanes] = (
                jnp.dot(score_grad, keys, preferred_element_type=F32) * SCALE
            ).astype(BF16)
            key_part = lax.dot_general(
                score_grad, queries, (((0,), (0,)), ((), ())), preferred_element_type=F32
            )
            value_part = lax.dot_general(
                probs.astype(BF16), grads, (((0,), (0,)), ((), ())), preferred_element_type=F32
            )
            if start == 0:
                dk_acc[...] = key_part
                dv_acc[...] = value_part
            else:
                dk_acc[...] += key_part
                dv_acc[...] += value_part
        dk_ref[:, lanes] = (dk_acc[...] * SCALE).astype(BF16)
        dv_ref[:, lanes] = dv_acc[...].astype(BF16)


def attend_back(queries, keys, values, grads, output, lse):
    frames, width = queries.shape
    return pl.pallas_call(
        attend_back_kernel,
        out_shape=[jax.ShapeDtypeStruct((frames, width), BF16)] * 3,
        scratch_shapes=[pltpu.VMEM((frames, HEAD_DIM), F32)] * 2,
        compiler_params=pltpu.CompilerParams(vmem_limit_bytes=VMEM_BYTES),
    )(queries, keys, values, grads, output, lse)


def layer_norm(values, gain, shift):
    center = values - jnp.mean(values, -1, keepdims=True)
    spread = jnp.mean(center * center, -1, keepdims=True)
    return center * lax.rsqrt(spread + EPS) * gain + shift


def gelu_exact(values):
    return jax.nn.gelu(values, approximate=False)


def front_norms(conv_pre, conv_gain, conv_shift, norm_gain, norm_shift):
    return layer_norm(
        gelu_exact(layer_norm(conv_pre, conv_gain, conv_shift)), norm_gain, norm_shift
    )


def inner_dot(first_mat, second_mat):
    return lax.dot_general(
        first_mat, second_mat, (((0,), (0,)), ((), ())), preferred_element_type=F32
    )


def dot(a, b):
    return jnp.dot(a, b, preferred_element_type=F32)


def shards(
    feats,
    mask_starts,
    grad_out,
    conv_weight,
    conv_gain,
    conv_shift,
    norm_gain,
    norm_shift,
    proj_weight,
    proj_bias,
    mask_embed,
    pos_weight,
    pos_bias,
    attn_gain,
    attn_shift,
    qkv_weight,
    query_bias,
    value_bias,
    out_weight,
    out_bias,
    ffn_gain,
    ffn_shift,
    up_weight,
    up_bias,
    down_weight,
    down_bias,
):
    num_utt, num_seq = lax.axis_size("utt"), lax.axis_size("seq")
    me_seq = lax.axis_index("seq")
    frames = grad_out.shape[1]
    length = frames * num_seq
    rows_all = num_utt * frames
    column = D // num_utt
    per_column = num_seq // num_utt
    width = column // per_column
    out_rows = grad_out.reshape(frames, D)
    steps_in = feats.reshape(frames, 2 * C)

    qkv_blocks = qkv_weight.reshape(column, 3, num_utt, column).transpose(2, 0, 1, 3)
    qkv_columns = permute_all(qkv_blocks.reshape(num_utt, column, 3 * column))
    qkv_columns = qkv_columns.reshape(D, 3 * column)
    hidden = up_bias.shape[0]
    up_blocks = up_weight.reshape(column, num_utt, hidden).transpose(1, 0, 2)
    up_columns = permute_all(up_blocks).reshape(D, hidden)

    vectors = [
        conv_gain,
        conv_shift,
        norm_gain,
        norm_shift,
        proj_bias,
        mask_embed,
        attn_gain,
        attn_shift,
        out_bias,
        ffn_gain,
        ffn_shift,
        down_bias,
    ]
    conv_all, proj_all, vectors_all = exchange(
        [
            (conv_weight, "utt", True),
            (proj_weight, "utt", True),
            (jnp.concatenate(vectors)[None, :], "utt", True),
        ],
        1,
    )
    conv_all = conv_all.reshape(2 * C, C)
    proj_all = proj_all.reshape(C, D)
    whole, start = [], 0
    for vector in vectors:
        end = start + vector.shape[0]
        whole.append(vectors_all[:, 0, start:end].reshape(-1))
        start = end
    (
        conv_gain,
        conv_shift,
        norm_gain,
        norm_shift,
        proj_bias,
        mask_embed,
        attn_gain,
        attn_shift,
        out_bias,
        ffn_gain,
        ffn_shift,
        down_bias,
    ) = whole

    conv_pre = dot(steps_in, conv_all)
    feat_norm, front_pull = jax.vjp(
        front_norms, conv_pre, conv_gain, conv_shift, norm_gain, norm_shift
    )
    feat_low = feat_norm.astype(BF16)
    proj_out = dot(feat_low, proj_all) + proj_bias
    frame_pos = me_seq * frames + jnp.arange(frames, dtype=jnp.int32)
    starts = mask_starts.reshape(1, -1)
    inside = (frame_pos[:, None] >= starts) & (frame_pos[:, None] < starts + SPAN)
    masked = jnp.any(inside, -1, keepdims=True)
    embed = jnp.where(masked, mask_embed[None, :], proj_out)

    def to_blocks(values):
        return values.reshape(frames, D // width, width).transpose(1, 0, 2)

    def from_blocks(blocks):
        return blocks.transpose(1, 0, 2).reshape(frames, D)

    block_id = me_seq // num_utt
    taps = lax.dynamic_slice_in_dim(pos_weight, block_id * width, width, 2)
    taps = taps.reshape(KPOS * GW, width)
    taps_bias = lax.dynamic_slice_in_dim(pos_bias, block_id * width, width, 0)[None, :]
    pos_in = regroup(to_blocks(embed.astype(BF16)), False, 2).reshape(length, width)
    pos_own = pos_forward(pos_in, taps, taps_bias)
    pos_pre = from_blocks(regroup(pos_own.reshape(num_seq, frames, width), True, 3))
    pos_act, pos_pull = jax.vjp(gelu_exact, pos_pre.astype(F32))
    resid_one = embed + pos_act
    attn_norm, attn_pull = jax.vjp(layer_norm, resid_one, attn_gain, attn_shift)
    attn_in, gout_all = exchange(
        [(attn_norm.astype(BF16), "utt", True), (out_rows, "utt", True)], 4
    )
    attn_in = attn_in.reshape(rows_all, D)
    gout_all = gout_all.reshape(rows_all, D)

    projected = dot(attn_in, qkv_columns).reshape(rows_all, 3, column)
    bias = jnp.stack([query_bias, jnp.zeros_like(query_bias), value_bias])
    projected = (projected + bias[None]).astype(BF16)

    def to_heads(values, parts):
        blocks = values.reshape(num_utt, frames, parts, per_column, width)
        return blocks.transpose(3, 0, 2, 1, 4).reshape(num_seq, parts, frames, width)

    def from_heads(blocks, parts):
        blocks = blocks.reshape(per_column, num_utt, parts, frames, width)
        return blocks.transpose(1, 3, 2, 0, 4).reshape(rows_all, parts * column)

    (qkv_heads,) = exchange([(to_heads(projected, 3), "seq", False)], 5)
    qkv_heads = qkv_heads.transpose(1, 0, 2, 3).reshape(3, length, width)
    queries, keys, values = qkv_heads[0], qkv_heads[1], qkv_heads[2]
    attn_f32, lse = attend(queries, keys, values)
    (attn_rows,) = exchange(
        [(attn_f32.astype(BF16).reshape(num_seq, 1, frames, width), "seq", False)], 6
    )
    attn_flat = from_heads(attn_rows, 1)

    def split_rows(values):
        return values.astype(BF16).reshape(num_utt, frames, D)

    (parts,) = exchange([(split_rows(dot(attn_flat, out_weight)), "utt", False)], 7)
    resid_two = resid_one + jnp.sum(parts.astype(F32), 0) + out_bias
    ffn_norm, ffn_pull = jax.vjp(layer_norm, resid_two, ffn_gain, ffn_shift)
    (ffn_in,) = exchange([(ffn_norm.astype(BF16), "utt", True)], 8)
    ffn_in = ffn_in.reshape(rows_all, D)
    hidden_pre = dot(ffn_in, up_columns) + up_bias
    hidden_act, hidden_pull = jax.vjp(gelu_exact, hidden_pre)
    hidden_low = hidden_act.astype(BF16)
    layer_parts = split_rows(dot(hidden_low, down_weight))
    (hidden_grad,) = hidden_pull(nt_dot(gout_all, down_weight))
    hidden_grad = hidden_grad.astype(BF16)
    (back_parts,) = exchange([(split_rows(nt_dot(hidden_grad, up_columns)), "utt", False)], 9)
    ffn_back, ffngain_grad, ffnshift_grad = ffn_pull(jnp.sum(back_parts.astype(F32), 0))
    resid2_grad = out_rows.astype(F32) + ffn_back
    attn_grad_own = resid2_grad.astype(BF16)
    (attn_grad,) = exchange([(attn_grad_own, "utt", True)], 10)
    attn_grad = attn_grad.reshape(rows_all, D)

    downweight_grad = inner_dot(hidden_low, gout_all).astype(BF16)
    upweight_grad = inner_dot(ffn_in, hidden_grad).astype(BF16)
    downweight_grad = lax.psum(downweight_grad, "seq").astype(F32)
    up_share = lax.psum_scatter(
        upweight_grad.reshape(num_utt, column, hidden), "seq", scatter_dimension=1, tiled=True
    )

    out_grad = nt_dot(attn_grad, out_weight).astype(BF16)
    out_grad_heads, layer_parts, up_share = exchange(
        [
            (to_heads(out_grad, 1), "seq", False),
            (layer_parts, "utt", False),
            (up_share, "utt", False),
        ],
        11,
    )
    upweight_grad = lax.all_gather(up_share, "seq", axis=1, tiled=True)
    upweight_grad = upweight_grad.transpose(1, 0, 2).reshape(column, num_utt * hidden).astype(F32)
    layer_value = resid_two + jnp.sum(layer_parts.astype(F32), 0) + down_bias
    layer_out = layer_value.astype(BF16).reshape(1, frames, D)
    qkv_grads = attend_back(
        queries, keys, values, out_grad_heads.reshape(length, width), attn_f32, lse
    )
    qkv_grads = jnp.stack([part.reshape(num_seq, frames, width) for part in qkv_grads], axis=1)
    (qkv_back,) = exchange([(qkv_grads, "seq", False)], 12)
    qkv_back = from_heads(qkv_back, 3)
    (qkv_parts,) = exchange([(split_rows(nt_dot(qkv_back, qkv_columns)), "utt", False)], 13)
    outweight_grad = lax.psum(inner_dot(attn_flat, attn_grad).astype(BF16), "seq").astype(F32)
    qkvweight_grad = inner_dot(attn_in, qkv_back).astype(BF16)
    qkv_share = lax.psum_scatter(
        qkvweight_grad.reshape(num_utt, column, 3 * column),
        "seq",
        scatter_dimension=1,
        tiled=True,
    )
    attn_back, attngain_grad, attnshift_grad = attn_pull(jnp.sum(qkv_parts.astype(F32), 0))
    resid1_grad = resid2_grad + attn_back
    (pos_grad,) = pos_pull(resid1_grad)
    pos_low = pos_grad.astype(BF16)
    grads_in = regroup(to_blocks(pos_low), False, 14).reshape(length, width)
    embed_own, taps_grad = pos_backward(pos_in, grads_in, taps)
    groups = [list(range(i * num_utt, (i + 1) * num_utt)) for i in range(per_column)]
    taps_share = lax.psum_scatter(
        taps_grad, "seq", scatter_dimension=0, axis_index_groups=groups, tiled=True
    )
    posweight_grad = lax.all_gather(taps_share, "seq", axis=0, tiled=True)
    posweight_grad = (
        posweight_grad.reshape(per_column, KPOS, GW, width)
        .transpose(1, 2, 0, 3)
        .reshape(KPOS, GW, column)
        .astype(F32)
    )
    embed_back = from_blocks(regroup(embed_own.reshape(num_seq, frames, width), True, 15))
    embed_grad = resid1_grad + embed_back.astype(F32)
    maskembed_grad = jnp.sum(jnp.where(masked, embed_grad, 0.0), 0)
    proj_grad = jnp.where(masked, 0.0, embed_grad).astype(BF16)
    projbias_grad = jnp.sum(proj_grad, 0, dtype=F32)
    projweight_grad = inner_dot(feat_low, proj_grad)
    conv_back, convgain_grad, convshift_grad, normgain_grad, normshift_grad = front_pull(
        nt_dot(proj_grad, proj_all)
    )
    conv_grad = conv_back.astype(BF16)
    convweight_grad = inner_dot(steps_in, conv_grad)
    feat_grad = nt_dot(conv_grad, conv_all).astype(BF16).reshape(1, 2 * frames, C)

    row_vectors = [
        convgain_grad,
        convshift_grad,
        normgain_grad,
        normshift_grad,
        projbias_grad,
        maskembed_grad,
        jnp.sum(pos_low, 0, dtype=F32),
        attngain_grad,
        attnshift_grad,
        jnp.sum(attn_grad_own, 0, dtype=F32),
        ffngain_grad,
        ffnshift_grad,
        jnp.sum(out_rows, 0, dtype=F32),
    ]
    column_vectors = [
        jnp.sum(qkv_back[:, :column], 0, dtype=F32),
        jnp.sum(qkv_back[:, 2 * column :], 0, dtype=F32),
        jnp.sum(hidden_grad, 0, dtype=F32),
    ]
    conv_parts, proj_parts, vector_parts, qkv_share = exchange(
        [
            (convweight_grad.astype(BF16).reshape(num_utt, -1, C), "utt", False),
            (projweight_grad.astype(BF16).reshape(num_utt, -1, D), "utt", False),
            (
                jnp.concatenate([v.reshape(num_utt, 1, -1) for v in row_vectors], axis=2),
                "utt",
                False,
            ),
            (qkv_share, "utt", False),
        ],
        16,
    )
    qkvweight_grad = lax.all_gather(qkv_share, "seq", axis=1, tiled=True)
    qkvweight_grad = (
        qkvweight_grad.reshape(num_utt, column, 3, column)
        .transpose(1, 2, 0, 3)
        .reshape(column, 3 * D)
        .astype(F32)
    )
    convweight_grad, projweight_grad, sums = lax.psum(
        (
            jnp.sum(conv_parts.astype(F32), 0).astype(BF16),
            jnp.sum(proj_parts.astype(F32), 0).astype(BF16),
            jnp.concatenate([jnp.sum(vector_parts, 0)[0]] + column_vectors),
        ),
        "seq",
    )
    outs, start = [], 0
    for vector in row_vectors:
        end = start + vector.shape[0] // num_utt
        outs.append(sums[start:end])
        start = end
    for vector in column_vectors:
        end = start + vector.shape[0]
        outs.append(sums[start:end])
        start = end
    (
        convgain_grad,
        convshift_grad,
        normgain_grad,
        normshift_grad,
        projbias_grad,
        maskembed_grad,
        posbias_grad,
        attngain_grad,
        attnshift_grad,
        outbias_grad,
        ffngain_grad,
        ffnshift_grad,
        downbias_grad,
        querybias_grad,
        valuebias_grad,
        upbias_grad,
    ) = outs
    return (
        layer_out,
        feat_grad,
        convweight_grad.astype(F32),
        convgain_grad,
        convshift_grad,
        normgain_grad,
        normshift_grad,
        projweight_grad.astype(F32),
        projbias_grad,
        maskembed_grad,
        posweight_grad,
        posbias_grad,
        attngain_grad,
        attnshift_grad,
        qkvweight_grad,
        querybias_grad,
        valuebias_grad,
        outweight_grad,
        outbias_grad,
        ffngain_grad,
        ffnshift_grad,
        upweight_grad,
        upbias_grad,
        downweight_grad,
        downbias_grad,
    )


def solution(mesh):
    rows, split, taps = P("utt", "seq", None), P("utt"), P(None, None, "utt")
    matrix = P("utt", None)
    in_specs = (
        (rows, matrix, rows, matrix, split, split, split, split, matrix, split, split, taps)
        + (split, split, split, matrix, split, split, matrix, split, split, split)
        + (matrix, split, matrix, split)
    )
    out_specs = (
        (rows, rows, matrix, split, split, split, split, matrix, split, split, taps)
        + (split, split, split, matrix, split, split, matrix, split, split, split)
        + (matrix, split, matrix, split)
    )
    return jax.shard_map(shards, mesh=mesh, in_specs=in_specs, out_specs=out_specs, check_vma=False)
```

time: 1620 us -> 673 us (0.42)
  waiting for transfers between devices: 842 us -> 88 us
  Pallas kernels: 0 us -> 329 us
  local copies, waits for them, and re-layouts: 329 us -> 87.2 us
  matrix products: 209 us -> 46 us
  blocking collectives: 155 us -> 32.5 us
    reduce_scatter x7 -> x3, waiting for transfers between devices: 352 us -> 0.02 us  [the longest x1 0.02 us: shards(): lax.psum_scatter(taps_grad, 'seq', scatter_dimension=0, axis_index_groups...]
    pallas_call x0 -> x20, Pallas kernels: none -> 329 us  [the longest x12 248 us: exchange(): pl.pallas_call(kernel, out_shape=shapes, in_specs=[pl.BlockSpec(memory_sp...]
    all_gather x9 -> x3, waiting for transfers between devices: 314 us -> 56.2 us  [the longest x1 37.9 us: shards(): posweight_grad = lax.all_gather(taps_share, 'seq', axis=0, tiled=True)]
    dot_general x74 -> x12, matrix products: 188 us -> 32.3 us  [the longest x6 18.3 us: nt_dot(): lax.dot_general(a, b, (((1,), (1,)), ((), ())), preferred_element_type=F32)]
    unnamed x253 -> x127, local copies, waits for them, and re-layouts: 166 us -> 19.7 us
    psum x1, waiting for transfers between devices: 172 us -> 30.5 us  [shards(): lax.psum((jnp.sum(conv_parts.astype(F32), 0).astype(BF16), jnp.sum(proj_p...]
    all_gather x16 -> x0, blocking collectives: 123 us -> none  [the longest x1 9.38 us: shards(): lax.all_gather(conv_shift, 'utt', axis=0, tiled=True)]
    while x383 -> x0, local copies, waits for them, and re-layouts: 58.5 us -> none  [the longest x1 36.2 us: tap_grad(): lax.fori_loop(0, KPOS // group_taps, absorb, jnp.zeros((KPOS, GW, G, GW),...]
  transfers between devices with their start and end apart: 23 -> 13, of which waited for: 10 -> 3; matrix products, arithmetic and copies ran while one was open for 29% -> 18% of each run, Pallas kernels for 0% -> 33%
where the time goes in v1:
time: 673 us; the launch traced here: 664 us
  Pallas kernels  329 us (49%)
  waiting for transfers between devices  88 us (13%)
  local copies, waits for them, and re-layouts  87.2 us (13%)
  other arithmetic  51.4 us (8%)
  matrix products  46 us (7%)
  blocking collectives  32.5 us (5%)
  between operations  15.5 us (2%)
  starting transfers between devices  13.7 us (2%)
    pallas_call x12, Pallas kernels, exchange(): pl.pallas_call(kernel, out_shape=shapes, in_specs=[pl.BlockSpec(memory_sp...  248 us
    pallas_call x4, Pallas kernels, regroup(): pl.pallas_call(kernel, out_shape=jax.ShapeDtypeStruct((receives,) + block...  47.9 us
    all_gather x1, waiting for transfers between devices, shards(): posweight_grad = lax.all_gather(taps_share, 'seq', axis=0, tiled=True)  37.9 us
    psum x1, blocking collectives, shards(): lax.psum((jnp.sum(conv_parts.astype(F32), 0).astype(BF16), jnp.sum(proj_p...  32.5 us
    psum x1, waiting for transfers between devices, shards(): lax.psum((jnp.sum(conv_parts.astype(F32), 0).astype(BF16), jnp.sum(proj_p...  30.5 us
    unnamed x127, local copies, waits for them, and re-layouts  19.7 us
    all_gather x1, waiting for transfers between devices, shards(): qkvweight_grad = lax.all_gather(qkv_share, 'seq', axis=1, tiled=True)  18.3 us
    dot_general x6, matrix products, nt_dot(): lax.dot_general(a, b, (((1,), (1,)), ((), ())), preferred_element_type=F32)  18.3 us
  transfers between devices with their start and end apart: 13, of which 3 were waited for; matrix products, arithmetic and copies ran while one was open for 18% of the time, Pallas kernels for 33%

profile of v1, /device:TPU:0, one launch (start us, length us, event | category | flops | bytes accessed | tf_op | source)
XLA Modules:
  0.0 663.6 jit_solution(15457221700393915154)
XLA Ops:
  7.3 2.7 copy.134
  14.4 2.9 collective-permute-start
  17.3 4.1 copy.140
  25.7 2.9 collective-permute-start.5
  29.4 44.3 %shard_map.441 = (bf16[4,256,512]{2,1,0:T(8,128)(2,1)}, bf16[4,128,1024]{2,1,0:T(8,128)(2,1)}, f32[4,1,2560]{2,1,0:T(1,128)}) custom-call(bf16[256,512]{1,0:T(8,128)(2,1)} %refs_0_.1, bf16[128,1024]{1,0:T(8,128)(2,1)} %refs_1_.1, f32[1,2560]{1,0:T(1,128)} %broadcast_in_dim.78.refs_2_), custom_call_target="tpu_custom_call" | custom-call | tf_op jit(solution)/shard_map/pallas_call | solution.py:98
  82.6 12.0 %shard_map.442 = bf16[8,128,128]{2,1,0:T(8,128)(2,1)} custom-call(bf16[8,128,128]{2,1,0:T(8,128)(2,1)} %bitcast_bitcast_fusion.x_ref), custom_call_target="tpu_custom_call" | custom-call | tf_op jit(solution)/shard_map/pallas_call | solution.py:209
  94.6 3.1 constant_dynamic-slice_fusion.3
  98.2 5.9 shard_map.443
  104.1 8.6 %shard_map.444 = bf16[8,128,128]{2,1,0:T(8,128)(2,1)} custom-call(bf16[8,128,128]{2,1,0:T(8,128)(2,1)} %bitcast.333), custom_call_target="tpu_custom_call" | custom-call | tf_op jit(solution)/shard_map/pallas_call | solution.py:209
  113.8 3.3 fusion.59
  120.6 3.1 collective-permute-start.1
  123.8 32.8 %shard_map.445 = (bf16[4,128,1024]{2,1,0:T(8,128)(2,1)}, bf16[4,128,1024]{2,1,0:T(8,128)(2,1)}) custom-call(bf16[128,1024]{1,0:T(8,128)(2,1)} %add_convert_fusion.4.refs_0_, bf16[128,1024]{1,0:T(8,128)(2,1)} %bitcast.307), custom_call_target="tpu_custom_call" | custom-call | tf_op jit(solution)/shard_map/pallas_call | solution.py:98
  164.9 3.9 copy.141
  176.5 3.6 add_convert_fusion.1
  180.1 2.7 reshape.407
  185.0 17.7 %shard_map.446 = bf16[8,3,128,128]{3,2,1,0:T(8,128)(2,1)} custom-call(bf16[8,3,128,128]{3,2,1,0:T(8,128)(2,1)} %bitcast.302), custom_call_target="tpu_custom_call" | custom-call | tf_op jit(solution)/shard_map/pallas_call | solution.py:98
  204.7 6.4 shard_map.447
  212.8 12.4 %shard_map.448 = bf16[8,1,128,128]{3,2,1,0:T(8,128)(2,1)} custom-call(bf16[8,1,128,128]{3,2,1,0:T(8,128)(2,1)} %bitcast.325), custom_call_target="tpu_custom_call" | custom-call | tf_op jit(solution)/shard_map/pallas_call | solution.py:98
  229.1 15.0 %shard_map.449 = bf16[4,128,1024]{2,1,0:T(8,128)(2,1)} custom-call(bf16[4,128,1024]{2,1,0:T(8,128)(2,1)} %bitcast.294), custom_call_target="tpu_custom_call" | custom-call | tf_op jit(solution)/shard_map/pallas_call | solution.py:98
  246.8 14.9 %shard_map.450 = bf16[4,128,1024]{2,1,0:T(8,128)(2,1)} custom-call(bf16[128,1024]{1,0:T(8,128)(2,1)} %add_convert_fusion.3.refs_0_), custom_call_target="tpu_custom_call" | custom-call | tf_op jit(solution)/shard_map/pallas_call | solution.py:98
  261.7 3.2 fusion.71
  265.0 7.4 %convert_reduce_fusion.4 = (f32[1024]{0:T(1024)S(1)}, bf16[512,1024]{1,0:T(8,128)(2,1)S(1)}, f32[512,1024]{1,0:T(8,128)}) fusion(f32[512,1024]{1,0:T(8,128)S(1)} %fusion.71, f32[1024]{0:T(1024)S(1)} %copy-done.31, bf16[512,1024]{1,0:T(8,128)(2,1)S(1)} %bitcast.380, bf16[1024,1024]{1,0:T(8,128)(2,1)S(1)} %copy-done), kind=kOutput, calls=%fused_computation.9 | convolution fusion | flops 1113062400 | bytes 8396800 | tf_op jit(solution)/shard_map/dot_general | solution.py:401
  275.2 4.2 convolution_convert_fusion.7
  279.4 14.9 %shard_map.451 = bf16[4,128,1024]{2,1,0:T(8,128)(2,1)} custom-call(bf16[4,128,1024]{2,1,0:T(8,128)(2,1)} %bitcast.327), custom_call_target="tpu_custom_call" | custom-call | tf_op jit(solution)/shard_map/pallas_call | solution.py:98
  298.3 13.3 %shard_map.452 = bf16[4,128,1024]{2,1,0:T(8,128)(2,1)} custom-call(bf16[128,1024]{1,0:T(8,128)(2,1)} %get-tuple-element.186.refs_0_), custom_call_target="tpu_custom_call" | custom-call | tf_op jit(solution)/shard_map/pallas_call | solution.py:98
  317.6 2.7 multiply_convert_fusion
  323.5 19.6 %shard_map.453 = (bf16[8,1,128,128]{3,2,1,0:T(8,128)(2,1)}, bf16[4,128,1024]{2,1,0:T(8,128)(2,1)}, bf16[4,32,1024]{2,1,0:T(8,128)(2,1)}) custom-call(bf16[8,1,128,128]{3,2,1,0:T(8,128)(2,1)} %bitcast.332, bf16[4,128,1024]{2,1,0:T(8,128)(2,1)} %bitcast.326, bf16[4,32,1024]{2,1,0:T(8,128)(2,1)} %reduce-scatter.4.cloned.1.call-done.refs_2_), custom_call_target="tpu_custom_call" | custom-call | tf_op jit(solution)/shard_map/pallas_call | solution.py:98
  343.2 9.2 %shard_map.454 = (bf16[1024,128]{1,0:T(8,128)(2,1)}, bf16[1024,128]{1,0:T(8,128)(2,1)}, bf16[1024,128]{1,0:T(8,128)(2,1)}) custom-call(bf16[1024,128]{1,0:T(8,128)(2,1)} %bitcast.315, bf16[1024,128]{1,0:T(8,128)(2,1)} %bitcast.313, bf16[1024,128]{1,0:T(8,128)(2,1)} %bitcast.311, bf16[1024,128]{1,0:T(8,128)(2,1)} %bitcast.338, ...), custom_call_target="tpu_custom_call" | custom-call | tf_op jit(solution)/shard_map/pallas_call | solution.py:466
  354.5 15.6 %shard_map.455 = bf16[8,3,128,128]{3,2,1,0:T(8,128)(2,1)} custom-call(bf16[8,3,128,128]{3,2,1,0:T(8,128)(2,1)} %pad_maximum_fusion.refs_0_), custom_call_target="tpu_custom_call" | custom-call | tf_op jit(solution)/shard_map/pallas_call | solution.py:98
  373.3 3.7 convolution_convert_fusion.2
  377.1 3.1 convolution_convert_fusion.5
  380.2 16.0 %shard_map.456 = bf16[4,128,1024]{2,1,0:T(8,128)(2,1)} custom-call(bf16[4,128,1024]{2,1,0:T(8,128)(2,1)} %bitcast.328), custom_call_target="tpu_custom_call" | custom-call | tf_op jit(solution)/shard_map/pallas_call | solution.py:98
  400.1 16.3 %shard_map.457 = bf16[8,128,128]{2,1,0:T(8,128)(2,1)} custom-call(bf16[8,128,128]{2,1,0:T(8,128)(2,1)} %bitcast.331), custom_call_target="tpu_custom_call" | custom-call | tf_op jit(solution)/shard_map/pallas_call | solution.py:209
  416.5 12.3 %shard_map.458 = (bf16[1024,128]{1,0:T(8,128)(2,1)}, bf16[8192,128]{1,0:T(8,128)(2,1)}) custom-call(bf16[1024,128]{1,0:T(8,128)(2,1)} %bitcast.309, bf16[1024,128]{1,0:T(8,128)(2,1)} %bitcast.324, bf16[8192,128]{1,0:T(8,128)(2,1)} %bitcast.282), custom_call_target="tpu_custom_call" | custom-call | tf_op jit(solution)/shard_map/pallas_call | solution.py:378
  430.4 4.2 convolution_convert_fusion
  434.5 11.0 %shard_map.459 = bf16[8,128,128]{2,1,0:T(8,128)(2,1)} custom-call(bf16[8,128,128]{2,1,0:T(8,128)(2,1)} %bitcast.334), custom_call_target="tpu_custom_call" | custom-call | tf_op jit(solution)/shard_map/pallas_call | solution.py:209
  454.3 31.1 %shard_map.460 = (bf16[4,256,512]{2,1,0:T(8,128)(2,1)}, bf16[4,128,1024]{2,1,0:T(8,128)(2,1)}, f32[4,1,2816]{2,1,0:T(1,128)}, bf16[4,32,768]{2,1,0:T(8,128)(2,1)}) custom-call(bf16[4,256,512]{2,1,0:T(8,128)(2,1)} %bitcast.299, bf16[4,128,1024]{2,1,0:T(8,128)(2,1)} %bitcast.300, f32[4,1,2816]{2,1,0:T(1,128)} %copy-done.29, ...), custom_call_target="tpu_custom_call" | custom-call | tf_op jit(solution)/shard_map/pallas_call | solution.py:98
  494.8 32.5 %psum.36 = f32[4352]{0:T(1024)S(1)} all-reduce(f32[4352]{0:T(1024)S(1)} %pad_maximum_fusion.1), channel_id=1, replica_groups=mesh['seq'=8,'utt'=4] {'seq'}, use_global_device_ids=true, to_apply=%region_42.43 | all-reduce | flops 4352 | bytes 34816 | tf_op jit(solution)/shard_map/psum | solution.py:771
  529.1 4.1 convert_bitcast_fusion.1
  533.2 5.4 copy.154
  538.6 5.7 copy.156
  544.3 30.5 %all-reduce.3.cloned.1.call-done = (bf16[256,512]{1,0:T(8,128)(2,1)}, bf16[128,1024]{1,0:T(8,128)(2,1)}, bf16[256,1024]{1,0:T(8,128)(2,1)}, bf16[1024,1024]{1,0:T(8,128)(2,1)}) async-done(((bf16[256,512]{1,0:T(8,128)(2,1)}, bf16[128,1024]{1,0:T(8,128)(2,1)}, bf16[256,1024]{1,0:T(8,128)(2,1)}, bf16[1024,1024]{1,0:T(8,128)(2,1)}), (bf16[256,512]{1,0:T(8,128)(2,1)}, bf16[128,1024]{1,0:T(8,128)(2,1)}, ...) | async-done | bytes 3145744 | tf_op jit(solution)/shard_map/psum | solution.py:771
  583.1 18.3 %all-gather.6.cloned.1.call-done = bf16[4,256,768]{2,1,0:T(8,128)(2,1)} async-done(((bf16[4,32,768]{2,1,0:T(8,128)(2,1)}), bf16[4,256,768]{2,1,0:T(8,128)(2,1)}) %all-gather.6.cloned.1.call-update) | async-done | bytes 1572880 | tf_op jit(solution)/shard_map/all_gather | solution.py:764
  601.4 3.1 copy.152
  604.4 3.8 copy.153
  608.2 3.7 copy.155
  611.9 37.9 %all-gather.4.cloned.1.call-done = bf16[16384,128]{1,0:T(8,128)(2,1)} async-done(((bf16[2048,128]{1,0:T(8,128)(2,1)}), bf16[16384,128]{1,0:T(8,128)(2,1)}) %all-gather.4.cloned.1.call-update) | async-done | bytes 4194320 | tf_op jit(solution)/shard_map/all_gather | solution.py:711
  649.8 6.8 %copy_bitcast_fusion = f32[128,64,256]{2,1,0:T(8,128)} fusion(bf16[2,128,64,128]{3,2,1,0:T(8,128)(2,1)} %bitcast.291), kind=kLoop, calls=%fused_computation | loop fusion | flops 2097152 | bytes 12582912 | tf_op jit(solution)/shard_map/convert_element_type | solution.py:716
  (256 shorter events, 106.1 us)
Async XLA Ops:
  7.2 257.8 %copy-start = (bf16[1024,1024]{1,0:T(8,128)(2,1)S(1)}, bf16[1024,1024]{1,0:T(8,128)(2,1)}, u32[]{:S(2)}) copy-start(bf16[1024,1024]{1,0:T(8,128)(2,1)} %param.50) | copy-start | bytes 6291460
  7.2 316.3 %reduce-scatter.4.cloned.1.call-start = ((), (), s32[]{:S(2)}) async-start(), calls=%async_computation.3 | async-start | bytes 2359296 | tf_op jit(solution)/shard_map/reduce_scatter | solution.py:669
  14.4 103.9 %collective-permute-start = (bf16[1,256,768]{1,2,0:T(8,128)(2,1)}, bf16[1,256,768]{1,2,0:T(8,128)(2,1)}, u32[]{:S(2)}, u32[]{:S(2)}) collective-permute-start(bf16[1,256,768]{1,2,0:T(8,128)(2,1)} %constant_dynamic-slice_fusion.2), channel_id=1, source_target_pairs={{0,1},{1,2},{2,3},{3,0},{4,5},{5,6},{6,7},{7,4},{8,9},{9,10},{10,1... | collective-permute-start | bytes 1179656 | tf_op jit(solution)/shard_map/ppermute | solution.py:231
  21.4 7.2 %copy-start.45 = (f32[128]{0:T(128)S(1)}, f32[128]{0:T(128)}, u32[]{:S(2)}) copy-start(f32[128]{0:T(128)} %param.30) | copy-start | bytes 1540
  21.4 7.2 %copy-start.46 = (f32[128]{0:T(128)S(1)}, f32[128]{0:T(128)}, u32[]{:S(2)}) copy-start(f32[128]{0:T(128)} %param.31) | copy-start | bytes 1540
  21.4 7.2 %copy-start.47 = (f32[128]{0:T(128)S(1)}, f32[128]{0:T(128)}, u32[]{:S(2)}) copy-start(f32[128]{0:T(128)} %param.32) | copy-start | bytes 1540
  21.4 7.2 %copy-start.48 = (f32[128]{0:T(128)S(1)}, f32[128]{0:T(128)}, u32[]{:S(2)}) copy-start(f32[128]{0:T(128)} %param.33) | copy-start | bytes 1540
  21.4 7.2 %copy-start.32 = (f32[256]{0:T(256)S(1)}, f32[256]{0:T(256)}, u32[]{:S(2)}) copy-start(f32[256]{0:T(256)} %param.35) | copy-start | bytes 3076
  21.4 7.3 %copy-start.33 = (f32[256]{0:T(256)S(1)}, f32[256]{0:T(256)}, u32[]{:S(2)}) copy-start(f32[256]{0:T(256)} %param.36) | copy-start | bytes 3076
  21.4 7.3 %copy-start.34 = (f32[256]{0:T(256)S(1)}, f32[256]{0:T(256)}, u32[]{:S(2)}) copy-start(f32[256]{0:T(256)} %param.39) | copy-start | bytes 3076
  21.4 7.3 %copy-start.35 = (f32[256]{0:T(256)S(1)}, f32[256]{0:T(256)}, u32[]{:S(2)}) copy-start(f32[256]{0:T(256)} %param.40) | copy-start | bytes 3076
  21.5 7.3 %copy-start.36 = (f32[256]{0:T(256)S(1)}, f32[256]{0:T(256)}, u32[]{:S(2)}) copy-start(f32[256]{0:T(256)} %param.45) | copy-start | bytes 3076
  21.5 7.3 %copy-start.37 = (f32[256]{0:T(256)S(1)}, f32[256]{0:T(256)}, u32[]{:S(2)}) copy-start(f32[256]{0:T(256)} %param.46) | copy-start | bytes 3076
  21.5 7.3 %copy-start.38 = (f32[256]{0:T(256)S(1)}, f32[256]{0:T(256)}, u32[]{:S(2)}) copy-start(f32[256]{0:T(256)} %param.47) | copy-start | bytes 3076
  21.5 7.3 %copy-start.39 = (f32[256]{0:T(256)S(1)}, f32[256]{0:T(256)}, u32[]{:S(2)}) copy-start(f32[256]{0:T(256)} %param.51) | copy-start | bytes 3076
  21.5 53.7 %copy-start.42 = (s32[1,85]{1,0:T(1,128)S(1)}, s32[1,85]{1,0:T(1,128)}, u32[]{:S(2)}) copy-start(s32[1,85]{1,0:T(1,128)} %param.27) | copy-start | bytes 1024
  24.1 135.1 %collective-permute-start.3 = (bf16[1,256,1024]{1,2,0:T(8,128)(2,1)}, bf16[1,256,1024]{1,2,0:T(8,128)(2,1)}, u32[]{:S(2)}, u32[]{:S(2)}) collective-permute-start(bf16[1,256,1024]{1,2,0:T(8,128)(2,1)} %get-tuple-element.209), channel_id=1, source_target_pairs={{0,1},{1,2},{2,3},{3,0},{4,5},{5,6},{6,7},{7,4},{8,9},{9,10},{10,1... | collective-permute-start | bytes 1572872 | tf_op jit(solution)/shard_map/ppermute | solution.py:231
  25.6 135.5 %collective-permute-start.4 = (bf16[1,256,1024]{1,2,0:T(8,128)(2,1)}, bf16[1,256,1024]{1,2,0:T(8,128)(2,1)}, u32[]{:S(2)}, u32[]{:S(2)}) collective-permute-start(bf16[1,256,1024]{1,2,0:T(8,128)(2,1)} %get-tuple-element.208), channel_id=1, source_target_pairs={{0,2},{1,3},{2,0},{3,1},{4,6},{5,7},{6,4},{7,5},{8,10},{9,11},{10,... | collective-permute-start | bytes 1572872 | tf_op jit(solution)/shard_map/ppermute | solution.py:231
  25.7 137.3 %collective-permute-start.5 = (bf16[1,256,1024]{1,2,0:T(8,128)(2,1)}, bf16[1,256,1024]{1,2,0:T(8,128)(2,1)}, u32[]{:S(2)}, u32[]{:S(2)}) collective-permute-start(bf16[1,256,1024]{1,2,0:T(8,128)(2,1)} %get-tuple-element.207), channel_id=1, source_target_pairs={{0,3},{1,0},{2,1},{3,2},{4,7},{5,4},{6,5},{7,6},{8,11},{9,8},{10,9... | collective-permute-start | bytes 1572872 | tf_op jit(solution)/shard_map/ppermute | solution.py:231
  73.7 6.7 %copy-start.14 = (bf16[4,128,1024]{2,1,0:T(8,128)(2,1)S(1)}, bf16[4,128,1024]{2,1,0:T(8,128)(2,1)}, u32[]{:S(2)}) copy-start(bf16[4,128,1024]{2,1,0:T(8,128)(2,1)} %get-tuple-element.46) | copy-start | bytes 3145732
  94.6 3.1 copy-start.44
  113.8 6.8 %copy-start.7 = (f32[8,16,8,128]{3,2,1,0:T(8,128)}, f32[8,16,8,128]{3,2,1,0:T(8,128)S(1)}, u32[]{:S(2)}) copy-start(f32[8,16,8,128]{3,2,1,0:T(8,128)S(1)} %get-tuple-element.218) | copy-start | bytes 1572868
  113.8 6.8 %copy-start.9 = (f32[8,16,8,128]{3,2,1,0:T(8,128)}, f32[8,16,8,128]{3,2,1,0:T(8,128)S(1)}, u32[]{:S(2)}) copy-start(f32[8,16,8,128]{3,2,1,0:T(8,128)S(1)} %get-tuple-element.219) | copy-start | bytes 1572868
  117.1 6.6 copy-start.40
  117.1 6.6 copy-start.41
  120.6 48.2 %collective-permute-start.1 = (bf16[1,256,768]{1,2,0:T(8,128)(2,1)}, bf16[1,256,768]{1,2,0:T(8,128)(2,1)S(1)}, u32[]{:S(2)}, u32[]{:S(2)}) collective-permute-start(bf16[1,256,768]{1,2,0:T(8,128)(2,1)} %get-tuple-element.211), channel_id=1, source_target_pairs={{0,2},{1,3},{2,0},{3,1},{4,6},{5,7},{6,4},{7,5},{8,10},{9,11},{10,... | collective-permute-start | bytes 1179656 | tf_op jit(solution)/shard_map/ppermute | solution.py:231
  156.6 13.0 %collective-permute-start.2 = (bf16[1,256,768]{1,2,0:T(8,128)(2,1)}, bf16[1,256,768]{1,2,0:T(8,128)(2,1)}, u32[]{:S(2)}, u32[]{:S(2)}) collective-permute-start(bf16[1,256,768]{1,2,0:T(8,128)(2,1)} %get-tuple-element.210), channel_id=1, source_target_pairs={{0,3},{1,0},{2,1},{3,2},{4,7},{5,4},{6,5},{7,6},{8,11},{9,8},{10,9... | collective-permute-start | bytes 1179656 | tf_op jit(solution)/shard_map/ppermute | solution.py:231
  226.5 19.0 %copy-start.16 = (bf16[2,4,1,128,128]{4,0,3,1,2:T(2,128)(2,1)}, bf16[2,4,1,128,128]{4,0,3,1,2:T(2,128)(2,1)S(1)}, u32[]{:S(2)}) copy-start(bf16[2,4,1,128,128]{4,0,3,1,2:T(2,128)(2,1)S(1)} %copy.139) | copy-start | bytes 786436
  261.7 3.3 copy-start.31
  261.7 3.3 copy-start.43
  265.0 7.5 %copy-start.24 = (f32[512,1024]{1,0:T(8,128)}, f32[512,1024]{1,0:T(8,128)S(1)}, u32[]{:S(2)}) copy-start(f32[512,1024]{1,0:T(8,128)S(1)} %fusion.71) | copy-start | bytes 6291460
  265.0 7.5 %copy-start.26 = (bf16[4,128,1024]{2,1,0:T(8,128)(2,1)S(1)}, bf16[4,128,1024]{2,1,0:T(8,128)(2,1)}, u32[]{:S(2)}) copy-start(bf16[4,128,1024]{2,1,0:T(8,128)(2,1)} %shard_map.450) | copy-start | bytes 3145732
  272.5 2.7 copy-start.49
  275.2 179.1 %reduce-scatter.6.cloned.1.call-start = ((), (), s32[]{:S(2)}) async-start(), calls=%async_computation.4 | async-start | bytes 1769472 | tf_op jit(solution)/shard_map/reduce_scatter | solution.py:695
  294.3 3.1 copy-start.18
  373.3 3.8 copy-start.4
  377.1 113.4 %reduce-scatter.8.cloned.1.call-start = ((), (), s32[]{:S(2)}) async-start(), calls=%async_computation.5 | async-start | bytes 2621440 | tf_op jit(solution)/shard_map/reduce_scatter | solution.py:708
  416.5 12.6 %copy-start.12 = (bf16[4,128,1024]{2,1,0:T(8,128)(2,1)S(1)}, bf16[4,128,1024]{2,1,0:T(8,128)(2,1)}, u32[]{:S(2)}) copy-start(bf16[4,128,1024]{2,1,0:T(8,128)(2,1)} %shard_map.452) | copy-start | bytes 3145732
  416.5 12.6 %copy-start.17 = (bf16[2,4,1,128,128]{4,0,3,1,2:T(2,128)(2,1)S(1)}, bf16[2,4,1,128,128]{4,0,3,1,2:T(2,128)(2,1)}, u32[]{:S(2)}) copy-start(bf16[2,4,1,128,128]{4,0,3,1,2:T(2,128)(2,1)} %copy-done.16) | copy-start | bytes 786436
  428.8 100.3 %all-gather.8.cloned.1.call-start = ((), (), s32[]{:S(2)}) async-start(), calls=%async_computation.8 | async-start | bytes 2359296 | tf_op jit(solution)/shard_map/all_gather | solution.py:682
  445.5 3.6 copy-start.15
  449.1 125.6 %all-reduce.3.cloned.1.call-start = ((), (), s32[]{:S(2)}) async-start(), calls=%async_computation.9 | async-start | bytes 6291456 | tf_op jit(solution)/shard_map/psum | solution.py:771
  489.8 2.6 copy-start.22
  489.8 111.6 %all-gather.6.cloned.1.call-start = ((), (), s32[]{:S(2)}) async-start(), calls=%async_computation.7 | async-start | bytes 1769472 | tf_op jit(solution)/shard_map/all_gather | solution.py:764
  490.4 159.4 %all-gather.4.cloned.1.call-start = ((), (), s32[]{:S(2)}) async-start(), calls=%async_computation.6 | async-start | bytes 4718592 | tf_op jit(solution)/shard_map/all_gather | solution.py:711
  491.6 3.1 copy-start.30
  574.7 5.9 copy-start.23
  649.8 6.8 %copy-start.1 = (bf16[1024,1024]{1,0:T(8,128)(2,1)S(1)}, bf16[1024,1024]{1,0:T(8,128)(2,1)}, u32[]{:S(2)}) copy-start(bf16[1024,1024]{1,0:T(8,128)(2,1)} %param.50) | copy-start | bytes 6291460
  (15 other events, 24.0 us)
Sparse Core Ops, SparseCore 0:
  275.3 36.4 reduce-scatter.3
  377.2 40.2 reduce-scatter.5
  429.0 32.9 reduce-scatter.7
  463.5 28.8 all-gather.7
  496.8 77.8 all-reduce.2
  576.3 25.0 all-gather.5
  603.0 46.6 all-gather.3

commit v2 on v1

--- a/solution.py
+++ b/solution.py
@@ -24,17 +24,63 @@
 VMEM_BYTES = 56 * 1024 * 1024
 
 
+class Item:
+    def __init__(self, array, axis, kind, parts=1, shared=False):
+        size = lax.axis_size(axis)
+        if kind == "columns" and (array.shape[1] // parts // size) % 128:
+            rows, wide = array.shape[0], array.shape[1] // parts // size
+            blocks = array.reshape(rows, parts, size, wide).transpose(2, 0, 1, 3)
+            array, kind, parts = blocks.reshape(size, rows, parts * wide), "blocks", 1
+        self.array, self.axis, self.kind, self.shared, self.size = array, axis, kind, shared, size
+        self.parts = parts
+        if kind == "gather":
+            self.shape = (size,) + array.shape
+        elif kind == "blocks":
+            self.shape = array.shape
+        else:
+            self.wide = array.shape[1] // parts // size
+            self.shape = (size, array.shape[0], parts * self.wide)
+
+    def source(self, ref, peer, part, rows):
+        if self.kind == "gather":
+            return ref if rows is None else ref.at[rows]
+        if self.kind == "blocks":
+            return ref.at[peer] if rows is None else ref.at[peer, rows]
+        first = pl.multiple_of(part * self.size * self.wide + peer * self.wide, 128)
+        rows = slice(None) if rows is None else rows
+        return ref.at[rows, pl.ds(first, self.wide)]
+
+    def target(self, ref, slot, part, rows):
+        if self.kind != "columns":
+            return ref.at[slot] if rows is None else ref.at[slot, rows]
+        rows = slice(None) if rows is None else rows
+        return ref.at[slot, rows, pl.ds(part * self.wide, self.wide)]
+
+    def half(self, core):
+        if not self.shared:
+            return None
+        rows = self.shape[1] // 2
+        return pl.ds(pl.multiple_of(core * rows, rows), rows)
+
+
 def exchange(items, collective_id):
+    items = [Item(*item) if isinstance(item, tuple) else item for item in items]
     count = len(items)
     axes = []
-    for _, axis, _ in items:
-        if axis not in axes:
-            axes.append(axis)
+    for item in items:
+        if item.axis not in axes:
+            axes.append(item.axis)
+    any_shared = any(item.shared for item in items)
+    assert not (any_shared and "seq" in axes and len(axes) == 1)
+    greet_core = any_shared and "seq" not in axes
     sizes = {axis: lax.axis_size(axis) for axis in axes}
 
     def kernel(*refs):
         ins, outs = refs[:count], refs[count : 2 * count]
-        sems = refs[2 * count :]
+        sems = [refs[(2 + n) * count : (3 + n) * count] for n in range(5)]
+        me_seq = lax.axis_index("seq")
+        core = lax.rem(me_seq, 2)
+        sibling = {"seq": me_seq + 1 - 2 * core}
         barrier = pltpu.get_barrier_semaphore()
         for axis in axes:
             me = lax.axis_index(axis)
@@ -47,64 +93,640 @@
                 return carry
 
             lax.fori_loop(1, sizes[axis], greet, 0)
+        if greet_core:
+            pl.semaphore_signal(barrier, inc=1, device_id=sibling, device_id_type=MESH)
         own = []
-        for n, (_, axis, gather) in enumerate(items):
-            me = lax.axis_index(axis)
-            source = ins[n] if gather else ins[n].at[me]
-            copy = pltpu.make_async_copy(source, outs[n].at[me], sems[3 * n + 2])
-            copy.start()
-            own.append(copy)
-        pl.semaphore_wait(barrier, sum(sizes[axis] - 1 for axis in axes))
-
-        def copy_to(n, i, slot_is_mine):
-            _, axis, gather = items[n]
-            me = lax.axis_index(axis)
-            peer = lax.rem(me + i, sizes[axis])
-            slot = me if slot_is_mine else peer
+        for n, item in enumerate(items):
+            me = lax.axis_index(item.axis)
+            for part in range(item.parts):
+                copy = pltpu.make_async_copy(
+                    item.source(ins[n], me, part, None),
+                    item.target(outs[n], me, part, None),
+                    sems[2][n].at[part],
+                )
+                copy.start()
+                own.append(copy)
+        pl.semaphore_wait(barrier, sum(sizes[axis] - 1 for axis in axes) + int(greet_core))
+
+        def copy_to(n, i, part, outgoing):
+            item = items[n]
+            me = lax.axis_index(item.axis)
+            peer = lax.rem(me + i, item.size)
+            slot = me if outgoing else peer
             return pltpu.make_async_remote_copy(
-                src_ref=ins[n] if gather else ins[n].at[peer],
-                dst_ref=outs[n].at[slot],
-                send_sem=sems[3 * n].at[peer],
-                recv_sem=sems[3 * n + 1].at[slot],
-                device_id={axis: peer},
+                src_ref=item.source(ins[n], peer, part, item.half(core)),
+                dst_ref=item.target(outs[n], slot, part, item.half(core)),
+                send_sem=sems[0][n].at[peer, part],
+                recv_sem=sems[1][n].at[slot, part],
+                device_id={item.axis: peer},
                 device_id_type=MESH,
             )
 
-        for n, (_, axis, _) in enumerate(items):
-
-            def send(i, carry, n=n):
-                copy_to(n, i, True).start()
+        def hand_over(n, slot, which):
+            item = items[n]
+            rows = item.half(which)
+            return pltpu.make_async_remote_copy(
+                src_ref=outs[n].at[slot, rows],
+                dst_ref=outs[n].at[slot, rows],
+                send_sem=sems[3][n].at[slot],
+                recv_sem=sems[4][n].at[slot],
+                device_id=sibling,
+                device_id_type=MESH,
+            )
+
+        for n, item in enumerate(items):
+
+            def send(i, carry, n=n, item=item):
+                for part in range(item.parts):
+                    copy_to(n, i, part, True).start()
                 return carry
 
-            lax.fori_loop(1, sizes[axis], send, 0)
-        for n, (_, axis, _) in enumerate(items):
-            own[n].wait()
-
-            def finish(i, carry, n=n):
-                copy_to(n, i, False).wait()
+            lax.fori_loop(1, item.size, send, 0)
+        for copy in own:
+            copy.wait()
+        for n, item in enumerate(items):
+
+            def arrived(i, carry, n=n, item=item):
+                for part in range(item.parts):
+                    copy_to(n, i, part, False).wait_recv()
+                if item.shared:
+                    hand_over(n, lax.rem(lax.axis_index(item.axis) + i, item.size), core).start()
                 return carry
 
-            lax.fori_loop(1, sizes[axis], finish, 0)
-
-    shapes, scratch = [], []
-    for array, axis, gather in items:
-        shape = ((sizes[axis],) + array.shape) if gather else array.shape
-        shapes.append(jax.ShapeDtypeStruct(shape, array.dtype))
-        scratch += [
-            pltpu.SemaphoreType.DMA((sizes[axis],)),
-            pltpu.SemaphoreType.DMA((sizes[axis],)),
-            pltpu.SemaphoreType.DMA,
-        ]
+            lax.fori_loop(1, item.size, arrived, 0)
+        for n, item in enumerate(items):
+
+            def finish(i, carry, n=n, item=item):
+                for part in range(item.parts):
+                    copy_to(n, i, part, False).wait_send()
+                if item.shared:
+                    slot = lax.rem(lax.axis_index(item.axis) + i, item.size)
+                    hand_over(n, slot, core).wait_send()
+                    hand_over(n, slot, 1 - core).wait_recv()
+                return carry
+
+            lax.fori_loop(1, item.size, finish, 0)
+
+    dma = pltpu.SemaphoreType.DMA
     return pl.pallas_call(
         kernel,
-        out_shape=shapes,
+        out_shape=[jax.ShapeDtypeStruct(item.shape, item.array.dtype) for item in items],
         in_specs=[pl.BlockSpec(memory_space=pl.ANY)] * count,
         out_specs=[pl.BlockSpec(memory_space=pl.ANY)] * count,
-        scratch_shapes=scratch,
+        scratch_shapes=(
+            [dma((item.size, item.parts)) for item in items] * 2
+            + [dma((item.parts,)) for item in items]
+            + [dma((item.size,)) for item in items] * 2
+        ),
         compiler_params=pltpu.CompilerParams(
             collective_id=collective_id, has_side_effects=True
         ),
-    )(*[array for array, _, _ in items])
+    )(*[item.array for item in items])
+
+
+HOP_LAG = 3
+CHUNK_ROWS = 128
+CHUNK_LANES = 256
+
+
+def sum_gradients(taps, out, qkv, conv, proj, vectors, up_sum, layer_parts, collective_id):
+    num_seq, num_utt = lax.axis_size("seq"), lax.axis_size("utt")
+    chips, blocks = num_seq // 2, num_seq // num_utt
+    width = taps.shape[1]
+    tap_rows = 2 * CHUNK_ROWS
+    tap_half = taps.shape[0] // 2 // tap_rows
+    column = out.shape[0]
+    half = column // 2
+    assert half == CHUNK_ROWS and width == CHUNK_ROWS and out.shape[1] % CHUNK_LANES == 0
+    proj_half = proj.shape[0] // num_utt // 2
+    proj_lanes = CHUNK_LANES * CHUNK_ROWS // proj_half
+    vector_half = vectors.shape[1] // 2
+    counts = [
+        blocks * tap_half,
+        out.shape[1] // CHUNK_LANES,
+        3 * num_utt * (column // CHUNK_LANES),
+        conv.shape[1] // CHUNK_LANES,
+        proj.shape[1] // proj_lanes,
+        1,
+    ]
+    assert column == CHUNK_LANES
+    starts = [sum(counts[:i]) for i in range(len(counts))]
+    total = sum(counts)
+
+    def kernel(
+        taps_ref,
+        out_ref,
+        qkv_ref,
+        conv_ref,
+        proj_ref,
+        vec_ref,
+        up_ref,
+        layer_ref,
+        taps_o,
+        out_o,
+        qkv_o,
+        conv_o,
+        proj_o,
+        vec_o,
+        up_o,
+        layer_o,
+        own_ref,
+        got_r,
+        got_l,
+        put_r,
+        put_l,
+        taps_mate,
+        out_mate,
+        *rest,
+    ):
+        mates, stages, gots = rest[0:4], rest[4:8], rest[8:12]
+        (
+            taps_send,
+            taps_recv,
+            out_send,
+            out_recv,
+            mate_send,
+            mate_recv,
+            peer_send,
+            peer_recv,
+            way_send_r,
+            way_send_l,
+            way_recv_r,
+            way_recv_l,
+            last_send,
+            last_recv,
+            up_send,
+            up_recv,
+            hand_send,
+            hand_recv,
+            layer_send,
+            layer_recv,
+            local_sem,
+        ) = rest[12:]
+        got_refs, put_refs = (got_r, got_l), (put_r, put_l)
+        way_send, way_recv = (way_send_r, way_send_l), (way_recv_r, way_recv_l)
+        grouped = (qkv_ref, conv_ref, proj_ref, vec_ref)
+        halves = (half, half, proj_half, vector_half)
+        me, me_utt = lax.axis_index("seq"), lax.axis_index("utt")
+        z, core = me // 2, lax.rem(me, 2)
+        block = me // num_utt
+        sibling = {"seq": me + 1 - 2 * core}
+        ends = (chips - 1, 0)
+        hops = ({"seq": me + 2}, {"seq": me - 2})
+        delays = (HOP_LAG * z, HOP_LAG * (chips - 1 - z))
+
+        def remote(src, dst, send, recv, device):
+            return pltpu.make_async_remote_copy(
+                src_ref=src,
+                dst_ref=dst,
+                send_sem=send,
+                recv_sem=recv,
+                device_id=device,
+                device_id_type=MESH,
+            )
+
+        def loop(first, last, body):
+            def run(i, carry):
+                body(i)
+                return carry
+
+            lax.fori_loop(first, last, run, 0)
+
+        def peer_of(i):
+            return lax.rem(me_utt + i, num_utt)
+
+        barrier = pltpu.get_barrier_semaphore()
+
+        def signal(device):
+            pl.semaphore_signal(barrier, inc=1, device_id=device, device_id_type=MESH)
+
+        signal(sibling)
+        loop(1, num_utt, lambda i: signal({"utt": peer_of(i)}))
+        for way in range(2):
+
+            @pl.when(z != ends[way])
+            def _(way=way):
+                signal(hops[way])
+
+        pl.semaphore_wait(
+            barrier,
+            num_utt
+            + (z != ends[0]).astype(jnp.int32)
+            + (z != ends[1]).astype(jnp.int32),
+        )
+
+        def tap_place(k, which):
+            return pl.ds(pl.multiple_of((which * tap_half + k) * tap_rows, tap_rows), tap_rows)
+
+        def half_rows(size, which):
+            return pl.ds(pl.multiple_of(which * size, size), size)
+
+        def group_place(n, b, which):
+            size = halves[n]
+            if n == 3:
+                return vec_ref.at[b, half_rows(size, which)]
+            return grouped[n].at[pl.ds(pl.multiple_of((2 * b + which) * size, size), size)]
+
+        def mate_taps(k):
+            return remote(
+                taps_ref.at[tap_place(k, 1 - core)],
+                taps_mate.at[pl.ds(pl.multiple_of(k * tap_rows, tap_rows), tap_rows)],
+                taps_send.at[k],
+                taps_recv.at[k],
+                sibling,
+            )
+
+        def mate_group(n, b):
+            return remote(
+                group_place(n, b, 1 - core),
+                mates[n].at[b],
+                mate_send.at[n, b],
+                mate_recv.at[n, b],
+                sibling,
+            )
+
+        mate_out = remote(
+            out_ref.at[half_rows(half, 1 - core)], out_mate, out_send, out_recv, sibling
+        )
+
+        def peer_group(n, b, slot):
+            return remote(
+                stages[n].at[b],
+                gots[n].at[slot],
+                peer_send.at[n, b],
+                peer_recv.at[n, slot],
+                {"utt": b},
+            )
+
+        def up_copy(b, slot):
+            rows = pl.ds(pl.multiple_of(b * column + core * half, half), half)
+            lanes = pl.ds(pl.multiple_of(slot * up_ref.shape[1], 128), up_ref.shape[1])
+            return remote(
+                up_ref.at[rows],
+                up_o.at[half_rows(half, core), lanes],
+                up_send.at[b],
+                up_recv.at[slot],
+                {"utt": b},
+            )
+
+        def up_hand(slot, which):
+            lanes = pl.ds(pl.multiple_of(slot * up_ref.shape[1], 128), up_ref.shape[1])
+            place = up_o.at[half_rows(half, which), lanes]
+            return remote(place, place, hand_send.at[slot], hand_recv.at[slot], sibling)
+
+        def layer_copy(b, slot):
+            return remote(
+                layer_ref.at[b], layer_o.at[slot], layer_send.at[b], layer_recv.at[slot], {"utt": b}
+            )
+
+        loop(0, 4, lambda k: mate_taps(k).start())
+        for n in range(4):
+            loop(0, num_utt, lambda b, n=n: mate_group(n, b).start())
+        mate_out.start()
+        loop(4, tap_half, lambda k: mate_taps(k).start())
+        own_up = pltpu.make_async_copy(
+            up_ref.at[pl.ds(pl.multiple_of(me_utt * column, column), column)],
+            up_o.at[
+                :, pl.ds(pl.multiple_of(me_utt * up_ref.shape[1], 128), up_ref.shape[1])
+            ],
+            local_sem.at[0],
+        )
+        own_up.start()
+        own_layer = pltpu.make_async_copy(
+            layer_ref.at[me_utt], layer_o.at[me_utt], local_sem.at[1]
+        )
+        own_layer.start()
+
+        def hand_on(b):
+            for n in range(4):
+                mate_group(n, b).wait_recv()
+                summed = (
+                    group_place(n, b, core)[...].astype(F32) + mates[n][b].astype(F32)
+                ).astype(BF16)
+
+                @pl.when(b != me_utt)
+                def _(n=n, summed=summed):
+                    stages[n][b] = summed
+                    peer_group(n, b, me_utt).start()
+
+                @pl.when(b == me_utt)
+                def _(n=n, summed=summed):
+                    gots[n][b] = summed
+
+        def chain_copy(way, chunk):
+            return remote(
+                put_refs[way].at[chunk],
+                got_refs[way].at[chunk],
+                way_send[way].at[chunk],
+                way_recv[way].at[chunk],
+                hops[way],
+            )
+
+        def lanes_of(k, size):
+            return pl.ds(pl.multiple_of(k * size, size), size)
+
+        def load_taps(k):
+            piece = lax.rem(k, tap_half)
+
+            @pl.when(k // tap_half == block)
+            def _():
+                mate_taps(piece).wait_recv()
+                for j in range(2):
+                    first = (core * tap_half + piece) * tap_rows + j * CHUNK_ROWS
+                    mine = taps_ref[pl.ds(pl.multiple_of(first, CHUNK_ROWS), CHUNK_ROWS), :]
+                    first = piece * tap_rows + j * CHUNK_ROWS
+                    other = taps_mate[pl.ds(pl.multiple_of(first, CHUNK_ROWS), CHUNK_ROWS), :]
+                    own_ref[k, :, j * width : (j + 1) * width] = mine.astype(F32) + other.astype(
+                        F32
+                    )
+
+            @pl.when(k // tap_half != block)
+            def _():
+                own_ref[k] = jnp.zeros((CHUNK_ROWS, CHUNK_LANES), F32)
+
+        def load_out(k):
+            @pl.when(k == 0)
+            def _():
+                mate_out.wait_recv()
+
+            lanes = lanes_of(k, CHUNK_LANES)
+            own_ref[starts[1] + k] = out_ref[half_rows(half, core), lanes].astype(
+                F32
+            ) + out_mate[:, lanes].astype(F32)
+
+        def load_qkv(k):
+            source, part = k // 3, lax.rem(k, 3)
+
+            @pl.when(jnp.logical_and(part == 0, source != me_utt))
+            def _():
+                peer_group(0, source, source).wait_recv()
+
+            own_ref[starts[2] + k] = gots[0][source, :, lanes_of(part, CHUNK_LANES)].astype(F32)
+
+        def peers_sum(n, lanes):
+            total = gots[n][0, :, lanes].astype(F32)
+            for b in range(1, num_utt):
+                total = total + gots[n][b, :, lanes].astype(F32)
+            return total
+
+        def await_peers(n):
+            def wait(b):
+                @pl.when(b != me_utt)
+                def _():
+                    peer_group(n, b, b).wait_recv()
+
+            loop(0, num_utt, wait)
+
+        def load_conv(k):
+            @pl.when(k == 0)
+            def _():
+                await_peers(1)
+
+            own_ref[starts[3] + k] = peers_sum(1, lanes_of(k, CHUNK_LANES))
+
+        def load_proj(k):
+            @pl.when(k == 0)
+            def _():
+                await_peers(2)
+
+            for j in range(proj_lanes // CHUNK_LANES):
+                first = k * proj_lanes + j * CHUNK_LANES
+                lanes = pl.ds(pl.multiple_of(first, CHUNK_LANES), CHUNK_LANES)
+                own_ref[starts[4] + k, j * proj_half : (j + 1) * proj_half, :] = peers_sum(2, lanes)
+
+        def load_vectors(k):
+            await_peers(3)
+            own_ref[starts[5]] = jnp.zeros((CHUNK_ROWS, CHUNK_LANES), F32)
+            own_ref[starts[5], 0:vector_half, 0:128] = peers_sum(3, slice(None))
+
+        loads = (load_taps, load_out, load_qkv, load_conv, load_proj, load_vectors)
+
+        def place_taps(k, which):
+            lanes = lanes_of(k // tap_half, width)
+            return taps_o.at[tap_place(lax.rem(k, tap_half), which), lanes]
+
+        def place_out(k, which):
+            return out_o.at[half_rows(half, which), lanes_of(k, CHUNK_LANES)]
+
+        def place_qkv(k, which):
+            lanes = lanes_of(lax.rem(k, 3) * num_utt + k // 3, CHUNK_LANES)
+            return qkv_o.at[half_rows(half, which), lanes]
+
+        def place_conv(k, which):
+            return conv_o.at[half_rows(half, which), lanes_of(k, CHUNK_LANES)]
+
+        def place_proj(k, which):
+            return proj_o.at[half_rows(proj_half, which), lanes_of(k, proj_lanes)]
+
+        def place_vectors(k, which):
+            return vec_o.at[half_rows(vector_half, which)]
+
+        places = (place_taps, place_out, place_qkv, place_conv, place_proj, place_vectors)
+
+        def store(n, k, value):
+            if n == 0:
+                for i in range(blocks):
+
+                    @pl.when(k // tap_half == i)
+                    def _(i=i):
+                        for j in range(2):
+                            first = (core * tap_half + lax.rem(k, tap_half)) * tap_rows
+                            first = pl.multiple_of(first + j * CHUNK_ROWS, CHUNK_ROWS)
+                            taps_o[pl.ds(first, CHUNK_ROWS), i * width : (i + 1) * width] = value[
+                                :, j * width : (j + 1) * width
+                            ]
+
+            elif n == 4:
+                for j in range(proj_lanes // CHUNK_LANES):
+                    first = k * proj_lanes + j * CHUNK_LANES
+                    proj_o[
+                        half_rows(proj_half, core),
+                        pl.ds(pl.multiple_of(first, CHUNK_LANES), CHUNK_LANES),
+                    ] = value[j * proj_half : (j + 1) * proj_half]
+            elif n == 5:
+                vec_o[half_rows(vector_half, core), :] = value[0:vector_half, 0:128]
+            else:
+                places[n](k, core)[...] = value
+
+        def last_copy(n, k, which):
+            place = places[n](k, which)
+            chunk = starts[n] + k
+            return remote(place, place, last_send.at[chunk], last_recv.at[chunk], sibling)
+
+        def within(chunk, n):
+            return jnp.logical_and(chunk >= starts[n], chunk < starts[n] + counts[n])
+
+        def step(t):
+            for n in range(6):
+
+                @pl.when(within(t, n))
+                def _(n=n):
+                    loads[n](t - starts[n])
+
+            @pl.when(jnp.logical_and(t >= 3, t < 3 + num_utt))
+            def _():
+                hand_on(lax.rem(me_utt + t - 2, num_utt))
+
+            @pl.when(t == 3 + num_utt)
+            def _():
+                loop(1, num_utt, lambda i: up_copy(peer_of(i), me_utt).start())
+                loop(1, num_utt, lambda i: layer_copy(peer_of(i), me_utt).start())
+
+            for way in range(2):
+                chunk = t - delays[way]
+
+                @pl.when(jnp.logical_and(chunk >= 0, chunk < total))
+                def _(way=way, chunk=chunk):
+                    first = ends[1 - way]
+
+                    @pl.when(z != first)
+                    def _():
+                        chain_copy(way, chunk).wait_recv()
+
+                        @pl.when(z != ends[way])
+                        def _():
+                            put_refs[way][chunk] = (
+                                own_ref[chunk] + got_refs[way][chunk].astype(F32)
+                            ).astype(BF16)
+
+                    @pl.when(z == first)
+                    def _():
+                        put_refs[way][chunk] = own_ref[chunk].astype(BF16)
+                        got_refs[way][chunk] = jnp.zeros((CHUNK_ROWS, CHUNK_LANES), BF16)
+
+                    @pl.when(z != ends[way])
+                    def _():
+                        chain_copy(way, chunk).start()
+
+            done = t - HOP_LAG * (chips - 1)
+
+            @pl.when(done >= 0)
+            def _():
+                value = (
+                    own_ref[done]
+                    + got_refs[0][done].astype(F32)
+                    + got_refs[1][done].astype(F32)
+                ).astype(BF16)
+                for n in range(6):
+
+                    @pl.when(within(done, n))
+                    def _(n=n):
+                        store(n, done - starts[n], value)
+                        last_copy(n, done - starts[n], core).start()
+
+        loop(0, total + HOP_LAG * (chips - 1), step)
+
+        def up_arrived(i):
+            up_copy(peer_of(i), peer_of(i)).wait_recv()
+            up_hand(peer_of(i), core).start()
+
+        loop(1, num_utt, up_arrived)
+        own_up.wait()
+        own_layer.wait()
+
+        def sent_chunk(chunk):
+            for way in range(2):
+
+                @pl.when(z != ends[way])
+                def _(way=way):
+                    chain_copy(way, chunk).wait_send()
+
+        loop(0, total, sent_chunk)
+        for n in range(6):
+
+            def handed(k, n=n):
+                last_copy(n, k, core).wait_send()
+                last_copy(n, k, 1 - core).wait_recv()
+
+            loop(0, counts[n], handed)
+        loop(0, tap_half, lambda k: mate_taps(k).wait_send())
+
+        mate_out.wait_send()
+
+        def sent_peer(i):
+            b = peer_of(i)
+            for n in range(4):
+                peer_group(n, b, me_utt).wait_send()
+            up_copy(b, me_utt).wait_send()
+            up_hand(b, core).wait_send()
+            up_hand(b, 1 - core).wait_recv()
+            layer_copy(b, me_utt).wait_send()
+            layer_copy(b, b).wait_recv()
+
+        loop(1, num_utt, sent_peer)
+        for n in range(4):
+            loop(0, num_utt, lambda b, n=n: mate_group(n, b).wait_send())
+
+    dma = pltpu.SemaphoreType.DMA
+    vmem, anywhere = pl.BlockSpec(memory_space=pltpu.VMEM), pl.BlockSpec(memory_space=pl.ANY)
+    chunk_shape = (total, CHUNK_ROWS, CHUNK_LANES)
+    group_shapes = [
+        (num_utt, half, qkv.shape[1]),
+        (num_utt, half, conv.shape[1]),
+        (num_utt, proj_half, proj.shape[1]),
+        (num_utt, vector_half, 128),
+    ]
+    return pl.pallas_call(
+        kernel,
+        out_shape=[
+            jax.ShapeDtypeStruct(shape, BF16)
+            for shape in (
+                (taps.shape[0], blocks * width),
+                out.shape,
+                (column, num_utt * qkv.shape[1]),
+                (column, conv.shape[1]),
+                (2 * proj_half, proj.shape[1]),
+                vectors.shape[1:],
+                (column, num_utt * up_sum.shape[1]),
+                layer_parts.shape,
+            )
+        ],
+        in_specs=[vmem] * 6 + [anywhere] * 2,
+        out_specs=[vmem] * 6 + [anywhere] * 2,
+        scratch_shapes=[pltpu.VMEM(chunk_shape, F32)]
+        + [pltpu.VMEM(chunk_shape, BF16)] * 4
+        + [
+            pltpu.VMEM((taps.shape[0] // 2, width), BF16),
+            pltpu.VMEM((half, out.shape[1]), BF16),
+        ]
+        + [pltpu.VMEM(shape, BF16) for shape in group_shapes] * 3
+        + [dma((tap_half,))] * 2
+        + [dma] * 2
+        + [dma((4, num_utt))] * 4
+        + [dma((total,))] * 6
+        + [dma((num_utt,))] * 6
+        + [dma((2,))],
+        compiler_params=pltpu.CompilerParams(
+            collective_id=collective_id, has_side_effects=True, vmem_limit_bytes=VMEM_BYTES
+        ),
+    )(taps, out, qkv, conv, proj, vectors, up_sum, layer_parts)
+
+
+def sum_gradients_plain(taps, out, qkv, conv, proj, vectors, up_sum, layer_parts):
+    num_seq, num_utt = lax.axis_size("seq"), lax.axis_size("utt")
+    blocks = num_seq // num_utt
+    split = [x.reshape((num_utt, -1) + x.shape[1:]) for x in (qkv, conv, proj)]
+    split += [vectors, up_sum.reshape((num_utt, -1) + up_sum.shape[1:]), layer_parts]
+    qkv, conv, proj, vectors, up_sum, layer_parts = exchange(
+        [Item(x, "utt", "blocks") for x in split], 16
+    )
+    groups = [list(range(i * num_utt, (i + 1) * num_utt)) for i in range(blocks)]
+    share = lax.psum_scatter(
+        taps, "seq", scatter_dimension=0, axis_index_groups=groups, tiled=True
+    )
+    taps = lax.all_gather(share, "seq", axis=0, tiled=True).reshape((blocks,) + taps.shape)
+    taps = taps.transpose(1, 0, 2).reshape(taps.shape[1], -1)
+
+    def over_utt(parts):
+        return jnp.sum(parts.astype(F32), 0).astype(BF16)
+
+    out, qkv, conv, proj, vectors = lax.psum(
+        (out, qkv, over_utt(conv), over_utt(proj), over_utt(vectors)), "seq"
+    )
+    rows = qkv.shape[1]
+    qkv = qkv.reshape(num_utt, rows, 3, -1).transpose(1, 2, 0, 3).reshape(rows, -1)
+    up_sum = up_sum.transpose(1, 0, 2).reshape(rows, -1)
+    return taps, out, qkv, conv, proj, vectors, up_sum, layer_parts
 
 
 def regroup(blocks, backward, collective_id):
@@ -220,19 +842,6 @@
             collective_id=collective_id, has_side_effects=True
         ),
     )(blocks)
-
-
-def permute_all(blocks):
-    size = lax.axis_size("utt")
-    me = lax.axis_index("utt")
-    result = blocks
-    for step in range(1, size):
-        piece = lax.dynamic_index_in_dim(blocks, lax.rem(me + step, size), 0)
-        moved = lax.ppermute(piece, "utt", [(i, (i + step) % size) for i in range(size)])
-        result = lax.dynamic_update_slice_in_dim(
-            result, moved, lax.rem(me + size - step, size), 0
-        )
-    return result
 
 
 def pack_frames(wide_ref, packed_ref, rows, groups):
@@ -536,12 +1145,7 @@
     out_rows = grad_out.reshape(frames, D)
     steps_in = feats.reshape(frames, 2 * C)
 
-    qkv_blocks = qkv_weight.reshape(column, 3, num_utt, column).transpose(2, 0, 1, 3)
-    qkv_columns = permute_all(qkv_blocks.reshape(num_utt, column, 3 * column))
-    qkv_columns = qkv_columns.reshape(D, 3 * column)
     hidden = up_bias.shape[0]
-    up_blocks = up_weight.reshape(column, num_utt, hidden).transpose(1, 0, 2)
-    up_columns = permute_all(up_blocks).reshape(D, hidden)
 
     vectors = [
         conv_gain,
@@ -557,14 +1161,16 @@
         ffn_shift,
         down_bias,
     ]
-    conv_all, proj_all, vectors_all = exchange(
+    conv_all, proj_all, vectors_all, qkv_columns = exchange(
         [
-            (conv_weight, "utt", True),
-            (proj_weight, "utt", True),
-            (jnp.concatenate(vectors)[None, :], "utt", True),
+            Item(conv_weight, "utt", "gather", shared=True),
+            Item(proj_weight, "utt", "gather", shared=True),
+            Item(jnp.concatenate(vectors)[None, :], "utt", "gather"),
+            Item(qkv_weight, "utt", "columns", 3, shared=True),
         ],
         1,
     )
+    qkv_columns = qkv_columns.reshape(D, 3 * column)
     conv_all = conv_all.reshape(2 * C, C)
     proj_all = proj_all.reshape(C, D)
     whole, start = [], 0
@@ -615,11 +1221,8 @@
     pos_act, pos_pull = jax.vjp(gelu_exact, pos_pre.astype(F32))
     resid_one = embed + pos_act
     attn_norm, attn_pull = jax.vjp(layer_norm, resid_one, attn_gain, attn_shift)
-    attn_in, gout_all = exchange(
-        [(attn_norm.astype(BF16), "utt", True), (out_rows, "utt", True)], 4
-    )
+    (attn_in,) = exchange([(attn_norm.astype(BF16), "utt", "gather")], 4)
     attn_in = attn_in.reshape(rows_all, D)
-    gout_all = gout_all.reshape(rows_all, D)
 
     projected = dot(attn_in, qkv_columns).reshape(rows_all, 3, column)
     bias = jnp.stack([query_bias, jnp.zeros_like(query_bias), value_bias])
@@ -633,88 +1236,70 @@
         blocks = blocks.reshape(per_column, num_utt, parts, frames, width)
         return blocks.transpose(1, 3, 2, 0, 4).reshape(rows_all, parts * column)
 
-    (qkv_heads,) = exchange([(to_heads(projected, 3), "seq", False)], 5)
+    qkv_heads, up_columns = exchange(
+        [
+            (to_heads(projected, 3), "seq", "blocks"),
+            Item(up_weight, "utt", "columns", shared=True),
+        ],
+        5,
+    )
+    up_columns = up_columns.reshape(D, hidden)
     qkv_heads = qkv_heads.transpose(1, 0, 2, 3).reshape(3, length, width)
     queries, keys, values = qkv_heads[0], qkv_heads[1], qkv_heads[2]
     attn_f32, lse = attend(queries, keys, values)
-    (attn_rows,) = exchange(
-        [(attn_f32.astype(BF16).reshape(num_seq, 1, frames, width), "seq", False)], 6
-    )
+    attn_rows, gout_all = exchange(
+        [
+            (attn_f32.astype(BF16).reshape(num_seq, 1, frames, width), "seq", "blocks"),
+            (out_rows, "utt", "gather"),
+        ],
+        6,
+    )
+    gout_all = gout_all.reshape(rows_all, D)
     attn_flat = from_heads(attn_rows, 1)
 
     def split_rows(values):
         return values.astype(BF16).reshape(num_utt, frames, D)
 
-    (parts,) = exchange([(split_rows(dot(attn_flat, out_weight)), "utt", False)], 7)
+    (parts,) = exchange([(split_rows(dot(attn_flat, out_weight)), "utt", "blocks")], 7)
     resid_two = resid_one + jnp.sum(parts.astype(F32), 0) + out_bias
     ffn_norm, ffn_pull = jax.vjp(layer_norm, resid_two, ffn_gain, ffn_shift)
-    (ffn_in,) = exchange([(ffn_norm.astype(BF16), "utt", True)], 8)
+    (ffn_in,) = exchange([(ffn_norm.astype(BF16), "utt", "gather")], 8)
     ffn_in = ffn_in.reshape(rows_all, D)
     hidden_pre = dot(ffn_in, up_columns) + up_bias
     hidden_act, hidden_pull = jax.vjp(gelu_exact, hidden_pre)
     hidden_low = hidden_act.astype(BF16)
-    layer_parts = split_rows(dot(hidden_low, down_weight))
     (hidden_grad,) = hidden_pull(nt_dot(gout_all, down_weight))
     hidden_grad = hidden_grad.astype(BF16)
-    (back_parts,) = exchange([(split_rows(nt_dot(hidden_grad, up_columns)), "utt", False)], 9)
+    downweight_grad = inner_dot(hidden_low, gout_all).astype(BF16)
+    upweight_grad = inner_dot(ffn_in, hidden_grad).astype(BF16)
+    downweight_grad, upweight_grad, hidden_grad = lax.optimization_barrier(
+        (downweight_grad, upweight_grad, hidden_grad)
+    )
+    downweight_sum, upweight_sum = lax.psum((downweight_grad, upweight_grad), "seq")
+    (back_parts,) = exchange([(split_rows(nt_dot(hidden_grad, up_columns)), "utt", "blocks")], 9)
     ffn_back, ffngain_grad, ffnshift_grad = ffn_pull(jnp.sum(back_parts.astype(F32), 0))
     resid2_grad = out_rows.astype(F32) + ffn_back
     attn_grad_own = resid2_grad.astype(BF16)
-    (attn_grad,) = exchange([(attn_grad_own, "utt", True)], 10)
+    (attn_grad,) = exchange([(attn_grad_own, "utt", "gather")], 10)
     attn_grad = attn_grad.reshape(rows_all, D)
 
-    downweight_grad = inner_dot(hidden_low, gout_all).astype(BF16)
-    upweight_grad = inner_dot(ffn_in, hidden_grad).astype(BF16)
-    downweight_grad = lax.psum(downweight_grad, "seq").astype(F32)
-    up_share = lax.psum_scatter(
-        upweight_grad.reshape(num_utt, column, hidden), "seq", scatter_dimension=1, tiled=True
-    )
-
     out_grad = nt_dot(attn_grad, out_weight).astype(BF16)
-    out_grad_heads, layer_parts, up_share = exchange(
-        [
-            (to_heads(out_grad, 1), "seq", False),
-            (layer_parts, "utt", False),
-            (up_share, "utt", False),
-        ],
-        11,
-    )
-    upweight_grad = lax.all_gather(up_share, "seq", axis=1, tiled=True)
-    upweight_grad = upweight_grad.transpose(1, 0, 2).reshape(column, num_utt * hidden).astype(F32)
-    layer_value = resid_two + jnp.sum(layer_parts.astype(F32), 0) + down_bias
-    layer_out = layer_value.astype(BF16).reshape(1, frames, D)
+    (out_grad_heads,) = exchange([(to_heads(out_grad, 1), "seq", "blocks")], 11)
     qkv_grads = attend_back(
         queries, keys, values, out_grad_heads.reshape(length, width), attn_f32, lse
     )
     qkv_grads = jnp.stack([part.reshape(num_seq, frames, width) for part in qkv_grads], axis=1)
-    (qkv_back,) = exchange([(qkv_grads, "seq", False)], 12)
+    (qkv_back,) = exchange([(qkv_grads, "seq", "blocks")], 12)
     qkv_back = from_heads(qkv_back, 3)
-    (qkv_parts,) = exchange([(split_rows(nt_dot(qkv_back, qkv_columns)), "utt", False)], 13)
-    outweight_grad = lax.psum(inner_dot(attn_flat, attn_grad).astype(BF16), "seq").astype(F32)
+    (qkv_parts,) = exchange([(split_rows(nt_dot(qkv_back, qkv_columns)), "utt", "blocks")], 13)
+    outweight_grad = inner_dot(attn_flat, attn_grad).astype(BF16)
     qkvweight_grad = inner_dot(attn_in, qkv_back).astype(BF16)
-    qkv_share = lax.psum_scatter(
-        qkvweight_grad.reshape(num_utt, column, 3 * column),
-        "seq",
-        scatter_dimension=1,
-        tiled=True,
-    )
     attn_back, attngain_grad, attnshift_grad = attn_pull(jnp.sum(qkv_parts.astype(F32), 0))
     resid1_grad = resid2_grad + attn_back
     (pos_grad,) = pos_pull(resid1_grad)
     pos_low = pos_grad.astype(BF16)
     grads_in = regroup(to_blocks(pos_low), False, 14).reshape(length, width)
     embed_own, taps_grad = pos_backward(pos_in, grads_in, taps)
-    groups = [list(range(i * num_utt, (i + 1) * num_utt)) for i in range(per_column)]
-    taps_share = lax.psum_scatter(
-        taps_grad, "seq", scatter_dimension=0, axis_index_groups=groups, tiled=True
-    )
-    posweight_grad = lax.all_gather(taps_share, "seq", axis=0, tiled=True)
-    posweight_grad = (
-        posweight_grad.reshape(per_column, KPOS, GW, width)
-        .transpose(1, 2, 0, 3)
-        .reshape(KPOS, GW, column)
-        .astype(F32)
-    )
     embed_back = from_blocks(regroup(embed_own.reshape(num_seq, frames, width), True, 15))
     embed_grad = resid1_grad + embed_back.astype(F32)
     maskembed_grad = jnp.sum(jnp.where(masked, embed_grad, 0.0), 0)
@@ -748,34 +1333,35 @@
         jnp.sum(qkv_back[:, 2 * column :], 0, dtype=F32),
         jnp.sum(hidden_grad, 0, dtype=F32),
     ]
-    conv_parts, proj_parts, vector_parts, qkv_share = exchange(
-        [
-            (convweight_grad.astype(BF16).reshape(num_utt, -1, C), "utt", False),
-            (projweight_grad.astype(BF16).reshape(num_utt, -1, D), "utt", False),
-            (
-                jnp.concatenate([v.reshape(num_utt, 1, -1) for v in row_vectors], axis=2),
-                "utt",
-                False,
-            ),
-            (qkv_share, "utt", False),
-        ],
-        16,
-    )
-    qkvweight_grad = lax.all_gather(qkv_share, "seq", axis=1, tiled=True)
-    qkvweight_grad = (
-        qkvweight_grad.reshape(num_utt, column, 3, column)
-        .transpose(1, 2, 0, 3)
-        .reshape(column, 3 * D)
-        .astype(F32)
-    )
-    convweight_grad, projweight_grad, sums = lax.psum(
-        (
-            jnp.sum(conv_parts.astype(F32), 0).astype(BF16),
-            jnp.sum(proj_parts.astype(F32), 0).astype(BF16),
-            jnp.concatenate([jnp.sum(vector_parts, 0)[0]] + column_vectors),
-        ),
-        "seq",
-    )
+    flat = jnp.concatenate([v.reshape(num_utt, -1) for v in row_vectors], axis=1)
+    mine = jnp.concatenate(column_vectors)
+    here = jnp.arange(num_utt)[:, None] == lax.axis_index("utt")
+    flat = jnp.concatenate([flat, jnp.where(here, mine[None, :], 0.0)], axis=1)
+    flat = jnp.pad(flat, ((0, 0), (0, -flat.shape[1] % (64 * 128))))
+    flat = flat.astype(BF16).reshape(num_utt, -1, 128)
+    layer_parts = split_rows(dot(hidden_low, down_weight))
+    grads = (
+        taps_grad,
+        outweight_grad,
+        qkvweight_grad,
+        convweight_grad.astype(BF16),
+        projweight_grad.astype(BF16),
+        flat,
+        upweight_sum,
+        layer_parts,
+    )
+    if width == CHUNK_ROWS:
+        grads = sum_gradients(*grads, 16)
+    else:
+        grads = sum_gradients_plain(*grads)
+    posweight_grad = grads[0].reshape(KPOS, GW, column).astype(F32)
+    outweight_grad, qkvweight_grad, convweight_grad, projweight_grad = (
+        grad.astype(F32) for grad in grads[1:5]
+    )
+    sums = grads[5].reshape(-1).astype(F32)
+    upweight_grad = grads[6].astype(F32)
+    layer_value = resid_two + jnp.sum(grads[7].astype(F32), 0) + down_bias
+    layer_out = layer_value.astype(BF16).reshape(1, frames, D)
     outs, start = [], 0
     for vector in row_vectors:
         end = start + vector.shape[0] // num_utt
@@ -806,12 +1392,12 @@
     return (
         layer_out,
         feat_grad,
-        convweight_grad.astype(F32),
+        convweight_grad,
         convgain_grad,
         convshift_grad,
         normgain_grad,
         normshift_grad,
-        projweight_grad.astype(F32),
+        projweight_grad,
         projbias_grad,
         maskembed_grad,
         posweight_grad,
@@ -827,7 +1413,7 @@
         ffnshift_grad,
         upweight_grad,
         upbias_grad,
-        downweight_grad,
+        downweight_sum.astype(F32),
         downbias_grad,
     )
 

time: 673 us -> 562 us (0.84)
  waiting for transfers between devices: 88 us -> 0.02 us
  Pallas kernels: 329 us -> 389 us
  local copies, waits for them, and re-layouts: 87.2 us -> 45.3 us
  blocking collectives: 32.5 us -> 0 us
  starting transfers between devices: 13.7 us -> 0.04 us
    pallas_call x12, Pallas kernels: 248 us -> 311 us  [the longest x11 209 us: exchange(): pl.pallas_call(kernel, out_shape=[jax.ShapeDtypeStruct(item.shape, item.a...]
    all_gather x3 -> x0, waiting for transfers between devices: 56.2 us -> none  [the longest x1 37.9 us: shards(): posweight_grad = lax.all_gather(taps_share, 'seq', axis=0, tiled=True)]
    psum x1 -> x0, blocking collectives: 32.5 us -> none  [shards(): lax.psum((jnp.sum(conv_parts.astype(F32), 0).astype(BF16), jnp.sum(proj_p...]
    psum x1, waiting for transfers between devices: 30.5 us -> 0.01 us  [shards(): lax.psum((downweight_grad, upweight_grad), 'seq')]
    dynamic_update_slice x7 -> x0, local copies, waits for them, and re-layouts: 14.7 us -> none  [permute_all(): lax.dynamic_update_slice_in_dim(result, moved, lax.rem(me + size - step,...]
    convert_element_type x4 -> x0, local copies, waits for them, and re-layouts: 13.5 us -> none  [the longest x2 6.82 us: shards(): qkvweight_grad = qkvweight_grad.reshape(num_utt, column, 3, column).trans...]
    ppermute x6 -> x0, starting transfers between devices: 13.2 us -> none  [permute_all(): lax.ppermute(piece, 'utt', [(i, (i + step) % size) for i in range(size)])]
    unnamed x127 -> x106, local copies, waits for them, and re-layouts: 19.7 us -> 10.8 us
  transfers between devices with their start and end apart: 13 -> 1, of which waited for: 3 -> 0; matrix products, arithmetic and copies ran while one was open for 18% -> 12% of each run, Pallas kernels for 33% -> 24%
where the time goes in v2:
time: 562 us; the launch traced here: 553 us
  Pallas kernels  389 us (69%)
  other arithmetic  54.5 us (10%)
  matrix products  48.3 us (9%)
  local copies, waits for them, and re-layouts  45.3 us (8%)
  between operations  15.3 us (3%)
    pallas_call x11, Pallas kernels, exchange(): pl.pallas_call(kernel, out_shape=[jax.ShapeDtypeStruct(item.shape, item.a...  209 us
    pallas_call x1, Pallas kernels, sum_gradients(): pl.pallas_call(kernel, out_shape=[jax.ShapeDtypeStruct(shape, BF16) for s...  102 us
    pallas_call x4, Pallas kernels, regroup(): pl.pallas_call(kernel, out_shape=jax.ShapeDtypeStruct((receives,) + block...  44.3 us
    dot_general x6, matrix products, nt_dot(): lax.dot_general(a, b, (((1,), (1,)), ((), ())), preferred_element_type=F32)  21.5 us
    dot_general x6, matrix products, dot(): return jnp.dot(a, b, preferred_element_type=F32)  14.1 us
    dot_general x6, matrix products, inner_dot(): lax.dot_general(first_mat, second_mat, (((0,), (0,)), ((), ())), preferre...  12.8 us
    pallas_call x1, Pallas kernels, pos_backward(): pl.pallas_call(pos_backward_kernel, out_shape=[jax.ShapeDtypeStruct((fram...  12.2 us
  transfers between devices with their start and end apart: 1, of which 0 were waited for; matrix products, arithmetic and copies ran while one was open for 12% of the time, Pallas kernels for 24%

profile of v2, /device:TPU:0, one launch (start us, length us, event | category | flops | bytes accessed | tf_op | source)
XLA Modules:
  0.0 552.5 jit_solution(10210522392521251466)
XLA Ops:
  16.2 33.4 %shard_map.441 = (bf16[4,256,512]{2,1,0:T(8,128)(2,1)}, bf16[4,128,1024]{2,1,0:T(8,128)(2,1)}, f32[4,1,2560]{2,1,0:T(1,128)}, bf16[4,256,768]{2,1,0:T(8,128)(2,1)}) custom-call(bf16[256,512]{1,0:T(8,128)(2,1)} %refs_0_.1, bf16[128,1024]{1,0:T(8,128)(2,1)} %refs_1_.2, f32[1,2560]{1,0:T(1,128)} %broadcast_in_dim.100.refs_2_, bf16[256,3072]{1,0:T(8,128)(2,1)} %refs_3_.1), custom_call_target="tpu_custom_call" | custom-call | tf_op jit(solution)/shard_map/pallas_call | solution.py:171
  56.8 14.1 %shard_map.442 = bf16[8,128,128]{2,1,0:T(8,128)(2,1)} custom-call(bf16[8,128,128]{2,1,0:T(8,128)(2,1)} %bitcast_bitcast_fusion.x_ref), custom_call_target="tpu_custom_call" | custom-call | tf_op jit(solution)/shard_map/pallas_call | solution.py:831
  71.0 3.1 constant_dynamic-slice_fusion
  74.7 5.9 %shard_map.443 = bf16[1024,128]{1,0:T(8,128)(2,1)} custom-call(bf16[1024,128]{1,0:T(8,128)(2,1)} %bitcast.298, bf16[8192,128]{1,0:T(8,128)(2,1)} %bitcast.282, f32[1,128]{1,0:T(1,128)} %dynamic-slice_bitcast_fusion.b_ref), custom_call_target="tpu_custom_call" | custom-call | tf_op jit(solution)/shard_map/pallas_call | solution.py:924
  80.6 7.5 %shard_map.444 = bf16[8,128,128]{2,1,0:T(8,128)(2,1)} custom-call(bf16[8,128,128]{2,1,0:T(8,128)(2,1)} %bitcast.323), custom_call_target="tpu_custom_call" | custom-call | tf_op jit(solution)/shard_map/pallas_call | solution.py:831
  89.2 1.9 fusion.62
  92.2 18.4 %shard_map.445 = bf16[4,128,1024]{2,1,0:T(8,128)(2,1)} custom-call(bf16[128,1024]{1,0:T(8,128)(2,1)} %add_convert_fusion.4.refs_0_), custom_call_target="tpu_custom_call" | custom-call | tf_op jit(solution)/shard_map/pallas_call | solution.py:171
  110.7 2.6 copy.78
  113.4 3.6 add_convert_fusion.1
  117.0 2.7 reshape.406
  119.7 2.2 copy.79
  121.9 22.9 %shard_map.446 = (bf16[8,3,128,128]{3,2,1,0:T(8,128)(2,1)}, bf16[4,256,1024]{2,1,0:T(8,128)(2,1)}) custom-call(bf16[8,3,128,128]{3,2,1,0:T(8,128)(2,1)} %bitcast.295, bf16[256,4096]{1,0:T(8,128)(2,1)} %refs_1_.3), custom_call_target="tpu_custom_call" | custom-call | tf_op jit(solution)/shard_map/pallas_call | solution.py:171
  144.8 2.0 fusion.67
  146.9 6.4 %shard_map.447 = (f32[1024,128]{1,0:T(8,128)}, f32[1024,2]{1,0:T(8,128)}) custom-call(bf16[1024,128]{1,0:T(8,128)(2,1)} %bitcast.304, bf16[1024,128]{1,0:T(8,128)(2,1)} %bitcast.302, bf16[1024,128]{1,0:T(8,128)(2,1)} %bitcast.300), custom_call_target="tpu_custom_call" | custom-call | tf_op jit(solution)/shard_map/pallas_call | solution.py:1031
  155.0 18.4 %shard_map.448 = (bf16[8,1,128,128]{3,2,1,0:T(8,128)(2,1)}, bf16[4,128,1024]{2,1,0:T(8,128)(2,1)}) custom-call(bf16[8,1,128,128]{3,2,1,0:T(8,128)(2,1)} %bitcast.316, bf16[128,1024]{1,0:T(8,128)(2,1)} %bitcast.292), custom_call_target="tpu_custom_call" | custom-call | tf_op jit(solution)/shard_map/pallas_call | solution.py:171
  174.6 2.5 convolution_convert_fusion.8
  177.2 15.3 %shard_map.449 = bf16[4,128,1024]{2,1,0:T(8,128)(2,1)} custom-call(bf16[4,128,1024]{2,1,0:T(8,128)(2,1)} %bitcast.287), custom_call_target="tpu_custom_call" | custom-call | tf_op jit(solution)/shard_map/pallas_call | solution.py:171
  195.2 14.3 %shard_map.450 = bf16[4,128,1024]{2,1,0:T(8,128)(2,1)} custom-call(bf16[128,1024]{1,0:T(8,128)(2,1)} %add_convert_fusion.3.refs_0_), custom_call_target="tpu_custom_call" | custom-call | tf_op jit(solution)/shard_map/pallas_call | solution.py:171
  209.5 3.2 fusion.72
  212.8 6.2 %add_convert_fusion = (bf16[512,1024]{1,0:T(8,128)(2,1)S(1)}, f32[512,1024]{1,0:T(8,128)S(1)}) fusion(f32[512,1024]{1,0:T(8,128)S(1)} %fusion.72, f32[1024]{0:T(1024)S(1)} %copy-done.34, bf16[512,1024]{1,0:T(8,128)(2,1)S(1)} %bitcast.360, bf16[1024,1024]{1,0:T(8,128)(2,1)S(1)} %copy-done), kind=kOutput, calls=%fused_computation.6 | convolution fusion | flops 1112014848 | bytes 8392704 | tf_op jit(solution)/shard_map/dot_general | solution.py:1010
  219.6 2.6 convolution_convert_fusion.1
  222.2 2.6 convolution_convert_fusion
  224.9 4.2 convolution_convert_fusion.7
  229.1 13.6 %shard_map.451 = bf16[4,128,1024]{2,1,0:T(8,128)(2,1)} custom-call(bf16[4,128,1024]{2,1,0:T(8,128)(2,1)} %bitcast.317), custom_call_target="tpu_custom_call" | custom-call | tf_op jit(solution)/shard_map/pallas_call | solution.py:171
  246.4 13.3 %shard_map.452 = bf16[4,128,1024]{2,1,0:T(8,128)(2,1)} custom-call(bf16[128,1024]{1,0:T(8,128)(2,1)} %get-tuple-element.91.refs_0_), custom_call_target="tpu_custom_call" | custom-call | tf_op jit(solution)/shard_map/pallas_call | solution.py:171
  259.8 2.6 convolution_convert_fusion.11
  265.7 17.0 %shard_map.453 = bf16[8,1,128,128]{3,2,1,0:T(8,128)(2,1)} custom-call(bf16[8,1,128,128]{3,2,1,0:T(8,128)(2,1)} %bitcast.319), custom_call_target="tpu_custom_call" | custom-call | tf_op jit(solution)/shard_map/pallas_call | solution.py:171
  282.7 9.3 %shard_map.454 = (bf16[1024,128]{1,0:T(8,128)(2,1)}, bf16[1024,128]{1,0:T(8,128)(2,1)}, bf16[1024,128]{1,0:T(8,128)(2,1)}) custom-call(bf16[1024,128]{1,0:T(8,128)(2,1)} %bitcast.305, bf16[1024,128]{1,0:T(8,128)(2,1)} %bitcast.303, bf16[1024,128]{1,0:T(8,128)(2,1)} %bitcast.301, bf16[1024,128]{1,0:T(8,128)(2,1)} %bitcast.322, ...), custom_call_target="tpu_custom_call" | custom-call | tf_op jit(solution)/shard_map/pallas_call | solution.py:1075
  291.9 2.1 pad_maximum_fusion.refs_0_
  294.0 27.2 %shard_map.455 = bf16[8,3,128,128]{3,2,1,0:T(8,128)(2,1)} custom-call(bf16[8,3,128,128]{3,2,1,0:T(8,128)(2,1)} %pad_maximum_fusion.refs_0_), custom_call_target="tpu_custom_call" | custom-call | tf_op jit(solution)/shard_map/pallas_call | solution.py:171
  321.3 2.8 copy.123
  324.1 3.1 reshape.422
  327.2 3.7 convolution_convert_fusion.5
  330.9 15.2 %shard_map.456 = bf16[4,128,1024]{2,1,0:T(8,128)(2,1)} custom-call(bf16[4,128,1024]{2,1,0:T(8,128)(2,1)} %bitcast.318), custom_call_target="tpu_custom_call" | custom-call | tf_op jit(solution)/shard_map/pallas_call | solution.py:171
  350.5 13.5 %shard_map.457 = bf16[8,128,128]{2,1,0:T(8,128)(2,1)} custom-call(bf16[8,128,128]{2,1,0:T(8,128)(2,1)} %bitcast.321), custom_call_target="tpu_custom_call" | custom-call | tf_op jit(solution)/shard_map/pallas_call | solution.py:831
  364.0 12.2 %shard_map.458 = (bf16[1024,128]{1,0:T(8,128)(2,1)}, bf16[8192,128]{1,0:T(8,128)(2,1)}) custom-call(bf16[1024,128]{1,0:T(8,128)(2,1)} %bitcast.299, bf16[1024,128]{1,0:T(8,128)(2,1)} %bitcast.315, bf16[8192,128]{1,0:T(8,128)(2,1)} %bitcast.283), custom_call_target="tpu_custom_call" | custom-call | tf_op jit(solution)/shard_map/pallas_call | solution.py:987
  376.3 9.2 %shard_map.459 = bf16[8,128,128]{2,1,0:T(8,128)(2,1)} custom-call(bf16[8,128,128]{2,1,0:T(8,128)(2,1)} %bitcast.326), custom_call_target="tpu_custom_call" | custom-call | tf_op jit(solution)/shard_map/pallas_call | solution.py:831
  398.2 2.4 fusion.71
  402.1 2.0 multiply_reduce_fusion.7
  407.0 2.4 convolution_convert_fusion.10
  411.2 2.6 fusion.6.conv_ref
  416.6 2.2 convolution_convert_fusion.2.qkv_ref
  418.8 2.2 convolution_convert_fusion.6
  421.0 101.9 %shard_map.460 = (bf16[8192,256]{1,0:T(8,128)(2,1)}, bf16[256,1024]{1,0:T(8,128)(2,1)}, bf16[256,3072]{1,0:T(8,128)(2,1)}, bf16[256,512]{1,0:T(8,128)(2,1)}, bf1...) custom-call(bf16[8192,128]{1,0:T(8,128)(2,1)} %get-tuple-element.65., ...), custom_call_target="tpu_custom_call" | custom-call | tf_op jit(solution)/shard_map/pallas_call | solution.py:669
  529.6 6.8 %convert.80 = f32[128,64,256]{2,1,0:T(8,128)} convert(bf16[128,64,256]{2,1,0:T(8,128)(2,1)} %bitcast.284) | non-fusion elementwise | flops 2097152 | bytes 12582912 | tf_op jit(solution)/shard_map/convert_element_type | solution.py:1357
  536.4 2.0 convert_element_type.202
  539.5 2.5 convert_element_type.204
  542.0 2.5 convert_element_type.205
  (203 shorter events, 66.8 us)
Async XLA Ops:
  7.2 205.6 %copy-start = (bf16[1024,1024]{1,0:T(8,128)(2,1)S(1)}, bf16[1024,1024]{1,0:T(8,128)(2,1)}, u32[]{:S(2)}) copy-start(bf16[1024,1024]{1,0:T(8,128)(2,1)} %param.50) | copy-start | bytes 6291460
  7.2 43.8 %copy-start.37 = (s32[1,85]{1,0:T(1,128)S(1)}, s32[1,85]{1,0:T(1,128)}, u32[]{:S(2)}) copy-start(s32[1,85]{1,0:T(1,128)} %param.27) | copy-start | bytes 1024
  7.2 43.8 %copy-start.33 = (bf16[1,256,512]{2,1,0:T(8,128)(2,1)S(1)}, bf16[1,256,512]{2,1,0:T(8,128)(2,1)}, u32[]{:S(2)}) copy-start(bf16[1,256,512]{2,1,0:T(8,128)(2,1)} %param.26) | copy-start | bytes 786436
  7.2 413.8 %all-reduce.4.cloned.1.call-start = ((), (), s32[]{:S(2)}) async-start(), calls=%async_computation | async-start | bytes 8388608 | tf_op jit(solution)/shard_map/psum | solution.py:1278
  51.1 2.0 copy-start.20
  51.1 3.5 copy-start.12
  53.0 18.0 %copy-start.1 = (f32[512,128]{1,0:T(8,128)}, f32[512,128]{1,0:T(8,128)S(1)}, u32[]{:S(2)}) copy-start(f32[512,128]{1,0:T(8,128)S(1)} %get-tuple-element.147) | copy-start | bytes 786436
  55.3 0.8 copy-start.3
  71.0 3.1 copy-start.39
  74.7 14.6 %copy-start.4 = (f32[128,1024]{1,0:T(8,128)S(1)}, f32[128,1024]{1,0:T(8,128)}, u32[]{:S(2)}) copy-start(f32[128,1024]{1,0:T(8,128)} %copy-done.3) | copy-start | bytes 1572868
  89.2 1.9 copy-start.7
  89.2 1.9 copy-start.9
  92.2 21.1 %copy-start.35 = (f32[256]{0:T(256)S(1)}, f32[256]{0:T(256)}, u32[]{:S(2)}) copy-start(f32[256]{0:T(256)} %param.43) | copy-start | bytes 3076
  92.2 21.1 %copy-start.36 = (f32[256]{0:T(256)S(1)}, f32[256]{0:T(256)}, u32[]{:S(2)}) copy-start(f32[256]{0:T(256)} %param.42) | copy-start | bytes 3076
  174.6 19.3 %copy-start.15 = (bf16[2,4,1,128,128]{4,0,3,1,2:T(2,128)(2,1)}, bf16[2,4,1,128,128]{4,0,3,1,2:T(2,128)(2,1)S(1)}, u32[]{:S(2)}) copy-start(bf16[2,4,1,128,128]{4,0,3,1,2:T(2,128)(2,1)S(1)} %copy.80) | copy-start | bytes 786436
  209.5 3.3 copy-start.34
  209.5 3.3 copy-start.38
  219.0 3.2 copy-start.28
  219.6 2.6 copy-start.29
  219.6 2.6 copy-start.27
  242.7 2.9 copy-start.13
  244.7 0.8 copy-start.5
  346.1 2.2 copy-start.6
  346.1 2.2 copy-start.8
  346.1 2.2 copy-start.10
  346.1 2.2 copy-start.14
  346.1 2.2 copy-start.24
  391.7 6.5 %copy-start.17 = (bf16[128,1024]{1,0:T(8,128)(2,1)S(1)}, bf16[128,1024]{1,0:T(8,128)(2,1)}, u32[]{:S(2)}) copy-start(bf16[128,1024]{1,0:T(8,128)(2,1)} %get-tuple-element.96) | copy-start | bytes 786436
  397.0 5.1 copy-start.2
  405.2 8.6 %copy-start.18 = (bf16[128,1024]{1,0:T(8,128)(2,1)S(1)}, bf16[128,1024]{1,0:T(8,128)(2,1)}, u32[]{:S(2)}) copy-start(bf16[128,1024]{1,0:T(8,128)(2,1)} %get-tuple-element.96) | copy-start | bytes 786436
  406.3 0.7 copy-start.19
  409.4 5.9 %copy-start.16 = (bf16[2,4,1,128,128]{4,0,3,1,2:T(2,128)(2,1)S(1)}, bf16[2,4,1,128,128]{4,0,3,1,2:T(2,128)(2,1)}, u32[]{:S(2)}) copy-start(bf16[2,4,1,128,128]{4,0,3,1,2:T(2,128)(2,1)} %copy-done.15) | copy-start | bytes 786436
  411.2 4.1 copy-start.11
  413.8 2.8 copy-start.21
  413.8 2.8 copy-start.26
  416.6 2.2 copy-start.30
  522.9 5.8 %copy-start.32 = (bf16[128,1024]{1,0:T(8,128)(2,1)S(1)}, bf16[128,1024]{1,0:T(8,128)(2,1)}, u32[]{:S(2)}) copy-start(bf16[128,1024]{1,0:T(8,128)(2,1)} %get-tuple-element.71) | copy-start | bytes 786436
  529.5 6.8 %copy-start.25 = (bf16[256,3072]{1,0:T(8,128)(2,1)S(1)}, bf16[256,3072]{1,0:T(8,128)(2,1)}, u32[]{:S(2)}) copy-start(bf16[256,3072]{1,0:T(8,128)(2,1)} %get-tuple-element.73) | copy-start | bytes 4718596
  536.4 2.0 copy-start.31
  536.4 3.1 copy-start.23
  539.5 2.5 copy-start.22
Sparse Core Ops, SparseCore 0:
  225.0 112.5 all-reduce.3

commit v3 on v2

--- a/solution.py
+++ b/solution.py
@@ -1080,6 +1080,706 @@
     )(queries, keys, values, grads, output, lse)
 
 
+def norm_parts(values):
+    center = values - jnp.mean(values, -1, keepdims=True)
+    scale = lax.rsqrt(jnp.mean(center * center, -1, keepdims=True) + EPS)
+    return center * scale, scale
+
+
+def norm_back(grad, normed, scale):
+    along = jnp.mean(grad * normed, -1, keepdims=True)
+    return (grad - jnp.mean(grad, -1, keepdims=True) - normed * along) * scale
+
+
+def gelu_parts(values):
+    phi = 0.5 + 0.5 * lax.erf(values * 0.7071067811865476)
+    density = jnp.exp(-0.5 * values * values) * 0.3989422804014327
+    return values * phi, phi + values * density
+
+
+def column_sum(values):
+    return jnp.sum(values, 0, keepdims=True)
+
+
+def front_back_kernel(
+    resid_ref,
+    blocks_ref,
+    masked_ref,
+    steps_ref,
+    pre_ref,
+    low_ref,
+    conv_ref,
+    proj_ref,
+    norms_ref,
+    feat_o,
+    conv_o,
+    proj_o,
+    sums_o,
+    wide_o,
+    grad_ref,
+):
+    count, _, width = blocks_ref.shape
+    for b in range(count):
+        lanes = slice(b * width, (b + 1) * width)
+        grad_ref[:, lanes] = resid_ref[:, lanes] + blocks_ref[b].astype(F32)
+    embed_grad = grad_ref[...]
+    masked = masked_ref[...] > 0.5
+    wide_o[0:1, :] = column_sum(jnp.where(masked, embed_grad, 0.0))
+    proj_grad = jnp.where(masked, 0.0, embed_grad).astype(BF16)
+    wide_o[1:2, :] = column_sum(proj_grad.astype(F32))
+    proj_o[...] = inner_dot(low_ref[...], proj_grad).astype(BF16)
+    feat_grad = nt_dot(proj_grad, proj_ref[...])
+    conv_gain, conv_shift, norm_gain = (norms_ref[i : i + 1, :] for i in range(3))
+    first, first_scale = norm_parts(pre_ref[...])
+    act, slope = gelu_parts(first * conv_gain + conv_shift)
+    second, second_scale = norm_parts(act)
+    sums_o[2:3, :] = column_sum(feat_grad * second)
+    sums_o[3:4, :] = column_sum(feat_grad)
+    act_grad = norm_back(feat_grad * norm_gain, second, second_scale) * slope
+    sums_o[0:1, :] = column_sum(act_grad * first)
+    sums_o[1:2, :] = column_sum(act_grad)
+    conv_grad = norm_back(act_grad * conv_gain, first, first_scale).astype(BF16)
+    conv_o[...] = inner_dot(steps_ref[...], conv_grad).astype(BF16)
+    feat_o[...] = nt_dot(conv_grad, conv_ref[...]).astype(BF16)
+
+
+def front_back(resid, blocks, masked, steps, conv_pre, low, conv, proj, norms):
+    frames = resid.shape[0]
+    return pl.pallas_call(
+        front_back_kernel,
+        out_shape=[
+            jax.ShapeDtypeStruct(steps.shape, BF16),
+            jax.ShapeDtypeStruct(conv.shape, BF16),
+            jax.ShapeDtypeStruct(proj.shape, BF16),
+            jax.ShapeDtypeStruct((4, C), F32),
+            jax.ShapeDtypeStruct((2, D), F32),
+        ],
+        scratch_shapes=[pltpu.VMEM((frames, D), F32)],
+        compiler_params=pltpu.CompilerParams(vmem_limit_bytes=VMEM_BYTES),
+    )(resid, blocks, masked, steps, conv_pre, low, conv, proj, norms)
+
+
+def half_rows(first, size, which):
+    return pl.ds(pl.multiple_of(first + which * size, size), size)
+
+
+def block_rows(index, size):
+    return pl.ds(pl.multiple_of(index * size, size), size)
+
+
+def remote(src, dst, send, recv, device):
+    return pltpu.make_async_remote_copy(
+        src_ref=src,
+        dst_ref=dst,
+        send_sem=send,
+        recv_sem=recv,
+        device_id=device,
+        device_id_type=MESH,
+    )
+
+
+def loop(first, last, body):
+    def run(i, carry):
+        body(i)
+        return carry
+
+    lax.fori_loop(first, last, run, 0)
+
+
+class Regroup:
+    def __init__(self):
+        self.num_seq, self.num_utt = lax.axis_size("seq"), lax.axis_size("utt")
+        self.per_column = self.num_seq // self.num_utt
+        self.me_seq, self.me_utt = lax.axis_index("seq"), lax.axis_index("utt")
+        self.is_own = (lax.rem(self.me_seq, self.num_utt) == self.me_utt).astype(jnp.int32)
+        self.my_block = self.me_utt * self.per_column + self.me_seq // self.num_utt
+
+    def by_block(self, b):
+        return {
+            "seq": lax.rem(b, self.per_column) * self.num_utt + self.me_utt,
+            "utt": b // self.per_column,
+        }
+
+    def by_shard(self, f):
+        return {"seq": f, "utt": lax.rem(self.me_seq, self.num_utt)}
+
+    def not_me(self, where):
+        return jnp.logical_or(where["seq"] != self.me_seq, where["utt"] != self.me_utt)
+
+    def each(self, count, where, body):
+        def run(i):
+            device = where(i)
+
+            @pl.when(self.not_me(device))
+            def _():
+                body(i, device)
+
+        loop(0, count, run)
+
+    def when_own(self, body):
+        @pl.when(self.is_own == 1)
+        def _():
+            body()
+
+
+class Names:
+    def __init__(self, **shapes):
+        self.names, self.shapes = list(shapes), list(shapes.values())
+
+    def bind(self, refs):
+        bound = type("Bound", (), {})()
+        for name, ref in zip(self.names, refs, strict=True):
+            setattr(bound, name, ref)
+        return bound
+
+
+def attend_head_block(q_ref, k_ref, v_ref, h, rows):
+    lanes = slice(h * HEAD_DIM, (h + 1) * HEAD_DIM)
+    scores = nt_dot(q_ref[rows, lanes], k_ref[:, lanes]) * SCALE
+    highest = jnp.max(scores, -1, keepdims=True)
+    weights = jnp.exp(scores - highest)
+    total = jnp.sum(weights, -1, keepdims=True)
+    summed = jnp.dot(weights.astype(BF16), v_ref[:, lanes], preferred_element_type=F32)
+    return summed / total, highest + jnp.log(total)
+
+
+def front_forward(
+    steps,
+    starts,
+    conv,
+    proj,
+    vectors,
+    qkv,
+    up,
+    grad_rows,
+    taps,
+    taps_bias,
+    bias,
+    collective_id,
+):
+    num_seq, num_utt = lax.axis_size("seq"), lax.axis_size("utt")
+    frames = steps.shape[0]
+    length = frames * num_seq
+    column = qkv.shape[0]
+    half = column // 2
+    proj_rows = proj.shape[0]
+    proj_half = proj_rows // 2
+    hidden = up.shape[1] // num_utt
+    per_column = num_seq // num_utt
+    width = column // per_column
+    groups = width // GW
+    rows = length // PACK
+    num_blocks = num_utt * per_column
+    low = C // num_utt
+    rows_all = num_utt * frames
+    dma = pltpu.SemaphoreType.DMA
+    scratch = Names(
+        wide=pltpu.VMEM((length + KPOS, width), F32),
+        packed=pltpu.VMEM((groups, (length + KPOS) // PACK, TILE), F32),
+        taps=pltpu.VMEM((KPOS * GW + 2 * TILE, width), BF16),
+        acc=pltpu.VMEM((groups, rows, TILE), F32),
+        embed=pltpu.VMEM((frames, D), F32),
+        blocks=pltpu.VMEM((num_blocks, frames, width), BF16),
+        pos_own=pltpu.VMEM((length, width), BF16),
+        pos_back=pltpu.VMEM((num_blocks, frames, width), BF16),
+        head_out=pltpu.VMEM((num_seq, 3, frames, width), BF16),
+        attn_low=pltpu.VMEM((length, width), BF16),
+        local=dma((12,)),
+        conv_send=dma((num_utt,)),
+        conv_recv=dma((num_utt,)),
+        conv_hand_send=dma((num_utt,)),
+        conv_hand_recv=dma((num_utt,)),
+        proj_send=dma((num_utt,)),
+        proj_recv=dma((num_utt,)),
+        proj_hand_send=dma((num_utt,)),
+        proj_hand_recv=dma((num_utt,)),
+        vec_send=dma((num_utt,)),
+        vec_recv=dma((num_utt,)),
+        qkv_send=dma((num_utt, 3)),
+        qkv_recv=dma((num_utt, 3)),
+        qkv_hand_send=dma((num_utt,)),
+        qkv_hand_recv=dma((num_utt,)),
+        up_send=dma((num_utt,)),
+        up_recv=dma((num_utt,)),
+        up_hand_send=dma((num_utt,)),
+        up_hand_recv=dma((num_utt,)),
+        gout_send=dma((num_utt,)),
+        gout_recv=dma((num_utt,)),
+        there_send=dma((num_blocks,)),
+        there_recv=dma((num_seq,)),
+        back_send=dma((num_seq,)),
+        back_recv=dma((num_blocks,)),
+        attn_send=dma((num_utt,)),
+        attn_recv=dma((num_utt,)),
+        head_send=dma((num_seq,)),
+        head_recv=dma((num_seq,)),
+        flat_send=dma((num_seq,)),
+        flat_recv=dma((num_seq,)),
+    )
+
+    def kernel(
+        steps_ref,
+        starts_ref,
+        conv_ref,
+        proj_ref,
+        vec_ref,
+        qkv_ref,
+        up_ref,
+        gout_ref,
+        taps_ref,
+        taps_bias_ref,
+        bias_ref,
+        conv_all,
+        proj_all,
+        vec_all,
+        qkv_all,
+        up_all,
+        gout_all,
+        pre_o,
+        low_o,
+        mask_o,
+        pos_in,
+        pos_pre,
+        resid_o,
+        attn_all,
+        heads,
+        attn_o,
+        lse_o,
+        flat_o,
+        *rest,
+    ):
+        s = scratch.bind(rest)
+        group = Regroup()
+        me, me_utt = group.me_seq, group.me_utt
+        core = lax.rem(me, 2)
+        sibling = {"seq": me + 1 - 2 * core}
+        block = me // num_utt
+
+        def peer_of(i):
+            return lax.rem(me_utt + i, num_utt)
+
+        def peers(body):
+            loop(1, num_utt, lambda i: body(peer_of(i)))
+
+        def seq_peers(body):
+            loop(1, num_seq, lambda i: body(lax.rem(me + i, num_seq)))
+
+        barrier = pltpu.get_barrier_semaphore()
+
+        def signal(device):
+            pl.semaphore_signal(barrier, inc=1, device_id=device, device_id_type=MESH)
+
+        peers(lambda b: signal({"utt": b}))
+        seq_peers(lambda f: signal({"seq": f}))
+        group.each(num_seq, group.by_shard, lambda i, device: signal(device))
+        group.each(num_blocks, group.by_block, lambda i, device: signal(device))
+
+        first_tap = pl.multiple_of(block * width, width)
+        taps_in = pltpu.make_async_copy(
+            taps_ref.at[:, pl.ds(first_tap, width)],
+            s.taps.at[pl.ds(TILE, KPOS * GW)],
+            s.local.at[0],
+        )
+        taps_in.start()
+
+        def own_qkv(part):
+            first = pl.multiple_of((part * num_utt + me_utt) * column, column)
+            return pltpu.make_async_copy(
+                qkv_ref.at[:, pl.ds(first, column)],
+                qkv_all.at[block_rows(me_utt, column), pl.ds(part * column, column)],
+                s.local.at[1 + part],
+            )
+
+        own_up = pltpu.make_async_copy(
+            up_ref.at[:, block_rows(me_utt, hidden)],
+            up_all.at[block_rows(me_utt, column)],
+            s.local.at[4],
+        )
+        own_gout = pltpu.make_async_copy(
+            gout_ref, gout_all.at[block_rows(me_utt, frames)], s.local.at[5]
+        )
+        for part in range(3):
+            own_qkv(part).start()
+        own_up.start()
+        own_gout.start()
+        pl.semaphore_wait(
+            barrier, num_utt - 1 + num_seq - 1 + num_blocks + num_seq - 2 * group.is_own
+        )
+
+        def conv_copy(b, slot):
+            return remote(
+                conv_ref.at[half_rows(0, half, core)],
+                conv_all.at[half_rows(slot * column, half, core)],
+                s.conv_send.at[b],
+                s.conv_recv.at[slot],
+                {"utt": b},
+            )
+
+        def conv_hand(slot, which):
+            place = conv_all.at[half_rows(slot * column, half, which)]
+            return remote(
+                place, place, s.conv_hand_send.at[slot], s.conv_hand_recv.at[slot], sibling
+            )
+
+        def proj_copy(b, slot):
+            return remote(
+                proj_ref.at[half_rows(0, proj_half, core)],
+                proj_all.at[half_rows(slot * proj_rows, proj_half, core)],
+                s.proj_send.at[b],
+                s.proj_recv.at[slot],
+                {"utt": b},
+            )
+
+        def proj_hand(slot, which):
+            place = proj_all.at[half_rows(slot * proj_rows, proj_half, which)]
+            return remote(
+                place, place, s.proj_hand_send.at[slot], s.proj_hand_recv.at[slot], sibling
+            )
+
+        def vec_copy(b, slot):
+            return remote(
+                vec_ref, vec_all.at[slot], s.vec_send.at[b], s.vec_recv.at[slot], {"utt": b}
+            )
+
+        def qkv_copy(b, slot, part):
+            first = pl.multiple_of((part * num_utt + b) * column, column)
+            return remote(
+                qkv_ref.at[half_rows(0, half, core), pl.ds(first, column)],
+                qkv_all.at[half_rows(slot * column, half, core), pl.ds(part * column, column)],
+                s.qkv_send.at[b, part],
+                s.qkv_recv.at[slot, part],
+                {"utt": b},
+            )
+
+        def qkv_hand(slot, which):
+            place = qkv_all.at[half_rows(slot * column, half, which)]
+            return remote(
+                place, place, s.qkv_hand_send.at[slot], s.qkv_hand_recv.at[slot], sibling
+            )
+
+        def up_copy(b, slot):
+            return remote(
+                up_ref.at[half_rows(0, half, core), block_rows(b, hidden)],
+                up_all.at[half_rows(slot * column, half, core)],
+                s.up_send.at[b],
+                s.up_recv.at[slot],
+                {"utt": b},
+            )
+
+        def up_hand(slot, which):
+            place = up_all.at[half_rows(slot * column, half, which)]
+            return remote(place, place, s.up_hand_send.at[slot], s.up_hand_recv.at[slot], sibling)
+
+        def gout_copy(b, slot):
+            return remote(
+                gout_ref,
+                gout_all.at[block_rows(slot, frames)],
+                s.gout_send.at[b],
+                s.gout_recv.at[slot],
+                {"utt": b},
+            )
+
+        peers(lambda b: conv_copy(b, me_utt).start())
+        peers(lambda b: vec_copy(b, me_utt).start())
+        peers(lambda b: proj_copy(b, me_utt).start())
+        conv_all[block_rows(me_utt, column), :] = conv_ref[...]
+        proj_all[block_rows(me_utt, proj_rows), :] = proj_ref[...]
+        vec_all[me_utt] = vec_ref[...]
+        position = me * frames + lax.broadcasted_iota(jnp.int32, (frames, 1), 0)
+        inside = jnp.logical_and(
+            position >= starts_ref[...], position < starts_ref[...] + SPAN
+        )
+        masked = jnp.max(jnp.where(inside, 1.0, 0.0), -1, keepdims=True)
+        mask_o[...] = masked
+        edge = jnp.zeros((TILE, width), BF16)
+        s.taps[0:TILE, :] = edge
+        s.taps[TILE + KPOS * GW :, :] = edge
+
+        def conv_arrived(b):
+            conv_copy(b, b).wait_recv()
+            conv_hand(b, core).start()
+
+        def proj_arrived(b):
+            proj_copy(b, b).wait_recv()
+            proj_hand(b, core).start()
+
+        peers(conv_arrived)
+        peers(proj_arrived)
+        for part in range(3):
+            peers(lambda b, part=part: qkv_copy(b, me_utt, part).start())
+        peers(lambda b: vec_copy(b, b).wait_recv())
+        peers(lambda b: conv_hand(b, 1 - core).wait_recv())
+
+        def vector(first, size):
+            return jnp.concatenate(
+                [vec_all[b, :, first : first + size] for b in range(num_utt)], axis=1
+            )
+
+        pre = jnp.dot(steps_ref[...], conv_all[...], preferred_element_type=F32)
+        pre_o[...] = pre
+        normed, _ = norm_parts(pre)
+        act, _ = gelu_parts(normed * vector(0, low) + vector(low, low))
+        normed, _ = norm_parts(act)
+        feat_low = (normed * vector(2 * low, low) + vector(3 * low, low)).astype(BF16)
+        low_o[...] = feat_low
+        peers(lambda b: proj_hand(b, 1 - core).wait_recv())
+        first = 4 * low
+        proj_out = jnp.dot(feat_low, proj_all[...], preferred_element_type=F32)
+        proj_out = proj_out + vector(first, column)
+        embed = jnp.where(masked > 0.5, vector(first + column, column), proj_out)
+        s.embed[...] = embed
+        embed_low = embed.astype(BF16)
+        for b in range(num_blocks):
+            s.blocks[b] = embed_low[:, b * width : (b + 1) * width]
+
+        def there(b, device):
+            return remote(
+                s.blocks.at[b],
+                pos_in.at[block_rows(me, frames)],
+                s.there_send.at[b],
+                s.there_recv.at[me],
+                device,
+            )
+
+        def there_from(f, device):
+            return remote(
+                s.blocks.at[0],
+                pos_in.at[block_rows(f, frames)],
+                s.there_send.at[0],
+                s.there_recv.at[f],
+                device,
+            )
+
+        group.each(num_blocks, group.by_block, lambda b, device: there(b, device).start())
+
+        def keep_there():
+            pos_in[block_rows(me, frames), :] = s.blocks[group.my_block]
+
+        group.when_own(keep_there)
+        taps_in.wait()
+        group.each(num_seq, group.by_shard, lambda f, device: there_from(f, device).wait_recv())
+        fill_frames(pos_in, s.wide, s.packed, length, groups)
+        for h in range(groups):
+            for step in range(NUM_TILES // STEP_TILES):
+                start = step * STEP_TILES
+                columns = jnp.concatenate(
+                    [s.packed[h, start + j : start + j + rows, :] for j in range(STEP_TILES)],
+                    axis=1,
+                ).astype(BF16)
+                part = jnp.dot(
+                    columns,
+                    tap_tile(s.taps, start * TILE, STEP_TILES * TILE, h),
+                    preferred_element_type=F32,
+                )
+                if step == 0:
+                    s.acc[h] = part
+                else:
+                    s.acc[h] += part
+        unpack_frames(
+            lambda h, r: s.acc[h, :, r * GW : (r + 1) * GW]
+            + taps_bias_ref[:, h * GW : (h + 1) * GW],
+            s.wide.at[0:length],
+            rows,
+            groups,
+        )
+        s.pos_own[...] = s.wide[0:length, :].astype(BF16)
+
+        def back(f, device):
+            return remote(
+                s.pos_own.at[block_rows(f, frames)],
+                s.pos_back.at[group.my_block],
+                s.back_send.at[f],
+                s.back_recv.at[group.my_block],
+                device,
+            )
+
+        def back_from(b, device):
+            return remote(
+                s.pos_own.at[block_rows(0, frames)],
+                s.pos_back.at[b],
+                s.back_send.at[0],
+                s.back_recv.at[b],
+                device,
+            )
+
+        group.each(num_seq, group.by_shard, lambda f, device: back(f, device).start())
+
+        def keep_back():
+            s.pos_back[group.my_block] = s.pos_own[block_rows(me, frames), :]
+
+        group.when_own(keep_back)
+        group.each(num_blocks, group.by_block, lambda b, device: back_from(b, device).wait_recv())
+        for b in range(num_blocks):
+            lanes = slice(b * width, (b + 1) * width)
+            pos_pre[:, lanes] = s.pos_back[b]
+        act, _ = gelu_parts(pos_pre[...].astype(F32))
+        resid = s.embed[...] + act
+        resid_o[...] = resid
+        normed, _ = norm_parts(resid)
+        first = first + 2 * column
+        attn_in = normed * vector(first, column) + vector(first + column, column)
+        attn_all[block_rows(me_utt, frames), :] = attn_in.astype(BF16)
+
+        def attn_copy(b, slot):
+            place = block_rows(slot, frames)
+            return remote(
+                attn_all.at[place],
+                attn_all.at[place],
+                s.attn_send.at[b],
+                s.attn_recv.at[slot],
+                {"utt": b},
+            )
+
+        peers(lambda b: attn_copy(b, me_utt).start())
+
+        def qkv_arrived(b):
+            for part in range(3):
+                qkv_copy(b, b, part).wait_recv()
+            qkv_hand(b, core).start()
+
+        peers(qkv_arrived)
+        peers(lambda b: qkv_hand(b, 1 - core).wait_recv())
+        for part in range(3):
+            own_qkv(part).wait()
+
+        def head_copy(dest, slot):
+            return remote(
+                s.head_out.at[dest],
+                heads.at[:, block_rows(slot, frames)],
+                s.head_send.at[dest],
+                s.head_recv.at[slot],
+                {"seq": dest},
+            )
+
+        for i in range(num_utt):
+            b = peer_of(i)
+            if i:
+                attn_copy(b, b).wait_recv()
+            projected = jnp.dot(
+                attn_all[block_rows(b, frames), :], qkv_all[...], preferred_element_type=F32
+            )
+            projected = (projected + bias_ref[...]).astype(BF16)
+            for j in range(per_column):
+                dest = j * num_utt + b
+                for part in range(3):
+                    lanes = part * column + j * width
+                    s.head_out[dest, part] = projected[:, lanes : lanes + width]
+
+                @pl.when(dest != me)
+                def _(dest=dest):
+                    head_copy(dest, me).start()
+
+                @pl.when(dest == me)
+                def _(dest=dest):
+                    for part in range(3):
+                        heads[part, block_rows(me, frames), :] = s.head_out[dest, part]
+
+        peers(lambda b: up_copy(b, me_utt).start())
+        peers(lambda b: gout_copy(b, me_utt).start())
+        seq_peers(lambda f: head_copy(f, f).wait_recv())
+
+        def flat_copy(f, slot):
+            lanes = pl.ds(pl.multiple_of(slot // num_utt * width, width), width)
+            return remote(
+                s.attn_low.at[block_rows(f, frames)],
+                flat_o.at[block_rows(lax.rem(slot, num_utt), frames), lanes],
+                s.flat_send.at[f],
+                s.flat_recv.at[slot],
+                {"seq": f},
+            )
+
+        for start in range(0, length, Q_BLOCK):
+            where = slice(start, start + Q_BLOCK)
+            for h in range(groups):
+                lanes = slice(h * HEAD_DIM, (h + 1) * HEAD_DIM)
+                value, lse = attend_head_block(heads.at[0], heads.at[1], heads.at[2], h, where)
+                attn_o[where, lanes] = value
+                lse_o[where, h : h + 1] = lse
+                s.attn_low[where, lanes] = value.astype(BF16)
+            for f in range(start // frames, (start + Q_BLOCK) // frames):
+
+                @pl.when(f != me)
+                def _(f=f):
+                    flat_copy(f, me).start()
+
+                @pl.when(f == me)
+                def _(f=f):
+                    lanes = pl.ds(pl.multiple_of(block * width, width), width)
+                    flat_o[block_rows(lax.rem(me, num_utt), frames), lanes] = s.attn_low[
+                        f * frames : (f + 1) * frames, :
+                    ]
+
+        def up_arrived(b):
+            up_copy(b, b).wait_recv()
+            up_hand(b, core).start()
+
+        peers(up_arrived)
+
+        seq_peers(lambda f: flat_copy(f, f).wait_recv())
+        peers(lambda b: gout_copy(b, b).wait_recv())
+        own_up.wait()
+        own_gout.wait()
+
+        def sent(b):
+            conv_copy(b, me_utt).wait_send()
+            conv_hand(b, core).wait_send()
+            proj_copy(b, me_utt).wait_send()
+            proj_hand(b, core).wait_send()
+            vec_copy(b, me_utt).wait_send()
+            for part in range(3):
+                qkv_copy(b, me_utt, part).wait_send()
+            qkv_hand(b, core).wait_send()
+            up_copy(b, me_utt).wait_send()
+            up_hand(b, core).wait_send()
+            up_hand(b, 1 - core).wait_recv()
+            gout_copy(b, me_utt).wait_send()
+            attn_copy(b, me_utt).wait_send()
+
+        peers(sent)
+
+        def sent_seq(f):
+            head_copy(f, me).wait_send()
+            flat_copy(f, me).wait_send()
+
+        seq_peers(sent_seq)
+        group.each(num_blocks, group.by_block, lambda b, device: there(b, device).wait_send())
+        group.each(num_seq, group.by_shard, lambda f, device: back(f, device).wait_send())
+
+    vmem, anywhere = pl.BlockSpec(memory_space=pltpu.VMEM), pl.BlockSpec(memory_space=pl.ANY)
+
+    def shape(*dims, dtype=BF16):
+        return jax.ShapeDtypeStruct(dims, dtype)
+
+    return pl.pallas_call(
+        kernel,
+        out_shape=[
+            shape(num_utt * column, C),
+            shape(num_utt * proj_rows, D),
+            shape(num_utt, 1, vectors.shape[1], dtype=F32),
+            shape(num_utt * column, 3 * column),
+            shape(num_utt * column, hidden),
+            shape(rows_all, D),
+            shape(frames, C, dtype=F32),
+            shape(frames, C),
+            shape(frames, 1, dtype=F32),
+            shape(length, width),
+            shape(frames, D),
+            shape(frames, D, dtype=F32),
+            shape(rows_all, D),
+            shape(3, length, width),
+            shape(length, width, dtype=F32),
+            shape(length, groups, dtype=F32),
+            shape(rows_all, column),
+        ],
+        in_specs=[vmem] * 5 + [anywhere] * 4 + [vmem] * 2,
+        out_specs=[vmem] * 4 + [anywhere] * 2 + [vmem] * 11,
+        scratch_shapes=scratch.shapes,
+        compiler_params=pltpu.CompilerParams(
+            collective_id=collective_id, has_side_effects=True, vmem_limit_bytes=VMEM_BYTES
+        ),
+    )(steps, starts, conv, proj, vectors, qkv, up, grad_rows, taps, taps_bias, bias)
+
+
 def layer_norm(values, gain, shift):
     center = values - jnp.mean(values, -1, keepdims=True)
     spread = jnp.mean(center * center, -1, keepdims=True)
@@ -1161,18 +1861,75 @@
         ffn_shift,
         down_bias,
     ]
-    conv_all, proj_all, vectors_all, qkv_columns = exchange(
-        [
-            Item(conv_weight, "utt", "gather", shared=True),
-            Item(proj_weight, "utt", "gather", shared=True),
-            Item(jnp.concatenate(vectors)[None, :], "utt", "gather"),
-            Item(qkv_weight, "utt", "columns", 3, shared=True),
-        ],
-        1,
-    )
-    qkv_columns = qkv_columns.reshape(D, 3 * column)
-    conv_all = conv_all.reshape(2 * C, C)
-    proj_all = proj_all.reshape(C, D)
+    def to_blocks(values):
+        return values.reshape(frames, D // width, width).transpose(1, 0, 2)
+
+    def from_blocks(blocks):
+        return blocks.transpose(1, 0, 2).reshape(frames, D)
+
+    def to_heads(values, parts):
+        blocks = values.reshape(num_utt, frames, parts, per_column, width)
+        return blocks.transpose(3, 0, 2, 1, 4).reshape(num_seq, parts, frames, width)
+
+    def from_heads(blocks, parts):
+        blocks = blocks.reshape(per_column, num_utt, parts, frames, width)
+        return blocks.transpose(1, 3, 2, 0, 4).reshape(rows_all, parts * column)
+
+    def split_rows(values):
+        return values.astype(BF16).reshape(num_utt, frames, D)
+
+    block_id = me_seq // num_utt
+    taps = lax.dynamic_slice_in_dim(pos_weight, block_id * width, width, 2)
+    taps = taps.reshape(KPOS * GW, width)
+    taps_bias = lax.dynamic_slice_in_dim(pos_bias, block_id * width, width, 0)[None, :]
+    fast = width == CHUNK_ROWS
+    if fast:
+        (
+            conv_all,
+            proj_all,
+            vectors_all,
+            qkv_columns,
+            up_columns,
+            gout_all,
+            conv_pre,
+            feat_low,
+            masked,
+            pos_in,
+            pos_pre,
+            resid_one,
+            attn_in,
+            qkv_heads,
+            attn_f32,
+            lse,
+            attn_flat,
+        ) = front_forward(
+            steps_in,
+            mask_starts,
+            conv_weight,
+            proj_weight,
+            jnp.concatenate(vectors)[None, :],
+            qkv_weight,
+            up_weight,
+            out_rows,
+            pos_weight.reshape(KPOS * GW, column),
+            taps_bias,
+            jnp.concatenate([query_bias, jnp.zeros_like(query_bias), value_bias])[None, :],
+            1,
+        )
+        queries, keys, values = qkv_heads[0], qkv_heads[1], qkv_heads[2]
+    else:
+        conv_all, proj_all, vectors_all, qkv_columns = exchange(
+            [
+                Item(conv_weight, "utt", "gather", shared=True),
+                Item(proj_weight, "utt", "gather", shared=True),
+                Item(jnp.concatenate(vectors)[None, :], "utt", "gather"),
+                Item(qkv_weight, "utt", "columns", 3, shared=True),
+            ],
+            1,
+        )
+        qkv_columns = qkv_columns.reshape(D, 3 * column)
+        conv_all = conv_all.reshape(2 * C, C)
+        proj_all = proj_all.reshape(C, D)
     whole, start = [], 0
     for vector in vectors:
         end = start + vector.shape[0]
@@ -1193,73 +1950,52 @@
         down_bias,
     ) = whole
 
-    conv_pre = dot(steps_in, conv_all)
-    feat_norm, front_pull = jax.vjp(
-        front_norms, conv_pre, conv_gain, conv_shift, norm_gain, norm_shift
-    )
-    feat_low = feat_norm.astype(BF16)
-    proj_out = dot(feat_low, proj_all) + proj_bias
-    frame_pos = me_seq * frames + jnp.arange(frames, dtype=jnp.int32)
-    starts = mask_starts.reshape(1, -1)
-    inside = (frame_pos[:, None] >= starts) & (frame_pos[:, None] < starts + SPAN)
-    masked = jnp.any(inside, -1, keepdims=True)
-    embed = jnp.where(masked, mask_embed[None, :], proj_out)
-
-    def to_blocks(values):
-        return values.reshape(frames, D // width, width).transpose(1, 0, 2)
-
-    def from_blocks(blocks):
-        return blocks.transpose(1, 0, 2).reshape(frames, D)
-
-    block_id = me_seq // num_utt
-    taps = lax.dynamic_slice_in_dim(pos_weight, block_id * width, width, 2)
-    taps = taps.reshape(KPOS * GW, width)
-    taps_bias = lax.dynamic_slice_in_dim(pos_bias, block_id * width, width, 0)[None, :]
-    pos_in = regroup(to_blocks(embed.astype(BF16)), False, 2).reshape(length, width)
-    pos_own = pos_forward(pos_in, taps, taps_bias)
-    pos_pre = from_blocks(regroup(pos_own.reshape(num_seq, frames, width), True, 3))
-    pos_act, pos_pull = jax.vjp(gelu_exact, pos_pre.astype(F32))
-    resid_one = embed + pos_act
-    attn_norm, attn_pull = jax.vjp(layer_norm, resid_one, attn_gain, attn_shift)
-    (attn_in,) = exchange([(attn_norm.astype(BF16), "utt", "gather")], 4)
-    attn_in = attn_in.reshape(rows_all, D)
-
-    projected = dot(attn_in, qkv_columns).reshape(rows_all, 3, column)
-    bias = jnp.stack([query_bias, jnp.zeros_like(query_bias), value_bias])
-    projected = (projected + bias[None]).astype(BF16)
-
-    def to_heads(values, parts):
-        blocks = values.reshape(num_utt, frames, parts, per_column, width)
-        return blocks.transpose(3, 0, 2, 1, 4).reshape(num_seq, parts, frames, width)
-
-    def from_heads(blocks, parts):
-        blocks = blocks.reshape(per_column, num_utt, parts, frames, width)
-        return blocks.transpose(1, 3, 2, 0, 4).reshape(rows_all, parts * column)
-
-    qkv_heads, up_columns = exchange(
-        [
-            (to_heads(projected, 3), "seq", "blocks"),
-            Item(up_weight, "utt", "columns", shared=True),
-        ],
-        5,
-    )
-    up_columns = up_columns.reshape(D, hidden)
-    qkv_heads = qkv_heads.transpose(1, 0, 2, 3).reshape(3, length, width)
-    queries, keys, values = qkv_heads[0], qkv_heads[1], qkv_heads[2]
-    attn_f32, lse = attend(queries, keys, values)
-    attn_rows, gout_all = exchange(
-        [
-            (attn_f32.astype(BF16).reshape(num_seq, 1, frames, width), "seq", "blocks"),
-            (out_rows, "utt", "gather"),
-        ],
-        6,
-    )
-    gout_all = gout_all.reshape(rows_all, D)
-    attn_flat = from_heads(attn_rows, 1)
-
-    def split_rows(values):
-        return values.astype(BF16).reshape(num_utt, frames, D)
-
+    if not fast:
+        conv_pre = dot(steps_in, conv_all)
+        feat_norm = front_norms(conv_pre, conv_gain, conv_shift, norm_gain, norm_shift)
+        feat_low = feat_norm.astype(BF16)
+        proj_out = dot(feat_low, proj_all) + proj_bias
+        frame_pos = me_seq * frames + jnp.arange(frames, dtype=jnp.int32)
+        starts = mask_starts.reshape(1, -1)
+        inside = (frame_pos[:, None] >= starts) & (frame_pos[:, None] < starts + SPAN)
+        masked = jnp.any(inside, -1, keepdims=True).astype(F32)
+        embed = jnp.where(masked > 0.5, mask_embed[None, :], proj_out)
+
+        pos_in = regroup(to_blocks(embed.astype(BF16)), False, 2).reshape(length, width)
+        pos_own = pos_forward(pos_in, taps, taps_bias)
+        pos_pre = from_blocks(regroup(pos_own.reshape(num_seq, frames, width), True, 3))
+        resid_one = embed + gelu_exact(pos_pre.astype(F32))
+        attn_norm = layer_norm(resid_one, attn_gain, attn_shift)
+        (attn_in,) = exchange([(attn_norm.astype(BF16), "utt", "gather")], 4)
+        attn_in = attn_in.reshape(rows_all, D)
+
+        projected = dot(attn_in, qkv_columns).reshape(rows_all, 3, column)
+        bias = jnp.stack([query_bias, jnp.zeros_like(query_bias), value_bias])
+        projected = (projected + bias[None]).astype(BF16)
+
+        qkv_heads, up_columns = exchange(
+            [
+                (to_heads(projected, 3), "seq", "blocks"),
+                Item(up_weight, "utt", "columns", shared=True),
+            ],
+            5,
+        )
+        up_columns = up_columns.reshape(D, hidden)
+        qkv_heads = qkv_heads.transpose(1, 0, 2, 3).reshape(3, length, width)
+        queries, keys, values = qkv_heads[0], qkv_heads[1], qkv_heads[2]
+        attn_f32, lse = attend(queries, keys, values)
+        attn_rows, gout_all = exchange(
+            [
+                (attn_f32.astype(BF16).reshape(num_seq, 1, frames, width), "seq", "blocks"),
+                (out_rows, "utt", "gather"),
+            ],
+            6,
+        )
+        gout_all = gout_all.reshape(rows_all, D)
+        attn_flat = from_heads(attn_rows, 1)
+
+    _, pos_pull = jax.vjp(gelu_exact, pos_pre.astype(F32))
+    _, attn_pull = jax.vjp(layer_norm, resid_one, attn_gain, attn_shift)
     (parts,) = exchange([(split_rows(dot(attn_flat, out_weight)), "utt", "blocks")], 7)
     resid_two = resid_one + jnp.sum(parts.astype(F32), 0) + out_bias
     ffn_norm, ffn_pull = jax.vjp(layer_norm, resid_two, ffn_gain, ffn_shift)
@@ -1291,35 +2027,35 @@
     qkv_grads = jnp.stack([part.reshape(num_seq, frames, width) for part in qkv_grads], axis=1)
     (qkv_back,) = exchange([(qkv_grads, "seq", "blocks")], 12)
     qkv_back = from_heads(qkv_back, 3)
-    (qkv_parts,) = exchange([(split_rows(nt_dot(qkv_back, qkv_columns)), "utt", "blocks")], 13)
     outweight_grad = inner_dot(attn_flat, attn_grad).astype(BF16)
     qkvweight_grad = inner_dot(attn_in, qkv_back).astype(BF16)
+    (qkv_parts,) = exchange([(split_rows(nt_dot(qkv_back, qkv_columns)), "utt", "blocks")], 13)
     attn_back, attngain_grad, attnshift_grad = attn_pull(jnp.sum(qkv_parts.astype(F32), 0))
     resid1_grad = resid2_grad + attn_back
     (pos_grad,) = pos_pull(resid1_grad)
     pos_low = pos_grad.astype(BF16)
     grads_in = regroup(to_blocks(pos_low), False, 14).reshape(length, width)
     embed_own, taps_grad = pos_backward(pos_in, grads_in, taps)
-    embed_back = from_blocks(regroup(embed_own.reshape(num_seq, frames, width), True, 15))
-    embed_grad = resid1_grad + embed_back.astype(F32)
-    maskembed_grad = jnp.sum(jnp.where(masked, embed_grad, 0.0), 0)
-    proj_grad = jnp.where(masked, 0.0, embed_grad).astype(BF16)
-    projbias_grad = jnp.sum(proj_grad, 0, dtype=F32)
-    projweight_grad = inner_dot(feat_low, proj_grad)
-    conv_back, convgain_grad, convshift_grad, normgain_grad, normshift_grad = front_pull(
-        nt_dot(proj_grad, proj_all)
+    embed_back = regroup(embed_own.reshape(num_seq, frames, width), True, 15)
+    feat_grad, convweight_grad, projweight_grad, norm_sums, embed_sums = front_back(
+        resid1_grad,
+        embed_back,
+        masked,
+        steps_in,
+        conv_pre,
+        feat_low,
+        conv_all,
+        proj_all,
+        jnp.stack([conv_gain, conv_shift, norm_gain]),
     )
-    conv_grad = conv_back.astype(BF16)
-    convweight_grad = inner_dot(steps_in, conv_grad)
-    feat_grad = nt_dot(conv_grad, conv_all).astype(BF16).reshape(1, 2 * frames, C)
-
+    feat_grad = feat_grad.reshape(1, 2 * frames, C)
     row_vectors = [
-        convgain_grad,
-        convshift_grad,
-        normgain_grad,
-        normshift_grad,
-        projbias_grad,
-        maskembed_grad,
+        norm_sums[0],
+        norm_sums[1],
+        norm_sums[2],
+        norm_sums[3],
+        embed_sums[1],
+        embed_sums[0],
         jnp.sum(pos_low, 0, dtype=F32),
         attngain_grad,
         attnshift_grad,
@@ -1344,13 +2080,13 @@
         taps_grad,
         outweight_grad,
         qkvweight_grad,
-        convweight_grad.astype(BF16),
-        projweight_grad.astype(BF16),
+        convweight_grad,
+        projweight_grad,
         flat,
         upweight_sum,
         layer_parts,
     )
-    if width == CHUNK_ROWS:
+    if fast:
         grads = sum_gradients(*grads, 16)
     else:
         grads = sum_gradients_plain(*grads)

time: 562 us -> 485 us (0.86)
  Pallas kernels: 389 us -> 350 us
  matrix products: 48.3 us -> 33.8 us
  other arithmetic: 54.5 us -> 42.8 us
  local copies, waits for them, and re-layouts: 45.3 us -> 34.1 us
    pallas_call x11 -> x7, Pallas kernels: 209 us -> 108 us  [exchange(): pl.pallas_call(kernel, out_shape=[jax.ShapeDtypeStruct(item.shape, item.a...]
    pallas_call x2, Pallas kernels: 12.3 us -> 97 us  [the longest x1 92 us: front_forward(): pl.pallas_call(kernel, out_shape=[shape(num_utt * column, C), shape(num_u...]
    pallas_call x4 -> x2, Pallas kernels: 44.3 us -> 22.4 us  [regroup(): pl.pallas_call(kernel, out_shape=jax.ShapeDtypeStruct((receives,) + block...]
    dot_general x6 -> x4, matrix products: 21.5 us -> 14.7 us  [nt_dot(): lax.dot_general(a, b, (((1,), (1,)), ((), ())), preferred_element_type=F32)]
    dot_general x6 -> x3, matrix products: 14.1 us -> 7.84 us  [dot(): return jnp.dot(a, b, preferred_element_type=F32)]
    dot_general x6 -> x4, matrix products: 12.8 us -> 11.3 us  [inner_dot(): lax.dot_general(first_mat, second_mat, (((0,), (0,)), ((), ())), preferre...]
  transfers between devices with their start and end apart: 1 -> 1, of which waited for: 0 -> 0; matrix products, arithmetic and copies ran while one was open for 12% -> 11% of each run, Pallas kernels for 24% -> 27%
where the time goes in v3:
time: 485 us; the launch traced here: 476 us
  Pallas kernels  350 us (72%)
  other arithmetic  42.8 us (9%)
  local copies, waits for them, and re-layouts  34.1 us (7%)
  matrix products  33.8 us (7%)
  between operations  15 us (3%)
    pallas_call x7, Pallas kernels, exchange(): pl.pallas_call(kernel, out_shape=[jax.ShapeDtypeStruct(item.shape, item.a...  108 us
    pallas_call x1, Pallas kernels, sum_gradients(): pl.pallas_call(kernel, out_shape=[jax.ShapeDtypeStruct(shape, BF16) for s...  102 us
    pallas_call x1, Pallas kernels, front_forward(): pl.pallas_call(kernel, out_shape=[shape(num_utt * column, C), shape(num_u...  92 us
    pallas_call x2, Pallas kernels, regroup(): pl.pallas_call(kernel, out_shape=jax.ShapeDtypeStruct((receives,) + block...  22.4 us
    dot_general x4, matrix products, nt_dot(): lax.dot_general(a, b, (((1,), (1,)), ((), ())), preferred_element_type=F32)  14.7 us
    pallas_call x1, Pallas kernels, pos_backward(): pl.pallas_call(pos_backward_kernel, out_shape=[jax.ShapeDtypeStruct((fram...  12.2 us
    dot_general x4, matrix products, inner_dot(): lax.dot_general(first_mat, second_mat, (((0,), (0,)), ((), ())), preferre...  11.3 us
    unnamed x74, local copies, waits for them, and re-layouts  10.1 us
  transfers between devices with their start and end apart: 1, of which 0 were waited for; matrix products, arithmetic and copies ran while one was open for 11% of the time, Pallas kernels for 27%

profile of v3, /device:TPU:0, one launch (start us, length us, event | category | flops | bytes accessed | tf_op | source)
XLA Modules:
  0.0 476.3 jit_solution(17222819567213037958)
XLA Ops:
  7.3 1.9 reshape.238.steps_ref
  19.2 1.3 dynamic-slice_bitcast_fusion.taps_bias_ref
  20.5 92.0 %shard_map.441 = (bf16[1024,512]{1,0:T(8,128)(2,1)}, bf16[512,1024]{1,0:T(8,128)(2,1)}, f32[4,1,2560]{2,1,0:T(1,128)}, bf16[1024,768]{1,0:T(8,128)(2,1)}, bf16[1...) custom-call(bf16[128,1024]{1,0:T(8,128)(2,1)} %reshape.238.steps_ref, ...), custom_call_target="tpu_custom_call" | custom-call | tf_op jit(solution)/shard_map/pallas_call | solution.py:1753
  112.5 2.4 convolution_convert_fusion.6
  114.9 13.8 %shard_map.442 = bf16[4,128,1024]{2,1,0:T(8,128)(2,1)} custom-call(bf16[4,128,1024]{2,1,0:T(8,128)(2,1)} %bitcast.128), custom_call_target="tpu_custom_call" | custom-call | tf_op jit(solution)/shard_map/pallas_call | solution.py:171
  128.7 2.3 convert_reduce_fusion.4
  133.4 14.4 %shard_map.443 = bf16[4,128,1024]{2,1,0:T(8,128)(2,1)} custom-call(bf16[128,1024]{1,0:T(8,128)(2,1)} %add_convert_fusion.2.refs_0_), custom_call_target="tpu_custom_call" | custom-call | tf_op jit(solution)/shard_map/pallas_call | solution.py:171
  147.8 3.2 fusion.55
  151.1 6.2 %add_convert_fusion = (bf16[512,1024]{1,0:T(8,128)(2,1)S(1)}, f32[512,1024]{1,0:T(8,128)S(1)}) fusion(f32[512,1024]{1,0:T(8,128)S(1)} %fusion.55, f32[1024]{0:T(1024)S(1)} %copy-done.21, bf16[512,1024]{1,0:T(8,128)(2,1)S(1)} %copy-done.23, bf16[1024,1024]{1,0:T(8,128)(2,1)S(1)} %copy-done), kind=kOutput, calls=%fused_computation.6 | convolution fusion | flops 1112014848 | bytes 8392704 | tf_op jit(solution)/shard_map/dot_general | solution.py:1010
  157.4 2.6 convolution_convert_fusion
  161.5 2.6 convolution_convert_fusion.1
  164.1 3.2 constant_dynamic-slice_fusion
  167.4 2.3 convolution_convert_fusion.5
  169.7 13.4 %shard_map.444 = bf16[4,128,1024]{2,1,0:T(8,128)(2,1)} custom-call(bf16[4,128,1024]{2,1,0:T(8,128)(2,1)} %bitcast.136), custom_call_target="tpu_custom_call" | custom-call | tf_op jit(solution)/shard_map/pallas_call | solution.py:171
  183.1 1.5 convert_reduce_fusion.3
  186.8 13.3 %shard_map.445 = bf16[4,128,1024]{2,1,0:T(8,128)(2,1)} custom-call(bf16[128,1024]{1,0:T(8,128)(2,1)} %get-tuple-element.116.refs_0_), custom_call_target="tpu_custom_call" | custom-call | tf_op jit(solution)/shard_map/pallas_call | solution.py:171
  200.2 2.6 convolution_convert_fusion.8
  202.7 1.7 reshape.245
  204.4 1.7 copy.53
  206.1 9.0 %shard_map.446 = bf16[8,1,128,128]{3,2,1,0:T(8,128)(2,1)} custom-call(bf16[8,1,128,128]{3,2,1,0:T(8,128)(2,1)} %bitcast.138), custom_call_target="tpu_custom_call" | custom-call | tf_op jit(solution)/shard_map/pallas_call | solution.py:171
  215.2 2.0 slice_bitcast_fusion
  217.2 9.3 %shard_map.447 = (bf16[1024,128]{1,0:T(8,128)(2,1)}, bf16[1024,128]{1,0:T(8,128)(2,1)}, bf16[1024,128]{1,0:T(8,128)(2,1)}) custom-call(bf16[1024,128]{1,0:T(8,128)(2,1)} %get-tuple-element.130.q_ref, bf16[1024,128]{1,0:T(8,128)(2,1)} %get-tuple-element.129.k_ref, bf16[1024,128]{1,0:T(8,128)(2,1)} %get-tuple-element.128.v_ref, bf16[1024,128]{1,0:T(8,128)(2,1)} %bitcast.139, ...), custom_call_target="tpu_custom_call" | custom-call | tf_op jit(solution)/shard_map/pallas_call | solution.py:1075
  226.4 2.1 pad_maximum_fusion.refs_0_
  228.5 28.4 %shard_map.448 = bf16[8,3,128,128]{3,2,1,0:T(8,128)(2,1)} custom-call(bf16[8,3,128,128]{3,2,1,0:T(8,128)(2,1)} %pad_maximum_fusion.refs_0_), custom_call_target="tpu_custom_call" | custom-call | tf_op jit(solution)/shard_map/pallas_call | solution.py:171
  256.9 2.8 copy.61
  259.8 3.2 reshape.249
  262.9 3.6 convolution_convert_fusion.3
  266.6 15.3 %shard_map.449 = bf16[4,128,1024]{2,1,0:T(8,128)(2,1)} custom-call(bf16[4,128,1024]{2,1,0:T(8,128)(2,1)} %bitcast.137), custom_call_target="tpu_custom_call" | custom-call | tf_op jit(solution)/shard_map/pallas_call | solution.py:171
  281.8 2.3 convert_reduce_fusion.2
  284.1 1.4 reduce.3
  285.5 1.4 reduce.5
  287.0 1.4 multiply_reduce_fusion.1
  288.4 1.3 fusion.50
  289.7 2.1 fusion.48
  292.6 13.0 %shard_map.450 = bf16[8,128,128]{2,1,0:T(8,128)(2,1)} custom-call(bf16[8,128,128]{2,1,0:T(8,128)(2,1)} %bitcast_bitcast_fusion.x_ref), custom_call_target="tpu_custom_call" | custom-call | tf_op jit(solution)/shard_map/pallas_call | solution.py:831
  305.6 12.2 %shard_map.451 = (bf16[1024,128]{1,0:T(8,128)(2,1)}, bf16[8192,128]{1,0:T(8,128)(2,1)}) custom-call(bf16[1024,128]{1,0:T(8,128)(2,1)} %get-tuple-element.66.x_ref, bf16[1024,128]{1,0:T(8,128)(2,1)} %bitcast.135, bf16[8192,128]{1,0:T(8,128)(2,1)} %bitcast.124), custom_call_target="tpu_custom_call" | custom-call | tf_op jit(solution)/shard_map/pallas_call | solution.py:987
  317.9 9.4 %shard_map.452.blocks_ref = bf16[8,128,128]{2,1,0:T(8,128)(2,1)} custom-call(bf16[8,128,128]{2,1,0:T(8,128)(2,1)} %bitcast.141), custom_call_target="tpu_custom_call" | custom-call | tf_op jit(solution)/shard_map/pallas_call | solution.py:831
  327.9 5.0 %shard_map.453 = (bf16[128,1024]{1,0:T(8,128)(2,1)}, bf16[1024,512]{1,0:T(8,128)(2,1)}, bf16[512,1024]{1,0:T(8,128)(2,1)}, f32[4,512]{1,0:T(4,128)}, f32[2,1024]{1,0:T(2,128)}) custom-call(f32[128,1024]{1,0:T(8,128)} %get-tuple-element.119.resid_ref, bf16[8,128,128]{2,1,0:T(8,128)(2,1)} %shard_map.452.blocks_ref, f32[128,1]{1,0:T(8,128)} %get-tuple-element.81.masked_ref, ...), custom_call_target="tpu_custom_call" | custom-call | tf_op jit(solution)/shard_map/pallas_call | solution.py:1148
  334.8 1.4 convert_reduce_fusion.1
  336.9 1.7 reshape.265
  338.7 2.6 convolution_convert_fusion.7.out_ref
  341.3 3.5 convolution_convert_fusion.2.qkv_ref
  344.8 2.2 convolution_convert_fusion.4
  347.0 101.9 %shard_map.454 = (bf16[8192,256]{1,0:T(8,128)(2,1)}, bf16[256,1024]{1,0:T(8,128)(2,1)}, bf16[256,3072]{1,0:T(8,128)(2,1)}, bf16[256,512]{1,0:T(8,128)(2,1)}, bf1...) custom-call(bf16[8192,128]{1,0:T(8,128)(2,1)} %get-tuple-element.78., ...), custom_call_target="tpu_custom_call" | custom-call | tf_op jit(solution)/shard_map/pallas_call | solution.py:669
  451.4 6.8 %convert.71 = f32[128,64,256]{2,1,0:T(8,128)} convert(bf16[128,64,256]{2,1,0:T(8,128)(2,1)} %bitcast.125) | non-fusion elementwise | flops 2097152 | bytes 12582912 | tf_op jit(solution)/shard_map/convert_element_type | solution.py:2093
  458.2 2.5 convert_element_type.143
  460.7 2.0 convert_element_type.141
  465.7 2.5 convert_element_type.144
  (129 shorter events, 26.5 us)
Async XLA Ops:
  7.2 143.9 %copy-start = (bf16[1024,1024]{1,0:T(8,128)(2,1)S(1)}, bf16[1024,1024]{1,0:T(8,128)(2,1)}, u32[]{:S(2)}) copy-start(bf16[1024,1024]{1,0:T(8,128)(2,1)} %param.50) | copy-start | bytes 6291460
  7.2 339.8 %all-reduce.4.cloned.1.call-start = ((), (), s32[]{:S(2)}) async-start(), calls=%async_computation | async-start | bytes 8388608 | tf_op jit(solution)/shard_map/psum | solution.py:2014
  20.5 92.0 %copy-start.15 = (bf16[256,1024]{1,0:T(8,128)(2,1)S(1)}, bf16[256,1024]{1,0:T(8,128)(2,1)}, u32[]{:S(2)}) copy-start(bf16[256,1024]{1,0:T(8,128)(2,1)} %param.44) | copy-start | bytes 1572868
  114.9 16.0 %copy-start.20 = (f32[4,1,2560]{2,1,0:T(1,128)S(1)}, f32[4,1,2560]{2,1,0:T(1,128)}, u32[]{:S(2)}) copy-start(f32[4,1,2560]{2,1,0:T(1,128)} %get-tuple-element.65) | copy-start | bytes 122884
  114.9 16.1 %copy-start.1 = (f32[128,1024]{1,0:T(8,128)S(1)}, f32[128,1024]{1,0:T(8,128)}, u32[]{:S(2)}) copy-start(f32[128,1024]{1,0:T(8,128)} %get-tuple-element.63) | copy-start | bytes 1572868
  147.8 3.3 copy-start.21
  147.8 3.3 copy-start.23
  151.1 6.2 %copy-start.9 = (bf16[4,128,1024]{2,1,0:T(8,128)(2,1)S(1)}, bf16[4,128,1024]{2,1,0:T(8,128)(2,1)}, u32[]{:S(2)}) copy-start(bf16[4,128,1024]{2,1,0:T(8,128)(2,1)} %shard_map.443) | copy-start | bytes 3145732
  157.3 2.6 copy-start.11
  160.5 1.0 copy-start.13
  164.1 3.3 copy-start.12
  164.1 3.3 copy-start.22
  183.1 2.9 copy-start.4
  185.2 0.8 copy-start.2
  287.0 2.7 copy-start.3
  287.0 2.7 copy-start.17
  317.9 16.8 %copy-start.5 = (bf16[512,768]{1,0:T(8,128)(2,1)S(1)}, bf16[512,768]{1,0:T(8,128)(2,1)}, u32[]{:S(2)}) copy-start(bf16[512,768]{1,0:T(8,128)(2,1)} %reshape.249) | copy-start | bytes 2359300
  341.3 3.5 copy-start.14
  451.4 6.9 %copy-start.7 = (bf16[256,4096]{1,0:T(8,128)(2,1)S(1)}, bf16[256,4096]{1,0:T(8,128)(2,1)}, u32[]{:S(2)}) copy-start(bf16[256,4096]{1,0:T(8,128)(2,1)} %get-tuple-element.99) | copy-start | bytes 6291460
  458.2 2.5 copy-start.8
  460.7 2.0 copy-start.16
  460.7 3.1 copy-start.10
  462.7 1.3 copy-start.19
  462.7 2.1 copy-start.18
  462.7 3.0 copy-start.6
Sparse Core Ops, SparseCore 0:
  164.2 115.8 all-reduce.3

commit v4 on v3

--- a/solution.py
+++ b/solution.py
@@ -189,519 +189,6 @@
 CHUNK_LANES = 256
 
 
-def sum_gradients(taps, out, qkv, conv, proj, vectors, up_sum, layer_parts, collective_id):
-    num_seq, num_utt = lax.axis_size("seq"), lax.axis_size("utt")
-    chips, blocks = num_seq // 2, num_seq // num_utt
-    width = taps.shape[1]
-    tap_rows = 2 * CHUNK_ROWS
-    tap_half = taps.shape[0] // 2 // tap_rows
-    column = out.shape[0]
-    half = column // 2
-    assert half == CHUNK_ROWS and width == CHUNK_ROWS and out.shape[1] % CHUNK_LANES == 0
-    proj_half = proj.shape[0] // num_utt // 2
-    proj_lanes = CHUNK_LANES * CHUNK_ROWS // proj_half
-    vector_half = vectors.shape[1] // 2
-    counts = [
-        blocks * tap_half,
-        out.shape[1] // CHUNK_LANES,
-        3 * num_utt * (column // CHUNK_LANES),
-        conv.shape[1] // CHUNK_LANES,
-        proj.shape[1] // proj_lanes,
-        1,
-    ]
-    assert column == CHUNK_LANES
-    starts = [sum(counts[:i]) for i in range(len(counts))]
-    total = sum(counts)
-
-    def kernel(
-        taps_ref,
-        out_ref,
-        qkv_ref,
-        conv_ref,
-        proj_ref,
-        vec_ref,
-        up_ref,
-        layer_ref,
-        taps_o,
-        out_o,
-        qkv_o,
-        conv_o,
-        proj_o,
-        vec_o,
-        up_o,
-        layer_o,
-        own_ref,
-        got_r,
-        got_l,
-        put_r,
-        put_l,
-        taps_mate,
-        out_mate,
-        *rest,
-    ):
-        mates, stages, gots = rest[0:4], rest[4:8], rest[8:12]
-        (
-            taps_send,
-            taps_recv,
-            out_send,
-            out_recv,
-            mate_send,
-            mate_recv,
-            peer_send,
-            peer_recv,
-            way_send_r,
-            way_send_l,
-            way_recv_r,
-            way_recv_l,
-            last_send,
-            last_recv,
-            up_send,
-            up_recv,
-            hand_send,
-            hand_recv,
-            layer_send,
-            layer_recv,
-            local_sem,
-        ) = rest[12:]
-        got_refs, put_refs = (got_r, got_l), (put_r, put_l)
-        way_send, way_recv = (way_send_r, way_send_l), (way_recv_r, way_recv_l)
-        grouped = (qkv_ref, conv_ref, proj_ref, vec_ref)
-        halves = (half, half, proj_half, vector_half)
-        me, me_utt = lax.axis_index("seq"), lax.axis_index("utt")
-        z, core = me // 2, lax.rem(me, 2)
-        block = me // num_utt
-        sibling = {"seq": me + 1 - 2 * core}
-        ends = (chips - 1, 0)
-        hops = ({"seq": me + 2}, {"seq": me - 2})
-        delays = (HOP_LAG * z, HOP_LAG * (chips - 1 - z))
-
-        def remote(src, dst, send, recv, device):
-            return pltpu.make_async_remote_copy(
-                src_ref=src,
-                dst_ref=dst,
-                send_sem=send,
-                recv_sem=recv,
-                device_id=device,
-                device_id_type=MESH,
-            )
-
-        def loop(first, last, body):
-            def run(i, carry):
-                body(i)
-                return carry
-
-            lax.fori_loop(first, last, run, 0)
-
-        def peer_of(i):
-            return lax.rem(me_utt + i, num_utt)
-
-        barrier = pltpu.get_barrier_semaphore()
-
-        def signal(device):
-            pl.semaphore_signal(barrier, inc=1, device_id=device, device_id_type=MESH)
-
-        signal(sibling)
-        loop(1, num_utt, lambda i: signal({"utt": peer_of(i)}))
-        for way in range(2):
-
-            @pl.when(z != ends[way])
-            def _(way=way):
-                signal(hops[way])
-
-        pl.semaphore_wait(
-            barrier,
-            num_utt
-            + (z != ends[0]).astype(jnp.int32)
-            + (z != ends[1]).astype(jnp.int32),
-        )
-
-        def tap_place(k, which):
-            return pl.ds(pl.multiple_of((which * tap_half + k) * tap_rows, tap_rows), tap_rows)
-
-        def half_rows(size, which):
-            return pl.ds(pl.multiple_of(which * size, size), size)
-
-        def group_place(n, b, which):
-            size = halves[n]
-            if n == 3:
-                return vec_ref.at[b, half_rows(size, which)]
-            return grouped[n].at[pl.ds(pl.multiple_of((2 * b + which) * size, size), size)]
-
-        def mate_taps(k):
-            return remote(
-                taps_ref.at[tap_place(k, 1 - core)],
-                taps_mate.at[pl.ds(pl.multiple_of(k * tap_rows, tap_rows), tap_rows)],
-                taps_send.at[k],
-                taps_recv.at[k],
-                sibling,
-            )
-
-        def mate_group(n, b):
-            return remote(
-                group_place(n, b, 1 - core),
-                mates[n].at[b],
-                mate_send.at[n, b],
-                mate_recv.at[n, b],
-                sibling,
-            )
-
-        mate_out = remote(
-            out_ref.at[half_rows(half, 1 - core)], out_mate, out_send, out_recv, sibling
-        )
-
-        def peer_group(n, b, slot):
-            return remote(
-                stages[n].at[b],
-                gots[n].at[slot],
-                peer_send.at[n, b],
-                peer_recv.at[n, slot],
-                {"utt": b},
-            )
-
-        def up_copy(b, slot):
-            rows = pl.ds(pl.multiple_of(b * column + core * half, half), half)
-            lanes = pl.ds(pl.multiple_of(slot * up_ref.shape[1], 128), up_ref.shape[1])
-            return remote(
-                up_ref.at[rows],
-                up_o.at[half_rows(half, core), lanes],
-                up_send.at[b],
-                up_recv.at[slot],
-                {"utt": b},
-            )
-
-        def up_hand(slot, which):
-            lanes = pl.ds(pl.multiple_of(slot * up_ref.shape[1], 128), up_ref.shape[1])
-            place = up_o.at[half_rows(half, which), lanes]
-            return remote(place, place, hand_send.at[slot], hand_recv.at[slot], sibling)
-
-        def layer_copy(b, slot):
-            return remote(
-                layer_ref.at[b], layer_o.at[slot], layer_send.at[b], layer_recv.at[slot], {"utt": b}
-            )
-
-        loop(0, 4, lambda k: mate_taps(k).start())
-        for n in range(4):
-            loop(0, num_utt, lambda b, n=n: mate_group(n, b).start())
-        mate_out.start()
-        loop(4, tap_half, lambda k: mate_taps(k).start())
-        own_up = pltpu.make_async_copy(
-            up_ref.at[pl.ds(pl.multiple_of(me_utt * column, column), column)],
-            up_o.at[
-                :, pl.ds(pl.multiple_of(me_utt * up_ref.shape[1], 128), up_ref.shape[1])
-            ],
-            local_sem.at[0],
-        )
-        own_up.start()
-        own_layer = pltpu.make_async_copy(
-            layer_ref.at[me_utt], layer_o.at[me_utt], local_sem.at[1]
-        )
-        own_layer.start()
-
-        def hand_on(b):
-            for n in range(4):
-                mate_group(n, b).wait_recv()
-                summed = (
-                    group_place(n, b, core)[...].astype(F32) + mates[n][b].astype(F32)
-                ).astype(BF16)
-
-                @pl.when(b != me_utt)
-                def _(n=n, summed=summed):
-                    stages[n][b] = summed
-                    peer_group(n, b, me_utt).start()
-
-                @pl.when(b == me_utt)
-                def _(n=n, summed=summed):
-                    gots[n][b] = summed
-
-        def chain_copy(way, chunk):
-            return remote(
-                put_refs[way].at[chunk],
-                got_refs[way].at[chunk],
-                way_send[way].at[chunk],
-                way_recv[way].at[chunk],
-                hops[way],
-            )
-
-        def lanes_of(k, size):
-            return pl.ds(pl.multiple_of(k * size, size), size)
-
-        def load_taps(k):
-            piece = lax.rem(k, tap_half)
-
-            @pl.when(k // tap_half == block)
-            def _():
-                mate_taps(piece).wait_recv()
-                for j in range(2):
-                    first = (core * tap_half + piece) * tap_rows + j * CHUNK_ROWS
-                    mine = taps_ref[pl.ds(pl.multiple_of(first, CHUNK_ROWS), CHUNK_ROWS), :]
-                    first = piece * tap_rows + j * CHUNK_ROWS
-                    other = taps_mate[pl.ds(pl.multiple_of(first, CHUNK_ROWS), CHUNK_ROWS), :]
-                    own_ref[k, :, j * width : (j + 1) * width] = mine.astype(F32) + other.astype(
-                        F32
-                    )
-
-            @pl.when(k // tap_half != block)
-            def _():
-                own_ref[k] = jnp.zeros((CHUNK_ROWS, CHUNK_LANES), F32)
-
-        def load_out(k):
-            @pl.when(k == 0)
-            def _():
-                mate_out.wait_recv()
-
-            lanes = lanes_of(k, CHUNK_LANES)
-            own_ref[starts[1] + k] = out_ref[half_rows(half, core), lanes].astype(
-                F32
-            ) + out_mate[:, lanes].astype(F32)
-
-        def load_qkv(k):
-            source, part = k // 3, lax.rem(k, 3)
-
-            @pl.when(jnp.logical_and(part == 0, source != me_utt))
-            def _():
-                peer_group(0, source, source).wait_recv()
-
-            own_ref[starts[2] + k] = gots[0][source, :, lanes_of(part, CHUNK_LANES)].astype(F32)
-
-        def peers_sum(n, lanes):
-            total = gots[n][0, :, lanes].astype(F32)
-            for b in range(1, num_utt):
-                total = total + gots[n][b, :, lanes].astype(F32)
-            return total
-
-        def await_peers(n):
-            def wait(b):
-                @pl.when(b != me_utt)
-                def _():
-                    peer_group(n, b, b).wait_recv()
-
-            loop(0, num_utt, wait)
-
-        def load_conv(k):
-            @pl.when(k == 0)
-            def _():
-                await_peers(1)
-
-            own_ref[starts[3] + k] = peers_sum(1, lanes_of(k, CHUNK_LANES))
-
-        def load_proj(k):
-            @pl.when(k == 0)
-            def _():
-                await_peers(2)
-
-            for j in range(proj_lanes // CHUNK_LANES):
-                first = k * proj_lanes + j * CHUNK_LANES
-                lanes = pl.ds(pl.multiple_of(first, CHUNK_LANES), CHUNK_LANES)
-                own_ref[starts[4] + k, j * proj_half : (j + 1) * proj_half, :] = peers_sum(2, lanes)
-
-        def load_vectors(k):
-            await_peers(3)
-            own_ref[starts[5]] = jnp.zeros((CHUNK_ROWS, CHUNK_LANES), F32)
-            own_ref[starts[5], 0:vector_half, 0:128] = peers_sum(3, slice(None))
-
-        loads = (load_taps, load_out, load_qkv, load_conv, load_proj, load_vectors)
-
-        def place_taps(k, which):
-            lanes = lanes_of(k // tap_half, width)
-            return taps_o.at[tap_place(lax.rem(k, tap_half), which), lanes]
-
-        def place_out(k, which):
-            return out_o.at[half_rows(half, which), lanes_of(k, CHUNK_LANES)]
-
-        def place_qkv(k, which):
-            lanes = lanes_of(lax.rem(k, 3) * num_utt + k // 3, CHUNK_LANES)
-            return qkv_o.at[half_rows(half, which), lanes]
-
-        def place_conv(k, which):
-            return conv_o.at[half_rows(half, which), lanes_of(k, CHUNK_LANES)]
-
-        def place_proj(k, which):
-            return proj_o.at[half_rows(proj_half, which), lanes_of(k, proj_lanes)]
-
-        def place_vectors(k, which):
-            return vec_o.at[half_rows(vector_half, which)]
-
-        places = (place_taps, place_out, place_qkv, place_conv, place_proj, place_vectors)
-
-        def store(n, k, value):
-            if n == 0:
-                for i in range(blocks):
-
-                    @pl.when(k // tap_half == i)
-                    def _(i=i):
-                        for j in range(2):
-                            first = (core * tap_half + lax.rem(k, tap_half)) * tap_rows
-                            first = pl.multiple_of(first + j * CHUNK_ROWS, CHUNK_ROWS)
-                            taps_o[pl.ds(first, CHUNK_ROWS), i * width : (i + 1) * width] = value[
-                                :, j * width : (j + 1) * width
-                            ]
-
-            elif n == 4:
-                for j in range(proj_lanes // CHUNK_LANES):
-                    first = k * proj_lanes + j * CHUNK_LANES
-                    proj_o[
-                        half_rows(proj_half, core),
-                        pl.ds(pl.multiple_of(first, CHUNK_LANES), CHUNK_LANES),
-                    ] = value[j * proj_half : (j + 1) * proj_half]
-            elif n == 5:
-                vec_o[half_rows(vector_half, core), :] = value[0:vector_half, 0:128]
-            else:
-                places[n](k, core)[...] = value
-
-        def last_copy(n, k, which):
-            place = places[n](k, which)
-            chunk = starts[n] + k
-            return remote(place, place, last_send.at[chunk], last_recv.at[chunk], sibling)
-
-        def within(chunk, n):
-            return jnp.logical_and(chunk >= starts[n], chunk < starts[n] + counts[n])
-
-        def step(t):
-            for n in range(6):
-
-                @pl.when(within(t, n))
-                def _(n=n):
-                    loads[n](t - starts[n])
-
-            @pl.when(jnp.logical_and(t >= 3, t < 3 + num_utt))
-            def _():
-                hand_on(lax.rem(me_utt + t - 2, num_utt))
-
-            @pl.when(t == 3 + num_utt)
-            def _():
-                loop(1, num_utt, lambda i: up_copy(peer_of(i), me_utt).start())
-                loop(1, num_utt, lambda i: layer_copy(peer_of(i), me_utt).start())
-
-            for way in range(2):
-                chunk = t - delays[way]
-
-                @pl.when(jnp.logical_and(chunk >= 0, chunk < total))
-                def _(way=way, chunk=chunk):
-                    first = ends[1 - way]
-
-                    @pl.when(z != first)
-                    def _():
-                        chain_copy(way, chunk).wait_recv()
-
-                        @pl.when(z != ends[way])
-                        def _():
-                            put_refs[way][chunk] = (
-                                own_ref[chunk] + got_refs[way][chunk].astype(F32)
-                            ).astype(BF16)
-
-                    @pl.when(z == first)
-                    def _():
-                        put_refs[way][chunk] = own_ref[chunk].astype(BF16)
-                        got_refs[way][chunk] = jnp.zeros((CHUNK_ROWS, CHUNK_LANES), BF16)
-
-                    @pl.when(z != ends[way])
-                    def _():
-                        chain_copy(way, chunk).start()
-
-            done = t - HOP_LAG * (chips - 1)
-
-            @pl.when(done >= 0)
-            def _():
-                value = (
-                    own_ref[done]
-                    + got_refs[0][done].astype(F32)
-                    + got_refs[1][done].astype(F32)
-                ).astype(BF16)
-                for n in range(6):
-
-                    @pl.when(within(done, n))
-                    def _(n=n):
-                        store(n, done - starts[n], value)
-                        last_copy(n, done - starts[n], core).start()
-
-        loop(0, total + HOP_LAG * (chips - 1), step)
-
-        def up_arrived(i):
-            up_copy(peer_of(i), peer_of(i)).wait_recv()
-            up_hand(peer_of(i), core).start()
-
-        loop(1, num_utt, up_arrived)
-        own_up.wait()
-        own_layer.wait()
-
-        def sent_chunk(chunk):
-            for way in range(2):
-
-                @pl.when(z != ends[way])
-                def _(way=way):
-                    chain_copy(way, chunk).wait_send()
-
-        loop(0, total, sent_chunk)
-        for n in range(6):
-
-            def handed(k, n=n):
-                last_copy(n, k, core).wait_send()
-                last_copy(n, k, 1 - core).wait_recv()
-
-            loop(0, counts[n], handed)
-        loop(0, tap_half, lambda k: mate_taps(k).wait_send())
-
-        mate_out.wait_send()
-
-        def sent_peer(i):
-            b = peer_of(i)
-            for n in range(4):
-                peer_group(n, b, me_utt).wait_send()
-            up_copy(b, me_utt).wait_send()
-            up_hand(b, core).wait_send()
-            up_hand(b, 1 - core).wait_recv()
-            layer_copy(b, me_utt).wait_send()
-            layer_copy(b, b).wait_recv()
-
-        loop(1, num_utt, sent_peer)
-        for n in range(4):
-            loop(0, num_utt, lambda b, n=n: mate_group(n, b).wait_send())
-
-    dma = pltpu.SemaphoreType.DMA
-    vmem, anywhere = pl.BlockSpec(memory_space=pltpu.VMEM), pl.BlockSpec(memory_space=pl.ANY)
-    chunk_shape = (total, CHUNK_ROWS, CHUNK_LANES)
-    group_shapes = [
-        (num_utt, half, qkv.shape[1]),
-        (num_utt, half, conv.shape[1]),
-        (num_utt, proj_half, proj.shape[1]),
-        (num_utt, vector_half, 128),
-    ]
-    return pl.pallas_call(
-        kernel,
-        out_shape=[
-            jax.ShapeDtypeStruct(shape, BF16)
-            for shape in (
-                (taps.shape[0], blocks * width),
-                out.shape,
-                (column, num_utt * qkv.shape[1]),
-                (column, conv.shape[1]),
-                (2 * proj_half, proj.shape[1]),
-                vectors.shape[1:],
-                (column, num_utt * up_sum.shape[1]),
-                layer_parts.shape,
-            )
-        ],
-        in_specs=[vmem] * 6 + [anywhere] * 2,
-        out_specs=[vmem] * 6 + [anywhere] * 2,
-        scratch_shapes=[pltpu.VMEM(chunk_shape, F32)]
-        + [pltpu.VMEM(chunk_shape, BF16)] * 4
-        + [
-            pltpu.VMEM((taps.shape[0] // 2, width), BF16),
-            pltpu.VMEM((half, out.shape[1]), BF16),
-        ]
-        + [pltpu.VMEM(shape, BF16) for shape in group_shapes] * 3
-        + [dma((tap_half,))] * 2
-        + [dma] * 2
-        + [dma((4, num_utt))] * 4
-        + [dma((total,))] * 6
-        + [dma((num_utt,))] * 6
-        + [dma((2,))],
-        compiler_params=pltpu.CompilerParams(
-            collective_id=collective_id, has_side_effects=True, vmem_limit_bytes=VMEM_BYTES
-        ),
-    )(taps, out, qkv, conv, proj, vectors, up_sum, layer_parts)
-
-
 def sum_gradients_plain(taps, out, qkv, conv, proj, vectors, up_sum, layer_parts):
     num_seq, num_utt = lax.axis_size("seq"), lax.axis_size("utt")
     blocks = num_seq // num_utt
@@ -861,7 +348,9 @@
 def tap_tile(taps_ref, first, depth, h):
     return jnp.concatenate(
         [
-            taps_ref[pl.ds(TILE + first - r * GW, depth), h * GW : (h + 1) * GW]
+            taps_ref[
+                pl.ds(pl.multiple_of(TILE + first - r * GW, GW), depth), h * GW : (h + 1) * GW
+            ]
             for r in range(PACK)
         ],
         axis=1,
@@ -1780,6 +1269,1164 @@
     )(steps, starts, conv, proj, vectors, qkv, up, grad_rows, taps, taps_bias, bias)
 
 
+RING = 16
+
+
+def back_forth(
+    flat,
+    out_weight,
+    resid_one,
+    vectors,
+    up_bias,
+    attn_in,
+    qkv_all,
+    heads,
+    attn_f32,
+    lse,
+    pos_pre,
+    pos_in,
+    masked,
+    steps,
+    conv_pre,
+    feat_low,
+    conv_all,
+    proj_all,
+    up_all,
+    down_weight,
+    gout_all,
+    taps,
+    collective_id,
+):
+    num_seq, num_utt = lax.axis_size("seq"), lax.axis_size("utt")
+    chips = num_seq // 2
+    frames = resid_one.shape[0]
+    length = frames * num_seq
+    rows_all = num_utt * frames
+    column = out_weight.shape[0]
+    half = column // 2
+    hidden = up_all.shape[1]
+    per_column = num_seq // num_utt
+    width = column // per_column
+    groups = width // GW
+    num_blocks = num_utt * per_column
+    rows = length // PACK
+    low = C // num_utt
+    proj_rows = C // num_utt
+    proj_half = proj_rows // 2
+    vec_rows = 64
+    vec_half = vec_rows // 2
+    final_lag = HOP_LAG * (chips - 1)
+    assert half == CHUNK_ROWS and width == CHUNK_ROWS and column == CHUNK_LANES
+    assert final_lag + 7 <= RING
+
+    DOWN, UP, OUT, QKV, TAPS, CONV, PROJ, VEC = range(8)
+    lane_blocks = {DOWN: D // CHUNK_LANES, UP: hidden // CHUNK_LANES, OUT: D // CHUNK_LANES}
+    lane_blocks[QKV] = 3 * column // CHUNK_LANES
+    row_blocks = {DOWN: hidden // column, UP: D // column, OUT: 1, QKV: D // column}
+    counts = [row_blocks[n] * lane_blocks[n] for n in range(4)]
+    tap_chunks = KPOS * GW // 2 // CHUNK_ROWS
+    counts += [tap_chunks, C // CHUNK_LANES, D // CHUNK_LANES, 1]
+    starts = [sum(counts[:n]) for n in range(8)]
+    total = sum(counts)
+    chunk_rows = [CHUNK_ROWS] * 6 + [proj_half, vec_half]
+    chunk_lanes = [CHUNK_LANES] * 7 + [128]
+    assert counts[CONV] + counts[PROJ] + counts[VEC] <= RING
+
+    dma = pltpu.SemaphoreType.DMA
+    chunk = (RING, CHUNK_ROWS, CHUNK_LANES)
+    group_shapes = [
+        (num_utt, half, C),
+        (num_utt, proj_half, D),
+        (num_utt, vec_half, 128),
+    ]
+    utt_rows = (num_utt, frames, D)
+    scratch = Names(
+        part_out=pltpu.VMEM(utt_rows, BF16),
+        layer_out=pltpu.VMEM(utt_rows, BF16),
+        got_out=pltpu.VMEM(utt_rows, BF16),
+        got_ffn=pltpu.VMEM(utt_rows, BF16),
+        got_qkv=pltpu.VMEM(utt_rows, BF16),
+        got_layer=pltpu.VMEM(utt_rows, BF16),
+        mine=pltpu.VMEM((frames, D), F32),
+        ffn_all=pltpu.VMEM((rows_all, D), BF16),
+        agrad_all=pltpu.VMEM((rows_all, D), BF16),
+        resid_two=pltpu.VMEM((frames, D), F32),
+        resid2_grad=pltpu.VMEM((frames, D), F32),
+        resid1_grad=pltpu.VMEM((frames, D), F32),
+        ghead_out=pltpu.VMEM((num_seq, frames, width), BF16),
+        ghead=pltpu.VMEM((length, width), BF16),
+        dqkv=pltpu.VMEM((3, length, width), BF16),
+        dk_acc=pltpu.VMEM((length, width), F32),
+        dv_acc=pltpu.VMEM((length, width), F32),
+        qback=pltpu.VMEM((3, rows_all, column), BF16),
+        blocks=pltpu.VMEM((num_blocks, frames, width), BF16),
+        pos_grad=pltpu.VMEM((length, width), BF16),
+        pos_own=pltpu.VMEM((length, width), BF16),
+        pos_back=pltpu.VMEM((num_blocks, frames, width), BF16),
+        vec_f32=pltpu.VMEM((num_utt, vec_rows, 128), F32),
+        part_down=pltpu.VMEM((hidden, D), BF16),
+        part_up=pltpu.VMEM((D, hidden), BF16),
+        part_outw=pltpu.VMEM((column, D), BF16),
+        part_qkv=pltpu.VMEM((D, 3 * column), BF16),
+        part_taps=pltpu.VMEM((KPOS * GW, width), BF16),
+        part_conv=pltpu.VMEM((2 * C, C), BF16),
+        part_proj=pltpu.VMEM((C, D), BF16),
+        part_vec=pltpu.VMEM((num_utt, vec_rows, 128), BF16),
+        mate_down=pltpu.VMEM((hidden // 2, D), BF16),
+        mate_up=pltpu.VMEM((D // 2, hidden), BF16),
+        mate_outw=pltpu.VMEM((half, D), BF16),
+        mate_qkv=pltpu.VMEM((D // 2, 3 * column), BF16),
+        mate_taps=pltpu.VMEM((KPOS * GW // 2, width), BF16),
+        mate_conv=pltpu.VMEM(group_shapes[0], BF16),
+        mate_proj=pltpu.VMEM(group_shapes[1], BF16),
+        mate_vec=pltpu.VMEM(group_shapes[2], BF16),
+        stage_conv=pltpu.VMEM(group_shapes[0], BF16),
+        stage_proj=pltpu.VMEM(group_shapes[1], BF16),
+        stage_vec=pltpu.VMEM(group_shapes[2], BF16),
+        got_conv=pltpu.VMEM(group_shapes[0], BF16),
+        got_proj=pltpu.VMEM(group_shapes[1], BF16),
+        got_vec=pltpu.VMEM(group_shapes[2], BF16),
+        own=pltpu.VMEM(chunk, F32),
+        got_r=pltpu.VMEM(chunk, BF16),
+        got_l=pltpu.VMEM(chunk, BF16),
+        put_r=pltpu.VMEM(chunk, BF16),
+        put_l=pltpu.VMEM(chunk, BF16),
+        result=pltpu.VMEM(chunk, BF16),
+        local=dma((8,)),
+        out_send=dma((num_utt,)),
+        out_recv=dma((num_utt,)),
+        ffn_send=dma((num_utt,)),
+        ffn_recv=dma((num_utt,)),
+        back_send=dma((num_utt,)),
+        back_recv=dma((num_utt,)),
+        agrad_send=dma((num_utt,)),
+        agrad_recv=dma((num_utt,)),
+        layer_send=dma((num_utt,)),
+        layer_recv=dma((num_utt,)),
+        qpart_send=dma((num_utt,)),
+        qpart_recv=dma((num_utt,)),
+        ghead_send=dma((num_seq,)),
+        ghead_recv=dma((num_seq,)),
+        dq_send=dma((num_seq,)),
+        dq_recv=dma((num_seq,)),
+        dkv_send=dma((num_seq,)),
+        dkv_recv=dma((num_seq,)),
+        there_send=dma((num_blocks,)),
+        there_recv=dma((num_seq,)),
+        home_send=dma((num_seq,)),
+        home_recv=dma((num_blocks,)),
+        mate_send=dma((5, tap_chunks)),
+        mate_recv=dma((5, tap_chunks)),
+        gmate_send=dma((3, num_utt)),
+        gmate_recv=dma((3, num_utt)),
+        peer_send=dma((3, num_utt)),
+        peer_recv=dma((3, num_utt)),
+        right_send=dma((total,)),
+        right_recv=dma((total,)),
+        left_send=dma((total,)),
+        left_recv=dma((total,)),
+        keep=dma((total,)),
+        last_send=dma((total,)),
+        last_recv=dma((total,)),
+        late_send=dma((2, num_utt, 3)),
+        late_recv=dma((2, num_utt, 3)),
+        hand_send=dma((2, num_utt, 3)),
+        hand_recv=dma((2, num_utt, 3)),
+        late_own=dma((2, 3)),
+    )
+    late_wide = (column, hidden)
+    late_parts = (3, 1)
+
+    def kernel(
+        flat_ref,
+        outw_ref,
+        resid_ref,
+        vec_ref,
+        up_bias_ref,
+        attn_in_ref,
+        qkv_ref,
+        heads_ref,
+        attn_ref,
+        lse_ref,
+        pos_pre_ref,
+        pos_in_ref,
+        mask_ref,
+        steps_ref,
+        pre_ref,
+        low_ref,
+        conv_ref,
+        proj_ref,
+        up_hbm,
+        down_hbm,
+        gout_hbm,
+        taps_hbm,
+        layer_o,
+        feat_o,
+        down_o,
+        up_mid,
+        outw_o,
+        qkv_mid,
+        taps_o,
+        conv_o,
+        proj_o,
+        vec_o,
+        up_o,
+        qkv_o,
+        *rest,
+    ):
+        s = scratch.bind(rest)
+        group = Regroup()
+        me, me_utt = group.me_seq, group.me_utt
+        z, core = me // 2, lax.rem(me, 2)
+        block = me // num_utt
+        sibling = {"seq": me + 1 - 2 * core}
+
+        def peer_of(i):
+            return lax.rem(me_utt + i, num_utt)
+
+        def peers(body):
+            loop(1, num_utt, lambda i: body(peer_of(i)))
+
+        def seq_peers(body):
+            loop(1, num_seq, lambda i: body(lax.rem(me + i, num_seq)))
+
+        barrier = pltpu.get_barrier_semaphore()
+
+        def signal(device):
+            pl.semaphore_signal(barrier, inc=1, device_id=device, device_id_type=MESH)
+
+        peers(lambda b: signal({"utt": b}))
+        seq_peers(lambda f: signal({"seq": f}))
+        group.each(num_seq, group.by_shard, lambda i, device: signal(device))
+        group.each(num_blocks, group.by_block, lambda i, device: signal(device))
+        s.vec_f32[...] = jnp.zeros_like(s.vec_f32)
+
+        def entered():
+            pl.semaphore_wait(
+                barrier, num_utt - 1 + num_seq - 1 + num_blocks + num_seq - 2 * group.is_own
+            )
+
+        def vector(first, size):
+            return jnp.concatenate(
+                [vec_ref[b, :, first : first + size] for b in range(num_utt)], axis=1
+            )
+
+        def own_rows(index):
+            return block_rows(index, frames)
+
+        def put_vector(first_row, value):
+            share = value.shape[1] // num_utt
+            for b in range(num_utt):
+                for j in range(share // 128):
+                    lanes = slice(b * share + j * 128, b * share + (j + 1) * 128)
+                    s.vec_f32[b, first_row + j : first_row + j + 1, :] = value[:, lanes]
+
+        def put_column(first_row, value):
+            for j in range(value.shape[1] // 128):
+                s.vec_f32[me_utt, first_row + j : first_row + j + 1, :] = value[
+                    :, j * 128 : (j + 1) * 128
+                ]
+
+        first = 4 * low + 2 * column
+        attn_gain = vector(first, column)
+        out_bias = vector(first + 2 * column, column)
+        ffn_gain = vector(first + 3 * column, column)
+        ffn_shift = vector(first + 4 * column, column)
+        down_bias = vector(first + 5 * column, column)
+
+        parts = (s.part_down, s.part_up, s.part_outw, s.part_qkv, s.part_taps)
+        part_mates = (s.mate_down, s.mate_up, s.mate_outw, s.mate_qkv, s.mate_taps)
+        finals = (down_o, up_mid, outw_o, qkv_mid, taps_o, conv_o, proj_o, vec_o)
+        grouped = (s.part_conv, s.part_proj, s.part_vec)
+        mates = (s.mate_conv, s.mate_proj, s.mate_vec)
+        stages = (s.stage_conv, s.stage_proj, s.stage_vec)
+        gots = (s.got_conv, s.got_proj, s.got_vec)
+        sizes = (half, proj_half, vec_half)
+        got_refs, put_refs = (s.got_r, s.got_l), (s.put_r, s.put_l)
+        way_send, way_recv = (s.right_send, s.left_send), (s.right_recv, s.left_recv)
+        ends = (chips - 1, 0)
+        hops = ({"seq": me + 2}, {"seq": me - 2})
+        delays = (HOP_LAG * z, HOP_LAG * (chips - 1 - z))
+
+        def mate_copy(n, k):
+            if n == TAPS:
+                source = half_rows(0, tap_chunks * CHUNK_ROWS, 1 - core)
+                place = pl.ds(
+                    pl.multiple_of(((1 - core) * tap_chunks + k) * CHUNK_ROWS, CHUNK_ROWS),
+                    CHUNK_ROWS,
+                )
+                source = place
+            else:
+                source = half_rows(k * column, half, 1 - core)
+            return remote(
+                parts[n].at[source],
+                part_mates[n].at[block_rows(k, CHUNK_ROWS)],
+                s.mate_send.at[n, k],
+                s.mate_recv.at[n, k],
+                sibling,
+            )
+
+        mate_counts = [row_blocks[n] for n in range(4)] + [tap_chunks]
+
+        def announce(n):
+            loop(0, mate_counts[n], lambda k: mate_copy(n, k).start())
+
+        def group_place(n, b, which):
+            if n == 2:
+                return s.part_vec.at[b, half_rows(0, vec_half, which)]
+            return grouped[n].at[half_rows(b * 2 * sizes[n], sizes[n], which)]
+
+        def group_mate(n, b):
+            return remote(
+                group_place(n, b, 1 - core),
+                mates[n].at[b],
+                s.gmate_send.at[n, b],
+                s.gmate_recv.at[n, b],
+                sibling,
+            )
+
+        def group_peer(n, b, slot):
+            return remote(
+                stages[n].at[b],
+                gots[n].at[slot],
+                s.peer_send.at[n, b],
+                s.peer_recv.at[n, slot],
+                {"utt": b},
+            )
+
+        def hand_on(n, b):
+            group_mate(n, b).wait_recv()
+            summed = (
+                group_place(n, b, core)[...].astype(F32) + mates[n][b].astype(F32)
+            ).astype(BF16)
+
+            @pl.when(b != me_utt)
+            def _():
+                stages[n][b] = summed
+                group_peer(n, b, me_utt).start()
+
+            @pl.when(b == me_utt)
+            def _():
+                gots[n][b] = summed
+
+        def lanes_of(k, size):
+            return pl.ds(pl.multiple_of(k * size, size), size)
+
+        def load(n, k, slot):
+            if n < 4:
+                b, j = k // lane_blocks[n], lax.rem(k, lane_blocks[n])
+
+                @pl.when(j == 0)
+                def _():
+                    mate_copy(n, b).wait_recv()
+
+                lanes = lanes_of(j, CHUNK_LANES)
+                s.own[slot] = parts[n][half_rows(b * column, half, core), lanes].astype(
+                    F32
+                ) + part_mates[n][block_rows(b, CHUNK_ROWS), lanes].astype(F32)
+            elif n == TAPS:
+                mate_copy(n, k).wait_recv()
+                place = pl.ds(
+                    pl.multiple_of((core * tap_chunks + k) * CHUNK_ROWS, CHUNK_ROWS), CHUNK_ROWS
+                )
+                value = s.part_taps[place, :].astype(F32) + s.mate_taps[
+                    block_rows(k, CHUNK_ROWS), :
+                ].astype(F32)
+                for i in range(per_column):
+                    s.own[slot, :, i * width : (i + 1) * width] = jnp.where(block == i, value, 0.0)
+            else:
+                g = n - CONV
+
+                @pl.when(k == 0)
+                def _():
+                    def wait(b):
+                        @pl.when(b != me_utt)
+                        def _():
+                            group_peer(g, b, b).wait_recv()
+
+                    loop(0, num_utt, wait)
+
+                lanes = lanes_of(k, chunk_lanes[n])
+                value = gots[g][0, :, lanes].astype(F32)
+                for b in range(1, num_utt):
+                    value = value + gots[g][b, :, lanes].astype(F32)
+                s.own[slot, 0 : chunk_rows[n], 0 : chunk_lanes[n]] = value
+
+        def place(n, k, which):
+            if n < 4:
+                b, j = k // lane_blocks[n], lax.rem(k, lane_blocks[n])
+                return finals[n].at[half_rows(b * column, half, which), lanes_of(j, CHUNK_LANES)]
+            if n == TAPS:
+                first = (which * tap_chunks + k) * CHUNK_ROWS
+                return finals[n].at[pl.ds(pl.multiple_of(first, CHUNK_ROWS), CHUNK_ROWS)]
+            return finals[n].at[
+                half_rows(0, chunk_rows[n], which), lanes_of(k, chunk_lanes[n])
+            ]
+
+        def keep_copy(n, k, slot):
+            source = s.result.at[slot, pl.ds(0, chunk_rows[n]), pl.ds(0, chunk_lanes[n])]
+            return pltpu.make_async_copy(source, place(n, k, core), s.keep.at[starts[n] + k])
+
+        def last_copy(n, k, slot, which):
+            index = starts[n] + k
+            source = s.result.at[slot, pl.ds(0, chunk_rows[n]), pl.ds(0, chunk_lanes[n])]
+            return remote(
+                source, place(n, k, which), s.last_send.at[index], s.last_recv.at[index], sibling
+            )
+
+        def whole_done(index):
+            slot = lax.rem(index, RING)
+            pltpu.make_async_copy(
+                s.result.at[slot], down_o.at[0:CHUNK_ROWS, 0:CHUNK_LANES], s.keep.at[index]
+            ).wait()
+            remote(
+                s.result.at[slot],
+                down_o.at[0:CHUNK_ROWS, 0:CHUNK_LANES],
+                s.last_send.at[index],
+                s.last_recv.at[index],
+                sibling,
+            ).wait_send()
+
+        def chain_copy(way, index):
+            slot = lax.rem(index, RING)
+            return remote(
+                put_refs[way].at[slot],
+                got_refs[way].at[slot],
+                way_send[way].at[index],
+                way_recv[way].at[index],
+                hops[way],
+            )
+
+        def sums(begin, end, shift=None):
+            def near(n, low_step, high_step):
+                return starts[n] < high_step and starts[n] + counts[n] > low_step
+
+            def step(t):
+                for n in range(8):
+                    if near(n, begin, end):
+
+                        @pl.when(jnp.logical_and(t >= starts[n], t < starts[n] + counts[n]))
+                        def _(n=n):
+                            load(n, t - starts[n], lax.rem(t, RING))
+
+                for way in range(2):
+                    index = t - delays[way]
+
+                    @pl.when(jnp.logical_and(index >= 0, index < total))
+                    def _(way=way, index=index):
+                        slot = lax.rem(index, RING)
+
+                        @pl.when(z != ends[way])
+                        def _():
+                            @pl.when(index >= RING)
+                            def _():
+                                chain_copy(way, index - RING).wait_send()
+
+                        @pl.when(z != ends[1 - way])
+                        def _():
+                            chain_copy(way, index).wait_recv()
+
+                            @pl.when(z != ends[way])
+                            def _():
+                                put_refs[way][slot] = (
+                                    s.own[slot] + got_refs[way][slot].astype(F32)
+                                ).astype(BF16)
+
+                        @pl.when(z == ends[1 - way])
+                        def _():
+                            put_refs[way][slot] = s.own[slot].astype(BF16)
+                            got_refs[way][slot] = jnp.zeros((CHUNK_ROWS, CHUNK_LANES), BF16)
+
+                        @pl.when(z != ends[way])
+                        def _():
+                            chain_copy(way, index).start()
+
+                done = t - final_lag
+
+                @pl.when(done >= 0)
+                def _():
+                    slot = lax.rem(done, RING)
+
+                    @pl.when(done >= RING)
+                    def _():
+                        whole_done(done - RING)
+
+                    s.result[slot] = (
+                        s.own[slot]
+                        + got_refs[0][slot].astype(F32)
+                        + got_refs[1][slot].astype(F32)
+                    ).astype(BF16)
+                    for n in range(8):
+                        if near(n, begin - final_lag, end - final_lag):
+
+                            @pl.when(
+                                jnp.logical_and(done >= starts[n], done < starts[n] + counts[n])
+                            )
+                            def _(n=n):
+                                keep_copy(n, done - starts[n], slot).start()
+                                last_copy(n, done - starts[n], slot, core).start()
+
+            if isinstance(shift, tuple):
+                loop(shift[0], shift[1], step)
+            elif end > begin:
+                loop(begin, end, step)
+
+        def out_copy(b, slot):
+            return remote(
+                s.part_out.at[b],
+                s.got_out.at[slot],
+                s.out_send.at[b],
+                s.out_recv.at[slot],
+                {"utt": b},
+            )
+
+        def ffn_copy(b, slot):
+            place = own_rows(slot)
+            return remote(
+                s.ffn_all.at[place],
+                s.ffn_all.at[place],
+                s.ffn_send.at[b],
+                s.ffn_recv.at[slot],
+                {"utt": b},
+            )
+
+        def back_copy(b, slot):
+            return remote(
+                s.part_out.at[b],
+                s.got_ffn.at[slot],
+                s.back_send.at[b],
+                s.back_recv.at[slot],
+                {"utt": b},
+            )
+
+        def agrad_copy(b, slot):
+            place = own_rows(slot)
+            return remote(
+                s.agrad_all.at[place],
+                s.agrad_all.at[place],
+                s.agrad_send.at[b],
+                s.agrad_recv.at[slot],
+                {"utt": b},
+            )
+
+        def layer_copy(b, slot):
+            return remote(
+                s.layer_out.at[b],
+                s.got_layer.at[slot],
+                s.layer_send.at[b],
+                s.layer_recv.at[slot],
+                {"utt": b},
+            )
+
+        def qpart_copy(b, slot):
+            return remote(
+                s.part_out.at[b],
+                s.got_qkv.at[slot],
+                s.qpart_send.at[b],
+                s.qpart_recv.at[slot],
+                {"utt": b},
+            )
+
+        def hand_out(b, part, copy):
+            @pl.when(b != me_utt)
+            def _():
+                s.part_out[b] = part.astype(BF16)
+                copy(b, me_utt).start()
+
+            @pl.when(b == me_utt)
+            def _():
+                s.mine[...] = part
+
+        def from_peers(got, own):
+            value = own
+            for i in range(1, num_utt):
+                value = value + got[peer_of(i)].astype(F32)
+            return value
+
+        def feed_forward(up, down, gout, hidden_low, hidden_grad, down_grad, sems):
+            loads = [
+                pltpu.make_async_copy(source, target, sems.at[i])
+                for i, (source, target) in enumerate(
+                    ((gout_hbm, gout), (down_hbm, down), (up_hbm, up))
+                )
+            ]
+            for copy in loads:
+                copy.start()
+            entered()
+
+            def out_block(i):
+                b = peer_of(i)
+                part = jnp.dot(flat_ref[own_rows(b), :], outw_ref[...], preferred_element_type=F32)
+                hand_out(b, part, out_copy)
+
+            loop(1, num_utt + 1, out_block)
+            loads[0].wait()
+            loads[1].wait()
+
+            def down_block(b):
+                down_grad[own_rows(b), :] = nt_dot(gout[own_rows(b), :], down[...])
+
+            loop(0, num_utt, down_block)
+            peers(lambda b: out_copy(b, b).wait_recv())
+            resid_two = resid_ref[...] + from_peers(s.got_out, s.mine[...]) + out_bias
+            s.resid_two[...] = resid_two
+            normed, _ = norm_parts(resid_two)
+            s.ffn_all[own_rows(me_utt), :] = (normed * ffn_gain + ffn_shift).astype(BF16)
+            peers(lambda b: ffn_copy(b, me_utt).start())
+            peers(lambda b: out_copy(b, me_utt).wait_send())
+            loads[2].wait()
+
+            def ffn_block(i):
+                b = peer_of(i)
+
+                @pl.when(i > 0)
+                def _():
+                    ffn_copy(b, b).wait_recv()
+
+                where = own_rows(b)
+
+                def cut_block(j):
+                    cut = block_rows(j, column)
+                    pre = jnp.dot(s.ffn_all[where, :], up[:, cut], preferred_element_type=F32)
+                    act, slope = gelu_parts(pre + up_bias_ref[:, cut])
+                    hidden_low[where, cut] = act.astype(BF16)
+                    hidden_grad[where, cut] = (down_grad[where, cut] * slope).astype(BF16)
+
+                loop(0, hidden // column, cut_block)
+                hand_out(b, nt_dot(hidden_grad[where, :], up[...]), back_copy)
+
+            loop(0, num_utt, ffn_block)
+
+            def down_grads(i):
+                cut = block_rows(i, column)
+                s.part_down[cut, :] = inner_dot(hidden_low[:, cut], gout[...]).astype(BF16)
+
+            loop(0, hidden // column, down_grads)
+            announce(DOWN)
+
+            def up_grads(i):
+                cut = block_rows(i, column)
+                s.part_up[cut, :] = inner_dot(s.ffn_all[:, cut], hidden_grad[...]).astype(BF16)
+
+            loop(0, D // column, up_grads)
+            announce(UP)
+            put_column(26, column_sum(hidden_grad[...].astype(F32)))
+            sums(*SITES[0])
+            peers(lambda b: back_copy(b, b).wait_recv())
+            back = from_peers(s.got_ffn, s.mine[...])
+            normed, scale = norm_parts(s.resid_two[...])
+            put_vector(16, column_sum(back * normed))
+            put_vector(18, column_sum(back))
+            own_grad = gout[own_rows(me_utt), :].astype(F32)
+            put_vector(20, column_sum(own_grad))
+            grad = own_grad + norm_back(back * ffn_gain, normed, scale)
+            s.resid2_grad[...] = grad
+            grad = grad.astype(BF16)
+            s.agrad_all[own_rows(me_utt), :] = grad
+            peers(lambda b: agrad_copy(b, me_utt).start())
+            put_vector(14, column_sum(grad.astype(F32)))
+            peers(lambda b: back_copy(b, me_utt).wait_send())
+            def layer_block(b):
+                part = jnp.dot(hidden_low[own_rows(b), :], down[...], preferred_element_type=F32)
+
+                @pl.when(b != me_utt)
+                def _():
+                    s.layer_out[b] = part.astype(BF16)
+
+                @pl.when(b == me_utt)
+                def _():
+                    s.resid_two[...] += part + down_bias
+
+            loop(0, num_utt, layer_block)
+            sums(*SITES[1])
+
+        vmem = pltpu.VMEM
+        pl.run_scoped(
+            feed_forward,
+            vmem((D, hidden), BF16),
+            vmem((hidden, D), BF16),
+            vmem((rows_all, D), BF16),
+            vmem((rows_all, hidden), BF16),
+            vmem((rows_all, hidden), BF16),
+            vmem((rows_all, hidden), F32),
+            dma((3,)),
+        )
+
+        def ghead_copy(dest, slot):
+            return remote(
+                s.ghead_out.at[dest],
+                s.ghead.at[own_rows(slot)],
+                s.ghead_send.at[dest],
+                s.ghead_recv.at[slot],
+                {"seq": dest},
+            )
+
+        def ghead_block(i):
+            b = peer_of(i)
+
+            @pl.when(i > 0)
+            def _():
+                agrad_copy(b, b).wait_recv()
+
+            grad = nt_dot(s.agrad_all[own_rows(b), :], outw_ref[...]).astype(BF16)
+            for j in range(per_column):
+                dest = j * num_utt + b
+                s.ghead_out[dest] = grad[:, j * width : (j + 1) * width]
+
+                @pl.when(dest != me)
+                def _(dest=dest):
+                    ghead_copy(dest, me).start()
+
+                @pl.when(dest == me)
+                def _(dest=dest):
+                    s.ghead[own_rows(me), :] = s.ghead_out[dest]
+
+        loop(0, num_utt, ghead_block)
+        peers(lambda b: layer_copy(b, me_utt).start())
+        s.part_outw[...] = inner_dot(flat_ref[...], s.agrad_all[...]).astype(BF16)
+        announce(OUT)
+        seq_peers(lambda f: ghead_copy(f, f).wait_recv())
+
+        my_rows = own_rows(lax.rem(me, num_utt))
+
+        def back_place(parts_, slot):
+            lanes = pl.ds(pl.multiple_of(slot // num_utt * width, width), width)
+            return s.qback.at[parts_, own_rows(lax.rem(slot, num_utt)), lanes]
+
+        def dq_copy(f, slot):
+            return remote(
+                s.dqkv.at[0, own_rows(f)],
+                back_place(0, slot),
+                s.dq_send.at[f],
+                s.dq_recv.at[slot],
+                {"seq": f},
+            )
+
+        def dkv_copy(f, slot):
+            return remote(
+                s.dqkv.at[pl.ds(1, 2), own_rows(f)],
+                back_place(pl.ds(1, 2), slot),
+                s.dkv_send.at[f],
+                s.dkv_recv.at[slot],
+                {"seq": f},
+            )
+
+        my_lanes = pl.ds(pl.multiple_of(block * width, width), width)
+        s.dk_acc[...] = jnp.zeros_like(s.dk_acc)
+        s.dv_acc[...] = jnp.zeros_like(s.dv_acc)
+        beside, q_blocks = SITES[2], length // Q_BLOCK
+        steps_beside = (beside[1] - beside[0]) // q_blocks
+
+        def query_block(i):
+            where = block_rows(i, Q_BLOCK)
+            for h in range(groups):
+                lanes = slice(h * HEAD_DIM, (h + 1) * HEAD_DIM)
+                keys, values = heads_ref[1, :, lanes], heads_ref[2, :, lanes]
+                queries, grads = heads_ref[0, where, lanes], s.ghead[where, lanes]
+                inner = jnp.sum(grads.astype(F32) * attn_ref[where, lanes], -1, keepdims=True)
+                probs = jnp.exp(nt_dot(queries, keys) * SCALE - lse_ref[where, h : h + 1])
+                score_grad = (probs * (nt_dot(grads, values) - inner)).astype(BF16)
+                s.dqkv[0, where, lanes] = (
+                    jnp.dot(score_grad, keys, preferred_element_type=F32) * SCALE
+                ).astype(BF16)
+                s.dk_acc[:, lanes] += inner_dot(score_grad, queries)
+                s.dv_acc[:, lanes] += inner_dot(probs.astype(BF16), grads)
+            for j in range(Q_BLOCK // frames):
+                f = i * (Q_BLOCK // frames) + j
+
+                @pl.when(f != me)
+                def _(f=f):
+                    dq_copy(f, me).start()
+
+            first_step = beside[0] + i * steps_beside
+            sums(*beside, shift=(first_step, first_step + steps_beside))
+
+        loop(0, q_blocks, query_block)
+        s.dqkv[1] = (s.dk_acc[...] * SCALE).astype(BF16)
+        s.dqkv[2] = s.dv_acc[...].astype(BF16)
+        seq_peers(lambda f: dkv_copy(f, me).start())
+        for part in range(3):
+            s.qback[part, my_rows, my_lanes] = s.dqkv[part, own_rows(me), :]
+
+        def qkv_block(i):
+            b = peer_of(i)
+            for j in range(per_column):
+                source = j * num_utt + b
+
+                @pl.when(source != me)
+                def _(source=source):
+                    dq_copy(source, source).wait_recv()
+                    dkv_copy(source, source).wait_recv()
+
+            value = jnp.concatenate([s.qback[part, own_rows(b), :] for part in range(3)], axis=1)
+            hand_out(b, nt_dot(value, qkv_ref[...]), qpart_copy)
+
+        loop(1, num_utt + 1, qkv_block)
+
+        def qkv_grads(i):
+            cut = block_rows(i, column)
+            for part in range(3):
+                s.part_qkv[cut, part * column : (part + 1) * column] = inner_dot(
+                    attn_in_ref[:, cut], s.qback[part]
+                ).astype(BF16)
+
+        loop(0, D // column, qkv_grads)
+        announce(QKV)
+        put_column(22, column_sum(s.qback[0].astype(F32)))
+        put_column(24, column_sum(s.qback[2].astype(F32)))
+        peers(lambda b: layer_copy(b, b).wait_recv())
+        layer_o[...] = from_peers(s.got_layer, s.resid_two[...]).astype(BF16)
+        sums(*SITES[3])
+        peers(lambda b: qpart_copy(b, b).wait_recv())
+        back = from_peers(s.got_qkv, s.mine[...])
+        normed, scale = norm_parts(resid_ref[...])
+        resid1_grad = s.resid2_grad[...] + norm_back(back * attn_gain, normed, scale)
+        s.resid1_grad[...] = resid1_grad
+        _, slope = gelu_parts(pos_pre_ref[...].astype(F32))
+        pos_low = (resid1_grad * slope).astype(BF16)
+        for b in range(num_blocks):
+            s.blocks[b] = pos_low[:, b * width : (b + 1) * width]
+
+        def there(b, device):
+            return remote(
+                s.blocks.at[b],
+                s.pos_grad.at[own_rows(me)],
+                s.there_send.at[b],
+                s.there_recv.at[me],
+                device,
+            )
+
+        def there_from(f, device):
+            return remote(
+                s.blocks.at[0],
+                s.pos_grad.at[own_rows(f)],
+                s.there_send.at[0],
+                s.there_recv.at[f],
+                device,
+            )
+
+        def home(f, device):
+            return remote(
+                s.pos_own.at[own_rows(f)],
+                s.pos_back.at[group.my_block],
+                s.home_send.at[f],
+                s.home_recv.at[group.my_block],
+                device,
+            )
+
+        def home_from(b, device):
+            return remote(
+                s.pos_own.at[own_rows(0)],
+                s.pos_back.at[b],
+                s.home_send.at[0],
+                s.home_recv.at[b],
+                device,
+            )
+
+        group.each(num_blocks, group.by_block, lambda b, device: there(b, device).start())
+
+        def keep_there():
+            s.pos_grad[own_rows(me), :] = s.blocks[group.my_block]
+
+        group.when_own(keep_there)
+        put_vector(10, column_sum(back * normed))
+        put_vector(12, column_sum(back))
+        put_vector(8, column_sum(pos_low.astype(F32)))
+
+        def position(wide, packed, grads, taps_ref, acc, total_ref, sem):
+            middle = HALF // PACK
+            taps_in = pltpu.make_async_copy(
+                taps_hbm.at[:, pl.ds(pl.multiple_of(block * width, width), width)],
+                taps_ref.at[pl.ds(TILE, KPOS * GW)],
+                sem,
+            )
+            taps_in.start()
+            edge = jnp.zeros((TILE, width), BF16)
+            taps_ref[0:TILE, :] = edge
+            taps_ref[TILE + KPOS * GW :, :] = edge
+            fill_frames(pos_in_ref, wide, packed, length, groups)
+            total_ref[...] = jnp.zeros_like(total_ref)
+            sums(*SITES[4])
+            taps_in.wait()
+            group.each(num_seq, group.by_shard, lambda f, device: there_from(f, device).wait_recv())
+            fill_frames(s.pos_grad, wide, grads, length, groups)
+            acc[...] = jnp.zeros_like(acc)
+
+            def input_tiles(first, windows, count):
+                for h in range(groups):
+                    for start in range(0, count, 4):
+                        tiles = range(start, min(start + 4, count))
+                        acc[h] += nt_dot(
+                            jnp.concatenate([windows[h](j) for j in tiles], axis=1),
+                            jnp.concatenate(
+                                [tap_tile(taps_ref, (first + j) * TILE, TILE, h) for j in tiles],
+                                axis=1,
+                            ),
+                        )
+
+            def eight_inputs(i):
+                base = pl.multiple_of(2 * middle - 8 - 8 * i, 8)
+                windows = []
+                for h in range(groups):
+                    window = grads[h, pl.ds(base, rows + 8), :]
+                    windows.append(lambda j, w=window: w[8 - j : 8 - j + rows].astype(BF16))
+                input_tiles(8 * i, windows, 8)
+
+            loop(0, NUM_TILES // 8, eight_inputs)
+            assert NUM_TILES % 8 == 1 and NUM_TILES == 2 * middle + 1
+            input_tiles(
+                NUM_TILES - 1,
+                [lambda j, h=h: grads[h, 0:rows, :].astype(BF16) for h in range(groups)],
+                1,
+            )
+            unpack_frames(
+                lambda h, r: acc[h, :, r * GW : (r + 1) * GW], wide.at[0:length], rows, groups
+            )
+            s.pos_own[...] = wide[0:length, :].astype(BF16)
+            group.each(num_seq, group.by_shard, lambda f, device: home(f, device).start())
+
+            def keep_home():
+                s.pos_back[group.my_block] = s.pos_own[own_rows(me), :]
+
+            group.when_own(keep_home)
+
+            def weight_tile(tile, frames_of):
+                pieces = [
+                    inner_dot(
+                        frames_of(h).astype(BF16),
+                        grads[h, middle : middle + rows, :].astype(BF16),
+                    )
+                    for h in range(groups)
+                ]
+                for r in range(PACK):
+                    where = pl.ds(pl.multiple_of(TILE + tile * TILE - r * GW, GW), TILE)
+                    total_ref[where, :] += jnp.concatenate(
+                        [piece[:, r * GW : (r + 1) * GW] for piece in pieces], axis=1
+                    )
+
+            def eight_weights(i):
+                base = pl.multiple_of(8 * i, 8)
+                windows = [packed[h, pl.ds(base, rows + 8), :] for h in range(groups)]
+                for j in range(8):
+                    weight_tile(8 * i + j, lambda h, j=j: windows[h][j : j + rows])
+
+            loop(0, NUM_TILES // 8, eight_weights)
+            weight_tile(NUM_TILES - 1, lambda h: packed[h, NUM_TILES - 1 :, :])
+            s.part_taps[...] = total_ref[TILE : TILE + KPOS * GW, :].astype(BF16)
+            announce(TAPS)
+
+        packed_rows = (groups, (length + KPOS) // PACK, TILE)
+        pl.run_scoped(
+            position,
+            vmem((length + KPOS, width), F32),
+            vmem(packed_rows, F32),
+            vmem(packed_rows, F32),
+            vmem((KPOS * GW + 2 * TILE, width), BF16),
+            vmem((groups, rows, TILE), F32),
+            vmem((KPOS * GW + 2 * TILE, width), F32),
+            dma,
+        )
+        sums(*SITES[5])
+
+        group.each(num_blocks, group.by_block, lambda b, device: home_from(b, device).wait_recv())
+        for b in range(num_blocks):
+            lanes = slice(b * width, (b + 1) * width)
+            s.resid1_grad[:, lanes] += s.pos_back[b].astype(F32)
+        embed_grad = s.resid1_grad[...]
+        hidden_frame = mask_ref[...] > 0.5
+        put_vector(6, column_sum(jnp.where(hidden_frame, embed_grad, 0.0)))
+        proj_grad = jnp.where(hidden_frame, 0.0, embed_grad).astype(BF16)
+        put_vector(4, column_sum(proj_grad.astype(F32)))
+        s.part_proj[...] = inner_dot(low_ref[...], proj_grad).astype(BF16)
+        loop(0, num_utt, lambda b: group_mate(1, b).start())
+        feat_grad = nt_dot(proj_grad, proj_ref[...])
+        conv_gain, conv_shift = vector(0, low), vector(low, low)
+        normed, first_scale = norm_parts(pre_ref[...])
+        act, slope = gelu_parts(normed * conv_gain + conv_shift)
+        second, second_scale = norm_parts(act)
+        put_vector(2, column_sum(feat_grad * second))
+        put_vector(3, column_sum(feat_grad))
+        grad = norm_back(feat_grad * vector(2 * low, low), second, second_scale) * slope
+        put_vector(0, column_sum(grad * normed))
+        put_vector(1, column_sum(grad))
+        conv_grad = norm_back(grad * conv_gain, normed, first_scale).astype(BF16)
+        s.part_conv[...] = inner_dot(steps_ref[...], conv_grad).astype(BF16)
+        loop(0, num_utt, lambda b: group_mate(0, b).start())
+        s.part_vec[...] = s.vec_f32[...].astype(BF16)
+        loop(0, num_utt, lambda b: group_mate(2, b).start())
+        feat_o[...] = nt_dot(conv_grad, conv_ref[...]).astype(BF16)
+
+        def late_lanes(n, slot, part):
+            first_lane = (part * num_utt + slot) * late_wide[n]
+            return pl.ds(pl.multiple_of(first_lane, 128), late_wide[n])
+
+        late_refs, late_outs = (qkv_mid, up_mid), (qkv_o, up_o)
+
+        def late_source(n, b, part):
+            return late_refs[n].at[
+                half_rows(b * column, half, core), pl.ds(part * late_wide[n], late_wide[n])
+            ]
+
+        def late_copy(n, b, slot, part):
+            return remote(
+                late_source(n, b, part),
+                late_outs[n].at[half_rows(0, half, core), late_lanes(n, slot, part)],
+                s.late_send.at[n, b, part],
+                s.late_recv.at[n, slot, part],
+                {"utt": b},
+            )
+
+        def late_hand(n, slot, part, which):
+            spot = late_outs[n].at[half_rows(0, half, which), late_lanes(n, slot, part)]
+            return remote(
+                spot, spot, s.hand_send.at[n, slot, part], s.hand_recv.at[n, slot, part], sibling
+            )
+
+        def late_own(n, part):
+            return pltpu.make_async_copy(
+                late_source(n, me_utt, part),
+                late_outs[n].at[half_rows(0, half, core), late_lanes(n, me_utt, part)],
+                s.late_own.at[n, part],
+            )
+
+        def late_start(n):
+            for part in range(late_parts[n]):
+                peers(lambda b, part=part: late_copy(n, b, me_utt, part).start())
+                late_own(n, part).start()
+
+        def late_arrived(n):
+            for part in range(late_parts[n]):
+
+                def arrived(b, part=part):
+                    late_copy(n, b, b, part).wait_recv()
+                    late_hand(n, b, part, core).start()
+
+                peers(arrived)
+                late_own(n, part).wait()
+                late_hand(n, me_utt, part, core).start()
+
+        begin = SITES[5][1]
+        stop = starts[OUT] + RING + final_lag
+        assert begin <= stop <= starts[CONV]
+        sums(begin, stop)
+        late_start(1)
+        for n in range(3):
+            loop(0, num_utt, lambda i, n=n: hand_on(n, lax.rem(me_utt + 1 + i, num_utt)))
+        after = starts[TAPS] + RING + final_lag
+        sums(stop, after)
+        late_start(0)
+        late_arrived(1)
+        sums(after, total + final_lag)
+        late_arrived(0)
+
+        for n in range(8):
+            tail = max(starts[n], total - RING)
+
+            def left(k, n=n):
+                slot = lax.rem(starts[n] + k, RING)
+                keep_copy(n, k, slot).wait()
+                last_copy(n, k, slot, core).wait_send()
+
+            if tail < starts[n] + counts[n]:
+                loop(tail - starts[n], counts[n], left)
+
+            def handed(k, n=n):
+                last_copy(n, k, 0, 1 - core).wait_recv()
+
+            loop(0, counts[n], handed)
+        for way in range(2):
+
+            @pl.when(z != ends[way])
+            def _(way=way):
+                loop(total - RING, total, lambda index: chain_copy(way, index).wait_send())
+
+        for n in range(5):
+            loop(0, mate_counts[n], lambda k, n=n: mate_copy(n, k).wait_send())
+        for n in range(3):
+            loop(0, num_utt, lambda b, n=n: group_mate(n, b).wait_send())
+            peers(lambda b, n=n: group_peer(n, b, me_utt).wait_send())
+        for n in range(2):
+            for part in range(late_parts[n]):
+                peers(lambda b, n=n, part=part: late_copy(n, b, me_utt, part).wait_send())
+
+                def both(b, n=n, part=part):
+                    late_hand(n, b, part, core).wait_send()
+                    late_hand(n, b, part, 1 - core).wait_recv()
+
+                loop(0, num_utt, both)
+
+        def sent(b):
+            ffn_copy(b, me_utt).wait_send()
+            agrad_copy(b, me_utt).wait_send()
+            layer_copy(b, me_utt).wait_send()
+            qpart_copy(b, me_utt).wait_send()
+
+        peers(sent)
+
+        def sent_seq(f):
+            ghead_copy(f, me).wait_send()
+            dq_copy(f, me).wait_send()
+            dkv_copy(f, me).wait_send()
+
+        seq_peers(sent_seq)
+        group.each(num_blocks, group.by_block, lambda b, device: there(b, device).wait_send())
+        group.each(num_seq, group.by_shard, lambda f, device: home(f, device).wait_send())
+
+    vmem, anywhere = pl.BlockSpec(memory_space=pltpu.VMEM), pl.BlockSpec(memory_space=pl.ANY)
+    shapes = [
+        (frames, D),
+        (frames, 2 * C),
+        (hidden, D),
+        (D, hidden),
+        (column, D),
+        (D, 3 * column),
+        (KPOS * GW, column),
+        (column, C),
+        (proj_rows, D),
+        (vec_rows, 128),
+        (column, num_utt * hidden),
+        (column, 3 * D),
+    ]
+    return pl.pallas_call(
+        kernel,
+        out_shape=[jax.ShapeDtypeStruct(shape, BF16) for shape in shapes],
+        in_specs=[vmem] * 18 + [anywhere] * 4,
+        out_specs=[vmem] * 2 + [anywhere] * 10,
+        scratch_shapes=scratch.shapes,
+        compiler_params=pltpu.CompilerParams(
+            collective_id=collective_id,
+            has_side_effects=True,
+            vmem_limit_bytes=62 * 1024 * 1024,
+        ),
+    )(
+        flat,
+        out_weight,
+        resid_one,
+        vectors,
+        up_bias,
+        attn_in,
+        qkv_all,
+        heads,
+        attn_f32,
+        lse,
+        pos_pre,
+        pos_in,
+        masked,
+        steps,
+        conv_pre,
+        feat_low,
+        conv_all,
+        proj_all,
+        up_all,
+        down_weight,
+        gout_all,
+        taps,
+    )
+
+
+SITES = [(0, 5), (5, 12), (12, 28), (28, 36), (36, 42), (42, 47)]
+
+
 def layer_norm(values, gain, shift):
     center = values - jnp.mean(values, -1, keepdims=True)
     spread = jnp.mean(center * center, -1, keepdims=True)
@@ -1994,119 +2641,158 @@
         gout_all = gout_all.reshape(rows_all, D)
         attn_flat = from_heads(attn_rows, 1)
 
-    _, pos_pull = jax.vjp(gelu_exact, pos_pre.astype(F32))
-    _, attn_pull = jax.vjp(layer_norm, resid_one, attn_gain, attn_shift)
-    (parts,) = exchange([(split_rows(dot(attn_flat, out_weight)), "utt", "blocks")], 7)
-    resid_two = resid_one + jnp.sum(parts.astype(F32), 0) + out_bias
-    ffn_norm, ffn_pull = jax.vjp(layer_norm, resid_two, ffn_gain, ffn_shift)
-    (ffn_in,) = exchange([(ffn_norm.astype(BF16), "utt", "gather")], 8)
-    ffn_in = ffn_in.reshape(rows_all, D)
-    hidden_pre = dot(ffn_in, up_columns) + up_bias
-    hidden_act, hidden_pull = jax.vjp(gelu_exact, hidden_pre)
-    hidden_low = hidden_act.astype(BF16)
-    (hidden_grad,) = hidden_pull(nt_dot(gout_all, down_weight))
-    hidden_grad = hidden_grad.astype(BF16)
-    downweight_grad = inner_dot(hidden_low, gout_all).astype(BF16)
-    upweight_grad = inner_dot(ffn_in, hidden_grad).astype(BF16)
-    downweight_grad, upweight_grad, hidden_grad = lax.optimization_barrier(
-        (downweight_grad, upweight_grad, hidden_grad)
-    )
-    downweight_sum, upweight_sum = lax.psum((downweight_grad, upweight_grad), "seq")
-    (back_parts,) = exchange([(split_rows(nt_dot(hidden_grad, up_columns)), "utt", "blocks")], 9)
-    ffn_back, ffngain_grad, ffnshift_grad = ffn_pull(jnp.sum(back_parts.astype(F32), 0))
-    resid2_grad = out_rows.astype(F32) + ffn_back
-    attn_grad_own = resid2_grad.astype(BF16)
-    (attn_grad,) = exchange([(attn_grad_own, "utt", "gather")], 10)
-    attn_grad = attn_grad.reshape(rows_all, D)
-
-    out_grad = nt_dot(attn_grad, out_weight).astype(BF16)
-    (out_grad_heads,) = exchange([(to_heads(out_grad, 1), "seq", "blocks")], 11)
-    qkv_grads = attend_back(
-        queries, keys, values, out_grad_heads.reshape(length, width), attn_f32, lse
-    )
-    qkv_grads = jnp.stack([part.reshape(num_seq, frames, width) for part in qkv_grads], axis=1)
-    (qkv_back,) = exchange([(qkv_grads, "seq", "blocks")], 12)
-    qkv_back = from_heads(qkv_back, 3)
-    outweight_grad = inner_dot(attn_flat, attn_grad).astype(BF16)
-    qkvweight_grad = inner_dot(attn_in, qkv_back).astype(BF16)
-    (qkv_parts,) = exchange([(split_rows(nt_dot(qkv_back, qkv_columns)), "utt", "blocks")], 13)
-    attn_back, attngain_grad, attnshift_grad = attn_pull(jnp.sum(qkv_parts.astype(F32), 0))
-    resid1_grad = resid2_grad + attn_back
-    (pos_grad,) = pos_pull(resid1_grad)
-    pos_low = pos_grad.astype(BF16)
-    grads_in = regroup(to_blocks(pos_low), False, 14).reshape(length, width)
-    embed_own, taps_grad = pos_backward(pos_in, grads_in, taps)
-    embed_back = regroup(embed_own.reshape(num_seq, frames, width), True, 15)
-    feat_grad, convweight_grad, projweight_grad, norm_sums, embed_sums = front_back(
-        resid1_grad,
-        embed_back,
-        masked,
-        steps_in,
-        conv_pre,
-        feat_low,
-        conv_all,
-        proj_all,
-        jnp.stack([conv_gain, conv_shift, norm_gain]),
-    )
-    feat_grad = feat_grad.reshape(1, 2 * frames, C)
-    row_vectors = [
-        norm_sums[0],
-        norm_sums[1],
-        norm_sums[2],
-        norm_sums[3],
-        embed_sums[1],
-        embed_sums[0],
-        jnp.sum(pos_low, 0, dtype=F32),
-        attngain_grad,
-        attnshift_grad,
-        jnp.sum(attn_grad_own, 0, dtype=F32),
-        ffngain_grad,
-        ffnshift_grad,
-        jnp.sum(out_rows, 0, dtype=F32),
-    ]
-    column_vectors = [
-        jnp.sum(qkv_back[:, :column], 0, dtype=F32),
-        jnp.sum(qkv_back[:, 2 * column :], 0, dtype=F32),
-        jnp.sum(hidden_grad, 0, dtype=F32),
-    ]
-    flat = jnp.concatenate([v.reshape(num_utt, -1) for v in row_vectors], axis=1)
-    mine = jnp.concatenate(column_vectors)
-    here = jnp.arange(num_utt)[:, None] == lax.axis_index("utt")
-    flat = jnp.concatenate([flat, jnp.where(here, mine[None, :], 0.0)], axis=1)
-    flat = jnp.pad(flat, ((0, 0), (0, -flat.shape[1] % (64 * 128))))
-    flat = flat.astype(BF16).reshape(num_utt, -1, 128)
-    layer_parts = split_rows(dot(hidden_low, down_weight))
-    grads = (
-        taps_grad,
-        outweight_grad,
-        qkvweight_grad,
-        convweight_grad,
-        projweight_grad,
-        flat,
-        upweight_sum,
-        layer_parts,
-    )
     if fast:
-        grads = sum_gradients(*grads, 16)
+        (
+            layer_out,
+            feat_grad,
+            downweight_sum,
+            _,
+            outweight_sum,
+            _,
+            taps_sum,
+            conv_sum,
+            proj_sum,
+            vector_sum,
+            up_sum,
+            qkv_sum,
+        ) = back_forth(
+            attn_flat,
+            out_weight,
+            resid_one,
+            vectors_all,
+            up_bias[None, :],
+            attn_in,
+            qkv_columns,
+            qkv_heads,
+            attn_f32,
+            lse,
+            pos_pre,
+            pos_in,
+            masked,
+            steps_in,
+            conv_pre,
+            feat_low,
+            conv_all,
+            proj_all,
+            up_columns,
+            down_weight,
+            gout_all,
+            pos_weight.reshape(KPOS * GW, column),
+            2,
+        )
+        layer_out = layer_out.reshape(1, frames, D)
+        feat_grad = feat_grad.reshape(1, 2 * frames, C)
+        grads = (taps_sum, outweight_sum, qkv_sum, conv_sum, proj_sum, vector_sum, up_sum)
+        small, wide = (C // num_utt,), (column,)
+        row_sizes, column_sizes = 4 * small + 9 * wide, 2 * wide + (hidden,)
     else:
+        _, pos_pull = jax.vjp(gelu_exact, pos_pre.astype(F32))
+        _, attn_pull = jax.vjp(layer_norm, resid_one, attn_gain, attn_shift)
+        (parts,) = exchange([(split_rows(dot(attn_flat, out_weight)), "utt", "blocks")], 7)
+        resid_two = resid_one + jnp.sum(parts.astype(F32), 0) + out_bias
+        ffn_norm, ffn_pull = jax.vjp(layer_norm, resid_two, ffn_gain, ffn_shift)
+        (ffn_in,) = exchange([(ffn_norm.astype(BF16), "utt", "gather")], 8)
+        ffn_in = ffn_in.reshape(rows_all, D)
+        hidden_pre = dot(ffn_in, up_columns) + up_bias
+        hidden_act, hidden_pull = jax.vjp(gelu_exact, hidden_pre)
+        hidden_low = hidden_act.astype(BF16)
+        (hidden_grad,) = hidden_pull(nt_dot(gout_all, down_weight))
+        hidden_grad = hidden_grad.astype(BF16)
+        downweight_grad = inner_dot(hidden_low, gout_all).astype(BF16)
+        upweight_grad = inner_dot(ffn_in, hidden_grad).astype(BF16)
+        downweight_grad, upweight_grad, hidden_grad = lax.optimization_barrier(
+            (downweight_grad, upweight_grad, hidden_grad)
+        )
+        downweight_sum, upweight_sum = lax.psum((downweight_grad, upweight_grad), "seq")
+        (back_parts,) = exchange([(split_rows(nt_dot(hidden_grad, up_columns)), "utt", "blocks")], 9)
+        ffn_back, ffngain_grad, ffnshift_grad = ffn_pull(jnp.sum(back_parts.astype(F32), 0))
+        resid2_grad = out_rows.astype(F32) + ffn_back
+        attn_grad_own = resid2_grad.astype(BF16)
+        (attn_grad,) = exchange([(attn_grad_own, "utt", "gather")], 10)
+        attn_grad = attn_grad.reshape(rows_all, D)
+
+        out_grad = nt_dot(attn_grad, out_weight).astype(BF16)
+        (out_grad_heads,) = exchange([(to_heads(out_grad, 1), "seq", "blocks")], 11)
+        qkv_grads = attend_back(
+            queries, keys, values, out_grad_heads.reshape(length, width), attn_f32, lse
+        )
+        qkv_grads = jnp.stack([part.reshape(num_seq, frames, width) for part in qkv_grads], axis=1)
+        (qkv_back,) = exchange([(qkv_grads, "seq", "blocks")], 12)
+        qkv_back = from_heads(qkv_back, 3)
+        outweight_grad = inner_dot(attn_flat, attn_grad).astype(BF16)
+        qkvweight_grad = inner_dot(attn_in, qkv_back).astype(BF16)
+        (qkv_parts,) = exchange([(split_rows(nt_dot(qkv_back, qkv_columns)), "utt", "blocks")], 13)
+        attn_back, attngain_grad, attnshift_grad = attn_pull(jnp.sum(qkv_parts.astype(F32), 0))
+        resid1_grad = resid2_grad + attn_back
+        (pos_grad,) = pos_pull(resid1_grad)
+        pos_low = pos_grad.astype(BF16)
+        grads_in = regroup(to_blocks(pos_low), False, 14).reshape(length, width)
+        embed_own, taps_grad = pos_backward(pos_in, grads_in, taps)
+        embed_back = regroup(embed_own.reshape(num_seq, frames, width), True, 15)
+        feat_grad, convweight_grad, projweight_grad, norm_sums, embed_sums = front_back(
+            resid1_grad,
+            embed_back,
+            masked,
+            steps_in,
+            conv_pre,
+            feat_low,
+            conv_all,
+            proj_all,
+            jnp.stack([conv_gain, conv_shift, norm_gain]),
+        )
+        feat_grad = feat_grad.reshape(1, 2 * frames, C)
+        row_vectors = [
+            norm_sums[0],
+            norm_sums[1],
+            norm_sums[2],
+            norm_sums[3],
+            embed_sums[1],
+            embed_sums[0],
+            jnp.sum(pos_low, 0, dtype=F32),
+            attngain_grad,
+            attnshift_grad,
+            jnp.sum(attn_grad_own, 0, dtype=F32),
+            ffngain_grad,
+            ffnshift_grad,
+            jnp.sum(out_rows, 0, dtype=F32),
+        ]
+        column_vectors = [
+            jnp.sum(qkv_back[:, :column], 0, dtype=F32),
+            jnp.sum(qkv_back[:, 2 * column :], 0, dtype=F32),
+            jnp.sum(hidden_grad, 0, dtype=F32),
+        ]
+        flat = jnp.concatenate([v.reshape(num_utt, -1) for v in row_vectors], axis=1)
+        mine = jnp.concatenate(column_vectors)
+        here = jnp.arange(num_utt)[:, None] == lax.axis_index("utt")
+        flat = jnp.concatenate([flat, jnp.where(here, mine[None, :], 0.0)], axis=1)
+        flat = jnp.pad(flat, ((0, 0), (0, -flat.shape[1] % (64 * 128))))
+        flat = flat.astype(BF16).reshape(num_utt, -1, 128)
+        layer_parts = split_rows(dot(hidden_low, down_weight))
+        grads = (
+            taps_grad,
+            outweight_grad,
+            qkvweight_grad,
+            convweight_grad,
+            projweight_grad,
+            flat,
+            upweight_sum,
+            layer_parts,
+        )
         grads = sum_gradients_plain(*grads)
+        layer_value = resid_two + jnp.sum(grads[7].astype(F32), 0) + down_bias
+        layer_out = layer_value.astype(BF16).reshape(1, frames, D)
+        row_sizes = [vector.shape[0] // num_utt for vector in row_vectors]
+        column_sizes = [vector.shape[0] for vector in column_vectors]
     posweight_grad = grads[0].reshape(KPOS, GW, column).astype(F32)
     outweight_grad, qkvweight_grad, convweight_grad, projweight_grad = (
         grad.astype(F32) for grad in grads[1:5]
     )
     sums = grads[5].reshape(-1).astype(F32)
     upweight_grad = grads[6].astype(F32)
-    layer_value = resid_two + jnp.sum(grads[7].astype(F32), 0) + down_bias
-    layer_out = layer_value.astype(BF16).reshape(1, frames, D)
     outs, start = [], 0
-    for vector in row_vectors:
-        end = start + vector.shape[0] // num_utt
-        outs.append(sums[start:end])
-        start = end
-    for vector in column_vectors:
-        end = start + vector.shape[0]
-        outs.append(sums[start:end])
-        start = end
+    for size in tuple(row_sizes) + tuple(column_sizes):
+        outs.append(sums[start : start + size])
+        start = start + size
     (
         convgain_grad,
         convshift_grad,

time: 485 us -> 376 us (0.78); the launches traced: 476 us -> 375 us
  matrix products: 33.8 us -> 0 us
  other arithmetic: 42.8 us -> 17.9 us
  local copies, waits for them, and re-layouts: 34.1 us -> 17.8 us
  between operations: 15 us -> 0.75 us
  Pallas kernels: 350 us -> 339 us
    dot_general x11 -> x0, matrix products: 33.8 us -> none  [the longest x4 14.7 us: nt_dot(): lax.dot_general(a, b, (((1,), (1,)), ((), ())), preferred_element_type=F32)]
    reduce_sum x18 -> x0, other arithmetic: 18.4 us -> none  [the longest x4 4.46 us: layer_norm(): return center * lax.rsqrt(spread + EPS) * gain + shift]
    pallas_call x13 -> x1, Pallas kernels: 258 us -> 247 us  [back_forth(): pl.pallas_call(kernel, out_shape=[jax.ShapeDtypeStruct(shape, BF16) for s...]
    reshape x11 -> x0, local copies, waits for them, and re-layouts: 9.46 us -> none  [the longest x2 3.41 us: to_heads(): blocks = values.reshape(num_utt, frames, parts, per_column, width)]
    unnamed x74 -> x26, local copies, waits for them, and re-layouts: 10.1 us -> 10.1 us
  transfers between devices with their start and end apart: 1 -> 0, of which waited for: 0 -> 0; matrix products, arithmetic and copies ran while one was open for 11% -> 0% of each run, Pallas kernels for 27% -> 0%
where the time goes in v4:
time: 376 us; the launch traced here: 375 us
  Pallas kernels  339 us (90%)
  other arithmetic  17.9 us (5%)
  local copies, waits for them, and re-layouts  17.8 us (5%)
    pallas_call x1, Pallas kernels, back_forth(): pl.pallas_call(kernel, out_shape=[jax.ShapeDtypeStruct(shape, BF16) for s...  247 us
    pallas_call x1, Pallas kernels, front_forward(): pl.pallas_call(kernel, out_shape=[shape(num_utt * column, C), shape(num_u...  91.4 us
    unnamed x26, local copies, waits for them, and re-layouts  10.1 us

profile of v4, /device:TPU:0, one launch (start us, length us, event | category | flops | bytes accessed | tf_op | source)
XLA Modules:
  0.0 375.0 jit_solution(15758456066879769447)
XLA Ops:
  0.7 0.0 copy-start
  0.7 0.7 copy-done
  1.4 0.6 dynamic-slice_bitcast_fusion.taps_bias_ref
  1.9 0.7 pad_maximum_fusion
  2.6 0.6 broadcast_in_dim.18.bias_ref
  3.2 0.7 constant_dynamic-update-slice_fusion.11
  3.9 0.7 constant_dynamic-update-slice_fusion.10
  4.5 0.7 constant_dynamic-update-slice_fusion.9
  5.2 0.7 constant_dynamic-update-slice_fusion.8
  5.9 0.7 constant_dynamic-update-slice_fusion.7
  6.6 0.7 constant_dynamic-update-slice_fusion.6
  7.2 0.7 constant_dynamic-update-slice_fusion.5
  7.9 0.7 constant_dynamic-update-slice_fusion.4
  8.6 0.7 constant_dynamic-update-slice_fusion.3
  9.3 0.7 constant_dynamic-update-slice_fusion.2
  10.0 0.7 constant_dynamic-update-slice_fusion.1
  10.7 0.7 constant_dynamic-update-slice_fusion
  11.4 0.6 broadcast_in_dim.15.vec_ref
  12.0 1.7 reshape.87.steps_ref
  13.7 91.4 %shard_map.441 = (bf16[1024,512]{1,0:T(8,128)(2,1)}, bf16[512,1024]{1,0:T(8,128)(2,1)}, f32[4,1,2560]{2,1,0:T(1,128)}, bf16[1024,768]{1,0:T(8,128)(2,1)}, bf16[1...) custom-call(bf16[128,1024]{1,0:T(8,128)(2,1)} %reshape.87.steps_ref,, ...), custom_call_target="tpu_custom_call" | custom-call | tf_op jit(solution)/shard_map/pallas_call | solution.py:1242
  105.1 247.2 %shard_map.442 = (bf16[128,1024]{1,0:T(8,128)(2,1)}, bf16[128,1024]{1,0:T(8,128)(2,1)}, bf16[1024,1024]{1,0:T(8,128)(2,1)}, bf16[1024,1024]{1,0:T(8,128)(2,1)}, ...) custom-call(bf16[512,256]{1,0:T(8,128)(2,1)} %get-tuple-element.52.f, ...), custom_call_target="tpu_custom_call" | custom-call | tf_op jit(solution)/shard_map/pallas_call | solution.py:2390
  352.3 0.0 copy-start.5
  352.4 0.0 copy-start.4
  352.4 0.9 convert_element_type.29
  353.2 0.5 slice_bitcast_fusion.12
  353.8 0.6 slice_bitcast_fusion
  354.4 0.6 slice_bitcast_fusion.1
  355.0 1.7 reshape.91
  356.7 1.8 convert_element_type.28
  358.5 1.8 convert_element_type.30
  360.3 0.0 copy-done.5
  360.3 1.1 convert_element_type.34
  361.4 0.0 copy-done.4
  361.4 0.0 copy-start.3
  361.4 2.0 convert_element_type.33
  363.4 0.2 copy-done.3
  363.6 0.0 copy-start.2
  363.6 2.5 convert_element_type.35
  366.1 0.0 copy-done.2
  366.1 0.0 copy-start.1
  366.1 2.6 convert_element_type.36
  368.7 1.1 copy-done.1
  369.8 0.0 copy-start.6
  369.8 4.5 %convert.1 = f32[128,64,256]{2,1,0:T(8,128)} convert(bf16[128,64,256]{2,1,0:T(8,128)(2,1)S(1)} %bitcast.42) | non-fusion elementwise | flops 2097152 | bytes 12582912 | tf_op jit(solution)/shard_map/convert_element_type | solution.py:2786
  374.3 0.0 copy-done.6
  374.3 0.7 copy.64
  (2 shorter events, 0.0 us)
Async XLA Ops:
  0.7 0.7 copy-start
  352.3 8.0 %copy-start.5 = (bf16[256,1024]{1,0:T(8,128)(2,1)S(1)}, bf16[256,1024]{1,0:T(8,128)(2,1)}, u32[]{:S(2)}) copy-start(bf16[256,1024]{1,0:T(8,128)(2,1)} %get-tuple-element.76) | copy-start | bytes 1572868
  352.4 9.0 %copy-start.4 = (bf16[256,3072]{1,0:T(8,128)(2,1)S(1)}, bf16[256,3072]{1,0:T(8,128)(2,1)}, u32[]{:S(2)}) copy-start(bf16[256,3072]{1,0:T(8,128)(2,1)} %get-tuple-element.75) | copy-start | bytes 4718596
  361.4 2.2 copy-start.3
  363.6 2.5 copy-start.2
  366.1 3.7 copy-start.1
  369.8 4.5 %copy-start.6 = (bf16[128,1024]{1,0:T(8,128)(2,1)S(1)}, bf16[128,1024]{1,0:T(8,128)(2,1)}, u32[]{:S(2)}) copy-start(bf16[128,1024]{1,0:T(8,128)(2,1)} %get-tuple-element.69) | copy-start | bytes 786436

commit v5 on v4

--- a/solution.py
+++ b/solution.py
@@ -711,6 +711,86 @@
             body()
 
 
+class Quarters:
+    def __init__(self, group, source, target, rows, parts, sems):
+        self.group, self.source, self.target = group, source, target
+        self.rows, self.parts, self.sems = rows // 4, parts, sems
+        me = group.me_seq
+        self.core, self.side = lax.rem(me, 2), lax.rem(me // 2, 2)
+        self.sibling = {"seq": me + 1 - 2 * self.core}
+        self.across = {"seq": me + 2 - 4 * self.side}
+
+    @staticmethod
+    def semaphores(num_utt, parts):
+        dma = pltpu.SemaphoreType.DMA
+        return [dma((num_utt, parts))] * 2 + [dma((num_utt,))] * 2 + [dma((num_utt, 2))] * 2
+
+    def place(self, block, side, core):
+        first = (block * 4 + 2 * side + core) * self.rows
+        return pl.ds(pl.multiple_of(first, self.rows), self.rows)
+
+    def fetch(self, b, slot, part):
+        mine = self.place(0, self.side, self.core)
+        source, lanes = self.source(b, part, mine)
+        place = self.place(slot, self.side, self.core)
+        target = self.target.at[place] if lanes is None else self.target.at[place, lanes]
+        return remote(
+            source, target, self.sems[0].at[b, part], self.sems[1].at[slot, part], {"utt": b}
+        )
+
+    def over(self, slot, side):
+        place = self.target.at[self.place(slot, side, self.core)]
+        return remote(place, place, self.sems[2].at[slot], self.sems[3].at[slot], self.across)
+
+    def hand(self, slot, which, core):
+        side = self.side if which == 0 else 1 - self.side
+        place = self.target.at[self.place(slot, side, core)]
+        return remote(
+            place, place, self.sems[4].at[slot, which], self.sems[5].at[slot, which], self.sibling
+        )
+
+    def peers(self, body):
+        size, me = self.group.num_utt, self.group.me_utt
+        loop(1, size, lambda i: body(lax.rem(me + i, size)))
+
+    def start(self):
+        for part in range(self.parts):
+            self.peers(lambda b, part=part: self.fetch(b, self.group.me_utt, part).start())
+
+    def pass_on(self):
+        def arrived(b):
+            for part in range(self.parts):
+                self.fetch(b, b, part).wait_recv()
+            self.over(b, self.side).start()
+            self.hand(b, 0, self.core).start()
+
+        self.peers(arrived)
+
+    def pass_over(self):
+        def arrived(b):
+            self.over(b, 1 - self.side).wait_recv()
+            self.hand(b, 1, self.core).start()
+
+        self.peers(arrived)
+
+    def arrive(self):
+        def arrived(b):
+            for which in range(2):
+                self.hand(b, which, 1 - self.core).wait_recv()
+
+        self.peers(arrived)
+
+    def sent(self):
+        def left(b):
+            for part in range(self.parts):
+                self.fetch(b, self.group.me_utt, part).wait_send()
+            self.over(b, self.side).wait_send()
+            for which in range(2):
+                self.hand(b, which, self.core).wait_send()
+
+        self.peers(left)
+
+
 class Names:
     def __init__(self, **shapes):
         self.names, self.shapes = list(shapes), list(shapes.values())
@@ -733,7 +813,7 @@
 
 
 def front_forward(
-    steps,
+    feats,
     starts,
     conv,
     proj,
@@ -743,11 +823,13 @@
     grad_rows,
     taps,
     taps_bias,
-    bias,
+    query_bias,
+    value_bias,
+    out_weight,
     collective_id,
 ):
     num_seq, num_utt = lax.axis_size("seq"), lax.axis_size("utt")
-    frames = steps.shape[0]
+    frames = grad_rows.shape[0]
     length = frames * num_seq
     column = qkv.shape[0]
     half = column // 2
@@ -763,6 +845,8 @@
     rows_all = num_utt * frames
     dma = pltpu.SemaphoreType.DMA
     scratch = Names(
+        feats=pltpu.VMEM((C // 128, 2 * frames, 128), F32),
+        vec_own=pltpu.VMEM((1, sum(vector.shape[0] for vector in vectors)), F32),
         wide=pltpu.VMEM((length + KPOS, width), F32),
         packed=pltpu.VMEM((groups, (length + KPOS) // PACK, TILE), F32),
         taps=pltpu.VMEM((KPOS * GW + 2 * TILE, width), BF16),
@@ -784,14 +868,6 @@
         proj_hand_recv=dma((num_utt,)),
         vec_send=dma((num_utt,)),
         vec_recv=dma((num_utt,)),
-        qkv_send=dma((num_utt, 3)),
-        qkv_recv=dma((num_utt, 3)),
-        qkv_hand_send=dma((num_utt,)),
-        qkv_hand_recv=dma((num_utt,)),
-        up_send=dma((num_utt,)),
-        up_recv=dma((num_utt,)),
-        up_hand_send=dma((num_utt,)),
-        up_hand_recv=dma((num_utt,)),
         gout_send=dma((num_utt,)),
         gout_recv=dma((num_utt,)),
         there_send=dma((num_blocks,)),
@@ -804,39 +880,48 @@
         head_recv=dma((num_seq,)),
         flat_send=dma((num_seq,)),
         flat_recv=dma((num_seq,)),
+        row_send=dma((num_seq,)),
+        row_recv=dma((num_blocks,)),
     )
-
-    def kernel(
-        steps_ref,
-        starts_ref,
-        conv_ref,
-        proj_ref,
-        vec_ref,
-        qkv_ref,
-        up_ref,
-        gout_ref,
-        taps_ref,
-        taps_bias_ref,
-        bias_ref,
-        conv_all,
-        proj_all,
-        vec_all,
-        qkv_all,
-        up_all,
-        gout_all,
-        pre_o,
-        low_o,
-        mask_o,
-        pos_in,
-        pos_pre,
-        resid_o,
-        attn_all,
-        heads,
-        attn_o,
-        lse_o,
-        flat_o,
-        *rest,
-    ):
+    quarter_sems = [Quarters.semaphores(num_utt, parts) for parts in (3, 1, 1)]
+
+    def kernel(*refs):
+        vec_refs, refs = refs[: len(vectors)], refs[len(vectors) :]
+        (
+            feats_ref,
+            starts_ref,
+            conv_ref,
+            proj_ref,
+            qkv_ref,
+            up_ref,
+            gout_ref,
+            taps_ref,
+            taps_bias_ref,
+            query_bias_ref,
+            value_bias_ref,
+            outw_ref,
+            conv_all,
+            proj_all,
+            vec_all,
+            qkv_all,
+            up_all,
+            gout_all,
+            pre_o,
+            low_o,
+            mask_o,
+            steps_o,
+            pos_in,
+            pos_pre,
+            resid_o,
+            attn_all,
+            heads,
+            attn_o,
+            lse_o,
+            flat_o,
+            rows_o,
+            outw_all,
+        ) = refs[:32]
+        rest, quarter_refs = refs[32:-18], refs[-18:]
         s = scratch.bind(rest)
         group = Regroup()
         me, me_utt = group.me_seq, group.me_utt
@@ -887,10 +972,18 @@
         own_gout = pltpu.make_async_copy(
             gout_ref, gout_all.at[block_rows(me_utt, frames)], s.local.at[5]
         )
+        own_outw = pltpu.make_async_copy(
+            outw_ref, outw_all.at[block_rows(me_utt, column)], s.local.at[6]
+        )
         for part in range(3):
             own_qkv(part).start()
+        own_outw.start()
         own_up.start()
         own_gout.start()
+        offset = 0
+        for ref in vec_refs:
+            s.vec_own[:, offset : offset + ref.shape[0]] = ref[...].reshape(1, ref.shape[0])
+            offset += ref.shape[0]
         pl.semaphore_wait(
             barrier, num_utt - 1 + num_seq - 1 + num_blocks + num_seq - 2 * group.is_own
         )
@@ -927,37 +1020,22 @@
 
         def vec_copy(b, slot):
             return remote(
-                vec_ref, vec_all.at[slot], s.vec_send.at[b], s.vec_recv.at[slot], {"utt": b}
-            )
-
-        def qkv_copy(b, slot, part):
+                s.vec_own, vec_all.at[slot], s.vec_send.at[b], s.vec_recv.at[slot], {"utt": b}
+            )
+
+        def qkv_source(b, part, mine):
             first = pl.multiple_of((part * num_utt + b) * column, column)
-            return remote(
-                qkv_ref.at[half_rows(0, half, core), pl.ds(first, column)],
-                qkv_all.at[half_rows(slot * column, half, core), pl.ds(part * column, column)],
-                s.qkv_send.at[b, part],
-                s.qkv_recv.at[slot, part],
-                {"utt": b},
-            )
-
-        def qkv_hand(slot, which):
-            place = qkv_all.at[half_rows(slot * column, half, which)]
-            return remote(
-                place, place, s.qkv_hand_send.at[slot], s.qkv_hand_recv.at[slot], sibling
-            )
-
-        def up_copy(b, slot):
-            return remote(
-                up_ref.at[half_rows(0, half, core), block_rows(b, hidden)],
-                up_all.at[half_rows(slot * column, half, core)],
-                s.up_send.at[b],
-                s.up_recv.at[slot],
-                {"utt": b},
-            )
-
-        def up_hand(slot, which):
-            place = up_all.at[half_rows(slot * column, half, which)]
-            return remote(place, place, s.up_hand_send.at[slot], s.up_hand_recv.at[slot], sibling)
+            return qkv_ref.at[mine, pl.ds(first, column)], pl.ds(part * column, column)
+
+        def up_source(b, part, mine):
+            return up_ref.at[mine, block_rows(b, hidden)], None
+
+        def outw_source(b, part, mine):
+            return outw_ref.at[mine], None
+
+        qkv_quarters = Quarters(group, qkv_source, qkv_all, column, 3, quarter_refs[0:6])
+        up_quarters = Quarters(group, up_source, up_all, column, 1, quarter_refs[6:12])
+        outw_quarters = Quarters(group, outw_source, outw_all, column, 1, quarter_refs[12:18])
 
         def gout_copy(b, slot):
             return remote(
@@ -973,7 +1051,13 @@
         peers(lambda b: proj_copy(b, me_utt).start())
         conv_all[block_rows(me_utt, column), :] = conv_ref[...]
         proj_all[block_rows(me_utt, proj_rows), :] = proj_ref[...]
-        vec_all[me_utt] = vec_ref[...]
+        vec_all[me_utt] = s.vec_own[...]
+        for j in range(C // 128):
+            s.feats[j] = feats_ref[:, j * 128 : (j + 1) * 128].astype(F32)
+        for step in range(2):
+            for j in range(C // 128):
+                lanes = slice(step * C + j * 128, step * C + (j + 1) * 128)
+                steps_o[:, lanes] = s.feats[j, pl.ds(step, frames, stride=2), :].astype(BF16)
         position = me * frames + lax.broadcasted_iota(jnp.int32, (frames, 1), 0)
         inside = jnp.logical_and(
             position >= starts_ref[...], position < starts_ref[...] + SPAN
@@ -994,8 +1078,7 @@
 
         peers(conv_arrived)
         peers(proj_arrived)
-        for part in range(3):
-            peers(lambda b, part=part: qkv_copy(b, me_utt, part).start())
+        qkv_quarters.start()
         peers(lambda b: vec_copy(b, b).wait_recv())
         peers(lambda b: conv_hand(b, 1 - core).wait_recv())
 
@@ -1004,7 +1087,7 @@
                 [vec_all[b, :, first : first + size] for b in range(num_utt)], axis=1
             )
 
-        pre = jnp.dot(steps_ref[...], conv_all[...], preferred_element_type=F32)
+        pre = jnp.dot(steps_o[...], conv_all[...], preferred_element_type=F32)
         pre_o[...] = pre
         normed, _ = norm_parts(pre)
         act, _ = gelu_parts(normed * vector(0, low) + vector(low, low))
@@ -1048,6 +1131,8 @@
         taps_in.wait()
         group.each(num_seq, group.by_shard, lambda f, device: there_from(f, device).wait_recv())
         fill_frames(pos_in, s.wide, s.packed, length, groups)
+        qkv_quarters.pass_on()
+        outw_quarters.start()
         for h in range(groups):
             for step in range(NUM_TILES // STEP_TILES):
                 start = step * STEP_TILES
@@ -1064,9 +1149,15 @@
                     s.acc[h] = part
                 else:
                     s.acc[h] += part
+        taps_bias_all = taps_bias_ref[...].reshape(1, column)
+        own_bias = taps_bias_all[:, 0:width]
+        for i in range(1, per_column):
+            own_bias = jnp.where(
+                block == i, taps_bias_all[:, i * width : (i + 1) * width], own_bias
+            )
         unpack_frames(
             lambda h, r: s.acc[h, :, r * GW : (r + 1) * GW]
-            + taps_bias_ref[:, h * GW : (h + 1) * GW],
+            + own_bias[:, h * GW : (h + 1) * GW],
             s.wide.at[0:length],
             rows,
             groups,
@@ -1098,6 +1189,7 @@
 
         group.when_own(keep_back)
         group.each(num_blocks, group.by_block, lambda b, device: back_from(b, device).wait_recv())
+        outw_quarters.pass_on()
         for b in range(num_blocks):
             lanes = slice(b * width, (b + 1) * width)
             pos_pre[:, lanes] = s.pos_back[b]
@@ -1121,13 +1213,8 @@
 
         peers(lambda b: attn_copy(b, me_utt).start())
 
-        def qkv_arrived(b):
-            for part in range(3):
-                qkv_copy(b, b, part).wait_recv()
-            qkv_hand(b, core).start()
-
-        peers(qkv_arrived)
-        peers(lambda b: qkv_hand(b, 1 - core).wait_recv())
+        qkv_quarters.pass_over()
+        qkv_quarters.arrive()
         for part in range(3):
             own_qkv(part).wait()
 
@@ -1140,6 +1227,11 @@
                 {"seq": dest},
             )
 
+        query_bias_row = query_bias_ref[...].reshape(1, column)
+        value_bias_row = value_bias_ref[...].reshape(1, column)
+        bias = jnp.concatenate(
+            [query_bias_row, jnp.zeros_like(query_bias_row), value_bias_row], axis=1
+        )
         for i in range(num_utt):
             b = peer_of(i)
             if i:
@@ -1147,7 +1239,7 @@
             projected = jnp.dot(
                 attn_all[block_rows(b, frames), :], qkv_all[...], preferred_element_type=F32
             )
-            projected = (projected + bias_ref[...]).astype(BF16)
+            projected = (projected + bias).astype(BF16)
             for j in range(per_column):
                 dest = j * num_utt + b
                 for part in range(3):
@@ -1163,9 +1255,11 @@
                     for part in range(3):
                         heads[part, block_rows(me, frames), :] = s.head_out[dest, part]
 
-        peers(lambda b: up_copy(b, me_utt).start())
+        up_quarters.start()
         peers(lambda b: gout_copy(b, me_utt).start())
+        outw_quarters.pass_over()
         seq_peers(lambda f: head_copy(f, f).wait_recv())
+        up_quarters.pass_on()
 
         def flat_copy(f, slot):
             lanes = pl.ds(pl.multiple_of(slot // num_utt * width, width), width)
@@ -1175,6 +1269,24 @@
                 s.flat_send.at[f],
                 s.flat_recv.at[slot],
                 {"seq": f},
+            )
+
+        def row_copy(f, device):
+            return remote(
+                s.attn_low.at[block_rows(f, frames)],
+                rows_o.at[group.my_block],
+                s.row_send.at[f],
+                s.row_recv.at[group.my_block],
+                device,
+            )
+
+        def row_from(b, device):
+            return remote(
+                s.attn_low.at[block_rows(0, frames)],
+                rows_o.at[b],
+                s.row_send.at[0],
+                s.row_recv.at[b],
+                device,
             )
 
         for start in range(0, length, Q_BLOCK):
@@ -1186,6 +1298,11 @@
                 lse_o[where, h : h + 1] = lse
                 s.attn_low[where, lanes] = value.astype(BF16)
             for f in range(start // frames, (start + Q_BLOCK) // frames):
+                device = group.by_shard(jnp.int32(f))
+
+                @pl.when(group.not_me(device))
+                def _(f=f, device=device):
+                    row_copy(f, device).start()
 
                 @pl.when(f != me)
                 def _(f=f):
@@ -1198,12 +1315,15 @@
                         f * frames : (f + 1) * frames, :
                     ]
 
-        def up_arrived(b):
-            up_copy(b, b).wait_recv()
-            up_hand(b, core).start()
-
-        peers(up_arrived)
-
+        def keep_rows():
+            rows_o[group.my_block] = s.attn_low[block_rows(me, frames), :]
+
+        group.when_own(keep_rows)
+
+        up_quarters.pass_over()
+
+        group.each(num_blocks, group.by_block, lambda b, device: row_from(b, device).wait_recv())
+        own_outw.wait()
         seq_peers(lambda f: flat_copy(f, f).wait_recv())
         peers(lambda b: gout_copy(b, b).wait_recv())
         own_up.wait()
@@ -1215,16 +1335,14 @@
             proj_copy(b, me_utt).wait_send()
             proj_hand(b, core).wait_send()
             vec_copy(b, me_utt).wait_send()
-            for part in range(3):
-                qkv_copy(b, me_utt, part).wait_send()
-            qkv_hand(b, core).wait_send()
-            up_copy(b, me_utt).wait_send()
-            up_hand(b, core).wait_send()
-            up_hand(b, 1 - core).wait_recv()
             gout_copy(b, me_utt).wait_send()
             attn_copy(b, me_utt).wait_send()
 
         peers(sent)
+        outw_quarters.arrive()
+        up_quarters.arrive()
+        for quarters in (qkv_quarters, up_quarters, outw_quarters):
+            quarters.sent()
 
         def sent_seq(f):
             head_copy(f, me).wait_send()
@@ -1233,6 +1351,7 @@
         seq_peers(sent_seq)
         group.each(num_blocks, group.by_block, lambda b, device: there(b, device).wait_send())
         group.each(num_seq, group.by_shard, lambda f, device: back(f, device).wait_send())
+        group.each(num_seq, group.by_shard, lambda f, device: row_copy(f, device).wait_send())
 
     vmem, anywhere = pl.BlockSpec(memory_space=pltpu.VMEM), pl.BlockSpec(memory_space=pl.ANY)
 
@@ -1244,13 +1363,14 @@
         out_shape=[
             shape(num_utt * column, C),
             shape(num_utt * proj_rows, D),
-            shape(num_utt, 1, vectors.shape[1], dtype=F32),
+            shape(num_utt, 1, sum(vector.shape[0] for vector in vectors), dtype=F32),
             shape(num_utt * column, 3 * column),
             shape(num_utt * column, hidden),
             shape(rows_all, D),
             shape(frames, C, dtype=F32),
             shape(frames, C),
             shape(frames, 1, dtype=F32),
+            shape(frames, 2 * C),
             shape(length, width),
             shape(frames, D),
             shape(frames, D, dtype=F32),
@@ -1259,14 +1379,30 @@
             shape(length, width, dtype=F32),
             shape(length, groups, dtype=F32),
             shape(rows_all, column),
+            shape(num_blocks, frames, width),
+            shape(num_utt * column, D),
         ],
-        in_specs=[vmem] * 5 + [anywhere] * 4 + [vmem] * 2,
-        out_specs=[vmem] * 4 + [anywhere] * 2 + [vmem] * 11,
-        scratch_shapes=scratch.shapes,
+        in_specs=[vmem] * (len(vectors) + 4) + [anywhere] * 4 + [vmem] * 3 + [anywhere],
+        out_specs=[vmem] * 4 + [anywhere] * 2 + [vmem] * 13 + [anywhere],
+        scratch_shapes=scratch.shapes + [sem for sems in quarter_sems for sem in sems],
         compiler_params=pltpu.CompilerParams(
             collective_id=collective_id, has_side_effects=True, vmem_limit_bytes=VMEM_BYTES
         ),
-    )(steps, starts, conv, proj, vectors, qkv, up, grad_rows, taps, taps_bias, bias)
+    )(
+        *vectors,
+        feats,
+        starts,
+        conv,
+        proj,
+        qkv,
+        up,
+        grad_rows,
+        taps,
+        taps_bias,
+        query_bias,
+        value_bias,
+        out_weight,
+    )
 
 
 RING = 16
@@ -1274,6 +1410,7 @@
 
 def back_forth(
     flat,
+    attn_rows,
     out_weight,
     resid_one,
     vectors,
@@ -1302,7 +1439,7 @@
     frames = resid_one.shape[0]
     length = frames * num_seq
     rows_all = num_utt * frames
-    column = out_weight.shape[0]
+    column = out_weight.shape[0] // num_utt
     half = column // 2
     hidden = up_all.shape[1]
     per_column = num_seq // num_utt
@@ -1343,11 +1480,11 @@
     scratch = Names(
         part_out=pltpu.VMEM(utt_rows, BF16),
         layer_out=pltpu.VMEM(utt_rows, BF16),
-        got_out=pltpu.VMEM(utt_rows, BF16),
         got_ffn=pltpu.VMEM(utt_rows, BF16),
         got_qkv=pltpu.VMEM(utt_rows, BF16),
         got_layer=pltpu.VMEM(utt_rows, BF16),
         mine=pltpu.VMEM((frames, D), F32),
+        up_bias=pltpu.VMEM((1, hidden), F32),
         ffn_all=pltpu.VMEM((rows_all, D), BF16),
         agrad_all=pltpu.VMEM((rows_all, D), BF16),
         resid_two=pltpu.VMEM((frames, D), F32),
@@ -1393,8 +1530,6 @@
         put_l=pltpu.VMEM(chunk, BF16),
         result=pltpu.VMEM(chunk, BF16),
         local=dma((8,)),
-        out_send=dma((num_utt,)),
-        out_recv=dma((num_utt,)),
         ffn_send=dma((num_utt,)),
         ffn_recv=dma((num_utt,)),
         back_send=dma((num_utt,)),
@@ -1439,6 +1574,7 @@
 
     def kernel(
         flat_ref,
+        rows_ref,
         outw_ref,
         resid_ref,
         vec_ref,
@@ -1500,6 +1636,7 @@
         group.each(num_seq, group.by_shard, lambda i, device: signal(device))
         group.each(num_blocks, group.by_block, lambda i, device: signal(device))
         s.vec_f32[...] = jnp.zeros_like(s.vec_f32)
+        s.up_bias[...] = up_bias_ref[...].reshape(1, hidden)
 
         def entered():
             pl.semaphore_wait(
@@ -1569,6 +1706,7 @@
         mate_counts = [row_blocks[n] for n in range(4)] + [tap_chunks]
 
         def announce(n):
+            steps_ready[0] = starts[n] + counts[n]
             loop(0, mate_counts[n], lambda k: mate_copy(n, k).start())
 
         def group_place(n, b, which):
@@ -1771,14 +1909,24 @@
             elif end > begin:
                 loop(begin, end, step)
 
-        def out_copy(b, slot):
-            return remote(
-                s.part_out.at[b],
-                s.got_out.at[slot],
-                s.out_send.at[b],
-                s.out_recv.at[slot],
-                {"utt": b},
-            )
+        steps_done, steps_ready = [0], [0]
+
+        def advance(count):
+            begin = steps_done[0]
+            steps_done[0] = begin + count
+            assert steps_done[0] <= steps_ready[0] or steps_ready[0] == total
+            return begin, steps_done[0]
+
+        def beside(count):
+            sums(*advance(count))
+
+        def beside_loop(iterations, count):
+            begin, end = advance(iterations * count)
+
+            def run(i):
+                sums(begin, end, shift=(begin + i * count, begin + (i + 1) * count))
+
+            return run
 
         def ffn_copy(b, slot):
             place = own_rows(slot)
@@ -1854,26 +2002,20 @@
                 copy.start()
             entered()
 
-            def out_block(i):
-                b = peer_of(i)
-                part = jnp.dot(flat_ref[own_rows(b), :], outw_ref[...], preferred_element_type=F32)
-                hand_out(b, part, out_copy)
-
-            loop(1, num_utt + 1, out_block)
-            loads[0].wait()
-            loads[1].wait()
-
-            def down_block(b):
-                down_grad[own_rows(b), :] = nt_dot(gout[own_rows(b), :], down[...])
-
-            loop(0, num_utt, down_block)
-            peers(lambda b: out_copy(b, b).wait_recv())
-            resid_two = resid_ref[...] + from_peers(s.got_out, s.mine[...]) + out_bias
+            rows_wide = jnp.concatenate([rows_ref[b] for b in range(num_blocks)], axis=1)
+            resid_two = resid_ref[...] + out_bias
+            resid_two = resid_two + jnp.dot(rows_wide, outw_ref[...], preferred_element_type=F32)
             s.resid_two[...] = resid_two
             normed, _ = norm_parts(resid_two)
             s.ffn_all[own_rows(me_utt), :] = (normed * ffn_gain + ffn_shift).astype(BF16)
             peers(lambda b: ffn_copy(b, me_utt).start())
-            peers(lambda b: out_copy(b, me_utt).wait_send())
+            loads[0].wait()
+            loads[1].wait()
+
+            def down_block(b):
+                down_grad[own_rows(b), :] = nt_dot(gout[own_rows(b), :], down[...])
+
+            loop(0, num_utt, down_block)
             loads[2].wait()
 
             def ffn_block(i):
@@ -1888,7 +2030,7 @@
                 def cut_block(j):
                     cut = block_rows(j, column)
                     pre = jnp.dot(s.ffn_all[where, :], up[:, cut], preferred_element_type=F32)
-                    act, slope = gelu_parts(pre + up_bias_ref[:, cut])
+                    act, slope = gelu_parts(pre + s.up_bias[:, cut])
                     hidden_low[where, cut] = act.astype(BF16)
                     hidden_grad[where, cut] = (down_grad[where, cut] * slope).astype(BF16)
 
@@ -1904,14 +2046,17 @@
             loop(0, hidden // column, down_grads)
             announce(DOWN)
 
+            up_steps = beside_loop(D // column, PACE["up"])
+
             def up_grads(i):
                 cut = block_rows(i, column)
                 s.part_up[cut, :] = inner_dot(s.ffn_all[:, cut], hidden_grad[...]).astype(BF16)
+                up_steps(i)
 
             loop(0, D // column, up_grads)
             announce(UP)
             put_column(26, column_sum(hidden_grad[...].astype(F32)))
-            sums(*SITES[0])
+            beside(PACE["back"])
             peers(lambda b: back_copy(b, b).wait_recv())
             back = from_peers(s.got_ffn, s.mine[...])
             normed, scale = norm_parts(s.resid_two[...])
@@ -1926,6 +2071,9 @@
             peers(lambda b: agrad_copy(b, me_utt).start())
             put_vector(14, column_sum(grad.astype(F32)))
             peers(lambda b: back_copy(b, me_utt).wait_send())
+            beside(PACE["before_layer"])
+            layer_steps = beside_loop(num_utt, PACE["layer"])
+
             def layer_block(b):
                 part = jnp.dot(hidden_low[own_rows(b), :], down[...], preferred_element_type=F32)
 
@@ -1937,8 +2085,10 @@
                 def _():
                     s.resid_two[...] += part + down_bias
 
+                layer_steps(b)
+
             loop(0, num_utt, layer_block)
-            sums(*SITES[1])
+            beside(PACE["after_layer"])
 
         vmem = pltpu.VMEM
         pl.run_scoped(
@@ -1968,7 +2118,9 @@
             def _():
                 agrad_copy(b, b).wait_recv()
 
-            grad = nt_dot(s.agrad_all[own_rows(b), :], outw_ref[...]).astype(BF16)
+            grad = nt_dot(
+                s.agrad_all[own_rows(b), :], outw_ref[block_rows(me_utt, column), :]
+            ).astype(BF16)
             for j in range(per_column):
                 dest = j * num_utt + b
                 s.ghead_out[dest] = grad[:, j * width : (j + 1) * width]
@@ -2014,8 +2166,8 @@
         my_lanes = pl.ds(pl.multiple_of(block * width, width), width)
         s.dk_acc[...] = jnp.zeros_like(s.dk_acc)
         s.dv_acc[...] = jnp.zeros_like(s.dv_acc)
-        beside, q_blocks = SITES[2], length // Q_BLOCK
-        steps_beside = (beside[1] - beside[0]) // q_blocks
+        q_blocks = length // Q_BLOCK
+        query_steps = beside_loop(q_blocks * groups, PACE["query"])
 
         def query_block(i):
             where = block_rows(i, Q_BLOCK)
@@ -2031,15 +2183,13 @@
                 ).astype(BF16)
                 s.dk_acc[:, lanes] += inner_dot(score_grad, queries)
                 s.dv_acc[:, lanes] += inner_dot(probs.astype(BF16), grads)
+                query_steps(i * groups + h)
             for j in range(Q_BLOCK // frames):
                 f = i * (Q_BLOCK // frames) + j
 
                 @pl.when(f != me)
                 def _(f=f):
                     dq_copy(f, me).start()
-
-            first_step = beside[0] + i * steps_beside
-            sums(*beside, shift=(first_step, first_step + steps_beside))
 
         loop(0, q_blocks, query_block)
         s.dqkv[1] = (s.dk_acc[...] * SCALE).astype(BF16)
@@ -2063,12 +2213,15 @@
 
         loop(1, num_utt + 1, qkv_block)
 
+        qkv_steps = beside_loop(D // column, PACE["qkv"])
+
         def qkv_grads(i):
             cut = block_rows(i, column)
             for part in range(3):
                 s.part_qkv[cut, part * column : (part + 1) * column] = inner_dot(
                     attn_in_ref[:, cut], s.qback[part]
                 ).astype(BF16)
+            qkv_steps(i)
 
         loop(0, D // column, qkv_grads)
         announce(QKV)
@@ -2076,7 +2229,7 @@
         put_column(24, column_sum(s.qback[2].astype(F32)))
         peers(lambda b: layer_copy(b, b).wait_recv())
         layer_o[...] = from_peers(s.got_layer, s.resid_two[...]).astype(BF16)
-        sums(*SITES[3])
+        beside(PACE["attn_back"])
         peers(lambda b: qpart_copy(b, b).wait_recv())
         back = from_peers(s.got_qkv, s.mine[...])
         normed, scale = norm_parts(resid_ref[...])
@@ -2146,50 +2299,10 @@
             taps_ref[TILE + KPOS * GW :, :] = edge
             fill_frames(pos_in_ref, wide, packed, length, groups)
             total_ref[...] = jnp.zeros_like(total_ref)
-            sums(*SITES[4])
+            beside(PACE["there"])
             taps_in.wait()
             group.each(num_seq, group.by_shard, lambda f, device: there_from(f, device).wait_recv())
             fill_frames(s.pos_grad, wide, grads, length, groups)
-            acc[...] = jnp.zeros_like(acc)
-
-            def input_tiles(first, windows, count):
-                for h in range(groups):
-                    for start in range(0, count, 4):
-                        tiles = range(start, min(start + 4, count))
-                        acc[h] += nt_dot(
-                            jnp.concatenate([windows[h](j) for j in tiles], axis=1),
-                            jnp.concatenate(
-                                [tap_tile(taps_ref, (first + j) * TILE, TILE, h) for j in tiles],
-                                axis=1,
-                            ),
-                        )
-
-            def eight_inputs(i):
-                base = pl.multiple_of(2 * middle - 8 - 8 * i, 8)
-                windows = []
-                for h in range(groups):
-                    window = grads[h, pl.ds(base, rows + 8), :]
-                    windows.append(lambda j, w=window: w[8 - j : 8 - j + rows].astype(BF16))
-                input_tiles(8 * i, windows, 8)
-
-            loop(0, NUM_TILES // 8, eight_inputs)
-            assert NUM_TILES % 8 == 1 and NUM_TILES == 2 * middle + 1
-            input_tiles(
-                NUM_TILES - 1,
-                [lambda j, h=h: grads[h, 0:rows, :].astype(BF16) for h in range(groups)],
-                1,
-            )
-            unpack_frames(
-                lambda h, r: acc[h, :, r * GW : (r + 1) * GW], wide.at[0:length], rows, groups
-            )
-            s.pos_own[...] = wide[0:length, :].astype(BF16)
-            group.each(num_seq, group.by_shard, lambda f, device: home(f, device).start())
-
-            def keep_home():
-                s.pos_back[group.my_block] = s.pos_own[own_rows(me), :]
-
-            group.when_own(keep_home)
-
             def weight_tile(tile, frames_of):
                 pieces = [
                     inner_dot(
@@ -2204,16 +2317,62 @@
                         [piece[:, r * GW : (r + 1) * GW] for piece in pieces], axis=1
                     )
 
+            weight_steps = beside_loop(NUM_TILES // 8, PACE["weight"])
+
             def eight_weights(i):
                 base = pl.multiple_of(8 * i, 8)
                 windows = [packed[h, pl.ds(base, rows + 8), :] for h in range(groups)]
                 for j in range(8):
                     weight_tile(8 * i + j, lambda h, j=j: windows[h][j : j + rows])
+                weight_steps(i)
 
             loop(0, NUM_TILES // 8, eight_weights)
             weight_tile(NUM_TILES - 1, lambda h: packed[h, NUM_TILES - 1 :, :])
             s.part_taps[...] = total_ref[TILE : TILE + KPOS * GW, :].astype(BF16)
             announce(TAPS)
+            beside(PACE["taps"])
+            acc[...] = jnp.zeros_like(acc)
+
+            def input_tiles(first, windows, count):
+                for h in range(groups):
+                    for start in range(0, count, 4):
+                        tiles = range(start, min(start + 4, count))
+                        acc[h] += nt_dot(
+                            jnp.concatenate([windows[h](j) for j in tiles], axis=1),
+                            jnp.concatenate(
+                                [tap_tile(taps_ref, (first + j) * TILE, TILE, h) for j in tiles],
+                                axis=1,
+                            ),
+                        )
+
+            input_steps = beside_loop(NUM_TILES // 8, PACE["input"])
+
+            def eight_inputs(i):
+                base = pl.multiple_of(2 * middle - 8 - 8 * i, 8)
+                windows = []
+                for h in range(groups):
+                    window = grads[h, pl.ds(base, rows + 8), :]
+                    windows.append(lambda j, w=window: w[8 - j : 8 - j + rows].astype(BF16))
+                input_tiles(8 * i, windows, 8)
+                input_steps(i)
+
+            loop(0, NUM_TILES // 8, eight_inputs)
+            assert NUM_TILES % 8 == 1 and NUM_TILES == 2 * middle + 1
+            input_tiles(
+                NUM_TILES - 1,
+                [lambda j, h=h: grads[h, 0:rows, :].astype(BF16) for h in range(groups)],
+                1,
+            )
+            unpack_frames(
+                lambda h, r: acc[h, :, r * GW : (r + 1) * GW], wide.at[0:length], rows, groups
+            )
+            s.pos_own[...] = wide[0:length, :].astype(BF16)
+            group.each(num_seq, group.by_shard, lambda f, device: home(f, device).start())
+
+            def keep_home():
+                s.pos_back[group.my_block] = s.pos_own[own_rows(me), :]
+
+            group.when_own(keep_home)
 
         packed_rows = (groups, (length + KPOS) // PACK, TILE)
         pl.run_scoped(
@@ -2226,7 +2385,7 @@
             vmem((KPOS * GW + 2 * TILE, width), F32),
             dma,
         )
-        sums(*SITES[5])
+        beside(PACE["home"])
 
         group.each(num_blocks, group.by_block, lambda b, device: home_from(b, device).wait_recv())
         for b in range(num_blocks):
@@ -2239,6 +2398,7 @@
         put_vector(4, column_sum(proj_grad.astype(F32)))
         s.part_proj[...] = inner_dot(low_ref[...], proj_grad).astype(BF16)
         loop(0, num_utt, lambda b: group_mate(1, b).start())
+        beside(PACE["proj"])
         feat_grad = nt_dot(proj_grad, proj_ref[...])
         conv_gain, conv_shift = vector(0, low), vector(low, low)
         normed, first_scale = norm_parts(pre_ref[...])
@@ -2249,12 +2409,23 @@
         grad = norm_back(feat_grad * vector(2 * low, low), second, second_scale) * slope
         put_vector(0, column_sum(grad * normed))
         put_vector(1, column_sum(grad))
+        beside(PACE["norms"])
         conv_grad = norm_back(grad * conv_gain, normed, first_scale).astype(BF16)
         s.part_conv[...] = inner_dot(steps_ref[...], conv_grad).astype(BF16)
         loop(0, num_utt, lambda b: group_mate(0, b).start())
         s.part_vec[...] = s.vec_f32[...].astype(BF16)
         loop(0, num_utt, lambda b: group_mate(2, b).start())
-        feat_o[...] = nt_dot(conv_grad, conv_ref[...]).astype(BF16)
+        back_steps = nt_dot(conv_grad, conv_ref[...])
+
+        def interleave(wide):
+            for step in range(2):
+                for j in range(C // 128):
+                    lanes = slice(step * C + j * 128, step * C + (j + 1) * 128)
+                    wide[j, pl.ds(step, frames, stride=2), :] = back_steps[:, lanes]
+            for j in range(C // 128):
+                feat_o[:, j * 128 : (j + 1) * 128] = wide[j].astype(BF16)
+
+        pl.run_scoped(interleave, vmem((C // 128, 2 * frames, 128), F32))
 
         def late_lanes(n, slot, part):
             first_lane = (part * num_utt + slot) * late_wide[n]
@@ -2305,14 +2476,14 @@
                 late_own(n, part).wait()
                 late_hand(n, me_utt, part, core).start()
 
-        begin = SITES[5][1]
-        stop = starts[OUT] + RING + final_lag
-        assert begin <= stop <= starts[CONV]
-        sums(begin, stop)
+        steps_ready[0] = total
+        stop = max(steps_done[0], starts[OUT] + RING + final_lag)
+        assert stop <= starts[CONV]
+        beside(stop - steps_done[0])
         late_start(1)
         for n in range(3):
             loop(0, num_utt, lambda i, n=n: hand_on(n, lax.rem(me_utt + 1 + i, num_utt)))
-        after = starts[TAPS] + RING + final_lag
+        after = max(stop, starts[TAPS] + RING + final_lag)
         sums(stop, after)
         late_start(0)
         late_arrived(1)
@@ -2375,7 +2546,7 @@
     vmem, anywhere = pl.BlockSpec(memory_space=pltpu.VMEM), pl.BlockSpec(memory_space=pl.ANY)
     shapes = [
         (frames, D),
-        (frames, 2 * C),
+        (2 * frames, C),
         (hidden, D),
         (D, hidden),
         (column, D),
@@ -2390,16 +2561,17 @@
     return pl.pallas_call(
         kernel,
         out_shape=[jax.ShapeDtypeStruct(shape, BF16) for shape in shapes],
-        in_specs=[vmem] * 18 + [anywhere] * 4,
+        in_specs=[vmem] * 19 + [anywhere] * 4,
         out_specs=[vmem] * 2 + [anywhere] * 10,
         scratch_shapes=scratch.shapes,
         compiler_params=pltpu.CompilerParams(
             collective_id=collective_id,
             has_side_effects=True,
-            vmem_limit_bytes=62 * 1024 * 1024,
+            vmem_limit_bytes=63 * 1024 * 1024,
         ),
     )(
         flat,
+        attn_rows,
         out_weight,
         resid_one,
         vectors,
@@ -2424,7 +2596,45 @@
     )
 
 
-SITES = [(0, 5), (5, 12), (12, 28), (28, 36), (36, 42), (42, 47)]
+PACE = {
+    "up": 1,
+    "back": 1,
+    "before_layer": 2,
+    "layer": 1,
+    "after_layer": 3,
+    "query": 1,
+    "qkv": 1,
+    "attn_back": 6,
+    "there": 3,
+    "weight": 1,
+    "taps": 1,
+    "input": 2,
+    "home": 4,
+    "proj": 2,
+    "norms": 2,
+}
+
+
+WIDEN_STEPS = 4
+
+
+def widen(arrays):
+    def kernel(*refs):
+        for source, target in zip(refs[: len(arrays)], refs[len(arrays) :], strict=True):
+            target[...] = source[...].astype(F32)
+
+    specs = [
+        pl.BlockSpec((array.shape[0] // WIDEN_STEPS, array.shape[1]), lambda i: (i, 0))
+        for array in arrays
+    ]
+    return pl.pallas_call(
+        kernel,
+        grid=(WIDEN_STEPS,),
+        out_shape=[jax.ShapeDtypeStruct(array.shape, F32) for array in arrays],
+        in_specs=specs,
+        out_specs=specs,
+        compiler_params=pltpu.CompilerParams(vmem_limit_bytes=VMEM_BYTES),
+    )(*arrays)
 
 
 def layer_norm(values, gain, shift):
@@ -2525,11 +2735,11 @@
     def split_rows(values):
         return values.astype(BF16).reshape(num_utt, frames, D)
 
+    fast = width == CHUNK_ROWS
     block_id = me_seq // num_utt
     taps = lax.dynamic_slice_in_dim(pos_weight, block_id * width, width, 2)
     taps = taps.reshape(KPOS * GW, width)
     taps_bias = lax.dynamic_slice_in_dim(pos_bias, block_id * width, width, 0)[None, :]
-    fast = width == CHUNK_ROWS
     if fast:
         (
             conv_all,
@@ -2541,6 +2751,7 @@
             conv_pre,
             feat_low,
             masked,
+            steps_in,
             pos_in,
             pos_pre,
             resid_one,
@@ -2549,18 +2760,22 @@
             attn_f32,
             lse,
             attn_flat,
+            attn_rows,
+            out_all,
         ) = front_forward(
-            steps_in,
+            feats.reshape(2 * frames, C),
             mask_starts,
             conv_weight,
             proj_weight,
-            jnp.concatenate(vectors)[None, :],
+            vectors,
             qkv_weight,
             up_weight,
             out_rows,
             pos_weight.reshape(KPOS * GW, column),
-            taps_bias,
-            jnp.concatenate([query_bias, jnp.zeros_like(query_bias), value_bias])[None, :],
+            pos_bias,
+            query_bias,
+            value_bias,
+            out_weight,
             1,
         )
         queries, keys, values = qkv_heads[0], qkv_heads[1], qkv_heads[2]
@@ -2657,10 +2872,11 @@
             qkv_sum,
         ) = back_forth(
             attn_flat,
-            out_weight,
+            attn_rows,
+            out_all,
             resid_one,
             vectors_all,
-            up_bias[None, :],
+            up_bias,
             attn_in,
             qkv_columns,
             qkv_heads,
@@ -2682,7 +2898,10 @@
         )
         layer_out = layer_out.reshape(1, frames, D)
         feat_grad = feat_grad.reshape(1, 2 * frames, C)
-        grads = (taps_sum, outweight_sum, qkv_sum, conv_sum, proj_sum, vector_sum, up_sum)
+        *wide_sums, downweight_sum = widen(
+            (taps_sum, outweight_sum, qkv_sum, conv_sum, proj_sum, up_sum, downweight_sum)
+        )
+        grads = (*wide_sums[:5], vector_sum, wide_sums[5])
         small, wide = (C // num_utt,), (column,)
         row_sizes, column_sizes = 4 * small + 9 * wide, 2 * wide + (hidden,)
     else:

time: 376 us -> 336 us (0.89)
  other arithmetic: 17.9 us -> 0.01 us
  local copies, waits for them, and re-layouts: 17.8 us -> 3.15 us
  Pallas kernels: 339 us -> 332 us
    pallas_call x1, Pallas kernels: 247 us -> 223 us  [back_forth(): pl.pallas_call(kernel, out_shape=[jax.ShapeDtypeStruct(shape, BF16) for s...]
    convert_element_type x7 -> x0, other arithmetic: 16.3 us -> none  [the longest x4 6.71 us: shards(): grad.astype(F32)]
    pallas_call x0 -> x1, Pallas kernels: none -> 11.4 us  [widen(): pl.pallas_call(kernel, grid=(WIDEN_STEPS,), out_shape=[jax.ShapeDtypeStru...]
    unnamed x26 -> x8, local copies, waits for them, and re-layouts: 10.1 us -> 1.42 us
    pallas_call x1, Pallas kernels: 91.4 us -> 97.5 us  [front_forward(): pl.pallas_call(kernel, out_shape=[shape(num_utt * column, C), shape(num_u...]
where the time goes in v5:
time: 336 us
  Pallas kernels  332 us (99%)
    pallas_call x1, Pallas kernels, back_forth(): pl.pallas_call(kernel, out_shape=[jax.ShapeDtypeStruct(shape, BF16) for s...  223 us
    pallas_call x1, Pallas kernels, front_forward(): pl.pallas_call(kernel, out_shape=[shape(num_utt * column, C), shape(num_u...  97.5 us
    pallas_call x1, Pallas kernels, widen(): pl.pallas_call(kernel, grid=(WIDEN_STEPS,), out_shape=[jax.ShapeDtypeStru...  11.4 us

profile of v5, /device:TPU:0, one launch (start us, length us, event | category | flops | bytes accessed | tf_op | source)
XLA Modules:
  0.0 336.1 jit_solution(4106954736357566791)
XLA Ops:
  0.7 97.5 %shard_map.441 = (bf16[1024,512]{1,0:T(8,128)(2,1)}, bf16[512,1024]{1,0:T(8,128)(2,1)}, f32[4,1,2560]{2,1,0:T(1,128)}, bf16[1024,768]{1,0:T(8,128)(2,1)}, bf16[1...) custom-call(f32[128]{0:T(128)} %refs_0_.1, ...), custom_call_target="tpu_custom_call" | custom-call | tf_op jit(solution)/shard_map/pallas_call | solution.py:1361
  98.2 223.2 %shard_map.442 = (bf16[128,1024]{1,0:T(8,128)(2,1)}, bf16[256,512]{1,0:T(8,128)(2,1)}, bf16[1024,1024]{1,0:T(8,128)(2,1)}, bf16[1024,1024]{1,0:T(8,128)(2,1)}, b...) custom-call(bf16[512,256]{1,0:T(8,128)(2,1)} %get-tuple-element.62.f, ...), custom_call_target="tpu_custom_call" | custom-call | tf_op jit(solution)/shard_map/pallas_call | solution.py:2561
  321.5 0.0 copy-start.2
  321.5 0.0 copy-start.1
  321.5 0.0 copy-start
  321.5 11.4 %shard_map.443 = (f32[8192,256]{1,0:T(8,128)}, f32[256,1024]{1,0:T(8,128)}, f32[256,3072]{1,0:T(8,128)}, f32[256,512]{1,0:T(8,128)}, f32[128,1024]{1,0:T(8,128)}...) custom-call(bf16[8192,256]{1,0:T(8,128)(2,1)} %get-tuple-element.84.refs_0_, bf16[256,1024]{1,0:T(8,128)(2,1)} %get-tuple-element.85.refs_1_, ...), custom_call_target="tpu_custom_call" | custom-call | tf_op jit(solution)/shard_map/pallas_call | solution.py:2630
  332.9 0.0 copy-done.2
  332.9 0.6 slice_bitcast_fusion.1
  333.5 0.6 slice_bitcast_fusion
  334.1 0.5 slice_bitcast_fusion.12
  334.7 0.0 copy-done.1
  334.7 0.7 copy.53
  335.4 0.0 copy-done
  335.4 0.7 copy.54
  (1 shorter events, 0.0 us)
Async XLA Ops:
  321.5 11.4 %copy-start.2 = (bf16[64,128]{1,0:T(8,128)(2,1)S(1)}, bf16[64,128]{1,0:T(8,128)(2,1)}, u32[]{:S(2)}) copy-start(bf16[64,128]{1,0:T(8,128)(2,1)} %get-tuple-element.92) | copy-start | bytes 49156
  321.5 13.2 %copy-start.1 = (bf16[128,1024]{1,0:T(8,128)(2,1)S(1)}, bf16[128,1024]{1,0:T(8,128)(2,1)}, u32[]{:S(2)}) copy-start(bf16[128,1024]{1,0:T(8,128)(2,1)} %get-tuple-element.82) | copy-start | bytes 786436
  321.5 13.9 %copy-start = (bf16[256,512]{1,0:T(8,128)(2,1)S(1)}, bf16[256,512]{1,0:T(8,128)(2,1)}, u32[]{:S(2)}) copy-start(bf16[256,512]{1,0:T(8,128)(2,1)} %get-tuple-element.83) | copy-start | bytes 786436

commit v6 on v5

--- a/solution.py
+++ b/solution.py
@@ -711,6 +711,166 @@
             body()
 
 
+class GroupMove:
+    def __init__(self):
+        self.num_seq, self.num_utt = lax.axis_size("seq"), lax.axis_size("utt")
+        self.me_seq, self.me_utt = lax.axis_index("seq"), lax.axis_index("utt")
+        self.here = self.num_utt // 2
+        self.per_column = self.num_seq // 2
+        assert self.per_column * self.num_utt == G
+        self.pieces = self.num_seq * self.here
+        self.z, self.core = self.me_seq // 2, lax.rem(self.me_seq, 2)
+        self.is_own = (self.core == self.me_utt // self.here).astype(jnp.int32)
+        self.my_group = self.per_column * self.me_utt + self.z
+        self.my_slot = lax.rem(self.me_utt, self.here)
+        self.my_piece = self.me_seq * self.here + self.my_slot
+
+    def by_group(self, g):
+        return {
+            "seq": 2 * lax.rem(g, self.per_column) + self.me_utt // self.here,
+            "utt": g // self.per_column,
+        }
+
+    def by_piece(self, i):
+        return {"seq": i // self.here, "utt": self.here * self.core + lax.rem(i, self.here)}
+
+    def each(self, count, where, body):
+        def run(i):
+            device = where(i)
+
+            @pl.when(
+                jnp.logical_or(device["seq"] != self.me_seq, device["utt"] != self.me_utt)
+            )
+            def _():
+                body(i, device)
+
+        loop(0, count, run)
+
+    def greet(self, signal):
+        self.each(self.pieces, self.by_piece, lambda i, device: signal(device))
+        self.each(G, self.by_group, lambda i, device: signal(device))
+
+    def out(self, blocks, whole, sems):
+        rows = blocks.shape[1]
+
+        def copy(g, device):
+            return remote(
+                blocks.at[g],
+                whole.at[self.my_slot, block_rows(self.me_seq, rows)],
+                sems[0].at[g],
+                sems[1].at[self.my_piece],
+                device,
+            )
+
+        def copy_from(i, device):
+            return remote(
+                blocks.at[0],
+                whole.at[lax.rem(i, self.here), block_rows(i // self.here, rows)],
+                sems[0].at[0],
+                sems[1].at[i],
+                device,
+            )
+
+        self.each(G, self.by_group, lambda g, device: copy(g, device).start())
+
+        @pl.when(self.is_own == 1)
+        def _():
+            whole[self.my_slot, block_rows(self.me_seq, rows), :] = blocks[self.my_group]
+
+        return (
+            lambda: self.each(
+                self.pieces, self.by_piece, lambda i, device: copy_from(i, device).wait_recv()
+            ),
+            lambda: self.each(G, self.by_group, lambda g, device: copy(g, device).wait_send()),
+        )
+
+    def home(self, whole, blocks, sems):
+        rows = blocks.shape[1]
+
+        def copy(i, device):
+            return remote(
+                whole.at[lax.rem(i, self.here), block_rows(i // self.here, rows)],
+                blocks.at[self.my_group],
+                sems[0].at[i],
+                sems[1].at[self.my_group],
+                device,
+            )
+
+        def copy_from(g, device):
+            return remote(
+                whole.at[0, block_rows(0, rows)],
+                blocks.at[g],
+                sems[0].at[0],
+                sems[1].at[g],
+                device,
+            )
+
+        self.each(self.pieces, self.by_piece, lambda i, device: copy(i, device).start())
+
+        @pl.when(self.is_own == 1)
+        def _():
+            blocks[self.my_group] = whole[self.my_slot, block_rows(self.me_seq, rows), :]
+
+        return (
+            lambda: self.each(G, self.by_group, lambda g, device: copy_from(g, device).wait_recv()),
+            lambda: self.each(
+                self.pieces, self.by_piece, lambda i, device: copy(i, device).wait_send()
+            ),
+        )
+
+    def semaphores(self, out):
+        dma = pltpu.SemaphoreType.DMA
+        return [dma((G,)), dma((self.pieces,))] if out else [dma((self.pieces,)), dma((G,))]
+
+
+def pack_rows(values, tiles, blocks):
+    rows = blocks.shape[1]
+    for p in range(tiles.shape[0]):
+        tiles[p] = values[:, p * 128 : (p + 1) * 128]
+    for p in range(tiles.shape[0]):
+        for r in range(PACK):
+            part = tiles[p, pl.ds(r, rows, stride=PACK), :].astype(BF16)
+            for h in range(128 // GW):
+                blocks[p * (128 // GW) + h, :, r * GW : (r + 1) * GW] = part[
+                    :, h * GW : (h + 1) * GW
+                ]
+
+
+def unpack_rows(blocks, tiles):
+    rows = blocks.shape[1]
+    for p in range(tiles.shape[0]):
+        for r in range(PACK):
+            tiles[p, pl.ds(r, rows, stride=PACK), :] = jnp.concatenate(
+                [
+                    blocks[p * (128 // GW) + h, :, r * GW : (r + 1) * GW].astype(F32)
+                    for h in range(128 // GW)
+                ],
+                axis=1,
+            )
+
+
+def pad_frames(whole, padded):
+    edge = HALF // PACK
+    for j in range(whole.shape[0]):
+        padded[j, 0:edge, :] = jnp.zeros((edge, TILE), F32)
+        padded[j, edge + whole.shape[1] :, :] = jnp.zeros((edge, TILE), F32)
+        padded[j, edge : edge + whole.shape[1], :] = whole[j].astype(F32)
+
+
+def own_taps(taps_ref, second):
+    edge = jnp.zeros((TILE, taps_ref.shape[1]), BF16)
+    taps_ref[0:TILE, :] = edge
+    taps_ref[TILE + KPOS * GW :, :] = edge
+
+    @pl.when(second)
+    def _():
+        def move(i):
+            rows = block_rows(i, 512)
+            taps_ref[rows, 0:GW] = taps_ref[rows, GW : 2 * GW]
+
+        loop(0, taps_ref.shape[0] // 512, move)
+
+
 class Quarters:
     def __init__(self, group, source, target, rows, parts, sems):
         self.group, self.source, self.target = group, source, target
@@ -840,21 +1000,37 @@
     width = column // per_column
     groups = width // GW
     rows = length // PACK
+    here = num_utt // 2
     num_blocks = num_utt * per_column
     low = C // num_utt
     rows_all = num_utt * frames
     dma = pltpu.SemaphoreType.DMA
+    vec_size = sum(vector.shape[0] for vector in vectors)
     scratch = Names(
+        out_conv_all=pltpu.VMEM((num_utt * column, C), BF16),
+        out_proj_all=pltpu.VMEM((num_utt * proj_rows, D), BF16),
+        out_vec_all=pltpu.VMEM((num_utt, 1, vec_size), F32),
+        out_qkv_all=pltpu.VMEM((num_utt * column, 3 * column), BF16),
+        out_pre_o=pltpu.VMEM((frames, C), F32),
+        out_low_o=pltpu.VMEM((frames, C), BF16),
+        out_mask_o=pltpu.VMEM((frames, 1), F32),
+        out_steps_o=pltpu.VMEM((frames, 2 * C), BF16),
+        out_pos_in=pltpu.VMEM((here, rows, TILE), BF16),
+        out_pos_pre=pltpu.VMEM((frames, D), BF16),
+        out_resid_o=pltpu.VMEM((frames, D), F32),
+        out_attn_all=pltpu.VMEM((rows_all, D), BF16),
+        out_heads=pltpu.VMEM((3, length, width), BF16),
+        store=dma((13,)),
         feats=pltpu.VMEM((C // 128, 2 * frames, 128), F32),
-        vec_own=pltpu.VMEM((1, sum(vector.shape[0] for vector in vectors)), F32),
-        wide=pltpu.VMEM((length + KPOS, width), F32),
-        packed=pltpu.VMEM((groups, (length + KPOS) // PACK, TILE), F32),
+        vec_own=pltpu.VMEM((1, vec_size), F32),
+        tiles=pltpu.VMEM((D // 128, frames, 128), F32),
+        packed=pltpu.VMEM((here, (length + KPOS) // PACK, TILE), F32),
         taps=pltpu.VMEM((KPOS * GW + 2 * TILE, width), BF16),
-        acc=pltpu.VMEM((groups, rows, TILE), F32),
+        acc=pltpu.VMEM((here * rows, TILE), F32),
         embed=pltpu.VMEM((frames, D), F32),
-        blocks=pltpu.VMEM((num_blocks, frames, width), BF16),
-        pos_own=pltpu.VMEM((length, width), BF16),
-        pos_back=pltpu.VMEM((num_blocks, frames, width), BF16),
+        blocks=pltpu.VMEM((G, frames // PACK, TILE), BF16),
+        pos_own=pltpu.VMEM((here, rows, TILE), BF16),
+        pos_back=pltpu.VMEM((G, frames // PACK, TILE), BF16),
         head_out=pltpu.VMEM((num_seq, 3, frames, width), BF16),
         attn_low=pltpu.VMEM((length, width), BF16),
         local=dma((12,)),
@@ -870,10 +1046,10 @@
         vec_recv=dma((num_utt,)),
         gout_send=dma((num_utt,)),
         gout_recv=dma((num_utt,)),
-        there_send=dma((num_blocks,)),
-        there_recv=dma((num_seq,)),
-        back_send=dma((num_seq,)),
-        back_recv=dma((num_blocks,)),
+        there_send=dma((G,)),
+        there_recv=dma((num_seq * here,)),
+        back_send=dma((num_seq * here,)),
+        back_recv=dma((G,)),
         attn_send=dma((num_utt,)),
         attn_recv=dma((num_utt,)),
         head_send=dma((num_seq,)),
@@ -900,21 +1076,21 @@
             query_bias_ref,
             value_bias_ref,
             outw_ref,
-            conv_all,
-            proj_all,
-            vec_all,
-            qkv_all,
+            conv_all_hbm,
+            proj_all_hbm,
+            vec_all_hbm,
+            qkv_all_hbm,
             up_all,
             gout_all,
-            pre_o,
-            low_o,
-            mask_o,
-            steps_o,
-            pos_in,
-            pos_pre,
-            resid_o,
-            attn_all,
-            heads,
+            pre_o_hbm,
+            low_o_hbm,
+            mask_o_hbm,
+            steps_o_hbm,
+            pos_in_hbm,
+            pos_pre_hbm,
+            resid_o_hbm,
+            attn_all_hbm,
+            heads_hbm,
             attn_o,
             lse_o,
             flat_o,
@@ -923,6 +1099,43 @@
         ) = refs[:32]
         rest, quarter_refs = refs[32:-18], refs[-18:]
         s = scratch.bind(rest)
+        conv_all = s.out_conv_all
+        proj_all = s.out_proj_all
+        vec_all = s.out_vec_all
+        qkv_all = s.out_qkv_all
+        pre_o = s.out_pre_o
+        low_o = s.out_low_o
+        mask_o = s.out_mask_o
+        steps_o = s.out_steps_o
+        pos_in = s.out_pos_in
+        pos_pre = s.out_pos_pre
+        resid_o = s.out_resid_o
+        attn_all = s.out_attn_all
+        heads = s.out_heads
+        early_outputs = {
+            "conv_all": (conv_all, conv_all_hbm),
+            "proj_all": (proj_all, proj_all_hbm),
+            "vec_all": (vec_all, vec_all_hbm),
+            "qkv_all": (qkv_all, qkv_all_hbm),
+            "pre_o": (pre_o, pre_o_hbm),
+            "low_o": (low_o, low_o_hbm),
+            "mask_o": (mask_o, mask_o_hbm),
+            "steps_o": (steps_o, steps_o_hbm),
+            "pos_in": (pos_in, pos_in_hbm),
+            "pos_pre": (pos_pre, pos_pre_hbm),
+            "resid_o": (resid_o, resid_o_hbm),
+            "attn_all": (attn_all, attn_all_hbm),
+            "heads": (heads, heads_hbm),
+        }
+        stores = {
+            name: pltpu.make_async_copy(source, target, s.store.at[i])
+            for i, (name, (source, target)) in enumerate(early_outputs.items())
+        }
+
+        def store(*names):
+            for name in names:
+                stores[name].start()
+
         group = Regroup()
         me, me_utt = group.me_seq, group.me_utt
         core = lax.rem(me, 2)
@@ -945,8 +1158,9 @@
 
         peers(lambda b: signal({"utt": b}))
         seq_peers(lambda f: signal({"seq": f}))
-        group.each(num_seq, group.by_shard, lambda i, device: signal(device))
         group.each(num_blocks, group.by_block, lambda i, device: signal(device))
+        move = GroupMove()
+        move.greet(signal)
 
         first_tap = pl.multiple_of(block * width, width)
         taps_in = pltpu.make_async_copy(
@@ -985,7 +1199,8 @@
             s.vec_own[:, offset : offset + ref.shape[0]] = ref[...].reshape(1, ref.shape[0])
             offset += ref.shape[0]
         pl.semaphore_wait(
-            barrier, num_utt - 1 + num_seq - 1 + num_blocks + num_seq - 2 * group.is_own
+            barrier,
+            num_utt - 1 + num_seq - 1 + num_seq - group.is_own + 2 * (G - move.is_own),
         )
 
         def conv_copy(b, slot):
@@ -1064,9 +1279,6 @@
         )
         masked = jnp.max(jnp.where(inside, 1.0, 0.0), -1, keepdims=True)
         mask_o[...] = masked
-        edge = jnp.zeros((TILE, width), BF16)
-        s.taps[0:TILE, :] = edge
-        s.taps[TILE + KPOS * GW :, :] = edge
 
         def conv_arrived(b):
             conv_copy(b, b).wait_recv()
@@ -1100,99 +1312,48 @@
         proj_out = proj_out + vector(first, column)
         embed = jnp.where(masked > 0.5, vector(first + column, column), proj_out)
         s.embed[...] = embed
-        embed_low = embed.astype(BF16)
-        for b in range(num_blocks):
-            s.blocks[b] = embed_low[:, b * width : (b + 1) * width]
-
-        def there(b, device):
-            return remote(
-                s.blocks.at[b],
-                pos_in.at[block_rows(me, frames)],
-                s.there_send.at[b],
-                s.there_recv.at[me],
-                device,
-            )
-
-        def there_from(f, device):
-            return remote(
-                s.blocks.at[0],
-                pos_in.at[block_rows(f, frames)],
-                s.there_send.at[0],
-                s.there_recv.at[f],
-                device,
-            )
-
-        group.each(num_blocks, group.by_block, lambda b, device: there(b, device).start())
-
-        def keep_there():
-            pos_in[block_rows(me, frames), :] = s.blocks[group.my_block]
-
-        group.when_own(keep_there)
+        pack_rows(embed, s.tiles, s.blocks)
+
+        there_arrived, there_sent = move.out(s.blocks, pos_in, (s.there_send, s.there_recv))
         taps_in.wait()
-        group.each(num_seq, group.by_shard, lambda f, device: there_from(f, device).wait_recv())
-        fill_frames(pos_in, s.wide, s.packed, length, groups)
+        own_taps(s.taps, lax.rem(move.z, 2) == 1)
+        there_arrived()
         qkv_quarters.pass_on()
         outw_quarters.start()
-        for h in range(groups):
-            for step in range(NUM_TILES // STEP_TILES):
-                start = step * STEP_TILES
-                columns = jnp.concatenate(
-                    [s.packed[h, start + j : start + j + rows, :] for j in range(STEP_TILES)],
-                    axis=1,
-                ).astype(BF16)
-                part = jnp.dot(
-                    columns,
-                    tap_tile(s.taps, start * TILE, STEP_TILES * TILE, h),
-                    preferred_element_type=F32,
-                )
-                if step == 0:
-                    s.acc[h] = part
-                else:
-                    s.acc[h] += part
+        pad_frames(pos_in, s.packed)
+        for step in range(NUM_TILES // STEP_TILES):
+            start = step * STEP_TILES
+            columns = jnp.concatenate(
+                [
+                    jnp.concatenate(
+                        [s.packed[u, start + j : start + j + rows, :] for u in range(here)], axis=0
+                    )
+                    for j in range(STEP_TILES)
+                ],
+                axis=1,
+            ).astype(BF16)
+            part = jnp.dot(
+                columns,
+                tap_tile(s.taps, start * TILE, STEP_TILES * TILE, 0),
+                preferred_element_type=F32,
+            )
+            if step == 0:
+                s.acc[...] = part
+            else:
+                s.acc[...] += part
         taps_bias_all = taps_bias_ref[...].reshape(1, column)
-        own_bias = taps_bias_all[:, 0:width]
-        for i in range(1, per_column):
-            own_bias = jnp.where(
-                block == i, taps_bias_all[:, i * width : (i + 1) * width], own_bias
-            )
-        unpack_frames(
-            lambda h, r: s.acc[h, :, r * GW : (r + 1) * GW]
-            + own_bias[:, h * GW : (h + 1) * GW],
-            s.wide.at[0:length],
-            rows,
-            groups,
-        )
-        s.pos_own[...] = s.wide[0:length, :].astype(BF16)
-
-        def back(f, device):
-            return remote(
-                s.pos_own.at[block_rows(f, frames)],
-                s.pos_back.at[group.my_block],
-                s.back_send.at[f],
-                s.back_recv.at[group.my_block],
-                device,
-            )
-
-        def back_from(b, device):
-            return remote(
-                s.pos_own.at[block_rows(0, frames)],
-                s.pos_back.at[b],
-                s.back_send.at[0],
-                s.back_recv.at[b],
-                device,
-            )
-
-        group.each(num_seq, group.by_shard, lambda f, device: back(f, device).start())
-
-        def keep_back():
-            s.pos_back[group.my_block] = s.pos_own[block_rows(me, frames), :]
-
-        group.when_own(keep_back)
-        group.each(num_blocks, group.by_block, lambda b, device: back_from(b, device).wait_recv())
+        own_bias = taps_bias_all[:, 0:GW]
+        for i in range(1, move.per_column):
+            own_bias = jnp.where(move.z == i, taps_bias_all[:, i * GW : (i + 1) * GW], own_bias)
+        own_bias = jnp.concatenate([own_bias] * PACK, axis=1)
+        for u in range(here):
+            s.pos_own[u] = (s.acc[u * rows : (u + 1) * rows, :] + own_bias).astype(BF16)
+        back_arrived, back_sent = move.home(s.pos_own, s.pos_back, (s.back_send, s.back_recv))
+        back_arrived()
         outw_quarters.pass_on()
-        for b in range(num_blocks):
-            lanes = slice(b * width, (b + 1) * width)
-            pos_pre[:, lanes] = s.pos_back[b]
+        unpack_rows(s.pos_back, s.tiles)
+        for p in range(D // 128):
+            pos_pre[:, p * 128 : (p + 1) * 128] = s.tiles[p].astype(BF16)
         act, _ = gelu_parts(pos_pre[...].astype(F32))
         resid = s.embed[...] + act
         resid_o[...] = resid
@@ -1212,7 +1373,8 @@
             )
 
         peers(lambda b: attn_copy(b, me_utt).start())
-
+        store("conv_all", "proj_all", "vec_all", "pre_o", "low_o", "mask_o", "steps_o")
+        store("pos_in", "pos_pre", "resid_o")
         qkv_quarters.pass_over()
         qkv_quarters.arrive()
         for part in range(3):
@@ -1255,11 +1417,13 @@
                     for part in range(3):
                         heads[part, block_rows(me, frames), :] = s.head_out[dest, part]
 
+        store("qkv_all", "attn_all")
         up_quarters.start()
         peers(lambda b: gout_copy(b, me_utt).start())
         outw_quarters.pass_over()
         seq_peers(lambda f: head_copy(f, f).wait_recv())
         up_quarters.pass_on()
+        store("heads")
 
         def flat_copy(f, slot):
             lanes = pl.ds(pl.multiple_of(slot // num_utt * width, width), width)
@@ -1322,6 +1486,8 @@
 
         up_quarters.pass_over()
 
+        for copy in stores.values():
+            copy.wait()
         group.each(num_blocks, group.by_block, lambda b, device: row_from(b, device).wait_recv())
         own_outw.wait()
         seq_peers(lambda f: flat_copy(f, f).wait_recv())
@@ -1349,8 +1515,8 @@
             flat_copy(f, me).wait_send()
 
         seq_peers(sent_seq)
-        group.each(num_blocks, group.by_block, lambda b, device: there(b, device).wait_send())
-        group.each(num_seq, group.by_shard, lambda f, device: back(f, device).wait_send())
+        there_sent()
+        back_sent()
         group.each(num_seq, group.by_shard, lambda f, device: row_copy(f, device).wait_send())
 
     vmem, anywhere = pl.BlockSpec(memory_space=pltpu.VMEM), pl.BlockSpec(memory_space=pl.ANY)
@@ -1363,7 +1529,7 @@
         out_shape=[
             shape(num_utt * column, C),
             shape(num_utt * proj_rows, D),
-            shape(num_utt, 1, sum(vector.shape[0] for vector in vectors), dtype=F32),
+            shape(num_utt, 1, vec_size, dtype=F32),
             shape(num_utt * column, 3 * column),
             shape(num_utt * column, hidden),
             shape(rows_all, D),
@@ -1371,7 +1537,7 @@
             shape(frames, C),
             shape(frames, 1, dtype=F32),
             shape(frames, 2 * C),
-            shape(length, width),
+            shape(here, rows, TILE),
             shape(frames, D),
             shape(frames, D, dtype=F32),
             shape(rows_all, D),
@@ -1383,7 +1549,7 @@
             shape(num_utt * column, D),
         ],
         in_specs=[vmem] * (len(vectors) + 4) + [anywhere] * 4 + [vmem] * 3 + [anywhere],
-        out_specs=[vmem] * 4 + [anywhere] * 2 + [vmem] * 13 + [anywhere],
+        out_specs=[anywhere] * 15 + [vmem] * 4 + [anywhere],
         scratch_shapes=scratch.shapes + [sem for sems in quarter_sems for sem in sems],
         compiler_params=pltpu.CompilerParams(
             collective_id=collective_id, has_side_effects=True, vmem_limit_bytes=VMEM_BYTES
@@ -1449,7 +1615,6 @@
     rows = length // PACK
     low = C // num_utt
     proj_rows = C // num_utt
-    proj_half = proj_rows // 2
     vec_rows = 64
     vec_half = vec_rows // 2
     final_lag = HOP_LAG * (chips - 1)
@@ -1461,11 +1626,15 @@
     lane_blocks[QKV] = 3 * column // CHUNK_LANES
     row_blocks = {DOWN: hidden // column, UP: D // column, OUT: 1, QKV: D // column}
     counts = [row_blocks[n] * lane_blocks[n] for n in range(4)]
-    tap_chunks = KPOS * GW // 2 // CHUNK_ROWS
-    counts += [tap_chunks, C // CHUNK_LANES, D // CHUNK_LANES, 1]
+    tap_half = KPOS * GW // PACK // 2 // CHUNK_ROWS
+    tap_chunks = chips * tap_half
+    assert chips == 4
+    here = num_utt // 2
+    counts += [tap_chunks, C // CHUNK_LANES, D // 2 // CHUNK_LANES, 1]
     starts = [sum(counts[:n]) for n in range(8)]
     total = sum(counts)
-    chunk_rows = [CHUNK_ROWS] * 6 + [proj_half, vec_half]
+    chunk_rows = [CHUNK_ROWS] * 7 + [vec_half]
+    assert proj_rows == CHUNK_ROWS
     chunk_lanes = [CHUNK_LANES] * 7 + [128]
     assert counts[CONV] + counts[PROJ] + counts[VEC] <= RING
 
@@ -1473,7 +1642,7 @@
     chunk = (RING, CHUNK_ROWS, CHUNK_LANES)
     group_shapes = [
         (num_utt, half, C),
-        (num_utt, proj_half, D),
+        (num_utt, proj_rows, D // 2),
         (num_utt, vec_half, 128),
     ]
     utt_rows = (num_utt, frames, D)
@@ -1484,6 +1653,21 @@
         got_qkv=pltpu.VMEM(utt_rows, BF16),
         got_layer=pltpu.VMEM(utt_rows, BF16),
         mine=pltpu.VMEM((frames, D), F32),
+        in_flat=pltpu.VMEM(flat.shape, flat.dtype),
+        in_attn_in=pltpu.VMEM(attn_in.shape, attn_in.dtype),
+        in_qkv=pltpu.VMEM(qkv_all.shape, qkv_all.dtype),
+        in_heads=pltpu.VMEM(heads.shape, heads.dtype),
+        in_attn=pltpu.VMEM(attn_f32.shape, attn_f32.dtype),
+        in_lse=pltpu.VMEM(lse.shape, lse.dtype),
+        in_pos_pre=pltpu.VMEM(pos_pre.shape, pos_pre.dtype),
+        in_pos_in=pltpu.VMEM(pos_in.shape, pos_in.dtype),
+        in_mask=pltpu.VMEM(masked.shape, masked.dtype),
+        in_steps=pltpu.VMEM(steps.shape, steps.dtype),
+        in_pre=pltpu.VMEM(conv_pre.shape, conv_pre.dtype),
+        in_low=pltpu.VMEM(feat_low.shape, feat_low.dtype),
+        in_conv=pltpu.VMEM(conv_all.shape, conv_all.dtype),
+        in_proj=pltpu.VMEM(proj_all.shape, proj_all.dtype),
+        load=dma((14,)),
         up_bias=pltpu.VMEM((1, hidden), F32),
         ffn_all=pltpu.VMEM((rows_all, D), BF16),
         agrad_all=pltpu.VMEM((rows_all, D), BF16),
@@ -1496,16 +1680,17 @@
         dk_acc=pltpu.VMEM((length, width), F32),
         dv_acc=pltpu.VMEM((length, width), F32),
         qback=pltpu.VMEM((3, rows_all, column), BF16),
-        blocks=pltpu.VMEM((num_blocks, frames, width), BF16),
-        pos_grad=pltpu.VMEM((length, width), BF16),
-        pos_own=pltpu.VMEM((length, width), BF16),
-        pos_back=pltpu.VMEM((num_blocks, frames, width), BF16),
+        blocks=pltpu.VMEM((G, frames // PACK, TILE), BF16),
+        pos_grad=pltpu.VMEM((here, rows, TILE), BF16),
+        pos_own=pltpu.VMEM((here, rows, TILE), BF16),
+        pos_back=pltpu.VMEM((G, frames // PACK, TILE), BF16),
+        tiles=pltpu.VMEM((D // 128, frames, 128), F32),
         vec_f32=pltpu.VMEM((num_utt, vec_rows, 128), F32),
         part_down=pltpu.VMEM((hidden, D), BF16),
         part_up=pltpu.VMEM((D, hidden), BF16),
         part_outw=pltpu.VMEM((column, D), BF16),
         part_qkv=pltpu.VMEM((D, 3 * column), BF16),
-        part_taps=pltpu.VMEM((KPOS * GW, width), BF16),
+        part_taps=pltpu.VMEM((KPOS * GW // PACK, TILE), BF16),
         part_conv=pltpu.VMEM((2 * C, C), BF16),
         part_proj=pltpu.VMEM((C, D), BF16),
         part_vec=pltpu.VMEM((num_utt, vec_rows, 128), BF16),
@@ -1513,7 +1698,7 @@
         mate_up=pltpu.VMEM((D // 2, hidden), BF16),
         mate_outw=pltpu.VMEM((half, D), BF16),
         mate_qkv=pltpu.VMEM((D // 2, 3 * column), BF16),
-        mate_taps=pltpu.VMEM((KPOS * GW // 2, width), BF16),
+        mate_taps=pltpu.VMEM((KPOS * GW // PACK // 2, TILE), BF16),
         mate_conv=pltpu.VMEM(group_shapes[0], BF16),
         mate_proj=pltpu.VMEM(group_shapes[1], BF16),
         mate_vec=pltpu.VMEM(group_shapes[2], BF16),
@@ -1546,12 +1731,12 @@
         dq_recv=dma((num_seq,)),
         dkv_send=dma((num_seq,)),
         dkv_recv=dma((num_seq,)),
-        there_send=dma((num_blocks,)),
-        there_recv=dma((num_seq,)),
-        home_send=dma((num_seq,)),
-        home_recv=dma((num_blocks,)),
-        mate_send=dma((5, tap_chunks)),
-        mate_recv=dma((5, tap_chunks)),
+        there_send=dma((G,)),
+        there_recv=dma((num_seq * here,)),
+        home_send=dma((num_seq * here,)),
+        home_recv=dma((G,)),
+        mate_send=dma((5, tap_half)),
+        mate_recv=dma((5, tap_half)),
         gmate_send=dma((3, num_utt)),
         gmate_recv=dma((3, num_utt)),
         peer_send=dma((3, num_utt)),
@@ -1573,25 +1758,25 @@
     late_parts = (3, 1)
 
     def kernel(
-        flat_ref,
+        flat_hbm,
         rows_ref,
         outw_ref,
         resid_ref,
         vec_ref,
         up_bias_ref,
-        attn_in_ref,
-        qkv_ref,
-        heads_ref,
-        attn_ref,
-        lse_ref,
-        pos_pre_ref,
-        pos_in_ref,
-        mask_ref,
-        steps_ref,
-        pre_ref,
-        low_ref,
-        conv_ref,
-        proj_ref,
+        attn_in_hbm,
+        qkv_hbm,
+        heads_hbm,
+        attn_hbm,
+        lse_hbm,
+        pos_pre_hbm,
+        pos_in_hbm,
+        mask_hbm,
+        steps_hbm,
+        pre_hbm,
+        low_hbm,
+        conv_hbm,
+        proj_hbm,
         up_hbm,
         down_hbm,
         gout_hbm,
@@ -1626,6 +1811,45 @@
         def seq_peers(body):
             loop(1, num_seq, lambda i: body(lax.rem(me + i, num_seq)))
 
+        late_inputs = {
+            "flat": (flat_hbm, s.in_flat),
+            "attn_in": (attn_in_hbm, s.in_attn_in),
+            "qkv": (qkv_hbm, s.in_qkv),
+            "heads": (heads_hbm, s.in_heads),
+            "attn": (attn_hbm, s.in_attn),
+            "lse": (lse_hbm, s.in_lse),
+            "pos_pre": (pos_pre_hbm, s.in_pos_pre),
+            "pos_in": (pos_in_hbm, s.in_pos_in),
+            "mask": (mask_hbm, s.in_mask),
+            "steps": (steps_hbm, s.in_steps),
+            "pre": (pre_hbm, s.in_pre),
+            "low": (low_hbm, s.in_low),
+            "conv": (conv_hbm, s.in_conv),
+            "proj": (proj_hbm, s.in_proj),
+        }
+        late_loads = {
+            name: pltpu.make_async_copy(source, target, s.load.at[i])
+            for i, (name, (source, target)) in enumerate(late_inputs.items())
+        }
+
+        def ready(*names):
+            for name in names:
+                late_loads[name].wait()
+
+        flat_ref = s.in_flat
+        attn_in_ref = s.in_attn_in
+        qkv_ref = s.in_qkv
+        heads_ref = s.in_heads
+        attn_ref = s.in_attn
+        lse_ref = s.in_lse
+        pos_pre_ref = s.in_pos_pre
+        pos_in_ref = s.in_pos_in
+        mask_ref = s.in_mask
+        steps_ref = s.in_steps
+        pre_ref = s.in_pre
+        low_ref = s.in_low
+        conv_ref = s.in_conv
+        proj_ref = s.in_proj
         barrier = pltpu.get_barrier_semaphore()
 
         def signal(device):
@@ -1633,14 +1857,14 @@
 
         peers(lambda b: signal({"utt": b}))
         seq_peers(lambda f: signal({"seq": f}))
-        group.each(num_seq, group.by_shard, lambda i, device: signal(device))
-        group.each(num_blocks, group.by_block, lambda i, device: signal(device))
+        move = GroupMove()
+        move.greet(signal)
         s.vec_f32[...] = jnp.zeros_like(s.vec_f32)
         s.up_bias[...] = up_bias_ref[...].reshape(1, hidden)
 
         def entered():
             pl.semaphore_wait(
-                barrier, num_utt - 1 + num_seq - 1 + num_blocks + num_seq - 2 * group.is_own
+                barrier, num_utt - 1 + num_seq - 1 + 2 * (G - move.is_own)
             )
 
         def vector(first, size):
@@ -1674,11 +1898,9 @@
         parts = (s.part_down, s.part_up, s.part_outw, s.part_qkv, s.part_taps)
         part_mates = (s.mate_down, s.mate_up, s.mate_outw, s.mate_qkv, s.mate_taps)
         finals = (down_o, up_mid, outw_o, qkv_mid, taps_o, conv_o, proj_o, vec_o)
-        grouped = (s.part_conv, s.part_proj, s.part_vec)
         mates = (s.mate_conv, s.mate_proj, s.mate_vec)
         stages = (s.stage_conv, s.stage_proj, s.stage_vec)
         gots = (s.got_conv, s.got_proj, s.got_vec)
-        sizes = (half, proj_half, vec_half)
         got_refs, put_refs = (s.got_r, s.got_l), (s.put_r, s.put_l)
         way_send, way_recv = (s.right_send, s.left_send), (s.right_recv, s.left_recv)
         ends = (chips - 1, 0)
@@ -1687,12 +1909,7 @@
 
         def mate_copy(n, k):
             if n == TAPS:
-                source = half_rows(0, tap_chunks * CHUNK_ROWS, 1 - core)
-                place = pl.ds(
-                    pl.multiple_of(((1 - core) * tap_chunks + k) * CHUNK_ROWS, CHUNK_ROWS),
-                    CHUNK_ROWS,
-                )
-                source = place
+                source = block_rows((1 - core) * tap_half + k, CHUNK_ROWS)
             else:
                 source = half_rows(k * column, half, 1 - core)
             return remote(
@@ -1703,7 +1920,12 @@
                 sibling,
             )
 
-        mate_counts = [row_blocks[n] for n in range(4)] + [tap_chunks]
+        mate_counts = [row_blocks[n] for n in range(4)] + [tap_half]
+        assert max(mate_counts) <= tap_half
+
+        def tap_group(k):
+            turn = lax.rem(k, chips)
+            return jnp.where(turn == 0, 0, jnp.where(turn == 1, 3, turn - 1)), k // chips
 
         def announce(n):
             steps_ready[0] = starts[n] + counts[n]
@@ -1712,7 +1934,9 @@
         def group_place(n, b, which):
             if n == 2:
                 return s.part_vec.at[b, half_rows(0, vec_half, which)]
-            return grouped[n].at[half_rows(b * 2 * sizes[n], sizes[n], which)]
+            if n == 1:
+                return s.part_proj.at[block_rows(b, proj_rows), block_rows(which, D // 2)]
+            return s.part_conv.at[half_rows(b * column, half, which)]
 
         def group_mate(n, b):
             return remote(
@@ -1763,15 +1987,19 @@
                     F32
                 ) + part_mates[n][block_rows(b, CHUNK_ROWS), lanes].astype(F32)
             elif n == TAPS:
-                mate_copy(n, k).wait_recv()
-                place = pl.ds(
-                    pl.multiple_of((core * tap_chunks + k) * CHUNK_ROWS, CHUNK_ROWS), CHUNK_ROWS
-                )
-                value = s.part_taps[place, :].astype(F32) + s.mate_taps[
-                    block_rows(k, CHUNK_ROWS), :
-                ].astype(F32)
-                for i in range(per_column):
-                    s.own[slot, :, i * width : (i + 1) * width] = jnp.where(block == i, value, 0.0)
+                tap, piece = tap_group(k)
+
+                @pl.when(tap == z)
+                def _():
+                    mate_copy(n, piece).wait_recv()
+                    s.own[slot] = s.part_taps[
+                        block_rows(core * tap_half + piece, CHUNK_ROWS), :
+                    ].astype(F32) + s.mate_taps[block_rows(piece, CHUNK_ROWS), :].astype(F32)
+
+                @pl.when(tap != z)
+                def _():
+                    s.own[slot] = jnp.zeros((CHUNK_ROWS, CHUNK_LANES), F32)
+
             else:
                 g = n - CONV
 
@@ -1795,8 +2023,10 @@
                 b, j = k // lane_blocks[n], lax.rem(k, lane_blocks[n])
                 return finals[n].at[half_rows(b * column, half, which), lanes_of(j, CHUNK_LANES)]
             if n == TAPS:
-                first = (which * tap_chunks + k) * CHUNK_ROWS
-                return finals[n].at[pl.ds(pl.multiple_of(first, CHUNK_ROWS), CHUNK_ROWS)]
+                tap, piece = tap_group(k)
+                return finals[n].at[tap, block_rows(which * tap_half + piece, CHUNK_ROWS)]
+            if n == PROJ:
+                return proj_o.at[:, lanes_of(which * (D // 2 // CHUNK_LANES) + k, CHUNK_LANES)]
             return finals[n].at[
                 half_rows(0, chunk_rows[n], which), lanes_of(k, chunk_lanes[n])
             ]
@@ -1835,6 +2065,20 @@
                 hops[way],
             )
 
+        def flows(way, index):
+            k = index - starts[TAPS]
+            is_tap = jnp.logical_and(k >= 0, k < tap_chunks)
+            tap, _ = tap_group(jnp.maximum(k, 0))
+            if way == 0:
+                sends, receives = tap <= z, tap <= z - 1
+            else:
+                sends, receives = tap >= z, tap >= z + 1
+            other = jnp.logical_not(is_tap)
+            return (
+                jnp.logical_and(z != ends[way], jnp.logical_or(other, sends)),
+                jnp.logical_and(z != ends[1 - way], jnp.logical_or(other, receives)),
+            )
+
         def sums(begin, end, shift=None):
             def near(n, low_step, high_step):
                 return starts[n] < high_step and starts[n] + counts[n] > low_step
@@ -1854,28 +2098,33 @@
                     def _(way=way, index=index):
                         slot = lax.rem(index, RING)
 
-                        @pl.when(z != ends[way])
+                        sends, receives = flows(way, index)
+
+                        @pl.when(index >= RING)
                         def _():
-                            @pl.when(index >= RING)
+                            @pl.when(flows(way, index - RING)[0])
                             def _():
                                 chain_copy(way, index - RING).wait_send()
 
-                        @pl.when(z != ends[1 - way])
+                        @pl.when(receives)
                         def _():
                             chain_copy(way, index).wait_recv()
 
-                            @pl.when(z != ends[way])
+                            @pl.when(sends)
                             def _():
                                 put_refs[way][slot] = (
                                     s.own[slot] + got_refs[way][slot].astype(F32)
                                 ).astype(BF16)
 
-                        @pl.when(z == ends[1 - way])
+                        @pl.when(jnp.logical_not(receives))
                         def _():
-                            put_refs[way][slot] = s.own[slot].astype(BF16)
                             got_refs[way][slot] = jnp.zeros((CHUNK_ROWS, CHUNK_LANES), BF16)
 
-                        @pl.when(z != ends[way])
+                            @pl.when(sends)
+                            def _():
+                                put_refs[way][slot] = s.own[slot].astype(BF16)
+
+                        @pl.when(sends)
                         def _():
                             chain_copy(way, index).start()
 
@@ -1999,6 +2248,8 @@
                 )
             ]
             for copy in loads:
+                copy.start()
+            for copy in late_loads.values():
                 copy.start()
             entered()
 
@@ -2135,6 +2386,7 @@
 
         loop(0, num_utt, ghead_block)
         peers(lambda b: layer_copy(b, me_utt).start())
+        ready("flat")
         s.part_outw[...] = inner_dot(flat_ref[...], s.agrad_all[...]).astype(BF16)
         announce(OUT)
         seq_peers(lambda f: ghead_copy(f, f).wait_recv())
@@ -2164,6 +2416,7 @@
             )
 
         my_lanes = pl.ds(pl.multiple_of(block * width, width), width)
+        ready("heads", "attn", "lse")
         s.dk_acc[...] = jnp.zeros_like(s.dk_acc)
         s.dv_acc[...] = jnp.zeros_like(s.dv_acc)
         q_blocks = length // Q_BLOCK
@@ -2211,7 +2464,9 @@
             value = jnp.concatenate([s.qback[part, own_rows(b), :] for part in range(3)], axis=1)
             hand_out(b, nt_dot(value, qkv_ref[...]), qpart_copy)
 
+        ready("qkv")
         loop(1, num_utt + 1, qkv_block)
+        ready("attn_in")
 
         qkv_steps = beside_loop(D // column, PACE["qkv"])
 
@@ -2235,58 +2490,19 @@
         normed, scale = norm_parts(resid_ref[...])
         resid1_grad = s.resid2_grad[...] + norm_back(back * attn_gain, normed, scale)
         s.resid1_grad[...] = resid1_grad
+        ready("pos_pre")
         _, slope = gelu_parts(pos_pre_ref[...].astype(F32))
         pos_low = (resid1_grad * slope).astype(BF16)
-        for b in range(num_blocks):
-            s.blocks[b] = pos_low[:, b * width : (b + 1) * width]
-
-        def there(b, device):
-            return remote(
-                s.blocks.at[b],
-                s.pos_grad.at[own_rows(me)],
-                s.there_send.at[b],
-                s.there_recv.at[me],
-                device,
-            )
-
-        def there_from(f, device):
-            return remote(
-                s.blocks.at[0],
-                s.pos_grad.at[own_rows(f)],
-                s.there_send.at[0],
-                s.there_recv.at[f],
-                device,
-            )
-
-        def home(f, device):
-            return remote(
-                s.pos_own.at[own_rows(f)],
-                s.pos_back.at[group.my_block],
-                s.home_send.at[f],
-                s.home_recv.at[group.my_block],
-                device,
-            )
-
-        def home_from(b, device):
-            return remote(
-                s.pos_own.at[own_rows(0)],
-                s.pos_back.at[b],
-                s.home_send.at[0],
-                s.home_recv.at[b],
-                device,
-            )
-
-        group.each(num_blocks, group.by_block, lambda b, device: there(b, device).start())
-
-        def keep_there():
-            s.pos_grad[own_rows(me), :] = s.blocks[group.my_block]
-
-        group.when_own(keep_there)
+        pack_rows(pos_low.astype(F32), s.tiles, s.blocks)
+
+        there_arrived, there_sent = move.out(s.blocks, s.pos_grad, (s.there_send, s.there_recv))
         put_vector(10, column_sum(back * normed))
         put_vector(12, column_sum(back))
         put_vector(8, column_sum(pos_low.astype(F32)))
 
-        def position(wide, packed, grads, taps_ref, acc, total_ref, sem):
+        home_waits = []
+
+        def position(packed, grads, taps_ref, acc, total_ref, sem):
             middle = HALF // PACK
             taps_in = pltpu.make_async_copy(
                 taps_hbm.at[:, pl.ds(pl.multiple_of(block * width, width), width)],
@@ -2294,104 +2510,103 @@
                 sem,
             )
             taps_in.start()
-            edge = jnp.zeros((TILE, width), BF16)
-            taps_ref[0:TILE, :] = edge
-            taps_ref[TILE + KPOS * GW :, :] = edge
-            fill_frames(pos_in_ref, wide, packed, length, groups)
+            ready("pos_in")
+            pad_frames(pos_in_ref, packed)
             total_ref[...] = jnp.zeros_like(total_ref)
             beside(PACE["there"])
             taps_in.wait()
-            group.each(num_seq, group.by_shard, lambda f, device: there_from(f, device).wait_recv())
-            fill_frames(s.pos_grad, wide, grads, length, groups)
+            own_taps(taps_ref, lax.rem(z, 2) == 1)
+            there_arrived()
+            pad_frames(s.pos_grad, grads)
+
             def weight_tile(tile, frames_of):
-                pieces = [
-                    inner_dot(
-                        frames_of(h).astype(BF16),
-                        grads[h, middle : middle + rows, :].astype(BF16),
-                    )
-                    for h in range(groups)
-                ]
+                piece = inner_dot(
+                    jnp.concatenate([frames_of(u) for u in range(here)], axis=0).astype(BF16),
+                    jnp.concatenate([s.pos_grad[u] for u in range(here)], axis=0),
+                )
                 for r in range(PACK):
                     where = pl.ds(pl.multiple_of(TILE + tile * TILE - r * GW, GW), TILE)
-                    total_ref[where, :] += jnp.concatenate(
-                        [piece[:, r * GW : (r + 1) * GW] for piece in pieces], axis=1
-                    )
+                    total_ref[where, :] += piece[:, r * GW : (r + 1) * GW]
 
             weight_steps = beside_loop(NUM_TILES // 8, PACE["weight"])
 
             def eight_weights(i):
                 base = pl.multiple_of(8 * i, 8)
-                windows = [packed[h, pl.ds(base, rows + 8), :] for h in range(groups)]
+                windows = [packed[u, pl.ds(base, rows + 8), :] for u in range(here)]
                 for j in range(8):
-                    weight_tile(8 * i + j, lambda h, j=j: windows[h][j : j + rows])
+                    weight_tile(8 * i + j, lambda u, j=j: windows[u][j : j + rows])
                 weight_steps(i)
 
             loop(0, NUM_TILES // 8, eight_weights)
-            weight_tile(NUM_TILES - 1, lambda h: packed[h, NUM_TILES - 1 :, :])
-            s.part_taps[...] = total_ref[TILE : TILE + KPOS * GW, :].astype(BF16)
+            weight_tile(NUM_TILES - 1, lambda u: packed[u, NUM_TILES - 1 :, :])
+            share = KPOS * GW // PACK
+            for q in range(PACK):
+                for m in range(share // TILE):
+                    first_row = TILE + q * share + m * TILE
+                    s.part_taps[m * TILE : (m + 1) * TILE, q * GW : (q + 1) * GW] = total_ref[
+                        first_row : first_row + TILE, :
+                    ].astype(BF16)
             announce(TAPS)
             beside(PACE["taps"])
             acc[...] = jnp.zeros_like(acc)
 
-            def input_tiles(first, windows, count):
-                for h in range(groups):
-                    for start in range(0, count, 4):
-                        tiles = range(start, min(start + 4, count))
-                        acc[h] += nt_dot(
-                            jnp.concatenate([windows[h](j) for j in tiles], axis=1),
-                            jnp.concatenate(
-                                [tap_tile(taps_ref, (first + j) * TILE, TILE, h) for j in tiles],
-                                axis=1,
-                            ),
-                        )
+            def input_tiles(first, frames_of, count):
+                for start in range(0, count, 4):
+                    tiles = range(start, min(start + 4, count))
+                    acc[...] += nt_dot(
+                        jnp.concatenate([frames_of(j) for j in tiles], axis=1),
+                        jnp.concatenate(
+                            [tap_tile(taps_ref, (first + j) * TILE, TILE, 0) for j in tiles],
+                            axis=1,
+                        ),
+                    )
 
             input_steps = beside_loop(NUM_TILES // 8, PACE["input"])
 
             def eight_inputs(i):
                 base = pl.multiple_of(2 * middle - 8 - 8 * i, 8)
-                windows = []
-                for h in range(groups):
-                    window = grads[h, pl.ds(base, rows + 8), :]
-                    windows.append(lambda j, w=window: w[8 - j : 8 - j + rows].astype(BF16))
-                input_tiles(8 * i, windows, 8)
+                windows = [grads[u, pl.ds(base, rows + 8), :] for u in range(here)]
+                input_tiles(
+                    8 * i,
+                    lambda j: jnp.concatenate(
+                        [window[8 - j : 8 - j + rows] for window in windows], axis=0
+                    ).astype(BF16),
+                    8,
+                )
                 input_steps(i)
 
             loop(0, NUM_TILES // 8, eight_inputs)
             assert NUM_TILES % 8 == 1 and NUM_TILES == 2 * middle + 1
             input_tiles(
                 NUM_TILES - 1,
-                [lambda j, h=h: grads[h, 0:rows, :].astype(BF16) for h in range(groups)],
+                lambda j: jnp.concatenate(
+                    [grads[u, 0:rows, :] for u in range(here)], axis=0
+                ).astype(BF16),
                 1,
             )
-            unpack_frames(
-                lambda h, r: acc[h, :, r * GW : (r + 1) * GW], wide.at[0:length], rows, groups
-            )
-            s.pos_own[...] = wide[0:length, :].astype(BF16)
-            group.each(num_seq, group.by_shard, lambda f, device: home(f, device).start())
-
-            def keep_home():
-                s.pos_back[group.my_block] = s.pos_own[own_rows(me), :]
-
-            group.when_own(keep_home)
-
-        packed_rows = (groups, (length + KPOS) // PACK, TILE)
+            for u in range(here):
+                s.pos_own[u] = acc[u * rows : (u + 1) * rows, :].astype(BF16)
+            home_waits.extend(move.home(s.pos_own, s.pos_back, (s.home_send, s.home_recv)))
+
+        packed_rows = (here, (length + KPOS) // PACK, TILE)
         pl.run_scoped(
             position,
-            vmem((length + KPOS, width), F32),
             vmem(packed_rows, F32),
             vmem(packed_rows, F32),
             vmem((KPOS * GW + 2 * TILE, width), BF16),
-            vmem((groups, rows, TILE), F32),
-            vmem((KPOS * GW + 2 * TILE, width), F32),
+            vmem((here * rows, TILE), F32),
+            vmem((KPOS * GW + 2 * TILE, GW), F32),
             dma,
         )
+        home_arrived, home_sent = home_waits
         beside(PACE["home"])
 
-        group.each(num_blocks, group.by_block, lambda b, device: home_from(b, device).wait_recv())
-        for b in range(num_blocks):
-            lanes = slice(b * width, (b + 1) * width)
-            s.resid1_grad[:, lanes] += s.pos_back[b].astype(F32)
+        home_arrived()
+        unpack_rows(s.pos_back, s.tiles)
+        for p in range(D // 128):
+            s.resid1_grad[:, p * 128 : (p + 1) * 128] += s.tiles[p]
         embed_grad = s.resid1_grad[...]
+        ready("mask", "low", "proj", "pre", "steps", "conv")
         hidden_frame = mask_ref[...] > 0.5
         put_vector(6, column_sum(jnp.where(hidden_frame, embed_grad, 0.0)))
         proj_grad = jnp.where(hidden_frame, 0.0, embed_grad).astype(BF16)
@@ -2507,9 +2722,12 @@
             loop(0, counts[n], handed)
         for way in range(2):
 
-            @pl.when(z != ends[way])
-            def _(way=way):
-                loop(total - RING, total, lambda index: chain_copy(way, index).wait_send())
+            def left_way(index, way=way):
+                @pl.when(flows(way, index)[0])
+                def _():
+                    chain_copy(way, index).wait_send()
+
+            loop(total - RING, total, left_way)
 
         for n in range(5):
             loop(0, mate_counts[n], lambda k, n=n: mate_copy(n, k).wait_send())
@@ -2540,8 +2758,8 @@
             dkv_copy(f, me).wait_send()
 
         seq_peers(sent_seq)
-        group.each(num_blocks, group.by_block, lambda b, device: there(b, device).wait_send())
-        group.each(num_seq, group.by_shard, lambda f, device: home(f, device).wait_send())
+        there_sent()
+        home_sent()
 
     vmem, anywhere = pl.BlockSpec(memory_space=pltpu.VMEM), pl.BlockSpec(memory_space=pl.ANY)
     shapes = [
@@ -2551,7 +2769,7 @@
         (D, hidden),
         (column, D),
         (D, 3 * column),
-        (KPOS * GW, column),
+        (chips, KPOS * GW // PACK, TILE),
         (column, C),
         (proj_rows, D),
         (vec_rows, 128),
@@ -2561,7 +2779,7 @@
     return pl.pallas_call(
         kernel,
         out_shape=[jax.ShapeDtypeStruct(shape, BF16) for shape in shapes],
-        in_specs=[vmem] * 19 + [anywhere] * 4,
+        in_specs=[anywhere] + [vmem] * 5 + [anywhere] * 17,
         out_specs=[vmem] * 2 + [anywhere] * 10,
         scratch_shapes=scratch.shapes,
         compiler_params=pltpu.CompilerParams(
@@ -2618,14 +2836,25 @@
 WIDEN_STEPS = 4
 
 
-def widen(arrays):
+def widen(taps, arrays):
+    arrays = (taps, *arrays)
+
     def kernel(*refs):
-        for source, target in zip(refs[: len(arrays)], refs[len(arrays) :], strict=True):
+        sources, targets = refs[: len(arrays)], refs[len(arrays) :]
+        for q in range(PACK):
+            lanes = slice(q * GW, (q + 1) * GW)
+            targets[0][q] = jnp.concatenate(
+                [sources[0][g, :, lanes].astype(F32) for g in range(taps.shape[0])], axis=1
+            )
+        for source, target in zip(sources[1:], targets[1:], strict=True):
             target[...] = source[...].astype(F32)
 
+    assert taps.shape[0] == PACK
     specs = [
+        pl.BlockSpec((PACK, taps.shape[1] // WIDEN_STEPS, taps.shape[2]), lambda i: (0, i, 0))
+    ] + [
         pl.BlockSpec((array.shape[0] // WIDEN_STEPS, array.shape[1]), lambda i: (i, 0))
-        for array in arrays
+        for array in arrays[1:]
     ]
     return pl.pallas_call(
         kernel,
@@ -2899,7 +3128,7 @@
         layer_out = layer_out.reshape(1, frames, D)
         feat_grad = feat_grad.reshape(1, 2 * frames, C)
         *wide_sums, downweight_sum = widen(
-            (taps_sum, outweight_sum, qkv_sum, conv_sum, proj_sum, up_sum, downweight_sum)
+            taps_sum, (outweight_sum, qkv_sum, conv_sum, proj_sum, up_sum, downweight_sum)
         )
         grads = (*wide_sums[:5], vector_sum, wide_sums[5])
         small, wide = (C // num_utt,), (column,)

time: 336 us -> 317 us (0.943)
  Pallas kernels: 332 us -> 311 us
    pallas_call x1, Pallas kernels: 223 us -> 204 us  [back_forth(): pl.pallas_call(kernel, out_shape=[jax.ShapeDtypeStruct(shape, BF16) for s...]
where the time goes in v6:
time: 317 us; the launch traced here: 315 us
  Pallas kernels  311 us (98%)
    pallas_call x1, Pallas kernels, back_forth(): pl.pallas_call(kernel, out_shape=[jax.ShapeDtypeStruct(shape, BF16) for s...  204 us
    pallas_call x1, Pallas kernels, front_forward(): pl.pallas_call(kernel, out_shape=[shape(num_utt * column, C), shape(num_u...  95.1 us
    pallas_call x1, Pallas kernels, widen(): pl.pallas_call(kernel, grid=(WIDEN_STEPS,), out_shape=[jax.ShapeDtypeStru...  12 us

profile of v6, /device:TPU:0, one launch (start us, length us, event | category | flops | bytes accessed | tf_op | source)
XLA Modules:
  0.0 315.3 jit_solution(4848455884115395032)
XLA Ops:
  0.7 95.1 %shard_map.441 = (bf16[1024,512]{1,0:T(8,128)(2,1)}, bf16[512,1024]{1,0:T(8,128)(2,1)}, f32[4,1,2560]{2,1,0:T(1,128)}, bf16[1024,768]{1,0:T(8,128)(2,1)}, bf16[1...) custom-call(f32[128]{0:T(128)} %refs_0_.1, ...), custom_call_target="tpu_custom_call" | custom-call | tf_op jit(solution)/shard_map/pallas_call | solution.py:1527
  95.7 204.3 %shard_map.442 = (bf16[128,1024]{1,0:T(8,128)(2,1)}, bf16[256,512]{1,0:T(8,128)(2,1)}, bf16[1024,1024]{1,0:T(8,128)(2,1)}, bf16[1024,1024]{1,0:T(8,128)(2,1)}, b...) custom-call(bf16[512,256]{1,0:T(8,128)(2,1)} %get-tuple-element.62.f, ...), custom_call_target="tpu_custom_call" | custom-call | tf_op jit(solution)/shard_map/pallas_call | solution.py:2779
  300.1 0.0 copy-start.2
  300.1 0.0 copy-start.1
  300.1 0.0 copy-start
  300.1 12.0 %shard_map.443 = (f32[4,2048,256]{2,1,0:T(8,128)}, f32[256,1024]{1,0:T(8,128)}, f32[256,3072]{1,0:T(8,128)}, f32[256,512]{1,0:T(8,128)}, f32[128,1024]{1,0:T(8,1...) custom-call(bf16[4,2048,256]{2,1,0:T(8,128)(2,1)} %get-tuple-element.84.refs_0_, ...), custom_call_target="tpu_custom_call" | custom-call | tf_op jit(solution)/shard_map/pallas_call | solution.py:2859
  312.1 0.0 copy-done.2
  312.1 0.6 slice_bitcast_fusion.1
  312.7 0.6 slice_bitcast_fusion
  313.3 0.5 slice_bitcast_fusion.12
  313.9 0.0 copy-done.1
  313.9 0.7 copy.53
  314.6 0.0 copy-done
  314.6 0.7 copy.54
  (1 shorter events, 0.0 us)
Async XLA Ops:
  300.1 12.0 %copy-start.2 = (bf16[64,128]{1,0:T(8,128)(2,1)S(1)}, bf16[64,128]{1,0:T(8,128)(2,1)}, u32[]{:S(2)}) copy-start(bf16[64,128]{1,0:T(8,128)(2,1)} %get-tuple-element.92) | copy-start | bytes 49156
  300.1 13.8 %copy-start.1 = (bf16[128,1024]{1,0:T(8,128)(2,1)S(1)}, bf16[128,1024]{1,0:T(8,128)(2,1)}, u32[]{:S(2)}) copy-start(bf16[128,1024]{1,0:T(8,128)(2,1)} %get-tuple-element.82) | copy-start | bytes 786436
  300.1 14.5 %copy-start = (bf16[256,512]{1,0:T(8,128)(2,1)S(1)}, bf16[256,512]{1,0:T(8,128)(2,1)}, u32[]{:S(2)}) copy-start(bf16[256,512]{1,0:T(8,128)(2,1)} %get-tuple-element.83) | copy-start | bytes 786436

commit v7 on v6

--- a/solution.py
+++ b/solution.py
@@ -1054,6 +1054,8 @@
         attn_recv=dma((num_utt,)),
         head_send=dma((num_seq,)),
         head_recv=dma((num_seq,)),
+        query_send=dma((num_seq,)),
+        query_recv=dma((num_seq,)),
         flat_send=dma((num_seq,)),
         flat_recv=dma((num_seq,)),
         row_send=dma((num_seq,)),
@@ -1382,10 +1384,19 @@
 
         def head_copy(dest, slot):
             return remote(
-                s.head_out.at[dest],
-                heads.at[:, block_rows(slot, frames)],
+                s.head_out.at[dest, pl.ds(1, 2)],
+                heads.at[pl.ds(1, 2), block_rows(slot, frames)],
                 s.head_send.at[dest],
                 s.head_recv.at[slot],
+                {"seq": dest},
+            )
+
+        def query_copy(dest, slot):
+            return remote(
+                s.head_out.at[dest, 0],
+                heads.at[0, block_rows(slot, frames)],
+                s.query_send.at[dest],
+                s.query_recv.at[slot],
                 {"seq": dest},
             )
 
@@ -1417,14 +1428,13 @@
                     for part in range(3):
                         heads[part, block_rows(me, frames), :] = s.head_out[dest, part]
 
+        seq_peers(lambda f: query_copy(f, me).start())
         store("qkv_all", "attn_all")
         up_quarters.start()
         peers(lambda b: gout_copy(b, me_utt).start())
         outw_quarters.pass_over()
         seq_peers(lambda f: head_copy(f, f).wait_recv())
         up_quarters.pass_on()
-        store("heads")
-
         def flat_copy(f, slot):
             lanes = pl.ds(pl.multiple_of(slot // num_utt * width, width), width)
             return remote(
@@ -1455,6 +1465,12 @@
 
         for start in range(0, length, Q_BLOCK):
             where = slice(start, start + Q_BLOCK)
+            for f in range(start // frames, (start + Q_BLOCK) // frames):
+
+                @pl.when(f != me)
+                def _(f=f):
+                    query_copy(f, f).wait_recv()
+
             for h in range(groups):
                 lanes = slice(h * HEAD_DIM, (h + 1) * HEAD_DIM)
                 value, lse = attend_head_block(heads.at[0], heads.at[1], heads.at[2], h, where)
@@ -1483,6 +1499,7 @@
             rows_o[group.my_block] = s.attn_low[block_rows(me, frames), :]
 
         group.when_own(keep_rows)
+        store("heads")
 
         up_quarters.pass_over()
 
@@ -1512,6 +1529,7 @@
 
         def sent_seq(f):
             head_copy(f, me).wait_send()
+            query_copy(f, me).wait_send()
             flat_copy(f, me).wait_send()
 
         seq_peers(sent_seq)
@@ -2251,14 +2269,13 @@
                 copy.start()
             for copy in late_loads.values():
                 copy.start()
-            entered()
-
             rows_wide = jnp.concatenate([rows_ref[b] for b in range(num_blocks)], axis=1)
             resid_two = resid_ref[...] + out_bias
             resid_two = resid_two + jnp.dot(rows_wide, outw_ref[...], preferred_element_type=F32)
             s.resid_two[...] = resid_two
             normed, _ = norm_parts(resid_two)
             s.ffn_all[own_rows(me_utt), :] = (normed * ffn_gain + ffn_shift).astype(BF16)
+            entered()
             peers(lambda b: ffn_copy(b, me_utt).start())
             loads[0].wait()
             loads[1].wait()
@@ -2290,12 +2307,17 @@
 
             loop(0, num_utt, ffn_block)
 
+            steps_ready[0] = counts[DOWN]
+            assert PACE["down"] <= lane_blocks[DOWN]
+            down_steps = beside_loop(hidden // column, PACE["down"])
+
             def down_grads(i):
                 cut = block_rows(i, column)
                 s.part_down[cut, :] = inner_dot(hidden_low[:, cut], gout[...]).astype(BF16)
+                mate_copy(DOWN, i).start()
+                down_steps(i)
 
             loop(0, hidden // column, down_grads)
-            announce(DOWN)
 
             up_steps = beside_loop(D // column, PACE["up"])
 
@@ -2815,6 +2837,7 @@
 
 
 PACE = {
+    "down": 1,
     "up": 1,
     "back": 1,
     "before_layer": 2,

time: 317 us -> 313 us (0.987)
  no operation moved by 1% of the time
where the time goes in v7:
time: 313 us
  Pallas kernels  309 us (99%)
  local copies, waits for them, and re-layouts  3.15 us (1%)
    pallas_call x1, Pallas kernels, back_forth(): pl.pallas_call(kernel, out_shape=[jax.ShapeDtypeStruct(shape, BF16) for s...  201 us
    pallas_call x1, Pallas kernels, front_forward(): pl.pallas_call(kernel, out_shape=[shape(num_utt * column, C), shape(num_u...  95.9 us
    pallas_call x1, Pallas kernels, widen(): pl.pallas_call(kernel, grid=(WIDEN_STEPS,), out_shape=[jax.ShapeDtypeStru...  12 us

profile of v7, /device:TPU:0, one launch (start us, length us, event | category | flops | bytes accessed | tf_op | source)
XLA Modules:
  0.0 313.0 jit_solution(3453428174401379455)
XLA Ops:
  0.7 95.9 %shard_map.441 = (bf16[1024,512]{1,0:T(8,128)(2,1)}, bf16[512,1024]{1,0:T(8,128)(2,1)}, f32[4,1,2560]{2,1,0:T(1,128)}, bf16[1024,768]{1,0:T(8,128)(2,1)}, bf16[1...) custom-call(f32[128]{0:T(128)} %refs_0_.1, ...), custom_call_target="tpu_custom_call" | custom-call | tf_op jit(solution)/shard_map/pallas_call | solution.py:1545
  96.6 201.2 %shard_map.442 = (bf16[128,1024]{1,0:T(8,128)(2,1)}, bf16[256,512]{1,0:T(8,128)(2,1)}, bf16[1024,1024]{1,0:T(8,128)(2,1)}, bf16[1024,1024]{1,0:T(8,128)(2,1)}, b...) custom-call(bf16[512,256]{1,0:T(8,128)(2,1)} %get-tuple-element.62.f, ...), custom_call_target="tpu_custom_call" | custom-call | tf_op jit(solution)/shard_map/pallas_call | solution.py:2801
  297.8 0.0 copy-start.2
  297.8 0.0 copy-start.1
  297.9 0.0 copy-start
  297.9 12.0 %shard_map.443 = (f32[4,2048,256]{2,1,0:T(8,128)}, f32[256,1024]{1,0:T(8,128)}, f32[256,3072]{1,0:T(8,128)}, f32[256,512]{1,0:T(8,128)}, f32[128,1024]{1,0:T(8,1...) custom-call(bf16[4,2048,256]{2,1,0:T(8,128)(2,1)} %get-tuple-element.84.refs_0_, ...), custom_call_target="tpu_custom_call" | custom-call | tf_op jit(solution)/shard_map/pallas_call | solution.py:2882
  309.9 0.0 copy-done.2
  309.9 0.6 slice_bitcast_fusion.1
  310.5 0.6 slice_bitcast_fusion
  311.1 0.5 slice_bitcast_fusion.12
  311.6 0.0 copy-done.1
  311.6 0.7 copy.53
  312.3 0.0 copy-done
  312.3 0.7 copy.54
  (1 shorter events, 0.0 us)
Async XLA Ops:
  297.8 12.0 %copy-start.2 = (bf16[64,128]{1,0:T(8,128)(2,1)S(1)}, bf16[64,128]{1,0:T(8,128)(2,1)}, u32[]{:S(2)}) copy-start(bf16[64,128]{1,0:T(8,128)(2,1)} %get-tuple-element.92) | copy-start | bytes 49156
  297.8 13.8 %copy-start.1 = (bf16[128,1024]{1,0:T(8,128)(2,1)S(1)}, bf16[128,1024]{1,0:T(8,128)(2,1)}, u32[]{:S(2)}) copy-start(bf16[128,1024]{1,0:T(8,128)(2,1)} %get-tuple-element.82) | copy-start | bytes 786436
  297.9 14.5 %copy-start = (bf16[256,512]{1,0:T(8,128)(2,1)S(1)}, bf16[256,512]{1,0:T(8,128)(2,1)}, u32[]{:S(2)}) copy-start(bf16[256,512]{1,0:T(8,128)(2,1)} %get-tuple-element.83) | copy-start | bytes 786436

commit v8 on v7

--- a/solution.py
+++ b/solution.py
@@ -1291,8 +1291,8 @@
             proj_hand(b, core).start()
 
         peers(conv_arrived)
+        qkv_quarters.start()
         peers(proj_arrived)
-        qkv_quarters.start()
         peers(lambda b: vec_copy(b, b).wait_recv())
         peers(lambda b: conv_hand(b, 1 - core).wait_recv())
 
@@ -2859,11 +2859,18 @@
 WIDEN_STEPS = 4
 
 
-def widen(taps, arrays):
+def widen(taps, arrays, vectors, sizes):
     arrays = (taps, *arrays)
 
     def kernel(*refs):
-        sources, targets = refs[: len(arrays)], refs[len(arrays) :]
+        sources, vec_ref = refs[: len(arrays)], refs[len(arrays)]
+        targets = refs[len(arrays) + 1 : 2 * len(arrays) + 1]
+        values = vec_ref[...].astype(F32)
+        row = 0
+        for size, target in zip(sizes, refs[2 * len(arrays) + 1 :], strict=True):
+            for j in range(size // 128):
+                target[j * 128 : (j + 1) * 128] = values[row + j]
+            row += size // 128
         for q in range(PACK):
             lanes = slice(q * GW, (q + 1) * GW)
             targets[0][q] = jnp.concatenate(
@@ -2882,11 +2889,12 @@
     return pl.pallas_call(
         kernel,
         grid=(WIDEN_STEPS,),
-        out_shape=[jax.ShapeDtypeStruct(array.shape, F32) for array in arrays],
-        in_specs=specs,
-        out_specs=specs,
+        out_shape=[jax.ShapeDtypeStruct(array.shape, F32) for array in arrays]
+        + [jax.ShapeDtypeStruct((size,), F32) for size in sizes],
+        in_specs=specs + [pl.BlockSpec(vectors.shape, lambda i: (0, 0))],
+        out_specs=specs + [pl.BlockSpec((size,), lambda i: (0,)) for size in sizes],
         compiler_params=pltpu.CompilerParams(vmem_limit_bytes=VMEM_BYTES),
-    )(*arrays)
+    )(*arrays, vectors)
 
 
 def layer_norm(values, gain, shift):
@@ -3150,12 +3158,16 @@
         )
         layer_out = layer_out.reshape(1, frames, D)
         feat_grad = feat_grad.reshape(1, 2 * frames, C)
-        *wide_sums, downweight_sum = widen(
-            taps_sum, (outweight_sum, qkv_sum, conv_sum, proj_sum, up_sum, downweight_sum)
+        small, wide = (C // num_utt,), (column,)
+        sizes = 4 * small + 9 * wide + 2 * wide + (hidden,)
+        wide_sums = widen(
+            taps_sum,
+            (outweight_sum, qkv_sum, conv_sum, proj_sum, up_sum, downweight_sum),
+            vector_sum,
+            sizes,
         )
-        grads = (*wide_sums[:5], vector_sum, wide_sums[5])
-        small, wide = (C // num_utt,), (column,)
-        row_sizes, column_sizes = 4 * small + 9 * wide, 2 * wide + (hidden,)
+        grads = (*wide_sums[:5], None, wide_sums[5])
+        downweight_sum, outs = wide_sums[6], wide_sums[7:]
     else:
         _, pos_pull = jax.vjp(gelu_exact, pos_pre.astype(F32))
         _, attn_pull = jax.vjp(layer_norm, resid_one, attn_gain, attn_shift)
@@ -3258,12 +3270,13 @@
     outweight_grad, qkvweight_grad, convweight_grad, projweight_grad = (
         grad.astype(F32) for grad in grads[1:5]
     )
-    sums = grads[5].reshape(-1).astype(F32)
     upweight_grad = grads[6].astype(F32)
-    outs, start = [], 0
-    for size in tuple(row_sizes) + tuple(column_sizes):
-        outs.append(sums[start : start + size])
-        start = start + size
+    if not fast:
+        sums = grads[5].reshape(-1).astype(F32)
+        outs, start = [], 0
+        for size in tuple(row_sizes) + tuple(column_sizes):
+            outs.append(sums[start : start + size])
+            start = start + size
     (
         convgain_grad,
         convshift_grad,

time: 313 us -> 311 us (level)
  no operation moved by 1% of the time
where the time goes in v8:
time: 311 us
  Pallas kernels  309 us (99%)
    pallas_call x1, Pallas kernels, back_forth(): pl.pallas_call(kernel, out_shape=[jax.ShapeDtypeStruct(shape, BF16) for s...  200 us
    pallas_call x1, Pallas kernels, front_forward(): pl.pallas_call(kernel, out_shape=[shape(num_utt * column, C), shape(num_u...  96.1 us
    pallas_call x1, Pallas kernels, widen(): pl.pallas_call(kernel, grid=(WIDEN_STEPS,), out_shape=[jax.ShapeDtypeStru...  12.1 us

profile of v8, /device:TPU:0, one launch (start us, length us, event | category | flops | bytes accessed | tf_op | source)
XLA Modules:
  0.0 310.8 jit_solution(9722194595514457552)
XLA Ops:
  0.7 96.1 %shard_map.441 = (bf16[1024,512]{1,0:T(8,128)(2,1)}, bf16[512,1024]{1,0:T(8,128)(2,1)}, f32[4,1,2560]{2,1,0:T(1,128)}, bf16[1024,768]{1,0:T(8,128)(2,1)}, bf16[1...) custom-call(f32[128]{0:T(128)} %refs_0_.1, ...), custom_call_target="tpu_custom_call" | custom-call | tf_op jit(solution)/shard_map/pallas_call | solution.py:1545
  96.8 200.4 %shard_map.442 = (bf16[128,1024]{1,0:T(8,128)(2,1)}, bf16[256,512]{1,0:T(8,128)(2,1)}, bf16[1024,1024]{1,0:T(8,128)(2,1)}, bf16[1024,1024]{1,0:T(8,128)(2,1)}, b...) custom-call(bf16[512,256]{1,0:T(8,128)(2,1)} %get-tuple-element.78.f, ...), custom_call_target="tpu_custom_call" | custom-call | tf_op jit(solution)/shard_map/pallas_call | solution.py:2801
  297.2 0.0 copy-start.1
  297.2 0.0 copy-start
  297.2 12.1 %shard_map.443 = (f32[4,2048,256]{2,1,0:T(8,128)}, f32[256,1024]{1,0:T(8,128)}, f32[256,3072]{1,0:T(8,128)}, f32[256,512]{1,0:T(8,128)}, f32[128,1024]{1,0:T(8,1...) custom-call(bf16[4,2048,256]{2,1,0:T(8,128)(2,1)} %get-tuple-element, ...), custom_call_target="tpu_custom_call" | custom-call | tf_op jit(solution)/shard_map/pallas_call | solution.py:2889
  309.3 0.0 copy-done.1
  309.3 0.7 copy.53
  310.0 0.0 copy-done
  310.1 0.7 copy.54
Async XLA Ops:
  297.2 12.1 %copy-start.1 = (bf16[128,1024]{1,0:T(8,128)(2,1)S(1)}, bf16[128,1024]{1,0:T(8,128)(2,1)}, u32[]{:S(2)}) copy-start(bf16[128,1024]{1,0:T(8,128)(2,1)} %get-tuple-element.98) | copy-start | bytes 786436
  297.2 12.8 %copy-start = (bf16[256,512]{1,0:T(8,128)(2,1)S(1)}, bf16[256,512]{1,0:T(8,128)(2,1)}, u32[]{:S(2)}) copy-start(bf16[256,512]{1,0:T(8,128)(2,1)} %get-tuple-element.99) | copy-start | bytes 786436
